TPU v7x, 32 devices: a whole 2x2x4 slice. The times are simulated.
32 devices in a mesh: rows: 16 (over z, y, core), feat: 2 (over x).
Axes of the slice: x: 2, y: 2, z: 4, core: 2. Of those that a mesh axis runs over, the one named last changes fastest.
Arguments:
- logits: float32 [49152, 32], P('rows'), may hold values from -6 to 6
- labels: int32 [49152], P('rows'), may hold values from 0 to 31
- node_ids: int32 [49152], P('rows'), may hold values from 0 to 7
- bin_codes: int32 [49152, 256], P('rows', 'feat'), may hold values from 0 to 63
- split_feature: int32 [8], replicated, may hold values from 0 to 255
- split_bin: int32 [8], replicated, may hold values from 1 to 63
- split_missing: int32 [8], replicated, may hold values from 0 to 1
Outputs:
- new_logits: float32 [49152, 32], P('rows')
- gain_table: float32 [16, 128, 128], P('rows', 'feat')
- leaves: float32 [8, 2, 32], replicated
Inputs may be any that keep to these rules, and one draw needn't show every extreme that they name: `split_missing`: 1 sends the missing code 64 - 1 to the left child, 0 to the right child.
All inputs are finite; a program needn't handle non-finite values.
Results may differ from a plain program's by a relative error of at most 0.0014.
Values sent between devices are 32-bit elements; how exact they have to be, the bound alone decides.
No kernel may reach another device: no remote copies, remote signals or barrier semaphores. Data moves between devices by JAX's collectives and lax.ppermute only.
A program may use at most 64 MiB of HBM per device.

v0:
```python
import math

import jax
import jax.numpy as jnp
from jax import lax
from jax.sharding import PartitionSpec as P

BINS = 64


reg_lambda = 1.0
step_size = 0.3


def split_score(sums, classes):
    grad_part = sums[..., :classes]
    hess_part = sums[..., classes:]
    return jnp.sum(grad_part * grad_part / (hess_part + reg_lambda), axis=-1)


def local(logits, labels, node_ids, bin_codes, split_feature, split_bin, split_missing):
    rows_dev, classes = logits.shape
    feats_dev = bin_codes.shape[1]
    node_count = split_feature.shape[0]
    bin_count = BINS
    per_node = lax.axis_size("rows") // node_count
    pairs_dev = feats_dev // per_node
    feat_pairs = feats_dev // 2
    width = 2 * classes
    expo_vals = jnp.exp(logits)
    soft_prob = expo_vals / jnp.sum(expo_vals, axis=1, keepdims=True)
    class_iota = jnp.arange(classes, dtype=jnp.int32)
    target = (labels[:, None] == class_iota[None, :]).astype(jnp.float32)
    grad_hess = jnp.concatenate(
        [
            (soft_prob - target).astype(jnp.bfloat16),
            (soft_prob * (1.0 - soft_prob)).astype(jnp.bfloat16),
        ],
        axis=1,
    )
    node_iota = jnp.arange(node_count, dtype=jnp.int32)
    node_match = node_ids[:, None] == node_iota[None, :]
    masked_rows = jnp.where(
        node_match[:, :, None], grad_hess[:, None, :], jnp.zeros((), jnp.bfloat16)
    ).reshape(rows_dev, node_count * width)
    bin_iota = jnp.arange(bin_count, dtype=jnp.int32)
    feat_block = math.gcd(feats_dev, 8)
    block_count = feats_dev // feat_block

    def make_hot(codes):
        return (
            (codes[:, :, None] == bin_iota[None, None, :])
            .astype(jnp.bfloat16)
            .reshape(rows_dev, codes.shape[1] * bin_count)
        )

    own_rows = node_count * feat_pairs * width // lax.axis_size("rows")
    groups = lax.axis_size("rows") * own_rows // width
    node_span = groups // feat_pairs

    def block_product(block):
        block_codes = lax.dynamic_slice_in_dim(bin_codes, block * feat_block, feat_block, 1)
        return lax.dot_general(
            masked_rows,
            make_hot(block_codes),
            (((0,), (0,)), ((), ())),
            preferred_element_type=jnp.float32,
        )

    stacked = lax.map(block_product, jnp.arange(block_count, dtype=jnp.int32))
    product = stacked.transpose(1, 0, 2).reshape(node_span * width, feats_dev * bin_count)
    product = product.reshape(node_span, width, feat_pairs, 2 * bin_count).transpose(0, 2, 1, 3)
    owned_hist = lax.psum_scatter(
        product.reshape(lax.axis_size("rows") * own_rows, 2 * bin_count),
        "rows",
        scatter_dimension=0,
        tiled=True,
    )
    owned = (
        owned_hist.reshape(pairs_dev // 2, width, 2, bin_count)
        .transpose(0, 2, 3, 1)
        .reshape(pairs_dev, bin_count, width)
    )
    lower_mask = (
        (bin_iota[:, None] < bin_iota[None, :]) & (bin_iota[:, None] < bin_count - 1)
    ).astype(jnp.float32)
    left_base = jnp.einsum("pbc,bt->ptc", owned, lower_mask, precision=lax.Precision.HIGHEST)
    node_total = jnp.sum(owned, axis=1, keepdims=True)
    missing_sum = owned[:, bin_count - 1 :, :]
    left_miss = left_base + missing_sum
    parent_score = split_score(node_total, classes)
    gain_left = (
        split_score(left_miss, classes)
        + split_score(node_total - left_miss, classes)
        - parent_score
    )
    gain_right = (
        split_score(left_base, classes)
        + split_score(node_total - left_base, classes)
        - parent_score
    )
    gain_rows = (jnp.concatenate([gain_left, gain_right], axis=1) / (2.0 * classes))[None]
    row_feature = jnp.sum(jnp.where(node_match, split_feature[None, :], 0), axis=1)
    row_bin = jnp.sum(jnp.where(node_match, split_bin[None, :], 0), axis=1)
    row_missing = jnp.sum(jnp.where(node_match, split_missing[None, :], 0), axis=1)
    feat_index = lax.axis_index("feat")
    local_col = row_feature - feat_index * feats_dev
    is_owned = (local_col >= 0) & (local_col < feats_dev)
    col_iota = jnp.arange(feats_dev, dtype=jnp.int32)
    row_code = jnp.sum(jnp.where(col_iota[None, :] == local_col[:, None], bin_codes, 0), axis=1)
    goes_left = (row_code < row_bin) | (row_code == bin_count - 1) & (row_missing == 1)
    right_flag = jnp.where(is_owned & jnp.logical_not(goes_left), 1.0, 0.0).astype(jnp.float32)
    side_count = lax.psum(right_flag, "feat")
    row_side = (side_count > 0.5).astype(jnp.int32)
    slot_iota = jnp.arange(2 * node_count, dtype=jnp.int32)
    slot_hot = (node_ids * 2 + row_side)[:, None] == slot_iota[None, :]
    row_index = lax.axis_index("rows")
    my_node = row_index // per_node
    base_feat = feat_index * feats_dev + row_index % per_node * pairs_dev
    local_feat = split_feature[my_node] - base_feat
    holds = ((local_feat >= 0) & (local_feat < pairs_dev)).astype(jnp.float32)
    chosen = owned[jnp.clip(local_feat, 0, pairs_dev - 1)]
    bin_mask = ((bin_iota < split_bin[my_node]) & (bin_iota < bin_count - 1)).astype(jnp.float32)
    left_sum = jnp.sum(chosen * bin_mask[:, None], axis=0) + chosen[bin_count - 1] * split_missing[
        my_node
    ].astype(jnp.float32)
    node_sum = jnp.sum(chosen, axis=0)
    entry = jnp.stack([left_sum, node_sum - left_sum], axis=0) * holds
    placed = jnp.where(
        (node_iota == my_node)[:, None, None], entry[None], jnp.zeros((), jnp.float32)
    )
    side_sums = lax.psum(placed, ("rows", "feat"))
    leaves = -side_sums[..., :classes] / (side_sums[..., classes:] + reg_lambda)
    update = jnp.dot(
        slot_hot.astype(jnp.float32),
        leaves.reshape(2 * node_count, classes),
        precision=lax.Precision.HIGHEST,
    )
    new_logits = logits + step_size * update
    return (new_logits, gain_rows, leaves)


def solution(mesh):
    return jax.shard_map(
        local,
        mesh=mesh,
        in_specs=(P("rows", None), P("rows"), P("rows"), P("rows", "feat"), P(), P(), P()),
        out_specs=(P("rows", None), P("rows", "feat", None), P()),
        check_vma=False,
    )
```

profile of v0, /device:TPU:0, one launch (start us, length us, event | category | flops | bytes accessed | tf_op | source)
XLA Modules:
  0.0 398.5 jit_solution(3833915012682438389)
XLA Ops:
  10.5 86.6 %while.11 = (s32[]{:T(128)}, f32[16,512,512]{1,2,0:T(8,128)}, s32[16]{0:T(128)S(1)}, s32[3072,128]{0,1:T(8,128)S(1)}, bf16[3072,64]{0,1:T(8,128)(2,1)S(1)}, /*in...) while((s32[]{:T(128)}, f32[16,512,512]{1,2,0:T(8,128)}, ...), condition=%wide.region_7.8_spmd.clone, body=%wide.region_6.7_spmd.clone.sunk | while | flops 1613758464 | bytes 11207331 | solution.py:70
  13.1 2.8 fusion.36
  18.5 2.9 fusion.36
  24.0 2.8 fusion.36
  29.4 2.8 fusion.36
  34.7 2.8 fusion.36
  40.1 2.8 fusion.36
  45.6 2.8 fusion.36
  51.0 2.8 fusion.36
  56.4 2.9 fusion.36
  61.8 2.8 fusion.36
  67.2 2.8 fusion.36
  78.0 2.9 fusion.36
  83.5 2.8 fusion.36
  88.8 2.8 fusion.36
  94.2 2.8 fusion.36
  97.1 20.2 %copy.39 = f32[512,16,512]{2,1,0:T(8,128)} copy(f32[512,16,512]{0,2,1:T(8,128)} %bitcast.72) | data formatting | bytes 33554432 | tf_op jit(solution)/shard_map/transpose | solution.py:71
  117.3 17.4 %reshape_reshape.3 = f32[8,64,64,128]{3,2,1,0:T(8,128)} reshape(f32[512,16,512]{2,1,0:T(8,128)} %copy.39) | data formatting | bytes 33554432 | tf_op jit(solution)/shard_map/reshape;reshape | solution.py:72
  134.7 17.7 %copy.40 = f32[8,64,64,128]{3,2,1,0:T(8,128)} copy(f32[8,64,64,128]{3,1,2,0:T(8,128)} %bitcast.70) | data formatting | bytes 33554432 | tf_op jit(solution)/shard_map/transpose | solution.py:72
  158.2 9.6 %psum.14 = f32[3072]{0:T(1024)S(1)} all-reduce(f32[3072]{0:T(1024)S(1)} %and_select_fusion), channel_id=1, replica_groups=mesh['rows'=16,'feat'=2] {'feat'}, use_global_device_ids=true, to_apply=%region_4.5 | all-reduce | flops 3072 | bytes 24576 | tf_op jit(solution)/shard_map/psum | solution.py:113
  169.5 164.3 %reduce-scatter.2.cloned.1.call-done = f32[2048,128]{1,0:T(8,128)} async-done(((f32[32768,128]{1,0:T(8,128)}), f32[2048,128]{1,0:T(8,128)}) %reduce-scatter.2.cloned.1.call-update) | async-done | bytes 1048592 | tf_op jit(solution)/shard_map/reduce_scatter | solution.py:73
  338.8 2.9 copy.43
  345.5 39.2 %psum.15 = f32[8,2,64]{2,1,0:T(2,128)S(1)} all-reduce(f32[8,2,64]{2,1,0:T(2,128)S(1)} %broadcast_select_fusion.1), channel_id=1, replica_groups=mesh['rows'=16,'feat'=2] {'rows','feat'}, use_global_device_ids=true, to_apply=%region_11.12 | all-reduce | flops 1024 | bytes 8192 | tf_op jit(solution)/shard_map/psum | solution.py:132
  384.8 3.5 broadcast_subtract_fusion.1
  (155 shorter events, 54.6 us)
Async XLA Ops:
  7.2 3.1 copy-start.1
  7.2 3.1 copy-start.2
  7.2 3.1 copy-start.4
  7.2 326.6 %reduce-scatter.2.cloned.1.call-start = ((), (), s32[]{:S(2)}) async-start(), calls=%async_computation.1 | async-start | bytes 17825792 | tf_op jit(solution)/shard_map/reduce_scatter | solution.py:73
  152.4 0.7 copy-start.5
  152.4 1.9 copy-start.7
  152.4 2.5 copy-start.6
  152.4 3.9 copy-start
  341.7 3.8 copy-start.8
  341.7 43.1 %copy-start.9 = (pred[64]{0:T(512)(128)(4,1)S(1)}, pred[64]{0:T(512)(128)(4,1)}, u32[]{:S(2)}) copy-start(pred[64]{0:T(512)(128)(4,1)} %iota_compare_fusion.6) | copy-start | bytes 196
  384.8 5.8 %copy-start.3 = (f32[8,2,32]{2,1,0:T(2,128)}, f32[8,2,32]{2,1,0:T(2,128)S(1)}, u32[]{:S(2)}) copy-start(f32[8,2,32]{2,1,0:T(2,128)S(1)} %fusion.23) | copy-start | bytes 6148
Sparse Core Ops, SparseCore 0:
  152.5 181.2 reduce-scatter.1
where the time goes:
time: 400 us; the launch traced here: 399 us
  waiting for transfers between devices  164 us (41%)
  local copies, waits for them, and re-layouts  79.3 us (20%)
  matrix products  49.8 us (12%)
  blocking collectives  48.8 us (12%)
  other arithmetic  29.6 us (7%)
  between operations  15.6 us (4%)
  loops' own time  11 us (3%)
    reduce_scatter x1, waiting for transfers between devices, local(): lax.psum_scatter(product.reshape(lax.axis_size('rows') * own_rows, 2 * bi...  164 us
    dot_general x16, matrix products, block_product(): lax.dot_general(masked_rows, make_hot(block_codes), (((0,), (0,)), ((), (...  45.2 us
    psum x1, blocking collectives, local(): side_sums = lax.psum(placed, ('rows', 'feat'))  39.2 us
    transpose x1, local copies, waits for them, and re-layouts, local(): stacked.transpose(1, 0, 2).reshape(node_span * width, feats_dev * bin_count)  20.2 us
    transpose x1, local copies, waits for them, and re-layouts, local(): product.reshape(node_span, width, feat_pairs, 2 * bin_count)  17.7 us
    another operation x1, local copies, waits for them, and re-layouts, local(): product.reshape(node_span, width, feat_pairs, 2 * bin_count)  17.4 us
    eq x16, other arithmetic, make_hot(): codes[:, :, None] == bin_iota[None, None, :]  14.8 us
    another operation x1, loops' own time, local(): stacked = lax.map(block_product, jnp.arange(block_count, dtype=jnp.int32))  11 us
  transfers between devices with their start and end apart: 1, of which 1 were waited for; matrix products, arithmetic and copies ran while one was open for 1% of the time, Pallas kernels for 0%

commit v1 on v0

v1 whole, which is shorter than its diff:
```python
import functools

import jax
import jax.numpy as jnp
from jax import lax
from jax.experimental import pallas as pl
from jax.experimental.pallas import tpu as pltpu
from jax.sharding import PartitionSpec as P

BINS = 64


reg_lambda = 1.0
step_size = 0.3


def split_score(sums, classes):
    grad_part = sums[..., :classes]
    hess_part = sums[..., classes:]
    return jnp.sum(grad_part * grad_part / (hess_part + reg_lambda), axis=-1)


def three_parts(x):
    first = x.astype(jnp.bfloat16)
    rest = x - first.astype(jnp.float32)
    second = rest.astype(jnp.bfloat16)
    third = (rest - second.astype(jnp.float32)).astype(jnp.bfloat16)
    return first, second, third


def threshold_masks():
    row = lax.broadcasted_iota(jnp.int32, (2 * BINS, 4 * BINS), 0)
    col = lax.broadcasted_iota(jnp.int32, (2 * BINS, 4 * BINS), 1)
    bin_of = row % BINS
    threshold = col % BINS
    first_dir = (col // BINS) % 2 == 0
    below = (bin_of < threshold) & (bin_of < BINS - 1)
    missing = (bin_of == BINS - 1) & first_dir
    same = row // BINS == col // (2 * BINS)
    return jnp.where((below | missing) & same, 1.0, 0.0).astype(jnp.bfloat16)


def add_rows(codes_ref, prob_ref, hist_ref, classes, node_count):
    prob = prob_ref[0, :classes, :]
    label = prob_ref[0, classes : classes + 1, :]
    node = prob_ref[0, classes + 1 : classes + 2, :]
    rows = prob.shape[1]
    class_iota = lax.broadcasted_iota(jnp.int32, (classes, rows), 0).astype(jnp.float32)
    target = jnp.where(class_iota == label, 1.0, 0.0)
    grad_hess = jnp.concatenate([prob - target, prob * (1.0 - prob)], axis=0)
    masked = jnp.concatenate(
        [jnp.where(node == float(n), grad_hess, 0.0).astype(jnp.bfloat16) for n in range(node_count)],
        axis=0,
    )
    bin_iota = lax.broadcasted_iota(jnp.int32, (BINS, rows), 0)
    hot = jnp.concatenate(
        [
            jnp.where(codes_ref[0, f : f + 1, :] == bin_iota, 1.0, 0.0).astype(jnp.bfloat16)
            for f in range(codes_ref.shape[1])
        ],
        axis=0,
    )
    hist_ref[...] += lax.dot_general(
        masked, hot, (((1,), (1,)), ((), ())), preferred_element_type=jnp.float32
    )


def hist_kernel(classes, node_count, codes_ref, prob_ref, hist_ref):
    @pl.when(pl.program_id(0) == 0)
    def _():
        hist_ref[...] = jnp.zeros_like(hist_ref)

    add_rows(codes_ref, prob_ref, hist_ref, classes, node_count)


def gain_kernel(classes, node_count, codes_ref, prob_ref, gain_ref, hist_ref):
    @pl.when(pl.program_id(0) == 0)
    def _():
        hist_ref[...] = jnp.zeros_like(hist_ref)

    add_rows(codes_ref, prob_ref, hist_ref, classes, node_count)

    @pl.when(pl.program_id(0) == pl.num_programs(0) - 1)
    def _():
        masks = threshold_masks()
        ones = jnp.where(
            lax.broadcasted_iota(jnp.int32, (2 * BINS, 4 * BINS), 0) < BINS, 1.0, 0.0
        ).astype(jnp.bfloat16)

        def times(parts, right):
            return sum(jnp.dot(part, right, preferred_element_type=jnp.float32) for part in parts)

        total = times(three_parts(hist_ref[:, : 2 * BINS]), ones)
        for pair in range(gain_ref.shape[1] // 2):
            span = slice(pair * 2 * BINS, (pair + 1) * 2 * BINS)
            left = times(three_parts(hist_ref[:, span]), masks)
            right = total - left
            for n in range(node_count):
                grads = slice(n * 2 * classes, n * 2 * classes + classes)
                hesss = slice(n * 2 * classes + classes, (n + 1) * 2 * classes)
                score = (
                    left[grads] * left[grads] / (left[hesss] + reg_lambda)
                    + right[grads] * right[grads] / (right[hesss] + reg_lambda)
                )
                parent = total[grads] * total[grads] / (total[hesss] + reg_lambda)
                gain = (
                    jnp.sum(score, axis=0, keepdims=True) - jnp.sum(parent, axis=0, keepdims=True)
                ) / (2.0 * classes)
                gain_ref[n, 2 * pair : 2 * pair + 1, :] = gain[:, : 2 * BINS]
                gain_ref[n, 2 * pair + 1 : 2 * pair + 2, :] = gain[:, 2 * BINS :]


def local(logits, labels, node_ids, bin_codes, split_feature, split_bin, split_missing):
    rows_dev, classes = logits.shape
    feats_dev = bin_codes.shape[1]
    node_count = split_feature.shape[0]
    n_rows = lax.axis_size("rows")
    per_node = n_rows // node_count
    pairs_dev = feats_dev // per_node
    width = 2 * classes
    feats_own = max(8, feats_dev // n_rows)
    group = feats_dev // feats_own
    group_count = n_rows // group
    row_index = lax.axis_index("rows")
    feat_index = lax.axis_index("feat")

    expo_vals = jnp.exp(logits.T)
    soft_prob = expo_vals / jnp.sum(expo_vals, axis=0, keepdims=True)
    row_info = jnp.concatenate(
        [
            soft_prob,
            labels[None, :].astype(jnp.float32),
            node_ids[None, :].astype(jnp.float32),
        ],
        axis=0,
    )
    if group_count == 1:
        order = (per_node, node_count, feats_own, rows_dev)
        codes_out = bin_codes.T.reshape(order).transpose(1, 0, 2, 3).reshape(group, feats_own, rows_dev)
        members = None
    else:
        codes_out = bin_codes.T.reshape(group, feats_own, rows_dev)
        members = [[g * group + r for r in range(group)] for g in range(group_count)]
    codes_in = lax.all_to_all(codes_out, "rows", 0, 0, tiled=True, axis_index_groups=members)
    info_in = lax.all_gather(row_info, "rows", axis=0, axis_index_groups=members)

    node_iota = jnp.arange(node_count, dtype=jnp.int32)
    node_match = node_ids[:, None] == node_iota[None, :]
    row_feature = jnp.sum(jnp.where(node_match, split_feature[None, :], 0), axis=1)
    row_bin = jnp.sum(jnp.where(node_match, split_bin[None, :], 0), axis=1)
    row_missing = jnp.sum(jnp.where(node_match, split_missing[None, :], 0), axis=1)
    local_col = row_feature - feat_index * feats_dev
    is_owned = (local_col >= 0) & (local_col < feats_dev)
    col_iota = jnp.arange(feats_dev, dtype=jnp.int32)
    row_code = jnp.sum(jnp.where(col_iota[None, :] == local_col[:, None], bin_codes, 0), axis=1)
    goes_left = (row_code < row_bin) | (row_code == BINS - 1) & (row_missing == 1)
    right_flag = jnp.where(is_owned & jnp.logical_not(goes_left), 1.0, 0.0).astype(jnp.float32)
    side_count = lax.psum(right_flag, "feat")
    row_side = (side_count > 0.5).astype(jnp.int32)
    slot_iota = jnp.arange(2 * node_count, dtype=jnp.int32)
    own_slot = node_ids * 2 + jnp.logical_not(goes_left).astype(jnp.int32)
    own_hot = ((own_slot[None, :] == slot_iota[:, None]) & is_owned[None, :]).astype(jnp.bfloat16)
    target = (labels[None, :] == jnp.arange(classes, dtype=jnp.int32)[:, None]).astype(jnp.float32)
    grad_hess = jnp.concatenate(
        [
            (soft_prob - target).astype(jnp.bfloat16),
            (soft_prob * (1.0 - soft_prob)).astype(jnp.bfloat16),
        ],
        axis=0,
    )
    own_sums = lax.dot_general(
        own_hot, grad_hess, (((1,), (1,)), ((), ())), preferred_element_type=jnp.float32
    )
    side_sums = lax.psum(own_sums, ("rows", "feat")).reshape(node_count, 2, width)
    leaves = -side_sums[..., :classes] / (side_sums[..., classes:] + reg_lambda)
    slot_hot = (node_ids * 2 + row_side)[:, None] == slot_iota[None, :]
    update = jnp.dot(
        slot_hot.astype(jnp.float32),
        leaves.reshape(2 * node_count, classes),
        precision=lax.Precision.HIGHEST,
    )
    new_logits = logits + step_size * update

    info_rows = row_info.shape[0]
    in_specs = [
        pl.BlockSpec((1, feats_own, rows_dev), lambda s: (s, 0, 0)),
        pl.BlockSpec((1, info_rows, rows_dev), lambda s: (s, 0, 0)),
    ]
    hist_shape = (node_count * width, feats_own * BINS)
    cost = pl.CostEstimate(
        flops=2 * hist_shape[0] * hist_shape[1] * group * rows_dev,
        bytes_accessed=4 * group * rows_dev * (feats_own + info_rows),
        transcendentals=0,
    )
    params = pltpu.CompilerParams(vmem_limit_bytes=48 * 1024 * 1024)
    if group_count == 1:
        gains = pl.pallas_call(
            functools.partial(gain_kernel, classes, node_count),
            grid=(group,),
            in_specs=in_specs,
            out_specs=pl.BlockSpec((node_count, feats_own, 2 * BINS), lambda s: (0, 0, 0)),
            out_shape=jax.ShapeDtypeStruct((node_count, feats_own, 2 * BINS), jnp.float32),
            scratch_shapes=[pltpu.VMEM(hist_shape, jnp.float32)],
            compiler_params=params,
            cost_estimate=cost,
        )(codes_in, info_in)
        halves = [[h + n * per_node for n in range(node_count)] for h in range(per_node)]
        gain_rows = lax.all_to_all(gains, "rows", 0, 0, tiled=True, axis_index_groups=halves)
        return (new_logits, gain_rows.reshape(1, pairs_dev, 2 * BINS), leaves)

    hist = pl.pallas_call(
        functools.partial(hist_kernel, classes, node_count),
        grid=(group,),
        in_specs=in_specs,
        out_specs=pl.BlockSpec(hist_shape, lambda s: (0, 0)),
        out_shape=jax.ShapeDtypeStruct(hist_shape, jnp.float32),
        compiler_params=params,
        cost_estimate=cost,
    )(codes_in, info_in)
    cuts = feats_own // pairs_dev
    hist = hist.reshape(node_count, width, cuts, pairs_dev, BINS).transpose(0, 2, 3, 4, 1)
    peers = [[g * group + r for g in range(group_count)] for r in range(group)]
    owned = lax.psum_scatter(
        hist.reshape(group_count, pairs_dev, BINS, width),
        "rows",
        scatter_dimension=0,
        axis_index_groups=peers,
    )
    bin_iota = jnp.arange(BINS, dtype=jnp.int32)
    lower_mask = (
        (bin_iota[:, None] < bin_iota[None, :]) & (bin_iota[:, None] < BINS - 1)
    ).astype(jnp.float32)
    left_base = jnp.einsum("pbc,bt->ptc", owned, lower_mask, precision=lax.Precision.HIGHEST)
    node_total = jnp.sum(owned, axis=1, keepdims=True)
    left_miss = left_base + owned[:, BINS - 1 :, :]
    parent_score = split_score(node_total, classes)
    gain_left = (
        split_score(left_miss, classes)
        + split_score(node_total - left_miss, classes)
        - parent_score
    )
    gain_right = (
        split_score(left_base, classes)
        + split_score(node_total - left_base, classes)
        - parent_score
    )
    gain = jnp.concatenate([gain_left, gain_right], axis=1) / (2.0 * classes)
    moves = [
        (n * per_node + cut * group + r, n * per_node + r * cuts + cut)
        for n in range(node_count)
        for cut in range(cuts)
        for r in range(group)
    ]
    gain_rows = lax.ppermute(gain, "rows", moves)
    return (new_logits, gain_rows[None], leaves)


def solution(mesh):
    return jax.shard_map(
        local,
        mesh=mesh,
        in_specs=(P("rows", None), P("rows"), P("rows"), P("rows", "feat"), P(), P(), P()),
        out_specs=(P("rows", None), P("rows", "feat", None), P()),
        check_vma=False,
    )
```

time: 400 us -> 175 us (0.44)
  waiting for transfers between devices: 164 us -> 18.2 us
  local copies, waits for them, and re-layouts: 79.3 us -> 2.45 us
  matrix products: 49.8 us -> 1.32 us
  blocking collectives: 48.8 us -> 86.9 us
  Pallas kernels: 0 us -> 32.7 us
  other arithmetic: 29.6 us -> 9.08 us
  loops' own time: 11 us -> 0 us
  starting transfers between devices: 0.04 us -> 9.39 us
    reduce_scatter x1 -> x0, waiting for transfers between devices: 164 us -> none  [local(): lax.psum_scatter(product.reshape(lax.axis_size('rows') * own_rows, 2 * bi...]
    dot_general x16 -> x1, matrix products: 45.2 us -> 0.21 us  [local(): lax.dot_general(own_hot, grad_hess, (((1,), (1,)), ((), ())), preferred_e...]
    transpose x3 -> x1, local copies, waits for them, and re-layouts: 40.4 us -> 1.34 us  [local(): bin_codes.T.reshape(order).transpose(1, 0, 2, 3)]
    psum x1, blocking collectives: 39.2 us -> 77.3 us  [local(): lax.psum(own_sums, ('rows', 'feat')).reshape(node_count, 2, width)]
    pallas_call x0 -> x1, Pallas kernels: none -> 32.7 us  [local(): pl.pallas_call(functools.partial(gain_kernel, classes, node_count), grid=...]
    another operation x1 -> x0, local copies, waits for them, and re-layouts: 17.4 us -> none  [local(): product.reshape(node_span, width, feat_pairs, 2 * bin_count)]
    eq x18 -> x0, other arithmetic: 15.4 us -> none  [the longest x16 14.8 us: make_hot(): codes[:, :, None] == bin_iota[None, None, :]]
    all_gather x0 -> x1, waiting for transfers between devices: none -> 12.7 us  [local(): lax.all_gather(row_info, 'rows', axis=0, axis_index_groups=members)]
  transfers between devices with their start and end apart: 1 -> 3, of which waited for: 1 -> 2; matrix products, arithmetic and copies ran while one was open for 1% -> 2% of each run, Pallas kernels for 0% -> 0%
where the time goes in v1:
time: 175 us; the launch traced here: 174 us
  blocking collectives  86.9 us (50%)
  Pallas kernels  32.7 us (19%)
  waiting for transfers between devices  18.2 us (10%)
  between operations  14.2 us (8%)
  starting transfers between devices  9.39 us (5%)
  other arithmetic  9.08 us (5%)
  local copies, waits for them, and re-layouts  2.45 us (1%)
    psum x1, blocking collectives, local(): lax.psum(own_sums, ('rows', 'feat')).reshape(node_count, 2, width)  77.3 us
    pallas_call x1, Pallas kernels, local(): pl.pallas_call(functools.partial(gain_kernel, classes, node_count), grid=...  32.7 us
    all_gather x1, waiting for transfers between devices, local(): lax.all_gather(row_info, 'rows', axis=0, axis_index_groups=members)  12.7 us
    psum x1, blocking collectives, local(): side_count = lax.psum(right_flag, 'feat')  9.59 us
    all_to_all x1, starting transfers between devices, local(): lax.all_to_all(codes_out, 'rows', 0, 0, tiled=True, axis_index_groups=mem...  6.01 us
    all_to_all x1, waiting for transfers between devices, local(): lax.all_to_all(gains, 'rows', 0, 0, tiled=True, axis_index_groups=halves)  5.5 us
  transfers between devices with their start and end apart: 3, of which 2 were waited for; matrix products, arithmetic and copies ran while one was open for 2% of the time, Pallas kernels for 0%

profile of v1, /device:TPU:0, one launch (start us, length us, event | category | flops | bytes accessed | tf_op | source)
XLA Modules:
  0.0 174.2 jit_solution(10433455661050602953)
XLA Ops:
  7.2 0.0 all-gather.4.cloned.1.call-start
  7.2 0.0 copy-start.3
  7.2 1.1 exponential_reduce_fusion
  8.3 0.7 convert_element_type.34
  9.0 1.8 %subtract_convert_fusion = (bf16[32,3072]{1,0:T(8,128)(2,1)}, f32[32,3072]{1,0:T(8,128)S(1)}) fusion(s32[3072]{0:T(1024)} %param.8, f32[3072]{0:T(1024)S(1)} %exponential_reduce_fusion, f32[3072,32]{0,1:T(8,128)} %param.7), kind=kLoop, calls=%fused_computation.11 | loop fusion | flops 491520 | bytes 1007616 | tf_op jit(solution)/shard_map/convert_element_type | solution.py:166
  10.8 0.9 select_reduce_fusion.2
  11.7 3.1 %select_reduce_fusion = s32[3072]{0:T(1024)S(1)} fusion(s32[3072,128]{1,0:T(8,128)} %param.10, s32[3072]{0:T(1024)S(1)} %broadcast_subtract_fusion), kind=kLoop, calls=%fused_computation.2 | loop fusion | flops 1176576 | bytes 1597440 | tf_op jit(solution)/shard_map/reduce_sum | solution.py:155
  14.8 9.6 %psum.14 = f32[3072]{0:T(1024)S(1)} all-reduce(f32[3072]{0:T(1024)S(1)} %get-tuple-element.6), channel_id=1, replica_groups=mesh['rows'=16,'feat'=2] {'feat'}, use_global_device_ids=true, to_apply=%region_4.5 | all-reduce | flops 3072 | bytes 24576 | tf_op jit(solution)/shard_map/psum | solution.py:158
  24.4 0.6 fusion.13
  25.0 0.8 maximum_bitcast_fusion
  25.8 0.0 all-gather.4.cloned.1.call-update
  25.9 0.5 copy.17
  26.3 1.3 copy.18
  27.7 6.0 %all-to-all-start = ((s32[16,8,3072]{2,1,0:T(8,128)}), s32[16,8,3072]{2,1,0:T(8,128)S(1)}, u32[]{:S(2)}, u32[]{:S(2)}) async-start(s32[16,8,3072]{2,1,0:T(8,128)} %bitcast.6), calls=%async_computation | async-start | bytes 3145728 | tf_op jit(solution)/shard_map/all_to_all | solution.py:144
  33.8 0.2 fusion.2
  34.0 77.3 %psum.15 = f32[8,2,64]{2,1,0:T(2,128)S(1)} all-reduce(f32[8,2,64]{2,1,0:T(2,128)S(1)} %bitcast.22), channel_id=1, replica_groups=mesh['rows'=16,'feat'=2] {'rows','feat'}, use_global_device_ids=true, to_apply=%region_6.7 | all-reduce | flops 1024 | bytes 8192 | tf_op jit(solution)/shard_map/psum | solution.py:174
  111.2 0.1 fusion.11
  111.3 0.0 copy-start.4
  111.4 12.7 %all-gather.4.cloned.1.call-done.prob_ref = f32[16,34,3072]{2,1,0:T(8,128)} async-done(((f32[1,34,3072]{2,1,0:T(8,128)}), f32[16,34,3072]{2,1,0:T(8,128)}) %all-gather.4.cloned.1.call-update) | async-done | bytes 6684688 | tf_op jit(solution)/shard_map/all_gather | solution.py:145
  124.1 32.7 %shard_map.94 = f32[8,8,128]{2,1,0:T(8,128)} custom-call(s32[16,8,3072]{2,1,0:T(8,128)S(1)} %all-to-all-done.codes_ref, f32[16,34,3072]{2,1,0:T(8,128)} %all-gather.4.cloned.1.call-done.prob_ref), custom_call_target="tpu_custom_call" | custom-call | flops 25769803776 | bytes 8257536 | tf_op jit(solution)/shard_map/pallas_call | solution.py:197
  156.8 3.3 %all-to-all-start.1 = ((f32[8,8,128]{2,1,0:T(8,128)}), f32[8,8,128]{2,1,0:T(8,128)S(1)}, u32[]{:S(2)}, u32[]{:S(2)}) async-start(f32[8,8,128]{2,1,0:T(8,128)} %shard_map.94), calls=%async_computation.1 | async-start | bytes 65536 | tf_op jit(solution)/shard_map/all_to_all | solution.py:208
  160.2 1.1 fusion
  161.3 5.5 %all-to-all-done.1 = f32[8,8,128]{2,1,0:T(8,128)S(1)} async-done(((f32[8,8,128]{2,1,0:T(8,128)}), f32[8,8,128]{2,1,0:T(8,128)S(1)}, u32[]{:S(2)}, u32[]{:S(2)}) %all-to-all-start.1) | async-done | bytes 32800 | tf_op jit(solution)/shard_map/all_to_all | solution.py:208
  166.8 0.6 copy.20
  (14 shorter events, 0.1 us)
Async XLA Ops:
  7.2 116.9 %all-gather.4.cloned.1.call-start = ((), (), s32[]{:S(2)}) async-start(), calls=%async_computation.2 | async-start | bytes 8355840 | tf_op jit(solution)/shard_map/all_gather | solution.py:145
  7.2 17.2 %copy-start.3 = (s32[3072]{0:T(1024)S(1)}, s32[3072]{0:T(1024)}, u32[]{:S(2)}) copy-start(s32[3072]{0:T(1024)} %param.9) | copy-start | bytes 36868
  11.7 14.2 %copy-start = (s32[3072,128]{1,0:T(8,128)S(1)}, s32[3072,128]{1,0:T(8,128)}, u32[]{:S(2)}) copy-start(s32[3072,128]{1,0:T(8,128)} %param.10) | copy-start | bytes 4718596
  27.7 6.1 %copy-start.2 = (bf16[32,3072]{1,0:T(8,128)(2,1)S(1)}, bf16[32,3072]{1,0:T(8,128)(2,1)}, u32[]{:S(2)}) copy-start(bf16[32,3072]{1,0:T(8,128)(2,1)} %get-tuple-element.9) | copy-start | bytes 589828
  27.7 6.1 %copy-start.5 = (s32[3072]{0:T(1024)S(1)}, s32[3072]{0:T(1024)}, u32[]{:S(2)}) copy-start(s32[3072]{0:T(1024)} %get-tuple-element.13) | copy-start | bytes 36868
  27.7 83.7 %all-to-all-start = ((s32[16,8,3072]{2,1,0:T(8,128)}), s32[16,8,3072]{2,1,0:T(8,128)S(1)}, u32[]{:S(2)}, u32[]{:S(2)}) async-start(s32[16,8,3072]{2,1,0:T(8,128)} %bitcast.6), calls=%async_computation | async-start | bytes 3145728 | tf_op jit(solution)/shard_map/all_to_all | solution.py:144
  111.3 48.8 %copy-start.4 = (f32[8,2,32]{2,1,0:T(2,128)}, f32[8,2,32]{2,1,0:T(2,128)S(1)}, u32[]{:S(2)}) copy-start(f32[8,2,32]{2,1,0:T(2,128)S(1)} %fusion.11) | copy-start | bytes 6148
  111.3 48.8 %copy-start.1 = (f32[3072,32]{0,1:T(8,128)S(1)}, f32[3072,32]{0,1:T(8,128)}, u32[]{:S(2)}) copy-start(f32[3072,32]{0,1:T(8,128)} %param.7) | copy-start | bytes 1179652
  156.8 10.0 %all-to-all-start.1 = ((f32[8,8,128]{2,1,0:T(8,128)}), f32[8,8,128]{2,1,0:T(8,128)S(1)}, u32[]{:S(2)}, u32[]{:S(2)}) async-start(f32[8,8,128]{2,1,0:T(8,128)} %shard_map.94), calls=%async_computation.1 | async-start | bytes 65536 | tf_op jit(solution)/shard_map/all_to_all | solution.py:208
Sparse Core Ops, SparseCore 0:
  26.0 98.0 all-gather.3

commit v2 on v1

v2 whole, which is shorter than its diff:
```python
import functools

import jax
import jax.numpy as jnp
from jax import lax
from jax.experimental import pallas as pl
from jax.experimental.pallas import tpu as pltpu
from jax.sharding import PartitionSpec as P

BINS = 64
LANES = 128


reg_lambda = 1.0
step_size = 0.3


def split_score(sums, classes):
    grad_part = sums[..., :classes]
    hess_part = sums[..., classes:]
    return jnp.sum(grad_part * grad_part / (hess_part + reg_lambda), axis=-1)


def three_parts(x):
    first = x.astype(jnp.bfloat16)
    rest = x - first.astype(jnp.float32)
    second = rest.astype(jnp.bfloat16)
    third = (rest - second.astype(jnp.float32)).astype(jnp.bfloat16)
    return first, second, third


def threshold_masks():
    row = lax.broadcasted_iota(jnp.int32, (2 * BINS, 4 * BINS), 0)
    col = lax.broadcasted_iota(jnp.int32, (2 * BINS, 4 * BINS), 1)
    bin_of = row % BINS
    threshold = col % BINS
    first_dir = (col // BINS) % 2 == 0
    below = (bin_of < threshold) & (bin_of < BINS - 1)
    missing = (bin_of == BINS - 1) & first_dir
    same = row // BINS == col // (2 * BINS)
    return jnp.where((below | missing) & same, 1.0, 0.0).astype(jnp.bfloat16)


def info_kernel(logits_ref, labels_ref, nodes_ref, info_ref):
    rows, classes = logits_ref.shape
    expo_vals = jnp.exp(logits_ref[...].T)
    info_ref[:, :rows] = expo_vals / jnp.sum(expo_vals, axis=0, keepdims=True)
    chunks = rows // LANES
    info_ref[:, rows:] = jnp.zeros((classes, 2 * LANES), jnp.float32)
    info_ref[:chunks, rows : rows + LANES] = labels_ref[...].astype(jnp.float32)
    info_ref[:chunks, rows + LANES :] = nodes_ref[...].astype(jnp.float32)


def read_info(info, rows):
    chunks = rows // LANES
    prob = info[:, :rows]
    labels = info[:, rows : rows + LANES]
    nodes = info[:, rows + LANES : rows + 2 * LANES]
    label = jnp.concatenate([labels[i : i + 1] for i in range(chunks)], axis=1)
    node = jnp.concatenate([nodes[i : i + 1] for i in range(chunks)], axis=1)
    return prob, label, node


def codes_kernel(group, own, starts_ref, codes_ref, *refs):
    outs, turned = refs[:-1], refs[-1]
    turned[...] = codes_ref[...].T
    for m in range(group):
        start = pl.multiple_of(starts_ref[m], own)
        outs[m][...] = turned[pl.ds(start, own), :]


def side_kernel(node_count, split_ref, info_ref, codes_ref, flag_ref, sums_ref, turned):
    rows, feats = codes_ref.shape
    prob, label, node = read_info(info_ref[...], rows)
    turned[...] = codes_ref[...].T
    side = jnp.zeros((1, rows), jnp.float32)
    for n in range(node_count):
        col = split_ref[0, n]
        held = (col >= 0) & (col < feats)
        code = turned[pl.ds(jnp.clip(col, 0, feats - 1), 1), :]
        threshold = jnp.where(held, split_ref[1, n], -1)
        last = jnp.where(held & (split_ref[2, n] == 1), BINS - 1, -1)
        left = (code < threshold) | (code == last)
        value = jnp.where(left, 1.0, jnp.where(held, 2.0, 0.0))
        side = jnp.where(node == float(n), value, side)
    flag_ref[...] = jnp.where(side == 2.0, 1.0, 0.0)
    grad_hess = gradients(prob, label)
    hot = jnp.concatenate(
        [
            jnp.where((node == float(slot // 2)) & (side == float(slot % 2 + 1)), 1.0, 0.0)
            for slot in range(2 * node_count)
        ],
        axis=0,
    ).astype(jnp.bfloat16)
    sums_ref[...] = lax.dot_general(
        hot,
        grad_hess.astype(jnp.bfloat16),
        (((1,), (1,)), ((), ())),
        preferred_element_type=jnp.float32,
    )


def gradients(prob, label):
    class_iota = lax.broadcasted_iota(jnp.int32, prob.shape, 0).astype(jnp.float32)
    target = jnp.where(class_iota == label, 1.0, 0.0)
    return jnp.concatenate([prob - target, prob * (1.0 - prob)], axis=0)


def add_rows(codes, info, hist_ref, node_count):
    feats, rows = codes.shape
    prob, label, node = read_info(info, rows)
    grad_hess = gradients(prob, label)
    masked = jnp.concatenate(
        [jnp.where(node == float(n), grad_hess, 0.0).astype(jnp.bfloat16) for n in range(node_count)],
        axis=0,
    )
    bin_iota = lax.broadcasted_iota(jnp.int32, (BINS, rows), 0)
    hot = jnp.concatenate(
        [
            jnp.where(codes[f : f + 1, :] == bin_iota, 1.0, 0.0).astype(jnp.bfloat16)
            for f in range(feats)
        ],
        axis=0,
    )
    hist_ref[...] += lax.dot_general(
        masked, hot, (((1,), (1,)), ((), ())), preferred_element_type=jnp.float32
    )


def write_gains(hist_ref, gain_ref, classes, node_count):
    masks = threshold_masks()
    ones = jnp.where(
        lax.broadcasted_iota(jnp.int32, (2 * BINS, 4 * BINS), 0) < BINS, 1.0, 0.0
    ).astype(jnp.bfloat16)

    def times(parts, right):
        return sum(jnp.dot(part, right, preferred_element_type=jnp.float32) for part in parts)

    total = times(three_parts(hist_ref[:, : 2 * BINS]), ones)
    for pair in range(gain_ref.shape[1] // 2):
        span = slice(pair * 2 * BINS, (pair + 1) * 2 * BINS)
        left = times(three_parts(hist_ref[:, span]), masks)
        right = total - left
        for n in range(node_count):
            grads = slice(n * 2 * classes, n * 2 * classes + classes)
            hesss = slice(n * 2 * classes + classes, (n + 1) * 2 * classes)
            score = (
                left[grads] * left[grads] / (left[hesss] + reg_lambda)
                + right[grads] * right[grads] / (right[hesss] + reg_lambda)
            )
            parent = total[grads] * total[grads] / (total[hesss] + reg_lambda)
            gain = (
                jnp.sum(score, axis=0, keepdims=True) - jnp.sum(parent, axis=0, keepdims=True)
            ) / (2.0 * classes)
            gain_ref[n, 2 * pair : 2 * pair + 1, :] = gain[:, : 2 * BINS]
            gain_ref[n, 2 * pair + 1 : 2 * pair + 2, :] = gain[:, 2 * BINS :]


def hist_kernel(classes, node_count, sources, first, gains, *refs):
    codes_refs, info_refs = refs[:sources], refs[sources : 2 * sources]
    rest = refs[2 * sources :]
    hist_in = None
    if not first:
        hist_in, rest = rest[0], rest[1:]
    out_ref, codes_buf, info_buf, code_sems, info_sems = rest[:5]
    hist_ref = rest[5] if gains else out_ref
    for s in range(sources):
        pltpu.make_async_copy(codes_refs[s], codes_buf.at[s], code_sems.at[s]).start()
        pltpu.make_async_copy(info_refs[s], info_buf.at[s], info_sems.at[s]).start()
    hist_ref[...] = jnp.zeros_like(hist_ref) if first else hist_in[...]

    @pl.loop(0, sources)
    def _(s):
        pltpu.make_async_copy(codes_buf.at[s], codes_buf.at[s], code_sems.at[s]).wait()
        pltpu.make_async_copy(info_buf.at[s], info_buf.at[s], info_sems.at[s]).wait()
        add_rows(codes_buf[s], info_buf[s], hist_ref, node_count)

    if gains:
        write_gains(hist_ref, out_ref, classes, node_count)


def add_sources(classes, node_count, codes, infos, hist, gains):
    sources = len(codes)
    own, rows = codes[0].shape
    info_shape = infos[0].shape
    hist_shape = (2 * classes * node_count, own * BINS)
    anywhere = pl.BlockSpec(memory_space=pl.ANY)
    whole = pl.BlockSpec(memory_space=pltpu.VMEM)
    out_shape = (node_count, own, 2 * BINS) if gains else hist_shape
    scratch = [
        pltpu.VMEM((sources, own, rows), jnp.int32),
        pltpu.VMEM((sources,) + info_shape, jnp.float32),
        pltpu.SemaphoreType.DMA((sources,)),
        pltpu.SemaphoreType.DMA((sources,)),
    ]
    if gains:
        scratch.append(pltpu.VMEM(hist_shape, jnp.float32))
    held = [] if hist is None else [hist]
    return pl.pallas_call(
        functools.partial(hist_kernel, classes, node_count, sources, hist is None, gains),
        in_specs=[anywhere] * (2 * sources) + [whole] * len(held),
        out_specs=whole,
        out_shape=jax.ShapeDtypeStruct(out_shape, jnp.float32),
        scratch_shapes=scratch,
        compiler_params=pltpu.CompilerParams(vmem_limit_bytes=48 * 1024 * 1024),
        cost_estimate=pl.CostEstimate(
            flops=2 * hist_shape[0] * hist_shape[1] * sources * rows,
            bytes_accessed=4 * sources * rows * (own + classes) + 8 * hist_shape[0] * hist_shape[1],
            transcendentals=0,
        ),
    )(*codes, *infos, *held)


def swap(x, axis, bit):
    size = lax.axis_size(axis)
    return lax.ppermute(x, axis, [(i, i ^ bit) for i in range(size)])


def sum_over(x, axis):
    bit = 1
    while bit < lax.axis_size(axis):
        x = x + swap(x, axis, bit)
        bit *= 2
    return x


def local(logits, labels, node_ids, bin_codes, split_feature, split_bin, split_missing):
    rows_dev, classes = logits.shape
    feats_dev = bin_codes.shape[1]
    node_count = split_feature.shape[0]
    n_rows = lax.axis_size("rows")
    per_node = n_rows // node_count
    pairs_dev = feats_dev // per_node
    width = 2 * classes
    feats_own = max(8, feats_dev // n_rows)
    group = feats_dev // feats_own
    group_count = n_rows // group
    row_index = lax.axis_index("rows")
    feat_index = lax.axis_index("feat")
    whole = pl.BlockSpec(memory_space=pltpu.VMEM)
    scalars = pl.BlockSpec(memory_space=pltpu.SMEM)
    params = pltpu.CompilerParams(vmem_limit_bytes=48 * 1024 * 1024)

    info = pl.pallas_call(
        info_kernel,
        in_specs=[whole] * 3,
        out_specs=whole,
        out_shape=jax.ShapeDtypeStruct((classes, rows_dev + 2 * LANES), jnp.float32),
        compiler_params=params,
    )(logits, labels.reshape(-1, LANES), node_ids.reshape(-1, LANES))

    taker = row_index ^ jnp.arange(group, dtype=jnp.int32)
    if group_count == 1:
        starts = (taker % per_node) * pairs_dev + (taker // per_node) * feats_own
    else:
        starts = (taker % group) * feats_own
    codes_out = pl.pallas_call(
        functools.partial(codes_kernel, group, feats_own),
        in_specs=[scalars, whole],
        out_specs=[whole] * group,
        out_shape=[jax.ShapeDtypeStruct((feats_own, rows_dev), jnp.int32)] * group,
        scratch_shapes=[pltpu.VMEM((feats_dev, rows_dev), jnp.int32)],
        compiler_params=params,
    )(starts, bin_codes)

    infos = [info] + [None] * (group - 1)
    for m in sorted(range(1, group), key=lambda m: -(m & -m)):
        low = m & -m
        infos[m] = swap(infos[m ^ low], "rows", low)
    codes_in = [codes_out[0]] + [swap(codes_out[m], "rows", m) for m in range(1, group)]

    splits = jnp.stack([split_feature - feat_index * feats_dev, split_bin, split_missing])
    right_flag, own_sums = pl.pallas_call(
        functools.partial(side_kernel, node_count),
        in_specs=[scalars, whole, whole],
        out_specs=[whole, whole],
        out_shape=[
            jax.ShapeDtypeStruct((1, rows_dev), jnp.float32),
            jax.ShapeDtypeStruct((2 * node_count, width), jnp.float32),
        ],
        scratch_shapes=[pltpu.VMEM((feats_dev, rows_dev), jnp.int32)],
        compiler_params=params,
    )(splits, info, bin_codes)
    side_count = sum_over(right_flag, "feat")[0]
    side_sums = sum_over(sum_over(own_sums, "rows"), "feat").reshape(node_count, 2, width)
    leaves = -side_sums[..., :classes] / (side_sums[..., classes:] + reg_lambda)
    row_side = (side_count > 0.5).astype(jnp.int32)
    slot_iota = jnp.arange(2 * node_count, dtype=jnp.int32)
    slot_hot = (node_ids * 2 + row_side)[:, None] == slot_iota[None, :]
    update = jnp.dot(
        slot_hot.astype(jnp.float32),
        leaves.reshape(2 * node_count, classes),
        precision=lax.Precision.HIGHEST,
    )
    new_logits = logits + step_size * update

    batch = 4
    hist = None
    for low in range(0, group, batch):
        span = slice(low, low + batch)
        gains = group_count == 1 and low + batch >= group
        hist = add_sources(classes, node_count, codes_in[span], infos[span], hist, gains)
    if group_count == 1:
        halves = [[h + n * per_node for n in range(node_count)] for h in range(per_node)]
        gain_rows = lax.all_to_all(hist, "rows", 0, 0, tiled=True, axis_index_groups=halves)
        return (new_logits, gain_rows.reshape(1, pairs_dev, 2 * BINS), leaves)

    cuts = feats_own // pairs_dev
    hist = hist.reshape(node_count, width, cuts, pairs_dev, BINS).transpose(0, 2, 3, 4, 1)
    peers = [[g * group + r for g in range(group_count)] for r in range(group)]
    owned = lax.psum_scatter(
        hist.reshape(group_count, pairs_dev, BINS, width),
        "rows",
        scatter_dimension=0,
        axis_index_groups=peers,
    )
    bin_iota = jnp.arange(BINS, dtype=jnp.int32)
    lower_mask = (
        (bin_iota[:, None] < bin_iota[None, :]) & (bin_iota[:, None] < BINS - 1)
    ).astype(jnp.float32)
    left_base = jnp.einsum("pbc,bt->ptc", owned, lower_mask, precision=lax.Precision.HIGHEST)
    node_total = jnp.sum(owned, axis=1, keepdims=True)
    left_miss = left_base + owned[:, BINS - 1 :, :]
    parent_score = split_score(node_total, classes)
    gain_left = (
        split_score(left_miss, classes)
        + split_score(node_total - left_miss, classes)
        - parent_score
    )
    gain_right = (
        split_score(left_base, classes)
        + split_score(node_total - left_base, classes)
        - parent_score
    )
    gain = jnp.concatenate([gain_left, gain_right], axis=1) / (2.0 * classes)
    moves = [
        (n * per_node + cut * group + r, n * per_node + r * cuts + cut)
        for n in range(node_count)
        for cut in range(cuts)
        for r in range(group)
    ]
    gain_rows = lax.ppermute(gain, "rows", moves)
    return (new_logits, gain_rows[None], leaves)


def solution(mesh):
    return jax.shard_map(
        local,
        mesh=mesh,
        in_specs=(P("rows", None), P("rows"), P("rows"), P("rows", "feat"), P(), P(), P()),
        out_specs=(P("rows", None), P("rows", "feat", None), P()),
        check_vma=False,
    )
```

time: 175 us -> 149 us (0.85)
  blocking collectives: 86.9 us -> 0 us
  waiting for transfers between devices: 18.2 us -> 52.9 us
  starting transfers between devices: 9.39 us -> 43.7 us
  between operations: 14.2 us -> 1.01 us
  other arithmetic: 9.08 us -> 0.15 us
  Pallas kernels: 32.7 us -> 40.9 us
  local copies, waits for them, and re-layouts: 2.45 us -> 9.4 us
    psum x2 -> x0, blocking collectives: 86.9 us -> none  [the longest x1 77.3 us: local(): lax.psum(own_sums, ('rows', 'feat')).reshape(node_count, 2, width)]
    ppermute x0 -> x36, waiting for transfers between devices: none -> 47.4 us  [swap(): return lax.ppermute(x, axis, [(i, i ^ bit) for i in range(size)])]
    ppermute x0 -> x36, starting transfers between devices: none -> 40 us  [swap(): return lax.ppermute(x, axis, [(i, i ^ bit) for i in range(size)])]
    all_gather x1 -> x0, waiting for transfers between devices: 12.7 us -> none  [local(): lax.all_gather(row_info, 'rows', axis=0, axis_index_groups=members)]
    unnamed x14 -> x56, local copies, waits for them, and re-layouts: 1.11 us -> 9.4 us
    pallas_call x1 -> x7, Pallas kernels: 32.7 us -> 40.9 us  [the longest x4 37.2 us: add_sources(): pl.pallas_call(functools.partial(hist_kernel, classes, node_count, source...]
    all_to_all x2 -> x1, starting transfers between devices: 9.35 us -> 3.75 us  [local(): lax.all_to_all(hist, 'rows', 0, 0, tiled=True, axis_index_groups=halves)]
    reduce_sum x3 -> x0, other arithmetic: 5.02 us -> none  [the longest x1 3.09 us: local(): jnp.sum(jnp.where(col_iota[None, :] == local_col[:, None], bin_codes, 0),...]
  transfers between devices with their start and end apart: 3 -> 37, of which waited for: 2 -> 12; matrix products, arithmetic and copies ran while one was open for 2% -> 2% of each run, Pallas kernels for 0% -> 19%
where the time goes in v2:
time: 149 us
  waiting for transfers between devices  52.9 us (36%)
  starting transfers between devices  43.7 us (29%)
  Pallas kernels  40.9 us (27%)
  local copies, waits for them, and re-layouts  9.4 us (6%)
    ppermute x36, waiting for transfers between devices, swap(): return lax.ppermute(x, axis, [(i, i ^ bit) for i in range(size)])  47.4 us
    ppermute x36, starting transfers between devices, swap(): return lax.ppermute(x, axis, [(i, i ^ bit) for i in range(size)])  40 us
    pallas_call x4, Pallas kernels, add_sources(): pl.pallas_call(functools.partial(hist_kernel, classes, node_count, source...  37.2 us
    unnamed x56, local copies, waits for them, and re-layouts  9.4 us
    all_to_all x1, waiting for transfers between devices, local(): lax.all_to_all(hist, 'rows', 0, 0, tiled=True, axis_index_groups=halves)  5.57 us
    all_to_all x1, starting transfers between devices, local(): lax.all_to_all(hist, 'rows', 0, 0, tiled=True, axis_index_groups=halves)  3.75 us
  transfers between devices with their start and end apart: 37, of which 12 were waited for; matrix products, arithmetic and copies ran while one was open for 2% of the time, Pallas kernels for 19%

profile of v2, /device:TPU:0, one launch (start us, length us, event | category | flops | bytes accessed | tf_op | source)
XLA Modules:
  0.0 149.3 jit_solution(4832431955703130873)
XLA Ops:
  10.0 2.5 %collective-permute-start.31 = (s32[8,3072]{1,0:T(8,128)}, s32[8,3072]{1,0:T(8,128)}, u32[]{:S(2)}, u32[]{:S(2)}) collective-permute-start(s32[8,3072]{1,0:T(8,128)} %get-tuple-element.37), channel_id=1, source_target_pairs={{0,4},{2,6},{4,0},{6,2},{8,12},{10,14},{12,8},{14,10},{16,20},{18,... | collective-permute-start | bytes 294920 | tf_op jit(solution)/shard_map/ppermute | solution.py:216
  20.9 2.1 %collective-permute-done.2 = f32[16,64]{1,0:T(8,128)S(1)} collective-permute-done((f32[16,64]{1,0:T(8,128)S(1)}, f32[16,64]{1,0:T(8,128)S(1)}, u32[]{:S(2)}, u32[]{:S(2)}) %collective-permute-start.2) | collective-permute-done | bytes 4128 | tf_op jit(solution)/shard_map/ppermute | solution.py:216
  23.3 3.4 %collective-permute-done.3 = f32[16,64]{1,0:T(8,128)S(1)} collective-permute-done((f32[16,64]{1,0:T(8,128)S(1)}, f32[16,64]{1,0:T(8,128)S(1)}, u32[]{:S(2)}, u32[]{:S(2)}) %collective-permute-start.3) | collective-permute-done | bytes 4128 | tf_op jit(solution)/shard_map/ppermute | solution.py:216
  26.7 2.6 %collective-permute-start.4 = (f32[16,64]{1,0:T(8,128)S(1)}, f32[16,64]{1,0:T(8,128)S(1)}, u32[]{:S(2)}, u32[]{:S(2)}) collective-permute-start(f32[16,64]{1,0:T(8,128)S(1)} %add.44), channel_id=1, source_target_pairs={{0,16},{2,18},{4,20},{6,22},{8,24},{10,26},{12,28},{14,30},{16,0},... | collective-permute-start | bytes 12296 | tf_op jit(solution)/shard_map/ppermute | solution.py:216
  29.3 2.0 %collective-permute-done.4 = f32[16,64]{1,0:T(8,128)S(1)} collective-permute-done((f32[16,64]{1,0:T(8,128)S(1)}, f32[16,64]{1,0:T(8,128)S(1)}, u32[]{:S(2)}, u32[]{:S(2)}) %collective-permute-start.4) | collective-permute-done | bytes 4128 | tf_op jit(solution)/shard_map/ppermute | solution.py:216
  32.7 2.2 %collective-permute-done = f32[1,3072]{1,0:T(1,128)S(1)} collective-permute-done((f32[1,3072]{1,0:T(1,128)S(1)}, f32[1,3072]{1,0:T(1,128)S(1)}, u32[]{:S(2)}, u32[]{:S(2)}) %collective-permute-start) | collective-permute-done | bytes 12320 | tf_op jit(solution)/shard_map/ppermute | solution.py:216
  36.4 2.2 %collective-permute-done.5 = f32[16,64]{1,0:T(8,128)S(1)} collective-permute-done((f32[16,64]{1,0:T(8,128)S(1)}, f32[16,64]{1,0:T(8,128)S(1)}, u32[]{:S(2)}, u32[]{:S(2)}) %collective-permute-start.5) | collective-permute-done | bytes 4128 | tf_op jit(solution)/shard_map/ppermute | solution.py:216
  42.2 2.3 %collective-permute-start.25 = (s32[8,3072]{1,0:T(8,128)S(1)}, s32[8,3072]{1,0:T(8,128)S(1)}, u32[]{:S(2)}, u32[]{:S(2)}) collective-permute-start(s32[8,3072]{1,0:T(8,128)S(1)} %copy-done.17), channel_id=1, source_target_pairs={{0,14},{2,12},{4,10},{6,8},{8,6},{10,4},{12,2},{14,0},{16,30},{18,... | collective-permute-start | bytes 294920 | tf_op jit(solution)/shard_map/ppermute | solution.py:216
  44.6 5.9 %collective-permute-done.23.refs_1_ = s32[8,3072]{1,0:T(8,128)S(1)} collective-permute-done((s32[8,3072]{1,0:T(8,128)S(1)}, s32[8,3072]{1,0:T(8,128)S(1)}, u32[]{:S(2)}, u32[]{:S(2)}) %collective-permute-start.23) | collective-permute-done | bytes 98336 | tf_op jit(solution)/shard_map/ppermute | solution.py:216
  50.4 2.0 %collective-permute-start.33 = (f32[32,3328]{1,0:T(8,128)S(1)}, f32[32,3328]{1,0:T(8,128)S(1)}, u32[]{:S(2)}, u32[]{:S(2)}) collective-permute-start(f32[32,3328]{1,0:T(8,128)S(1)} %shard_map.94.info_ref.refs_4_), channel_id=1, source_target_pairs={{0,2},{2,0},{4,6},{6,4},{8,10},{10,8},{12,14},{14,12},{16,18},{18,... | collective-permute-start | bytes 1277960 | tf_op jit(solution)/shard_map/ppermute | solution.py:216
  53.1 2.8 %collective-permute-start.10 = (f32[32,3328]{1,0:T(8,128)S(1)}, f32[32,3328]{1,0:T(8,128)S(1)}, u32[]{:S(2)}, u32[]{:S(2)}) collective-permute-start(f32[32,3328]{1,0:T(8,128)S(1)} %shard_map.94.info_ref.refs_4_), channel_id=1, source_target_pairs={{0,16},{2,18},{4,20},{6,22},{8,24},{10,26},{12,28},{14,30},{16,0},... | collective-permute-start | bytes 1277960 | tf_op jit(solution)/shard_map/ppermute | solution.py:216
  58.5 19.9 %collective-permute-done.15.refs_0_ = s32[8,3072]{1,0:T(8,128)S(1)} collective-permute-done((s32[8,3072]{1,0:T(8,128)S(1)}, s32[8,3072]{1,0:T(8,128)S(1)}, u32[]{:S(2)}, u32[]{:S(2)}) %collective-permute-start.15) | collective-permute-done | bytes 98336 | tf_op jit(solution)/shard_map/ppermute | solution.py:216
  78.5 7.2 %collective-permute-done.16.refs_1_ = s32[8,3072]{1,0:T(8,128)S(1)} collective-permute-done((s32[8,3072]{1,0:T(8,128)S(1)}, s32[8,3072]{1,0:T(8,128)S(1)}, u32[]{:S(2)}, u32[]{:S(2)}) %collective-permute-start.16) | collective-permute-done | bytes 98336 | tf_op jit(solution)/shard_map/ppermute | solution.py:216
  86.8 2.3 %collective-permute-start.11 = (f32[32,3328]{1,0:T(8,128)S(1)}, f32[32,3328]{1,0:T(8,128)S(1)}, u32[]{:S(2)}, u32[]{:S(2)}) collective-permute-start(f32[32,3328]{1,0:T(8,128)S(1)} %collective-permute-done.10.refs_4_), channel_id=1, source_target_pairs={{0,8},{2,10},{4,12},{6,14},{8,0},{10,2},{12,4},{14,6},{16,24},{18,... | collective-permute-start | bytes 1277960 | tf_op jit(solution)/shard_map/ppermute | solution.py:216
  89.1 8.7 %shard_map.97.refs_8_ = f32[512,512]{1,0:T(8,128)S(1)} custom-call(s32[8,3072]{1,0:T(8,128)S(1)} %copy-done.11, s32[8,3072]{1,0:T(8,128)} %collective-permute-done.30.refs_1_, s32[8,3072]{1,0:T(8,128)} %collective-permute-done.31.refs_2_, s32[8,3072]{1,0:T(8,128)} %collective-permute-done.32.refs_3_, f32[32,3328]{1,0:T(8,128)S(1)} %shard_map.94.info_ref.refs_4_, ...), custom_call_target="tpu_custom_call" | custom-call | flops 6442450944 | bytes 4063232 | tf_op jit(solution)/shard_map/pallas_call | solution.py:199
  98.8 1.8 %collective-permute-start.6 = (s32[8,3072]{1,0:T(8,128)S(1)}, s32[8,3072]{1,0:T(8,128)S(1)}, u32[]{:S(2)}, u32[]{:S(2)}) collective-permute-start(s32[8,3072]{1,0:T(8,128)S(1)} %copy-done.5), channel_id=1, source_target_pairs={{0,24},{2,26},{4,28},{6,30},{8,16},{10,18},{12,20},{14,22},{16,8},... | collective-permute-start | bytes 294920 | tf_op jit(solution)/shard_map/ppermute | solution.py:216
  102.2 8.8 %shard_map.98.refs_8_ = f32[512,512]{1,0:T(8,128)S(1)} custom-call(s32[8,3072]{1,0:T(8,128)} %collective-permute-done.22.refs_0_, s32[8,3072]{1,0:T(8,128)S(1)} %collective-permute-done.23.refs_1_, s32[8,3072]{1,0:T(8,128)S(1)} %collective-permute-done.24.refs_2_, s32[8,3072]{1,0:T(8,128)S(1)} %collective-permute-done.25.refs_3_, ...), custom_call_target="tpu_custom_call" | custom-call | flops 6442450944 | bytes 4063232 | tf_op jit(solution)/shard_map/pallas_call | solution.py:199
  111.0 2.1 %collective-permute-start.7 = (s32[8,3072]{1,0:T(8,128)S(1)}, s32[8,3072]{1,0:T(8,128)S(1)}, u32[]{:S(2)}, u32[]{:S(2)}) collective-permute-start(s32[8,3072]{1,0:T(8,128)S(1)} %get-tuple-element.24), channel_id=1, source_target_pairs={{0,26},{2,24},{4,30},{6,28},{8,18},{10,16},{12,22},{14,20},{16,10}... | collective-permute-start | bytes 294920 | tf_op jit(solution)/shard_map/ppermute | solution.py:216
  113.1 2.1 %collective-permute-start.8 = (s32[8,3072]{1,0:T(8,128)S(1)}, s32[8,3072]{1,0:T(8,128)S(1)}, u32[]{:S(2)}, u32[]{:S(2)}) collective-permute-start(s32[8,3072]{1,0:T(8,128)S(1)} %get-tuple-element.25), channel_id=1, source_target_pairs={{0,28},{2,30},{4,24},{6,26},{8,20},{10,22},{12,16},{14,18},{16,12}... | collective-permute-start | bytes 294920 | tf_op jit(solution)/shard_map/ppermute | solution.py:216
  115.2 2.7 %collective-permute-start.9 = (s32[8,3072]{1,0:T(8,128)S(1)}, s32[8,3072]{1,0:T(8,128)S(1)}, u32[]{:S(2)}, u32[]{:S(2)}) collective-permute-start(s32[8,3072]{1,0:T(8,128)S(1)} %get-tuple-element.26), channel_id=1, source_target_pairs={{0,30},{2,28},{4,26},{6,24},{8,22},{10,20},{12,18},{14,16},{16,14}... | collective-permute-start | bytes 294920 | tf_op jit(solution)/shard_map/ppermute | solution.py:216
  118.4 8.8 %shard_map.99.refs_8_ = f32[512,512]{1,0:T(8,128)S(1)} custom-call(s32[8,3072]{1,0:T(8,128)S(1)} %collective-permute-done.15.refs_0_, s32[8,3072]{1,0:T(8,128)S(1)} %collective-permute-done.16.refs_1_, s32[8,3072]{1,0:T(8,128)S(1)} %collective-permute-done.17.refs_2_, s32[8,3072]{1,0:T(8,128)S(1)} %collective-permute-done.18.refs_3_, ...), custom_call_target="tpu_custom_call" | custom-call | flops 6442450944 | bytes 4063232 | tf_op jit(solution)/shard_map/pallas_call | solution.py:199
  127.3 10.9 %shard_map.100 = f32[8,8,128]{2,1,0:T(8,128)} custom-call(s32[8,3072]{1,0:T(8,128)S(1)} %collective-permute-done.6.refs_0_, s32[8,3072]{1,0:T(8,128)S(1)} %collective-permute-done.7.refs_1_, s32[8,3072]{1,0:T(8,128)S(1)} %collective-permute-done.8.refs_2_, s32[8,3072]{1,0:T(8,128)S(1)} %collective-permute-done.9.refs_3_, ...), custom_call_target="tpu_custom_call" | custom-call | flops 6442450944 | bytes 4063232 | tf_op jit(solution)/shard_map/pallas_call | solution.py:199
  138.2 3.8 %all-to-all-start = ((f32[8,8,128]{2,1,0:T(8,128)}), f32[8,8,128]{2,1,0:T(8,128)S(1)}, u32[]{:S(2)}, u32[]{:S(2)}) async-start(f32[8,8,128]{2,1,0:T(8,128)} %shard_map.100), calls=%async_computation | async-start | bytes 65536 | tf_op jit(solution)/shard_map/all_to_all | solution.py:305
  143.1 5.6 %all-to-all-done = f32[8,8,128]{2,1,0:T(8,128)S(1)} async-done(((f32[8,8,128]{2,1,0:T(8,128)}), f32[8,8,128]{2,1,0:T(8,128)S(1)}, u32[]{:S(2)}, u32[]{:S(2)}) %all-to-all-start) | async-done | bytes 32800 | tf_op jit(solution)/shard_map/all_to_all | solution.py:305
  (125 shorter events, 33.7 us)
Async XLA Ops:
  9.6 30.5 %collective-permute-start.30 = (s32[8,3072]{1,0:T(8,128)}, s32[8,3072]{1,0:T(8,128)}, u32[]{:S(2)}, u32[]{:S(2)}) collective-permute-start(s32[8,3072]{1,0:T(8,128)} %get-tuple-element.36), channel_id=1, source_target_pairs={{0,2},{2,0},{4,6},{6,4},{8,10},{10,8},{12,14},{14,12},{16,18},{18,... | collective-permute-start | bytes 294920 | tf_op jit(solution)/shard_map/ppermute | solution.py:216
  10.0 30.5 %collective-permute-start.31 = (s32[8,3072]{1,0:T(8,128)}, s32[8,3072]{1,0:T(8,128)}, u32[]{:S(2)}, u32[]{:S(2)}) collective-permute-start(s32[8,3072]{1,0:T(8,128)} %get-tuple-element.37), channel_id=1, source_target_pairs={{0,4},{2,6},{4,0},{6,2},{8,12},{10,14},{12,8},{14,10},{16,20},{18,... | collective-permute-start | bytes 294920 | tf_op jit(solution)/shard_map/ppermute | solution.py:216
  12.6 28.0 %collective-permute-start.32 = (s32[8,3072]{1,0:T(8,128)}, s32[8,3072]{1,0:T(8,128)}, u32[]{:S(2)}, u32[]{:S(2)}) collective-permute-start(s32[8,3072]{1,0:T(8,128)} %get-tuple-element.38), channel_id=1, source_target_pairs={{0,6},{2,4},{4,2},{6,0},{8,14},{10,12},{12,10},{14,8},{16,22},{18,... | collective-permute-start | bytes 294920 | tf_op jit(solution)/shard_map/ppermute | solution.py:216
  12.7 29.5 %collective-permute-start.22 = (s32[8,3072]{1,0:T(8,128)}, s32[8,3072]{1,0:T(8,128)}, u32[]{:S(2)}, u32[]{:S(2)}) collective-permute-start(s32[8,3072]{1,0:T(8,128)} %get-tuple-element.31), channel_id=1, source_target_pairs={{0,8},{2,10},{4,12},{6,14},{8,0},{10,2},{12,4},{14,6},{16,24},{18,... | collective-permute-start | bytes 294920 | tf_op jit(solution)/shard_map/ppermute | solution.py:216
  38.6 17.5 %collective-permute-start.34 = (f32[32,3328]{1,0:T(8,128)S(1)}, f32[32,3328]{1,0:T(8,128)S(1)}, u32[]{:S(2)}, u32[]{:S(2)}) collective-permute-start(f32[32,3328]{1,0:T(8,128)S(1)} %shard_map.94.info_ref.refs_4_), channel_id=1, source_target_pairs={{0,4},{2,6},{4,0},{6,2},{8,12},{10,14},{12,8},{14,10},{16,20},{18,... | collective-permute-start | bytes 1277960 | tf_op jit(solution)/shard_map/ppermute | solution.py:216
  40.1 17.2 %collective-permute-start.26 = (f32[32,3328]{1,0:T(8,128)S(1)}, f32[32,3328]{1,0:T(8,128)S(1)}, u32[]{:S(2)}, u32[]{:S(2)}) collective-permute-start(f32[32,3328]{1,0:T(8,128)S(1)} %shard_map.94.info_ref.refs_4_), channel_id=1, source_target_pairs={{0,8},{2,10},{4,12},{6,14},{8,0},{10,2},{12,4},{14,6},{16,24},{18,... | collective-permute-start | bytes 1277960 | tf_op jit(solution)/shard_map/ppermute | solution.py:216
  40.6 12.5 %collective-permute-start.24 = (s32[8,3072]{1,0:T(8,128)S(1)}, s32[8,3072]{1,0:T(8,128)S(1)}, u32[]{:S(2)}, u32[]{:S(2)}) collective-permute-start(s32[8,3072]{1,0:T(8,128)S(1)} %copy-done.19), channel_id=1, source_target_pairs={{0,12},{2,14},{4,8},{6,10},{8,4},{10,6},{12,0},{14,2},{16,28},{18,... | collective-permute-start | bytes 294920 | tf_op jit(solution)/shard_map/ppermute | solution.py:216
  42.2 13.7 %collective-permute-start.25 = (s32[8,3072]{1,0:T(8,128)S(1)}, s32[8,3072]{1,0:T(8,128)S(1)}, u32[]{:S(2)}, u32[]{:S(2)}) collective-permute-start(s32[8,3072]{1,0:T(8,128)S(1)} %copy-done.17), channel_id=1, source_target_pairs={{0,14},{2,12},{4,10},{6,8},{8,6},{10,4},{12,2},{14,0},{16,30},{18,... | collective-permute-start | bytes 294920 | tf_op jit(solution)/shard_map/ppermute | solution.py:216
  50.4 35.3 %collective-permute-start.33 = (f32[32,3328]{1,0:T(8,128)S(1)}, f32[32,3328]{1,0:T(8,128)S(1)}, u32[]{:S(2)}, u32[]{:S(2)}) collective-permute-start(f32[32,3328]{1,0:T(8,128)S(1)} %shard_map.94.info_ref.refs_4_), channel_id=1, source_target_pairs={{0,2},{2,0},{4,6},{6,4},{8,10},{10,8},{12,14},{14,12},{16,18},{18,... | collective-permute-start | bytes 1277960 | tf_op jit(solution)/shard_map/ppermute | solution.py:216
  53.1 32.8 %collective-permute-start.10 = (f32[32,3328]{1,0:T(8,128)S(1)}, f32[32,3328]{1,0:T(8,128)S(1)}, u32[]{:S(2)}, u32[]{:S(2)}) collective-permute-start(f32[32,3328]{1,0:T(8,128)S(1)} %shard_map.94.info_ref.refs_4_), channel_id=1, source_target_pairs={{0,16},{2,18},{4,20},{6,22},{8,24},{10,26},{12,28},{14,30},{16,0},... | collective-permute-start | bytes 1277960 | tf_op jit(solution)/shard_map/ppermute | solution.py:216
  55.9 22.5 %collective-permute-start.15 = (s32[8,3072]{1,0:T(8,128)S(1)}, s32[8,3072]{1,0:T(8,128)S(1)}, u32[]{:S(2)}, u32[]{:S(2)}) collective-permute-start(s32[8,3072]{1,0:T(8,128)S(1)} %copy-done.15), channel_id=1, source_target_pairs={{0,16},{2,18},{4,20},{6,22},{8,24},{10,26},{12,28},{14,30},{16,0},... | collective-permute-start | bytes 294920 | tf_op jit(solution)/shard_map/ppermute | solution.py:216
  56.1 30.7 %collective-permute-start.35 = (f32[32,3328]{1,0:T(8,128)S(1)}, f32[32,3328]{1,0:T(8,128)S(1)}, u32[]{:S(2)}, u32[]{:S(2)}) collective-permute-start(f32[32,3328]{1,0:T(8,128)S(1)} %collective-permute-done.34.refs_6_), channel_id=1, source_target_pairs={{0,2},{2,0},{4,6},{6,4},{8,10},{10,8},{12,14},{14,12},{16,18},{18,... | collective-permute-start | bytes 1277960 | tf_op jit(solution)/shard_map/ppermute | solution.py:216
  57.3 31.8 %collective-permute-start.28 = (f32[32,3328]{1,0:T(8,128)S(1)}, f32[32,3328]{1,0:T(8,128)S(1)}, u32[]{:S(2)}, u32[]{:S(2)}) collective-permute-start(f32[32,3328]{1,0:T(8,128)S(1)} %collective-permute-done.26.refs_4_), channel_id=1, source_target_pairs={{0,4},{2,6},{4,0},{6,2},{8,12},{10,14},{12,8},{14,10},{16,20},{18,... | collective-permute-start | bytes 1277960 | tf_op jit(solution)/shard_map/ppermute | solution.py:216
  85.8 13.0 %collective-permute-start.27 = (f32[32,3328]{1,0:T(8,128)S(1)}, f32[32,3328]{1,0:T(8,128)S(1)}, u32[]{:S(2)}, u32[]{:S(2)}) collective-permute-start(f32[32,3328]{1,0:T(8,128)S(1)} %collective-permute-done.26.refs_4_), channel_id=1, source_target_pairs={{0,2},{2,0},{4,6},{6,4},{8,10},{10,8},{12,14},{14,12},{16,18},{18,... | collective-permute-start | bytes 1277960 | tf_op jit(solution)/shard_map/ppermute | solution.py:216
  85.9 14.7 %collective-permute-start.20 = (f32[32,3328]{1,0:T(8,128)S(1)}, f32[32,3328]{1,0:T(8,128)S(1)}, u32[]{:S(2)}, u32[]{:S(2)}) collective-permute-start(f32[32,3328]{1,0:T(8,128)S(1)} %collective-permute-done.10.refs_4_), channel_id=1, source_target_pairs={{0,4},{2,6},{4,0},{6,2},{8,12},{10,14},{12,8},{14,10},{16,20},{18,... | collective-permute-start | bytes 1277960 | tf_op jit(solution)/shard_map/ppermute | solution.py:216
  86.8 14.4 %collective-permute-start.11 = (f32[32,3328]{1,0:T(8,128)S(1)}, f32[32,3328]{1,0:T(8,128)S(1)}, u32[]{:S(2)}, u32[]{:S(2)}) collective-permute-start(f32[32,3328]{1,0:T(8,128)S(1)} %collective-permute-done.10.refs_4_), channel_id=1, source_target_pairs={{0,8},{2,10},{4,12},{6,14},{8,0},{10,2},{12,4},{14,6},{16,24},{18,... | collective-permute-start | bytes 1277960 | tf_op jit(solution)/shard_map/ppermute | solution.py:216
  89.1 12.2 %collective-permute-start.29 = (f32[32,3328]{1,0:T(8,128)S(1)}, f32[32,3328]{1,0:T(8,128)S(1)}, u32[]{:S(2)}, u32[]{:S(2)}) collective-permute-start(f32[32,3328]{1,0:T(8,128)S(1)} %collective-permute-done.28.refs_6_), channel_id=1, source_target_pairs={{0,2},{2,0},{4,6},{6,4},{8,10},{10,8},{12,14},{14,12},{16,18},{18,... | collective-permute-start | bytes 1277960 | tf_op jit(solution)/shard_map/ppermute | solution.py:216
  97.8 13.2 %collective-permute-start.18 = (s32[8,3072]{1,0:T(8,128)S(1)}, s32[8,3072]{1,0:T(8,128)S(1)}, u32[]{:S(2)}, u32[]{:S(2)}) collective-permute-start(s32[8,3072]{1,0:T(8,128)S(1)} %copy-done.7), channel_id=1, source_target_pairs={{0,22},{2,20},{4,18},{6,16},{8,30},{10,28},{12,26},{14,24},{16,6},... | collective-permute-start | bytes 294920 | tf_op jit(solution)/shard_map/ppermute | solution.py:216
  98.8 14.3 %collective-permute-start.6 = (s32[8,3072]{1,0:T(8,128)S(1)}, s32[8,3072]{1,0:T(8,128)S(1)}, u32[]{:S(2)}, u32[]{:S(2)}) collective-permute-start(s32[8,3072]{1,0:T(8,128)S(1)} %copy-done.5), channel_id=1, source_target_pairs={{0,24},{2,26},{4,28},{6,30},{8,16},{10,18},{12,20},{14,22},{16,8},... | collective-permute-start | bytes 294920 | tf_op jit(solution)/shard_map/ppermute | solution.py:216
  100.6 14.6 %collective-permute-start.19 = (f32[32,3328]{1,0:T(8,128)S(1)}, f32[32,3328]{1,0:T(8,128)S(1)}, u32[]{:S(2)}, u32[]{:S(2)}) collective-permute-start(f32[32,3328]{1,0:T(8,128)S(1)} %collective-permute-done.10.refs_4_), channel_id=1, source_target_pairs={{0,2},{2,0},{4,6},{6,4},{8,10},{10,8},{12,14},{14,12},{16,18},{18,... | collective-permute-start | bytes 1277960 | tf_op jit(solution)/shard_map/ppermute | solution.py:216
  101.2 16.6 %collective-permute-start.21 = (f32[32,3328]{1,0:T(8,128)S(1)}, f32[32,3328]{1,0:T(8,128)S(1)}, u32[]{:S(2)}, u32[]{:S(2)}) collective-permute-start(f32[32,3328]{1,0:T(8,128)S(1)} %collective-permute-done.20.refs_6_), channel_id=1, source_target_pairs={{0,2},{2,0},{4,6},{6,4},{8,10},{10,8},{12,14},{14,12},{16,18},{18,... | collective-permute-start | bytes 1277960 | tf_op jit(solution)/shard_map/ppermute | solution.py:216
  101.3 16.6 %collective-permute-start.13 = (f32[32,3328]{1,0:T(8,128)S(1)}, f32[32,3328]{1,0:T(8,128)S(1)}, u32[]{:S(2)}, u32[]{:S(2)}) collective-permute-start(f32[32,3328]{1,0:T(8,128)S(1)} %collective-permute-done.11.refs_4_), channel_id=1, source_target_pairs={{0,4},{2,6},{4,0},{6,2},{8,12},{10,14},{12,8},{14,10},{16,20},{18,... | collective-permute-start | bytes 1277960 | tf_op jit(solution)/shard_map/ppermute | solution.py:216
  111.0 16.2 %collective-permute-start.7 = (s32[8,3072]{1,0:T(8,128)S(1)}, s32[8,3072]{1,0:T(8,128)S(1)}, u32[]{:S(2)}, u32[]{:S(2)}) collective-permute-start(s32[8,3072]{1,0:T(8,128)S(1)} %get-tuple-element.24), channel_id=1, source_target_pairs={{0,26},{2,24},{4,30},{6,28},{8,18},{10,16},{12,22},{14,20},{16,10}... | collective-permute-start | bytes 294920 | tf_op jit(solution)/shard_map/ppermute | solution.py:216
  113.1 14.2 %collective-permute-start.8 = (s32[8,3072]{1,0:T(8,128)S(1)}, s32[8,3072]{1,0:T(8,128)S(1)}, u32[]{:S(2)}, u32[]{:S(2)}) collective-permute-start(s32[8,3072]{1,0:T(8,128)S(1)} %get-tuple-element.25), channel_id=1, source_target_pairs={{0,28},{2,30},{4,24},{6,26},{8,20},{10,22},{12,16},{14,18},{16,12}... | collective-permute-start | bytes 294920 | tf_op jit(solution)/shard_map/ppermute | solution.py:216
  (40 other events, 560.9 us)

commit v3 on v2

--- a/solution.py
+++ b/solution.py
@@ -9,6 +9,8 @@
 
 BINS = 64
 LANES = 128
+BATCHES = ((2, 4, 6, 8), (10, 12), (14,))
+SMALL_COST = pl.CostEstimate(flops=1000000, bytes_accessed=1000000, transcendentals=0)
 
 
 reg_lambda = 1.0
@@ -42,8 +44,8 @@
 
 
 def info_kernel(logits_ref, labels_ref, nodes_ref, info_ref):
-    rows, classes = logits_ref.shape
-    expo_vals = jnp.exp(logits_ref[...].T)
+    classes, rows = logits_ref.shape
+    expo_vals = jnp.exp(logits_ref[...])
     info_ref[:, :rows] = expo_vals / jnp.sum(expo_vals, axis=0, keepdims=True)
     chunks = rows // LANES
     info_ref[:, rows:] = jnp.zeros((classes, 2 * LANES), jnp.float32)
@@ -61,23 +63,25 @@
     return prob, label, node
 
 
-def codes_kernel(group, own, starts_ref, codes_ref, *refs):
-    outs, turned = refs[:-1], refs[-1]
+def codes_kernel(own, starts_ref, split_ref, codes_ref, sent_ref, kept_ref, picked_ref, turned):
     turned[...] = codes_ref[...].T
-    for m in range(group):
-        start = pl.multiple_of(starts_ref[m], own)
-        outs[m][...] = turned[pl.ds(start, own), :]
-
-
-def side_kernel(node_count, split_ref, info_ref, codes_ref, flag_ref, sums_ref, turned):
-    rows, feats = codes_ref.shape
+    for half, out_ref in ((1, sent_ref), (0, kept_ref)):
+        for m in range(out_ref.shape[0]):
+            start = pl.multiple_of(starts_ref[half, m], own)
+            out_ref[m] = turned[pl.ds(start, own), :]
+    for n in range(picked_ref.shape[0]):
+        col = jnp.clip(split_ref[0, n], 0, turned.shape[0] - 1)
+        picked_ref[n : n + 1, :] = turned[pl.ds(col, 1), :]
+
+
+def side_kernel(feats, split_ref, info_ref, picked_ref, flag_ref, sums_ref):
+    node_count, rows = picked_ref.shape
     prob, label, node = read_info(info_ref[...], rows)
-    turned[...] = codes_ref[...].T
     side = jnp.zeros((1, rows), jnp.float32)
     for n in range(node_count):
         col = split_ref[0, n]
         held = (col >= 0) & (col < feats)
-        code = turned[pl.ds(jnp.clip(col, 0, feats - 1), 1), :]
+        code = picked_ref[n : n + 1, :]
         threshold = jnp.where(held, split_ref[1, n], -1)
         last = jnp.where(held & (split_ref[2, n] == 1), BINS - 1, -1)
         left = (code < threshold) | (code == last)
@@ -106,24 +110,24 @@
     return jnp.concatenate([prob - target, prob * (1.0 - prob)], axis=0)
 
 
-def add_rows(codes, info, hist_ref, node_count):
-    feats, rows = codes.shape
+def masked_gradients(info, rows, node_count):
     prob, label, node = read_info(info, rows)
     grad_hess = gradients(prob, label)
-    masked = jnp.concatenate(
+    return jnp.concatenate(
         [jnp.where(node == float(n), grad_hess, 0.0).astype(jnp.bfloat16) for n in range(node_count)],
         axis=0,
     )
+
+
+def one_hot(codes):
+    feats, rows = codes.shape
     bin_iota = lax.broadcasted_iota(jnp.int32, (BINS, rows), 0)
-    hot = jnp.concatenate(
+    return jnp.concatenate(
         [
             jnp.where(codes[f : f + 1, :] == bin_iota, 1.0, 0.0).astype(jnp.bfloat16)
             for f in range(feats)
         ],
         axis=0,
-    )
-    hist_ref[...] += lax.dot_general(
-        masked, hot, (((1,), (1,)), ((), ())), preferred_element_type=jnp.float32
     )
 
 
@@ -156,72 +160,46 @@
             gain_ref[n, 2 * pair + 1 : 2 * pair + 2, :] = gain[:, 2 * BINS :]
 
 
-def hist_kernel(classes, node_count, sources, first, gains, *refs):
-    codes_refs, info_refs = refs[:sources], refs[sources : 2 * sources]
-    rest = refs[2 * sources :]
-    hist_in = None
-    if not first:
-        hist_in, rest = rest[0], rest[1:]
-    out_ref, codes_buf, info_buf, code_sems, info_sems = rest[:5]
-    hist_ref = rest[5] if gains else out_ref
-    for s in range(sources):
-        pltpu.make_async_copy(codes_refs[s], codes_buf.at[s], code_sems.at[s]).start()
-        pltpu.make_async_copy(info_refs[s], info_buf.at[s], info_sems.at[s]).start()
-    hist_ref[...] = jnp.zeros_like(hist_ref) if first else hist_in[...]
-
-    @pl.loop(0, sources)
-    def _(s):
-        pltpu.make_async_copy(codes_buf.at[s], codes_buf.at[s], code_sems.at[s]).wait()
-        pltpu.make_async_copy(info_buf.at[s], info_buf.at[s], info_sems.at[s]).wait()
-        add_rows(codes_buf[s], info_buf[s], hist_ref, node_count)
-
-    if gains:
-        write_gains(hist_ref, out_ref, classes, node_count)
-
-
-def add_sources(classes, node_count, codes, infos, hist, gains):
-    sources = len(codes)
-    own, rows = codes[0].shape
-    info_shape = infos[0].shape
+def hist_kernel(node_count, places, first, places_ref, codes_ref, *refs):
+    info_refs = refs[: len(places)]
+    out_ref = refs[-1]
+    for s, place in enumerate(places):
+        codes = codes_ref[places_ref[place]]
+        masked = masked_gradients(info_refs[s][...], codes.shape[1], node_count)
+        product = lax.dot_general(
+            masked, one_hot(codes), (((1,), (1,)), ((), ())), preferred_element_type=jnp.float32
+        )
+        if s > 0:
+            out_ref[...] += product
+        elif first:
+            out_ref[...] = product
+        else:
+            out_ref[...] = refs[len(places)][...] + product
+
+
+def add_sources(classes, node_count, sources, places, codes, infos, hist):
+    own = codes.shape[1]
     hist_shape = (2 * classes * node_count, own * BINS)
-    anywhere = pl.BlockSpec(memory_space=pl.ANY)
     whole = pl.BlockSpec(memory_space=pltpu.VMEM)
-    out_shape = (node_count, own, 2 * BINS) if gains else hist_shape
-    scratch = [
-        pltpu.VMEM((sources, own, rows), jnp.int32),
-        pltpu.VMEM((sources,) + info_shape, jnp.float32),
-        pltpu.SemaphoreType.DMA((sources,)),
-        pltpu.SemaphoreType.DMA((sources,)),
-    ]
-    if gains:
-        scratch.append(pltpu.VMEM(hist_shape, jnp.float32))
     held = [] if hist is None else [hist]
     return pl.pallas_call(
-        functools.partial(hist_kernel, classes, node_count, sources, hist is None, gains),
-        in_specs=[anywhere] * (2 * sources) + [whole] * len(held),
+        functools.partial(hist_kernel, node_count, [m // 2 for m in sources], hist is None),
+        in_specs=[pl.BlockSpec(memory_space=pltpu.SMEM)] + [whole] * (1 + len(sources) + len(held)),
         out_specs=whole,
-        out_shape=jax.ShapeDtypeStruct(out_shape, jnp.float32),
-        scratch_shapes=scratch,
-        compiler_params=pltpu.CompilerParams(vmem_limit_bytes=48 * 1024 * 1024),
-        cost_estimate=pl.CostEstimate(
-            flops=2 * hist_shape[0] * hist_shape[1] * sources * rows,
-            bytes_accessed=4 * sources * rows * (own + classes) + 8 * hist_shape[0] * hist_shape[1],
-            transcendentals=0,
-        ),
-    )(*codes, *infos, *held)
+        out_shape=jax.ShapeDtypeStruct(hist_shape, jnp.float32),
+        compiler_params=pltpu.CompilerParams(vmem_limit_bytes=32 * 1024 * 1024),
+        cost_estimate=SMALL_COST,
+    )(places, codes, *[infos[m] for m in sources], *held)
+
+
+def gain_kernel(classes, node_count, kept_ref, came_ref, gain_ref, hist_ref):
+    hist_ref[...] = kept_ref[...] + came_ref[...]
+    write_gains(hist_ref, gain_ref, classes, node_count)
 
 
 def swap(x, axis, bit):
     size = lax.axis_size(axis)
     return lax.ppermute(x, axis, [(i, i ^ bit) for i in range(size)])
-
-
-def sum_over(x, axis):
-    bit = 1
-    while bit < lax.axis_size(axis):
-        x = x + swap(x, axis, bit)
-        bit *= 2
-    return x
 
 
 def local(logits, labels, node_ids, bin_codes, split_feature, split_bin, split_missing):
@@ -239,71 +217,111 @@
     feat_index = lax.axis_index("feat")
     whole = pl.BlockSpec(memory_space=pltpu.VMEM)
     scalars = pl.BlockSpec(memory_space=pltpu.SMEM)
-    params = pltpu.CompilerParams(vmem_limit_bytes=48 * 1024 * 1024)
-
+    params = pltpu.CompilerParams(vmem_limit_bytes=16 * 1024 * 1024)
+
+    logits_t = logits.T
     info = pl.pallas_call(
         info_kernel,
         in_specs=[whole] * 3,
         out_specs=whole,
         out_shape=jax.ShapeDtypeStruct((classes, rows_dev + 2 * LANES), jnp.float32),
         compiler_params=params,
-    )(logits, labels.reshape(-1, LANES), node_ids.reshape(-1, LANES))
-
-    taker = row_index ^ jnp.arange(group, dtype=jnp.int32)
+        cost_estimate=SMALL_COST,
+    )(logits_t, labels.reshape(-1, LANES), node_ids.reshape(-1, LANES))
+
+    parity = row_index % 2
+    sources = list(range(0, group, 2))
+    chip_count = len(sources)
+    chip = jnp.arange(chip_count, dtype=jnp.int32)
+    half_of = jnp.stack([parity, 1 - parity])[:, None]
     if group_count == 1:
-        starts = (taker % per_node) * pairs_dev + (taker // per_node) * feats_own
+        starts = half_of * pairs_dev + (chip * 2 // per_node)[None, :] * feats_own
     else:
-        starts = (taker % group) * feats_own
-    codes_out = pl.pallas_call(
-        functools.partial(codes_kernel, group, feats_own),
-        in_specs=[scalars, whole],
-        out_specs=[whole] * group,
-        out_shape=[jax.ShapeDtypeStruct((feats_own, rows_dev), jnp.int32)] * group,
+        starts = (chip[None, :] * 2 + half_of) * feats_own
+    splits = jnp.stack([split_feature - feat_index * feats_dev, split_bin, split_missing])
+    block_shape = jax.ShapeDtypeStruct((chip_count, feats_own, rows_dev), jnp.int32)
+    codes_sent, codes_kept, picked = pl.pallas_call(
+        functools.partial(codes_kernel, feats_own),
+        in_specs=[scalars, scalars, whole],
+        out_specs=[whole] * 3,
+        out_shape=[
+            block_shape,
+            block_shape,
+            jax.ShapeDtypeStruct((node_count, rows_dev), jnp.int32),
+        ],
         scratch_shapes=[pltpu.VMEM((feats_dev, rows_dev), jnp.int32)],
         compiler_params=params,
-    )(starts, bin_codes)
-
-    infos = [info] + [None] * (group - 1)
-    for m in sorted(range(1, group), key=lambda m: -(m & -m)):
+        cost_estimate=SMALL_COST,
+    )(starts, splits, bin_codes)
+    members = [
+        [g * group + 2 * r + k for r in range(chip_count)] for g in range(group_count) for k in range(2)
+    ]
+    places = (row_index % group // 2) ^ chip
+    here = jnp.zeros((chip_count,), jnp.int32) + row_index % group // 2
+
+    def exchange(blocks):
+        return lax.all_to_all(blocks, "rows", 0, 0, tiled=True, axis_index_groups=members)
+
+    add = functools.partial(add_sources, classes, node_count)
+    infos = {0: info}
+    came_sent = exchange(codes_sent)
+    for m in sources[1:]:
+        if m & (m - 1) == 0:
+            infos[m] = swap(info, "rows", m)
+    own_sent = add((0,), here, codes_sent, infos, None)
+    own_kept = add((0,), here, codes_kept, infos, None)
+    for m in sorted(sources[1:], key=lambda m: -(m & -m)):
         low = m & -m
-        infos[m] = swap(infos[m ^ low], "rows", low)
-    codes_in = [codes_out[0]] + [swap(codes_out[m], "rows", m) for m in range(1, group)]
-
-    splits = jnp.stack([split_feature - feat_index * feats_dev, split_bin, split_missing])
+        if m != low:
+            infos[m] = swap(infos[m ^ low], "rows", low)
+
     right_flag, own_sums = pl.pallas_call(
-        functools.partial(side_kernel, node_count),
+        functools.partial(side_kernel, feats_dev),
         in_specs=[scalars, whole, whole],
         out_specs=[whole, whole],
         out_shape=[
             jax.ShapeDtypeStruct((1, rows_dev), jnp.float32),
             jax.ShapeDtypeStruct((2 * node_count, width), jnp.float32),
         ],
-        scratch_shapes=[pltpu.VMEM((feats_dev, rows_dev), jnp.int32)],
         compiler_params=params,
-    )(splits, info, bin_codes)
-    side_count = sum_over(right_flag, "feat")[0]
-    side_sums = sum_over(sum_over(own_sums, "rows"), "feat").reshape(node_count, 2, width)
+        cost_estimate=SMALL_COST,
+    )(splits, info, picked)
+    side_count = jnp.sum(lax.all_gather(right_flag, "feat"), axis=0)
+    all_sums = lax.all_gather(own_sums, ("rows", "feat"))
+    side_sums = jnp.sum(all_sums, axis=0).reshape(node_count, 2, width)
     leaves = -side_sums[..., :classes] / (side_sums[..., classes:] + reg_lambda)
     row_side = (side_count > 0.5).astype(jnp.int32)
     slot_iota = jnp.arange(2 * node_count, dtype=jnp.int32)
-    slot_hot = (node_ids * 2 + row_side)[:, None] == slot_iota[None, :]
+    slot_hot = (node_ids[None, :] * 2 + row_side) == slot_iota[:, None]
     update = jnp.dot(
+        leaves.reshape(2 * node_count, classes).T,
         slot_hot.astype(jnp.float32),
-        leaves.reshape(2 * node_count, classes),
         precision=lax.Precision.HIGHEST,
     )
-    new_logits = logits + step_size * update
-
-    batch = 4
-    hist = None
-    for low in range(0, group, batch):
-        span = slice(low, low + batch)
-        gains = group_count == 1 and low + batch >= group
-        hist = add_sources(classes, node_count, codes_in[span], infos[span], hist, gains)
+    new_logits = (logits_t + step_size * update).T
+
+    came_sent, codes_kept = lax.optimization_barrier((came_sent, codes_kept))
+    came_kept = exchange(codes_kept)
+    batches = BATCHES if chip_count == 8 else tuple((m,) for m in sources[1:])
+    hist = own_sent
+    for batch in batches:
+        hist = add(batch, places, came_sent, infos, hist)
+    came = swap(hist, "rows", 1)
+    kept = add(tuple(sources[1:]), places, came_kept, infos, own_kept)
     if group_count == 1:
+        gains = pl.pallas_call(
+            functools.partial(gain_kernel, classes, node_count),
+            in_specs=[whole] * 2,
+            out_specs=whole,
+            out_shape=jax.ShapeDtypeStruct((node_count, feats_own, 2 * BINS), jnp.float32),
+            scratch_shapes=[pltpu.VMEM(kept.shape, jnp.float32)],
+            compiler_params=params,
+            cost_estimate=SMALL_COST,
+        )(kept, came)
         halves = [[h + n * per_node for n in range(node_count)] for h in range(per_node)]
-        gain_rows = lax.all_to_all(hist, "rows", 0, 0, tiled=True, axis_index_groups=halves)
+        gain_rows = lax.all_to_all(gains, "rows", 0, 0, tiled=True, axis_index_groups=halves)
         return (new_logits, gain_rows.reshape(1, pairs_dev, 2 * BINS), leaves)
+    hist = kept + came
 
     cuts = feats_own // pairs_dev
     hist = hist.reshape(node_count, width, cuts, pairs_dev, BINS).transpose(0, 2, 3, 4, 1)

time: 149 us -> 207 us (1.39)
  blocking collectives: 0 us -> 74 us
  starting transfers between devices: 43.7 us -> 23.9 us
  waiting for transfers between devices: 52.9 us -> 60.5 us
  local copies, waits for them, and re-layouts: 9.4 us -> 3.06 us
    all_gather x0 -> x2, blocking collectives: none -> 74 us  [the longest x1 69.4 us: local(): all_sums = lax.all_gather(own_sums, ('rows', 'feat'))]
    ppermute x36 -> x8, starting transfers between devices: 40 us -> 9.58 us  [swap(): return lax.ppermute(x, axis, [(i, i ^ bit) for i in range(size)])]
    all_to_all x1 -> x3, starting transfers between devices: 3.75 us -> 14.3 us  [the longest x2 11 us: exchange(): lax.all_to_all(blocks, 'rows', 0, 0, tiled=True, axis_index_groups=members)]
    ppermute x36 -> x8, waiting for transfers between devices: 47.4 us -> 55 us  [swap(): return lax.ppermute(x, axis, [(i, i ^ bit) for i in range(size)])]
    unnamed x56 -> x21, local copies, waits for them, and re-layouts: 9.4 us -> 3.06 us
    pallas_call x6 -> x9, Pallas kernels: 40.5 us -> 41.6 us  [the longest x6 35 us: add_sources(): pl.pallas_call(functools.partial(hist_kernel, node_count, [m // 2 for m i...]
    all_to_all x1 -> x3, waiting for transfers between devices: 5.57 us -> 5.5 us  [the longest x1 5.5 us: local(): lax.all_to_all(gains, 'rows', 0, 0, tiled=True, axis_index_groups=halves)]
  transfers between devices with their start and end apart: 37 -> 11, of which waited for: 12 -> 6; matrix products, arithmetic and copies ran while one was open for 2% -> 1% of each run, Pallas kernels for 19% -> 17%
where the time goes in v3:
time: 207 us
  blocking collectives  74 us (36%)
  waiting for transfers between devices  60.5 us (29%)
  Pallas kernels  41.7 us (20%)
  starting transfers between devices  23.9 us (12%)
  local copies, waits for them, and re-layouts  3.06 us (1%)
    all_gather x1, blocking collectives, local(): all_sums = lax.all_gather(own_sums, ('rows', 'feat'))  69.4 us
    ppermute x8, waiting for transfers between devices, swap(): return lax.ppermute(x, axis, [(i, i ^ bit) for i in range(size)])  55 us
    pallas_call x6, Pallas kernels, add_sources(): pl.pallas_call(functools.partial(hist_kernel, node_count, [m // 2 for m i...  35 us
    all_to_all x2, starting transfers between devices, exchange(): lax.all_to_all(blocks, 'rows', 0, 0, tiled=True, axis_index_groups=members)  11 us
    ppermute x8, starting transfers between devices, swap(): return lax.ppermute(x, axis, [(i, i ^ bit) for i in range(size)])  9.58 us
    all_to_all x1, waiting for transfers between devices, local(): lax.all_to_all(gains, 'rows', 0, 0, tiled=True, axis_index_groups=halves)  5.5 us
    all_gather x1, blocking collectives, local(): side_count = jnp.sum(lax.all_gather(right_flag, 'feat'), axis=0)  4.58 us
  transfers between devices with their start and end apart: 11, of which 6 were waited for; matrix products, arithmetic and copies ran while one was open for 1% of the time, Pallas kernels for 17%

profile of v3, /device:TPU:0, one launch (start us, length us, event | category | flops | bytes accessed | tf_op | source)
XLA Modules:
  0.0 206.8 jit_solution(13619303787997643176)
XLA Ops:
  2.2 1.4 copy-done.6
  3.6 2.3 %shard_map.95 = (s32[8,8,3072]{2,1,0:T(8,128)}, s32[8,8,3072]{2,1,0:T(8,128)}, s32[8,3072]{1,0:T(8,128)S(1)}) custom-call(s32[2,8]{1,0:T(2,128)S(1)} %broadcast_add_fusion.starts_ref, s32[3,8]{1,0:T(4,128)S(1)} %pad_add_fusion.split_ref, s32[3072,128]{1,0:T(8,128)S(1)} %copy-done.6), custom_call_target="tpu_custom_call" | custom-call | flops 1000000 | bytes 1000000 | tf_op jit(solution)/shard_map/pallas_call | solution.py:243
  5.9 7.3 %all-to-all-start = ((s32[8,8,3072]{2,1,0:T(8,128)}), s32[8,8,3072]{2,1,0:T(8,128)S(1)}, u32[]{:S(2)}, u32[]{:S(2)}) async-start(s32[8,8,3072]{2,1,0:T(8,128)} %get-tuple-element.13.codes_ref), calls=%async_computation | async-start | bytes 1572864 | tf_op jit(solution)/shard_map/all_to_all | solution.py:263
  13.3 3.0 %collective-permute-start.3 = (f32[32,3328]{1,0:T(8,128)S(1)}, f32[32,3328]{1,0:T(8,128)S(1)}, u32[]{:S(2)}, u32[]{:S(2)}) collective-permute-start(f32[32,3328]{1,0:T(8,128)S(1)} %shard_map.94.info_ref.refs_0_), channel_id=1, source_target_pairs={{0,16},{2,18},{4,20},{6,22},{8,24},{10,26},{12,28},{14,30},{16,0},... | collective-permute-start | bytes 1277960 | tf_op jit(solution)/shard_map/ppermute | solution.py:202
  16.2 1.5 collective-permute-start.1
  17.7 33.9 %collective-permute-done.3.refs_3_ = f32[32,3328]{1,0:T(8,128)S(1)} collective-permute-done((f32[32,3328]{1,0:T(8,128)S(1)}, f32[32,3328]{1,0:T(8,128)S(1)}, u32[]{:S(2)}, u32[]{:S(2)}) %collective-permute-start.3) | collective-permute-done | bytes 426016 | tf_op jit(solution)/shard_map/ppermute | solution.py:202
  51.6 1.4 collective-permute-start
  55.0 7.1 %collective-permute-done.5.refs_5_.refs_1_ = f32[32,3328]{1,0:T(8,128)} collective-permute-done((f32[32,3328]{1,0:T(8,128)S(1)}, f32[32,3328]{1,0:T(8,128)}, u32[]{:S(2)}, u32[]{:S(2)}) %collective-permute-start.5) | collective-permute-done | bytes 426016 | tf_op jit(solution)/shard_map/ppermute | solution.py:202
  62.1 1.7 collective-permute-start.6
  63.9 3.7 %all-to-all-start.1 = ((s32[8,8,3072]{2,1,0:T(8,128)}), s32[8,8,3072]{2,1,0:T(8,128)S(1)}, u32[]{:S(2)}, u32[]{:S(2)}) async-start(s32[8,8,3072]{2,1,0:T(8,128)} %get-tuple-element.15.codes_ref), calls=%async_computation.1 | async-start | bytes 1572864 | tf_op jit(solution)/shard_map/all_to_all | solution.py:263
  67.6 3.0 %shard_map.99.refs_4_ = f32[512,512]{1,0:T(8,128)S(1)} custom-call(s32[8]{0:T(128)S(1)} %xor.6.places_ref, s32[8,8,3072]{2,1,0:T(8,128)} %get-tuple-element.13.codes_ref, f32[32,3328]{1,0:T(8,128)S(1)} %shard_map.94.info_ref.refs_0_), custom_call_target="tpu_custom_call" | custom-call | flops 1000000 | bytes 1000000 | tf_op jit(solution)/shard_map/pallas_call | solution.py:185
  70.6 7.2 %collective-permute-done.2.refs_2_ = f32[32,3328]{1,0:T(8,128)} collective-permute-done((f32[32,3328]{1,0:T(8,128)S(1)}, f32[32,3328]{1,0:T(8,128)}, u32[]{:S(2)}, u32[]{:S(2)}) %collective-permute-start.2) | collective-permute-done | bytes 426016 | tf_op jit(solution)/shard_map/ppermute | solution.py:202
  77.8 7.7 %shard_map.100.refs_2_ = f32[512,512]{1,0:T(8,128)S(1)} custom-call(s32[8]{0:T(128)S(1)} %iota_xor_fusion.places_ref, s32[8,8,3072]{2,1,0:T(8,128)S(1)} %all-to-all-done.codes_ref, f32[32,3328]{1,0:T(8,128)S(1)} %collective-permute-done.refs_0_, f32[32,3328]{1,0:T(8,128)S(1)} %collective-permute-done.1.refs_1_, f32[32,3328]{1,0:T(8,128)} %collective-permute-done.2.refs_2_, ...), custom_call_target="tpu_custom_call" | custom-call | flops 1000000 | bytes 1000000 | tf_op jit(solution)/shard_map/pallas_call | solution.py:185
  85.5 3.5 %collective-permute-done.4.refs_4_.refs_0_ = f32[32,3328]{1,0:T(8,128)} collective-permute-done((f32[32,3328]{1,0:T(8,128)S(1)}, f32[32,3328]{1,0:T(8,128)}, u32[]{:S(2)}, u32[]{:S(2)}) %collective-permute-start.4) | collective-permute-done | bytes 426016 | tf_op jit(solution)/shard_map/ppermute | solution.py:202
  89.0 4.6 %shard_map.101.refs_1_ = f32[512,512]{1,0:T(8,128)S(1)} custom-call(s32[8]{0:T(128)S(1)} %iota_xor_fusion.places_ref, s32[8,8,3072]{2,1,0:T(8,128)S(1)} %all-to-all-done.codes_ref, f32[32,3328]{1,0:T(8,128)} %collective-permute-done.4.refs_4_.refs_0_, f32[32,3328]{1,0:T(8,128)} %collective-permute-done.5.refs_5_.refs_1_, f32[512,512]{1,0:T(8,128)S(1)} %shard_map.100.refs_2_), custom_call_target="tpu_custom_call" | custom-call | flops 1000000 | bytes 1000000 | tf_op jit(solution)/shard_map/pallas_call | solution.py:185
  93.6 3.3 %collective-permute-done.6.refs_6_.refs_0_ = f32[32,3328]{1,0:T(8,128)} collective-permute-done((f32[32,3328]{1,0:T(8,128)}, f32[32,3328]{1,0:T(8,128)}, u32[]{:S(2)}, u32[]{:S(2)}) %collective-permute-start.6) | collective-permute-done | bytes 426016 | tf_op jit(solution)/shard_map/ppermute | solution.py:202
  96.9 3.8 %shard_map.102 = f32[512,512]{1,0:T(8,128)} custom-call(s32[8]{0:T(128)S(1)} %iota_xor_fusion.places_ref, s32[8,8,3072]{2,1,0:T(8,128)S(1)} %all-to-all-done.codes_ref, f32[32,3328]{1,0:T(8,128)} %collective-permute-done.6.refs_6_.refs_0_, f32[512,512]{1,0:T(8,128)S(1)} %shard_map.101.refs_1_), custom_call_target="tpu_custom_call" | custom-call | flops 1000000 | bytes 1000000 | tf_op jit(solution)/shard_map/pallas_call | solution.py:185
  101.8 69.4 %all-gather.1 = f32[512,64]{1,0:T(8,128)S(1)} all-gather(f32[16,64]{1,0:T(8,128)S(1)} %get-tuple-element.12), channel_id=3, replica_groups=mesh['rows'=16,'feat'=2] {'rows','feat'}, dimensions={0}, use_global_device_ids=true | all-gather | bytes 135168 | tf_op jit(solution)/shard_map/all_gather | solution.py:290
  171.2 4.6 %all-gather.2 = f32[2,1,3072]{2,1,0:T(1,128)S(1)} all-gather(f32[1,1,3072]{2,1,0:T(1,128)S(1)} %bitcast.17), channel_id=2, replica_groups=mesh['rows'=16,'feat'=2] {'feat'}, dimensions={0}, use_global_device_ids=true | all-gather | bytes 36864 | tf_op jit(solution)/shard_map/all_gather | solution.py:289
  175.8 3.0 %shard_map.97.refs_7_ = f32[512,512]{1,0:T(8,128)S(1)} custom-call(s32[8]{0:T(128)S(1)} %xor.6.places_ref, s32[8,8,3072]{2,1,0:T(8,128)} %get-tuple-element.15.codes_ref, f32[32,3328]{1,0:T(8,128)S(1)} %shard_map.94.info_ref.refs_0_), custom_call_target="tpu_custom_call" | custom-call | flops 1000000 | bytes 1000000 | tf_op jit(solution)/shard_map/pallas_call | solution.py:185
  180.0 12.9 %shard_map.98.kept_ref = f32[512,512]{1,0:T(8,128)S(1)} custom-call(s32[8]{0:T(128)S(1)} %iota_xor_fusion.places_ref, s32[8,8,3072]{2,1,0:T(8,128)S(1)} %all-to-all-done.1.codes_ref, f32[32,3328]{1,0:T(8,128)S(1)} %copy-done.3, f32[32,3328]{1,0:T(8,128)S(1)} %copy-done.1, f32[32,3328]{1,0:T(8,128)} %collective-permute-done.2.refs_2_, ...), custom_call_target="tpu_custom_call" | custom-call | flops 1000000 | bytes 1000000 | tf_op jit(solution)/shard_map/pallas_call | solution.py:185
  192.9 3.3 %shard_map.103 = f32[8,8,128]{2,1,0:T(8,128)} custom-call(f32[512,512]{1,0:T(8,128)S(1)} %shard_map.98.kept_ref, f32[512,512]{1,0:T(8,128)} %collective-permute-done.7.came_ref), custom_call_target="tpu_custom_call" | custom-call | flops 1000000 | bytes 1000000 | tf_op jit(solution)/shard_map/pallas_call | solution.py:312
  196.2 3.3 %all-to-all-start.2 = ((f32[8,8,128]{2,1,0:T(8,128)}), f32[8,8,128]{2,1,0:T(8,128)S(1)}, u32[]{:S(2)}, u32[]{:S(2)}) async-start(f32[8,8,128]{2,1,0:T(8,128)} %shard_map.103), calls=%async_computation.2 | async-start | bytes 65536 | tf_op jit(solution)/shard_map/all_to_all | solution.py:322
  200.7 5.5 %all-to-all-done.2 = f32[8,8,128]{2,1,0:T(8,128)S(1)} async-done(((f32[8,8,128]{2,1,0:T(8,128)}), f32[8,8,128]{2,1,0:T(8,128)S(1)}, u32[]{:S(2)}, u32[]{:S(2)}) %all-to-all-start.2) | async-done | bytes 32800 | tf_op jit(solution)/shard_map/all_to_all | solution.py:322
  (43 shorter events, 7.6 us)
Async XLA Ops:
  2.2 1.4 copy-start.6
  3.6 9.6 %copy-start.4 = (f32[3072,32]{0,1:T(8,128)S(1)}, f32[3072,32]{0,1:T(8,128)}, u32[]{:S(2)}) copy-start(f32[3072,32]{0,1:T(8,128)} %param.7) | copy-start | bytes 1179652
  3.6 9.6 %copy-start.7 = (s32[3072]{0:T(1024)S(1)}, s32[3072]{0:T(1024)}, u32[]{:S(2)}) copy-start(s32[3072]{0:T(1024)} %param.9) | copy-start | bytes 36868
  3.6 9.6 %copy-start.8 = (s32[3072]{0:T(1024)S(1)}, s32[3072]{0:T(1024)}, u32[]{:S(2)}) copy-start(s32[3072]{0:T(1024)} %param.8) | copy-start | bytes 36868
  5.9 58.0 %all-to-all-start = ((s32[8,8,3072]{2,1,0:T(8,128)}), s32[8,8,3072]{2,1,0:T(8,128)S(1)}, u32[]{:S(2)}, u32[]{:S(2)}) async-start(s32[8,8,3072]{2,1,0:T(8,128)} %get-tuple-element.13.codes_ref), calls=%async_computation | async-start | bytes 1572864 | tf_op jit(solution)/shard_map/all_to_all | solution.py:263
  13.3 38.3 %collective-permute-start.3 = (f32[32,3328]{1,0:T(8,128)S(1)}, f32[32,3328]{1,0:T(8,128)S(1)}, u32[]{:S(2)}, u32[]{:S(2)}) collective-permute-start(f32[32,3328]{1,0:T(8,128)S(1)} %shard_map.94.info_ref.refs_0_), channel_id=1, source_target_pairs={{0,16},{2,18},{4,20},{6,22},{8,24},{10,26},{12,28},{14,30},{16,0},... | collective-permute-start | bytes 1277960 | tf_op jit(solution)/shard_map/ppermute | solution.py:202
  16.2 36.7 %collective-permute-start.1 = (f32[32,3328]{1,0:T(8,128)S(1)}, f32[32,3328]{1,0:T(8,128)S(1)}, u32[]{:S(2)}, u32[]{:S(2)}) collective-permute-start(f32[32,3328]{1,0:T(8,128)S(1)} %shard_map.94.info_ref.refs_0_), channel_id=1, source_target_pairs={{0,8},{2,10},{4,12},{6,14},{8,0},{10,2},{12,4},{14,6},{16,24},{18,... | collective-permute-start | bytes 1277960 | tf_op jit(solution)/shard_map/ppermute | solution.py:202
  51.6 10.5 %collective-permute-start.5 = (f32[32,3328]{1,0:T(8,128)S(1)}, f32[32,3328]{1,0:T(8,128)}, u32[]{:S(2)}, u32[]{:S(2)}) collective-permute-start(f32[32,3328]{1,0:T(8,128)S(1)} %collective-permute-done.3.refs_3_), channel_id=1, source_target_pairs={{0,8},{2,10},{4,12},{6,14},{8,0},{10,2},{12,4},{14,6},{16,24},{18,... | collective-permute-start | bytes 1277960 | tf_op jit(solution)/shard_map/ppermute | solution.py:202
  51.6 19.0 %collective-permute-start = (f32[32,3328]{1,0:T(8,128)S(1)}, f32[32,3328]{1,0:T(8,128)S(1)}, u32[]{:S(2)}, u32[]{:S(2)}) collective-permute-start(f32[32,3328]{1,0:T(8,128)S(1)} %shard_map.94.info_ref.refs_0_), channel_id=1, source_target_pairs={{0,4},{2,6},{4,0},{6,2},{8,12},{10,14},{12,8},{14,10},{16,20},{18,... | collective-permute-start | bytes 1277960 | tf_op jit(solution)/shard_map/ppermute | solution.py:202
  53.0 24.8 %copy-start = (f32[32,3328]{1,0:T(8,128)}, f32[32,3328]{1,0:T(8,128)S(1)}, u32[]{:S(2)}) copy-start(f32[32,3328]{1,0:T(8,128)S(1)} %collective-permute-done.1.refs_1_) | copy-start | bytes 1277956
  53.0 24.8 %collective-permute-start.2 = (f32[32,3328]{1,0:T(8,128)S(1)}, f32[32,3328]{1,0:T(8,128)}, u32[]{:S(2)}, u32[]{:S(2)}) collective-permute-start(f32[32,3328]{1,0:T(8,128)S(1)} %collective-permute-done.1.refs_1_), channel_id=1, source_target_pairs={{0,4},{2,6},{4,0},{6,2},{8,12},{10,14},{12,8},{14,10},{16,20},{18,... | collective-permute-start | bytes 1277960 | tf_op jit(solution)/shard_map/ppermute | solution.py:202
  53.6 35.4 %collective-permute-start.4 = (f32[32,3328]{1,0:T(8,128)S(1)}, f32[32,3328]{1,0:T(8,128)}, u32[]{:S(2)}, u32[]{:S(2)}) collective-permute-start(f32[32,3328]{1,0:T(8,128)S(1)} %collective-permute-done.3.refs_3_), channel_id=1, source_target_pairs={{0,4},{2,6},{4,0},{6,2},{8,12},{10,14},{12,8},{14,10},{16,20},{18,... | collective-permute-start | bytes 1277960 | tf_op jit(solution)/shard_map/ppermute | solution.py:202
  62.1 34.8 %collective-permute-start.6 = (f32[32,3328]{1,0:T(8,128)}, f32[32,3328]{1,0:T(8,128)}, u32[]{:S(2)}, u32[]{:S(2)}) collective-permute-start(f32[32,3328]{1,0:T(8,128)} %collective-permute-done.5.refs_5_.refs_1_), channel_id=1, source_target_pairs={{0,4},{2,6},{4,0},{6,2},{8,12},{10,14},{12,8},{14,10},{16,20},{18,... | collective-permute-start | bytes 1277960 | tf_op jit(solution)/shard_map/ppermute | solution.py:202
  63.9 115.1 %all-to-all-start.1 = ((s32[8,8,3072]{2,1,0:T(8,128)}), s32[8,8,3072]{2,1,0:T(8,128)S(1)}, u32[]{:S(2)}, u32[]{:S(2)}) async-start(s32[8,8,3072]{2,1,0:T(8,128)} %get-tuple-element.15.codes_ref), calls=%async_computation.1 | async-start | bytes 1572864 | tf_op jit(solution)/shard_map/all_to_all | solution.py:263
  70.6 14.9 %copy-start.2 = (f32[32,3328]{1,0:T(8,128)}, f32[32,3328]{1,0:T(8,128)S(1)}, u32[]{:S(2)}) copy-start(f32[32,3328]{1,0:T(8,128)S(1)} %collective-permute-done.refs_0_) | copy-start | bytes 1277956
  100.7 92.2 %collective-permute-start.7 = (f32[512,512]{1,0:T(8,128)}, f32[512,512]{1,0:T(8,128)}, u32[]{:S(2)}, u32[]{:S(2)}) collective-permute-start(f32[512,512]{1,0:T(8,128)} %shard_map.102), channel_id=1, source_target_pairs={{0,2},{2,0},{4,6},{6,4},{8,10},{10,8},{12,14},{14,12},{16,18},{18,... | collective-permute-start | bytes 3145736 | tf_op jit(solution)/shard_map/ppermute | solution.py:202
  101.8 77.2 %copy-start.1 = (f32[32,3328]{1,0:T(8,128)S(1)}, f32[32,3328]{1,0:T(8,128)}, u32[]{:S(2)}) copy-start(f32[32,3328]{1,0:T(8,128)} %copy-done) | copy-start | bytes 1277956
  178.9 20.7 %copy-start.9 = (f32[8,2,32]{2,1,0:T(2,128)}, f32[8,2,32]{2,1,0:T(2,128)S(1)}, u32[]{:S(2)}) copy-start(f32[8,2,32]{2,1,0:T(2,128)S(1)} %fusion.2) | copy-start | bytes 6148
  178.9 1.0 copy-start.3
  192.9 6.7 %copy-start.5 = (f32[3072,32]{0,1:T(8,128)S(1)}, f32[3072,32]{0,1:T(8,128)}, u32[]{:S(2)}) copy-start(f32[3072,32]{0,1:T(8,128)} %param.7) | copy-start | bytes 1179652
  196.2 10.0 %all-to-all-start.2 = ((f32[8,8,128]{2,1,0:T(8,128)}), f32[8,8,128]{2,1,0:T(8,128)S(1)}, u32[]{:S(2)}, u32[]{:S(2)}) async-start(f32[8,8,128]{2,1,0:T(8,128)} %shard_map.103), calls=%async_computation.2 | async-start | bytes 65536 | tf_op jit(solution)/shard_map/all_to_all | solution.py:322

commit v4 on v2

v4 whole, which is shorter than its diff:
```python
import functools

import jax
import jax.numpy as jnp
from jax import lax
from jax.experimental import pallas as pl
from jax.experimental.pallas import tpu as pltpu
from jax.sharding import PartitionSpec as P

BINS = 64
LANES = 128
SMALL_COST = pl.CostEstimate(flops=1000000, bytes_accessed=1000000, transcendentals=0)


reg_lambda = 1.0
step_size = 0.3


def split_score(sums, classes):
    grad_part = sums[..., :classes]
    hess_part = sums[..., classes:]
    return jnp.sum(grad_part * grad_part / (hess_part + reg_lambda), axis=-1)


def three_parts(x):
    first = x.astype(jnp.bfloat16)
    rest = x - first.astype(jnp.float32)
    second = rest.astype(jnp.bfloat16)
    third = (rest - second.astype(jnp.float32)).astype(jnp.bfloat16)
    return first, second, third


def threshold_masks():
    row = lax.broadcasted_iota(jnp.int32, (2 * BINS, 4 * BINS), 0)
    col = lax.broadcasted_iota(jnp.int32, (2 * BINS, 4 * BINS), 1)
    bin_of = row % BINS
    threshold = col % BINS
    first_dir = (col // BINS) % 2 == 0
    below = (bin_of < threshold) & (bin_of < BINS - 1)
    missing = (bin_of == BINS - 1) & first_dir
    same = row // BINS == col // (2 * BINS)
    return jnp.where((below | missing) & same, 1.0, 0.0).astype(jnp.bfloat16)


def read_info(info, rows):
    chunks = rows // LANES
    prob = info[:, :rows]
    labels = info[:, rows : rows + LANES]
    nodes = info[:, rows + LANES : rows + 2 * LANES]
    label = jnp.concatenate([labels[i : i + 1] for i in range(chunks)], axis=1)
    node = jnp.concatenate([nodes[i : i + 1] for i in range(chunks)], axis=1)
    return prob, label, node


def prep_kernel(
    own, blocks, starts_ref, split_ref, logits_ref, labels_ref, nodes_ref, codes_ref, *refs
):
    outs, flag_ref, turned = refs[: len(blocks)], refs[-2], refs[-1]
    classes, rows = logits_ref.shape
    chunks = rows // LANES
    turned[...] = codes_ref[...].T
    for (with_info, pieces), out_ref in zip(blocks, outs):
        base = classes if with_info else 0
        for i, (taker, quarter) in enumerate(pieces):
            start = pl.multiple_of(starts_ref[taker, quarter], own)
            low = base + i * own
            out_ref[low : low + own, :rows] = turned[pl.ds(start, own), :].astype(out_ref.dtype)
            if with_info:
                out_ref[low : low + own, rows:] = jnp.zeros((own, 2 * LANES), out_ref.dtype)
    expo_vals = jnp.exp(logits_ref[...])
    prob = expo_vals / jnp.sum(expo_vals, axis=0, keepdims=True)
    labels = labels_ref[...].astype(jnp.float32)
    nodes = nodes_ref[...].astype(jnp.float32)
    label = jnp.concatenate([labels[i : i + 1] for i in range(chunks)], axis=1)
    node = jnp.concatenate([nodes[i : i + 1] for i in range(chunks)], axis=1)

    feats = turned.shape[0]
    node_count = split_ref.shape[1]
    side = jnp.zeros((1, rows), jnp.float32)
    for n in range(node_count):
        col = split_ref[0, n]
        held = (col >= 0) & (col < feats)
        code = turned[pl.ds(jnp.clip(col, 0, feats - 1), 1), :]
        threshold = jnp.where(held, split_ref[1, n], -1)
        missing = jnp.where(held & (split_ref[2, n] == 1), BINS - 1, -1)
        left = (code < threshold) | (code == missing)
        value = jnp.where(left, 1.0, jnp.where(held, 2.0, 0.0))
        side = jnp.where(node == float(n), value, side)
    flag_ref[...] = jnp.where(side == 2.0, 1.0, 0.0)
    hot = jnp.concatenate(
        [
            jnp.where((node == float(slot // 2)) & (side == float(slot % 2 + 1)), 1.0, 0.0)
            for slot in range(2 * node_count)
        ],
        axis=0,
    ).astype(jnp.bfloat16)
    sums = lax.dot_general(
        hot,
        gradients(prob, label).astype(jnp.bfloat16),
        (((1,), (1,)), ((), ())),
        preferred_element_type=jnp.float32,
    )
    sums = jnp.concatenate([sums[:node_count], sums[node_count:]], axis=1)
    for (with_info, _), out_ref in zip(blocks, outs):
        if with_info:
            out_ref[:classes, :rows] = prob
            out_ref[:chunks, rows : rows + LANES] = labels
            out_ref[:chunks, rows + LANES :] = nodes
            if chunks < classes - node_count:
                out_ref[chunks : classes - node_count, rows : rows + LANES] = jnp.zeros(
                    (classes - node_count - chunks, LANES), jnp.float32
                )
            out_ref[classes - node_count : classes, rows : rows + LANES] = sums
            out_ref[chunks:classes, rows + LANES :] = jnp.zeros(
                (classes - chunks, LANES), jnp.float32
            )


def gradients(prob, label):
    class_iota = lax.broadcasted_iota(jnp.int32, prob.shape, 0).astype(jnp.float32)
    target = jnp.where(class_iota == label, 1.0, 0.0)
    return jnp.concatenate([prob - target, prob * (1.0 - prob)], axis=0)


def masked_gradients(info, rows, node_count):
    prob, label, node = read_info(info, rows)
    grad_hess = gradients(prob, label)
    return jnp.concatenate(
        [jnp.where(node == float(n), grad_hess, 0.0).astype(jnp.bfloat16) for n in range(node_count)],
        axis=0,
    )


def one_hot(codes):
    feats, rows = codes.shape
    bin_iota = lax.broadcasted_iota(jnp.int32, (BINS, rows), 0).astype(codes.dtype)
    return jnp.concatenate(
        [
            jnp.where(codes[f : f + 1, :] == bin_iota, 1.0, 0.0).astype(jnp.bfloat16)
            for f in range(feats)
        ],
        axis=0,
    )


def write_gains(hist_ref, gain_ref, classes, node_count):
    masks = threshold_masks()
    ones = jnp.where(
        lax.broadcasted_iota(jnp.int32, (2 * BINS, 4 * BINS), 0) < BINS, 1.0, 0.0
    ).astype(jnp.bfloat16)

    def times(parts, right):
        return sum(jnp.dot(part, right, preferred_element_type=jnp.float32) for part in parts)

    total = times(three_parts(hist_ref[:, : 2 * BINS]), ones)
    for pair in range(gain_ref.shape[1] // 2):
        span = slice(pair * 2 * BINS, (pair + 1) * 2 * BINS)
        left = times(three_parts(hist_ref[:, span]), masks)
        right = total - left
        for n in range(node_count):
            grads = slice(n * 2 * classes, n * 2 * classes + classes)
            hesss = slice(n * 2 * classes + classes, (n + 1) * 2 * classes)
            score = (
                left[grads] * left[grads] / (left[hesss] + reg_lambda)
                + right[grads] * right[grads] / (right[hesss] + reg_lambda)
            )
            parent = total[grads] * total[grads] / (total[hesss] + reg_lambda)
            gain = (
                jnp.sum(score, axis=0, keepdims=True) - jnp.sum(parent, axis=0, keepdims=True)
            ) / (2.0 * classes)
            gain_ref[n, 2 * pair : 2 * pair + 1, :] = gain[:, : 2 * BINS]
            gain_ref[n, 2 * pair + 1 : 2 * pair + 2, :] = gain[:, 2 * BINS :]


def add_kernel(classes, node_count, own, plan, place_ref, *refs):
    outs = len(plan[0][2])
    arrays = 1 + max(max(c, i) for c, i, _ in plan)
    out_refs = refs[-outs:]
    held_refs = refs[arrays:-outs]
    pairs = 2 * classes * node_count
    for s, (codes_at, info_at, firsts) in enumerate(plan):
        codes_ref, info_ref = refs[codes_at], refs[info_at]
        rows = info_ref.shape[1] - 2 * LANES
        if len(codes_ref.shape) == 3:
            codes_ref = codes_ref.at[place_ref[0, s]]
        info = info_ref[:classes, :]
        masked = masked_gradients(info, rows, node_count)
        sums = info[classes - node_count :, rows : rows + LANES]
        for i, first in enumerate(firsts):
            out_ref = out_refs[i]
            product = lax.dot_general(
                masked,
                one_hot(codes_ref[first : first + own, :rows]),
                (((1,), (1,)), ((), ())),
                preferred_element_type=jnp.float32,
            )
            if s == 0:
                if held_refs:
                    out_ref[...] = sum(ref[...] for ref in held_refs[i::outs])
                else:
                    out_ref[...] = jnp.zeros(out_ref.shape, out_ref.dtype)
            out_ref[:pairs, :] += product
            for line in range(out_ref.shape[1] // LANES):
                here = jnp.where(place_ref[0, s] == line, 1.0, 0.0)
                band = pl.ds(pl.multiple_of(pairs + place_ref[1, s] * node_count, node_count), node_count)
                out_ref[band, line * LANES : (line + 1) * LANES] += here * sums


def add_rows(classes, node_count, own, plan, places, arrays, *held):
    shape = (2 * classes * node_count + 4 * node_count, own * BINS)
    whole = pl.BlockSpec(memory_space=pltpu.VMEM)
    outs = len(plan[0][2])
    return pl.pallas_call(
        functools.partial(add_kernel, classes, node_count, own, plan),
        in_specs=[pl.BlockSpec(memory_space=pltpu.SMEM)]
        + [whole] * (len(arrays) + len(held) * outs),
        out_specs=[whole] * outs,
        out_shape=[jax.ShapeDtypeStruct(shape, jnp.float32)] * outs,
        compiler_params=pltpu.CompilerParams(vmem_limit_bytes=32 * 1024 * 1024),
        cost_estimate=SMALL_COST,
    )(places, *arrays, *[hist for hists in held for hist in hists])


def gain_kernel(classes, node_count, *refs):
    gain_ref, hist_ref = refs[-2:]
    hist_ref[...] = sum(ref[: hist_ref.shape[0], :] for ref in refs[:-2])
    write_gains(hist_ref, gain_ref, classes, node_count)


def swap(x, axis, bit):
    size = lax.axis_size(axis)
    return lax.ppermute(x, axis, [(i, i ^ bit) for i in range(size)])


def sum_over(x, axis):
    bit = 1
    while bit < lax.axis_size(axis):
        x = x + swap(x, axis, bit)
        bit *= 2
    return x


def prepare(blocks, starts, logits_t, labels, node_ids, bin_codes, splits):
    classes, rows_dev = logits_t.shape
    feats_dev = bin_codes.shape[1]
    own = 8
    whole = pl.BlockSpec(memory_space=pltpu.VMEM)
    scalars = pl.BlockSpec(memory_space=pltpu.SMEM)
    shapes = []
    for with_info, pieces in blocks:
        codes = len(pieces) * own
        if with_info:
            shape = (classes + codes, rows_dev + 2 * LANES)
            shapes.append(jax.ShapeDtypeStruct(shape, jnp.float32))
        else:
            shapes.append(jax.ShapeDtypeStruct((codes, rows_dev), jnp.int32))
    return pl.pallas_call(
        functools.partial(prep_kernel, own, blocks),
        in_specs=[scalars, scalars] + [whole] * 4,
        out_specs=[whole] * (len(blocks) + 1),
        out_shape=shapes + [jax.ShapeDtypeStruct((1, rows_dev), jnp.float32)],
        scratch_shapes=[pltpu.VMEM((feats_dev, rows_dev), jnp.int32)],
        compiler_params=pltpu.CompilerParams(vmem_limit_bytes=20 * 1024 * 1024),
        cost_estimate=SMALL_COST,
    )(
        starts,
        splits,
        logits_t,
        labels.reshape(-1, LANES),
        node_ids.reshape(-1, LANES),
        bin_codes,
    )


def child_sums(info, rows_dev, classes, node_count):
    return info[classes - node_count : classes, rows_dev : rows_dev + LANES]


def finish(logits_t, node_ids, side_count, sums, node_count):
    classes = logits_t.shape[0]
    width = 2 * classes
    side_sums = jnp.concatenate([sums[:, :width], sums[:, width:]], axis=0)
    side_sums = side_sums.reshape(node_count, 2, width)
    leaves = -side_sums[..., :classes] / (side_sums[..., classes:] + reg_lambda)
    row_side = (side_count > 0.5).astype(jnp.int32)
    slot_iota = jnp.arange(2 * node_count, dtype=jnp.int32)
    slot_hot = (node_ids[None, :] * 2 + row_side) == slot_iota[:, None]
    update = jnp.dot(
        leaves.reshape(2 * node_count, classes).T,
        slot_hot.astype(jnp.float32),
        precision=lax.Precision.HIGHEST,
    )
    return (logits_t + step_size * update).T, leaves


def local(logits, labels, node_ids, bin_codes, split_feature, split_bin, split_missing):
    rows_dev, classes = logits.shape
    feats_dev = bin_codes.shape[1]
    node_count = split_feature.shape[0]
    n_rows = lax.axis_size("rows")
    per_node = n_rows // node_count
    pairs_dev = feats_dev // per_node
    width = 2 * classes
    own = 8
    row_index = lax.axis_index("rows")
    feat_index = lax.axis_index("feat")
    splits = jnp.stack([split_feature - feat_index * feats_dev, split_bin, split_missing])
    logits_t = logits.T
    add = functools.partial(add_rows, classes, node_count, own)
    if feats_dev != own * n_rows or n_rows != 16:
        return by_groups(
            logits_t, labels, node_ids, bin_codes, splits, row_index, per_node, pairs_dev
        )

    starts = []
    for taker in [row_index ^ m for m in (0, 4, 8, 12)] + [z * 4 + row_index % 4 for z in range(4)]:
        takers = [taker ^ low for low in (3, 2, 1, 0)]
        starts.append(jnp.stack([t % per_node * pairs_dev + t // per_node * own for t in takers]))
    starts = jnp.stack(starts)
    blocks = (
        (True, ((0, 0), (0, 1), (0, 2), (0, 3))),
        (True, ((1, 0), (1, 1))),
        (True, ((2, 0), (2, 1))),
        (False, ((3, 0), (3, 1))),
        (False, tuple((4 + z, quarter) for z in range(4) for quarter in (2, 3))),
    )
    rows_0, rows_4, rows_8, codes_12, codes_late, flags = prepare(
        blocks, starts, logits_t, labels, node_ids, bin_codes, splits
    )

    def place(*lines):
        line = jnp.stack([row_index // 4 ^ m // 4 for m in lines])
        return jnp.stack([line, jnp.zeros_like(line) + row_index % 4])

    first, second, third, fourth = [classes + i * own for i in range(4)]
    rows_8 = swap(rows_8, "rows", 8)
    rows_4 = swap(rows_4, "rows", 4)
    codes_12 = swap(codes_12, "rows", 12)
    hist_a, hist_b, hist_c, hist_d = add(((0, 0, (first, second, third, fourth)),), place(0), [rows_0])
    hist_a, hist_b, codes_late, rows_8 = lax.optimization_barrier(
        (hist_a, hist_b, codes_late, rows_8)
    )
    lines = [[4 * z + low for z in range(4)] for low in range(4)]
    codes_late = lax.all_to_all(
        codes_late.reshape(4, 2 * own, rows_dev), "rows", 0, 0, tiled=True, axis_index_groups=lines
    )
    info_12 = swap(rows_8[:classes], "rows", 4)
    hists = add(((0, 0, (first, second)),), place(4), [rows_4], [hist_a, hist_b])
    hist_a, hist_b = add(((0, 0, (first, second)),), place(8), [rows_8], hists)
    (to_core,) = add(((0, 1, (0,)),), place(12), [codes_12, info_12], [hist_a])
    from_core = swap(to_core, "rows", 1)
    (to_plane,) = add(((0, 1, (own,)),), place(12), [codes_12, info_12], [hist_b], [from_core])
    to_plane, codes_late = lax.optimization_barrier((to_plane, codes_late))
    from_plane = swap(to_plane, "rows", 2)
    late = [codes_late, rows_4, rows_8, info_12]
    (to_core,) = add(tuple((0, i, (0,)) for i in (1, 2, 3)), place(4, 8, 12), late, [hist_c])
    from_core = swap(to_core, "rows", 1)
    (kept,) = add(tuple((0, i, (own,)) for i in (1, 2, 3)), place(4, 8, 12), late, [hist_d])

    pairs = node_count * width
    parts = from_core[pairs:] + from_plane[pairs:] + kept[pairs:]
    sums = jnp.sum(parts.reshape(4, node_count, -1, LANES), axis=(0, 2))
    children = jnp.concatenate([sums, flags.reshape(-1, LANES)], axis=0)
    children = sum_over(children, "feat")
    side_count = children[node_count:].reshape(1, rows_dev)
    new_logits, leaves = finish(logits_t, node_ids, side_count, children[:node_count], node_count)

    gains = pl.pallas_call(
        functools.partial(gain_kernel, classes, node_count),
        in_specs=[pl.BlockSpec(memory_space=pltpu.VMEM)] * 3,
        out_specs=pl.BlockSpec(memory_space=pltpu.VMEM),
        out_shape=jax.ShapeDtypeStruct((node_count, own, 2 * BINS), jnp.float32),
        scratch_shapes=[pltpu.VMEM((pairs, own * BINS), jnp.float32)],
        compiler_params=pltpu.CompilerParams(vmem_limit_bytes=16 * 1024 * 1024),
        cost_estimate=SMALL_COST,
    )(from_core, from_plane, kept)
    halves = [[h + n * per_node for n in range(node_count)] for h in range(per_node)]
    gain_rows = lax.all_to_all(gains, "rows", 0, 0, tiled=True, axis_index_groups=halves)
    return (new_logits, gain_rows.reshape(1, pairs_dev, 2 * BINS), leaves)


def by_groups(logits_t, labels, node_ids, bin_codes, splits, row_index, per_node, pairs_dev):
    classes, rows_dev = logits_t.shape
    feats_dev = bin_codes.shape[1]
    node_count = splits.shape[1]
    n_rows = lax.axis_size("rows")
    width = 2 * classes
    own = 8
    group = feats_dev // own
    group_count = n_rows // group
    starts = jnp.arange(group, dtype=jnp.int32)[:, None] * own
    blocks = tuple((True, ((r, 0),)) for r in range(group))
    *rows_out, flags = prepare(blocks, starts, logits_t, labels, node_ids, bin_codes, splits)
    members = [[g * group + r for r in range(group)] for g in range(group_count)]
    rows_in = lax.all_to_all(
        jnp.stack(rows_out), "rows", 0, 0, tiled=True, axis_index_groups=members
    )
    hists = []
    for r in range(group):
        held = [hists] if hists else []
        nowhere = jnp.full((2, 1), -1, jnp.int32) * jnp.array([[1], [0]], jnp.int32)
        hists = add_rows(
            classes, node_count, own, ((0, 0, (classes,)),), nowhere, [rows_in[r]], *held
        )
    sums = lax.psum(child_sums(rows_out[0], rows_dev, classes, node_count), ("rows", "feat"))
    side_count = lax.psum(flags, "feat")
    new_logits, leaves = finish(logits_t, node_ids, side_count, sums, node_count)

    cuts = own // pairs_dev
    hist = hists[0][: node_count * width]
    hist = hist.reshape(node_count, width, cuts, pairs_dev, BINS).transpose(0, 2, 3, 4, 1)
    peers = [[g * group + r for g in range(group_count)] for r in range(group)]
    owned = lax.psum_scatter(
        hist.reshape(group_count, pairs_dev, BINS, width),
        "rows",
        scatter_dimension=0,
        axis_index_groups=peers,
    )
    bin_iota = jnp.arange(BINS, dtype=jnp.int32)
    lower_mask = (
        (bin_iota[:, None] < bin_iota[None, :]) & (bin_iota[:, None] < BINS - 1)
    ).astype(jnp.float32)
    left_base = jnp.einsum("pbc,bt->ptc", owned, lower_mask, precision=lax.Precision.HIGHEST)
    node_total = jnp.sum(owned, axis=1, keepdims=True)
    left_miss = left_base + owned[:, BINS - 1 :, :]
    parent_score = split_score(node_total, classes)
    gain_left = (
        split_score(left_miss, classes)
        + split_score(node_total - left_miss, classes)
        - parent_score
    )
    gain_right = (
        split_score(left_base, classes)
        + split_score(node_total - left_base, classes)
        - parent_score
    )
    gain = jnp.concatenate([gain_left, gain_right], axis=1) / (2.0 * classes)
    moves = [
        (n * per_node + cut * group + r, n * per_node + r * cuts + cut)
        for n in range(node_count)
        for cut in range(cuts)
        for r in range(group)
    ]
    gain_rows = lax.ppermute(gain, "rows", moves)
    return (new_logits, gain_rows[None], leaves)


def solution(mesh):
    return jax.shard_map(
        local,
        mesh=mesh,
        in_specs=(P("rows", None), P("rows"), P("rows"), P("rows", "feat"), P(), P(), P()),
        out_specs=(P("rows", None), P("rows", "feat", None), P()),
        check_vma=False,
    )
```

time: 149 us -> 124 us (0.83)
  starting transfers between devices: 43.7 us -> 22.3 us
  Pallas kernels: 40.9 us -> 36.1 us
  waiting for transfers between devices: 52.9 us -> 48.3 us
  local copies, waits for them, and re-layouts: 9.4 us -> 12.9 us
  between operations: 1.01 us -> 2.53 us
    ppermute x36 -> x8, starting transfers between devices: 40 us -> 12.4 us  [swap(): return lax.ppermute(x, axis, [(i, i ^ bit) for i in range(size)])]
    ppermute x36 -> x8, waiting for transfers between devices: 47.4 us -> 38.7 us  [swap(): return lax.ppermute(x, axis, [(i, i ^ bit) for i in range(size)])]
    all_to_all x1 -> x2, starting transfers between devices: 3.75 us -> 9.95 us  [the longest x1 6.28 us: local(): lax.all_to_all(gains, 'rows', 0, 0, tiled=True, axis_index_groups=halves)]
    pallas_call x7 -> x9, Pallas kernels: 40.9 us -> 36.1 us  [the longest x7 31.4 us: add_rows(): pl.pallas_call(functools.partial(add_kernel, classes, node_count, own, pl...]
    all_to_all x1 -> x2, waiting for transfers between devices: 5.57 us -> 9.57 us  [the longest x1 5.36 us: local(): lax.all_to_all(gains, 'rows', 0, 0, tiled=True, axis_index_groups=halves)]
    unnamed x56 -> x41, local copies, waits for them, and re-layouts: 9.4 us -> 12 us
  transfers between devices with their start and end apart: 37 -> 10, of which waited for: 12 -> 6; matrix products, arithmetic and copies ran while one was open for 2% -> 2% of each run, Pallas kernels for 19% -> 23%
where the time goes in v4:
time: 124 us
  waiting for transfers between devices  48.3 us (39%)
  Pallas kernels  36.1 us (29%)
  starting transfers between devices  22.3 us (18%)
  local copies, waits for them, and re-layouts  12.9 us (10%)
  between operations  2.53 us (2%)
    ppermute x8, waiting for transfers between devices, swap(): return lax.ppermute(x, axis, [(i, i ^ bit) for i in range(size)])  38.7 us
    pallas_call x7, Pallas kernels, add_rows(): pl.pallas_call(functools.partial(add_kernel, classes, node_count, own, pl...  31.4 us
    ppermute x8, starting transfers between devices, swap(): return lax.ppermute(x, axis, [(i, i ^ bit) for i in range(size)])  12.4 us
    unnamed x41, local copies, waits for them, and re-layouts  12 us
    all_to_all x1, starting transfers between devices, local(): lax.all_to_all(gains, 'rows', 0, 0, tiled=True, axis_index_groups=halves)  6.28 us
    all_to_all x1, waiting for transfers between devices, local(): lax.all_to_all(gains, 'rows', 0, 0, tiled=True, axis_index_groups=halves)  5.36 us
    all_to_all x1, waiting for transfers between devices, local(): lax.all_to_all(codes_late.reshape(4, 2 * own, rows_dev), 'rows', 0, 0, ti...  4.21 us
    all_to_all x1, starting transfers between devices, local(): lax.all_to_all(codes_late.reshape(4, 2 * own, rows_dev), 'rows', 0, 0, ti...  3.67 us
  transfers between devices with their start and end apart: 10, of which 6 were waited for; matrix products, arithmetic and copies ran while one was open for 2% of the time, Pallas kernels for 23%

profile of v4, /device:TPU:0, one launch (start us, length us, event | category | flops | bytes accessed | tf_op | source)
XLA Modules:
  0.0 123.7 jit_solution(7427119774652729470)
XLA Ops:
  4.4 2.6 %shard_map.94 = (f32[64,3328]{1,0:T(8,128)S(1)}, f32[48,3328]{1,0:T(8,128)S(1)}, f32[48,3328]{1,0:T(8,128)}, s32[16,3072]{1,0:T(8,128)}, s32[64,3072]{1,0:T(8,128)S(1)}, /*index=5*/f32[1,3072]{1,0:T(1,128)S(1)}) custom-call(s32[8,4]{1,0:T(8,128)S(1)} %stack.253.starts_ref, s32[3,8]{1,0:T(4,128)S(1)} %pad_add_fusion.split_ref, f32[32,3072]{1,0:T(8,128)S(1)} %bitcast.77, ...), custom_call_target="tpu_custom_call" | custom-call | flops 1000000 | bytes 1000000 | tf_op jit(solution)/shard_map/pallas_call | solution.py:257
  7.9 4.0 %collective-permute-start.1 = (f32[48,3328]{1,0:T(8,128)}, f32[48,3328]{1,0:T(8,128)S(1)}, u32[]{:S(2)}, u32[]{:S(2)}) collective-permute-start(f32[48,3328]{1,0:T(8,128)} %get-tuple-element.28), channel_id=1, source_target_pairs={{0,16},{2,18},{4,20},{6,22},{8,24},{10,26},{12,28},{14,30},{16,0},... | collective-permute-start | bytes 1916936 | tf_op jit(solution)/shard_map/ppermute | solution.py:232
  12.0 1.6 %collective-permute-start.3 = (f32[48,3328]{1,0:T(8,128)S(1)}, f32[48,3328]{1,0:T(8,128)S(1)}, u32[]{:S(2)}, u32[]{:S(2)}) collective-permute-start(f32[48,3328]{1,0:T(8,128)S(1)} %get-tuple-element.30), channel_id=1, source_target_pairs={{0,8},{2,10},{4,12},{6,14},{8,0},{10,2},{12,4},{14,6},{16,24},{18,... | collective-permute-start | bytes 1916936 | tf_op jit(solution)/shard_map/ppermute | solution.py:232
  13.5 7.2 %shard_map.95 = (f32[544,512]{1,0:T(8,128)S(1)}, f32[544,512]{1,0:T(8,128)S(1)}, f32[544,512]{1,0:T(8,128)S(1)}, f32[544,512]{1,0:T(8,128)S(1)}) custom-call(s32[2,1]{1,0:T(2,128)S(1)} %pad_add_fusion.3.place_ref, f32[64,3328]{1,0:T(8,128)S(1)} %get-tuple-element.24.refs_0_), custom_call_target="tpu_custom_call" | custom-call | flops 1000000 | bytes 1000000 | tf_op jit(solution)/shard_map/pallas_call | solution.py:213
  24.8 15.5 %collective-permute-done.1.refs_0_.refs_2_ = f32[48,3328]{1,0:T(8,128)S(1)} collective-permute-done((f32[48,3328]{1,0:T(8,128)}, f32[48,3328]{1,0:T(8,128)S(1)}, u32[]{:S(2)}, u32[]{:S(2)}) %collective-permute-start.1) | collective-permute-done | bytes 639008 | tf_op jit(solution)/shard_map/ppermute | solution.py:232
  41.9 2.7 %collective-permute-start = (s32[16,3072]{1,0:T(8,128)}, s32[16,3072]{1,0:T(8,128)S(1)}, u32[]{:S(2)}, u32[]{:S(2)}) collective-permute-start(s32[16,3072]{1,0:T(8,128)} %get-tuple-element.23), channel_id=1, source_target_pairs={{0,24},{2,26},{4,28},{6,30},{8,16},{10,18},{12,20},{14,22},{16,8},... | collective-permute-start | bytes 589832 | tf_op jit(solution)/shard_map/ppermute | solution.py:232
  44.6 3.7 %all-to-all-start = ((s32[4,16,3072]{2,1,0:T(8,128)}), s32[4,16,3072]{2,1,0:T(8,128)S(1)}, u32[]{:S(2)}, u32[]{:S(2)}) async-start(s32[4,16,3072]{2,1,0:T(8,128)} %bitcast.78), calls=%async_computation | async-start | bytes 1572864 | tf_op jit(solution)/shard_map/all_to_all | solution.py:344
  48.3 1.2 %copy-done.10 = f32[544,512]{1,0:T(8,128)S(1)} copy-done((f32[544,512]{1,0:T(8,128)S(1)}, f32[544,512]{1,0:T(8,128)}, u32[]{:S(2)}) %copy-start.10) | copy-done | bytes 1114136
  49.5 1.2 %copy-done.12 = f32[544,512]{1,0:T(8,128)S(1)} copy-done((f32[544,512]{1,0:T(8,128)S(1)}, f32[544,512]{1,0:T(8,128)}, u32[]{:S(2)}) %copy-start.12) | copy-done | bytes 1114136
  50.8 4.0 %shard_map.96 = (f32[544,512]{1,0:T(8,128)S(1)}, f32[544,512]{1,0:T(8,128)S(1)}) custom-call(s32[2,1]{1,0:T(2,128)S(1)} %get-tuple-element.53.place_ref, f32[48,3328]{1,0:T(8,128)S(1)} %collective-permute-done.3.refs_0_.refs_1_, f32[544,512]{1,0:T(8,128)S(1)} %copy-done.10, f32[544,512]{1,0:T(8,128)S(1)} %copy-done.12), custom_call_target="tpu_custom_call" | custom-call | flops 1000000 | bytes 1000000 | tf_op jit(solution)/shard_map/pallas_call | solution.py:213
  54.8 4.0 %shard_map.97 = (f32[544,512]{1,0:T(8,128)S(1)}, f32[544,512]{1,0:T(8,128)S(1)}) custom-call(s32[2,1]{1,0:T(2,128)S(1)} %get-tuple-element.54.place_ref, f32[48,3328]{1,0:T(8,128)S(1)} %collective-permute-done.1.refs_0_.refs_2_, f32[544,512]{1,0:T(8,128)S(1)} %get-tuple-element.33.refs_1_, f32[544,512]{1,0:T(8,128)S(1)} %get-tuple-element.34.refs_2_), custom_call_target="tpu_custom_call" | custom-call | flops 1000000 | bytes 1000000 | tf_op jit(solution)/shard_map/pallas_call | solution.py:213
  59.8 2.4 %shard_map.98 = f32[544,512]{1,0:T(8,128)S(1)} custom-call(s32[2,1]{1,0:T(2,128)S(1)} %pad_add_fusion.4.place_ref, s32[16,3072]{1,0:T(8,128)S(1)} %collective-permute-done.refs_0_, f32[32,3328]{1,0:T(8,128)S(1)} %collective-permute-done.2.refs_1_.refs_3_, f32[544,512]{1,0:T(8,128)S(1)} %get-tuple-element.36.refs_2_), custom_call_target="tpu_custom_call" | custom-call | flops 1000000 | bytes 1000000 | tf_op jit(solution)/shard_map/pallas_call | solution.py:213
  62.3 2.7 %collective-permute-done.4.refs_3_ = f32[544,512]{1,0:T(8,128)S(1)} collective-permute-done((f32[544,512]{1,0:T(8,128)S(1)}, f32[544,512]{1,0:T(8,128)S(1)}, u32[]{:S(2)}, u32[]{:S(2)}) %collective-permute-start.4) | collective-permute-done | bytes 1114144 | tf_op jit(solution)/shard_map/ppermute | solution.py:232
  65.0 2.4 %shard_map.99 = f32[544,512]{1,0:T(8,128)S(1)} custom-call(s32[2,1]{1,0:T(2,128)S(1)} %pad_add_fusion.4.place_ref, s32[16,3072]{1,0:T(8,128)S(1)} %collective-permute-done.refs_0_, f32[32,3328]{1,0:T(8,128)S(1)} %collective-permute-done.2.refs_1_.refs_3_, f32[544,512]{1,0:T(8,128)S(1)} %get-tuple-element.35.refs_2_, ...), custom_call_target="tpu_custom_call" | custom-call | flops 1000000 | bytes 1000000 | tf_op jit(solution)/shard_map/pallas_call | solution.py:213
  68.3 4.2 %all-to-all-done.refs_0_ = s32[4,16,3072]{2,1,0:T(8,128)S(1)} async-done(((s32[4,16,3072]{2,1,0:T(8,128)}), s32[4,16,3072]{2,1,0:T(8,128)S(1)}, u32[]{:S(2)}, u32[]{:S(2)}) %all-to-all-start) | async-done | bytes 786464 | tf_op jit(solution)/shard_map/all_to_all | solution.py:344
  72.6 1.2 %copy-done.6 = f32[544,512]{1,0:T(8,128)S(1)} copy-done((f32[544,512]{1,0:T(8,128)S(1)}, f32[544,512]{1,0:T(8,128)}, u32[]{:S(2)}) %copy-start.6) | copy-done | bytes 1114136
  73.8 5.6 %shard_map.100 = f32[544,512]{1,0:T(8,128)S(1)} custom-call(s32[2,3]{1,0:T(2,128)S(1)} %stack.203.place_ref, s32[4,16,3072]{2,1,0:T(8,128)S(1)} %all-to-all-done.refs_0_, f32[48,3328]{1,0:T(8,128)S(1)} %collective-permute-done.3.refs_0_.refs_1_, f32[48,3328]{1,0:T(8,128)S(1)} %collective-permute-done.1.refs_0_.refs_2_, ...), custom_call_target="tpu_custom_call" | custom-call | flops 1000000 | bytes 1000000 | tf_op jit(solution)/shard_map/pallas_call | solution.py:213
  79.5 1.6 %collective-permute-start.6 = (f32[544,512]{1,0:T(8,128)S(1)}, f32[544,512]{1,0:T(8,128)S(1)}, u32[]{:S(2)}, u32[]{:S(2)}) collective-permute-start(f32[544,512]{1,0:T(8,128)S(1)} %copy-done.8), channel_id=1, source_target_pairs={{0,4},{2,6},{4,0},{6,2},{8,12},{10,14},{12,8},{14,10},{16,20},{18,... | collective-permute-start | bytes 3342344 | tf_op jit(solution)/shard_map/ppermute | solution.py:232
  81.1 5.8 %shard_map.101.refs_2_ = f32[544,512]{1,0:T(8,128)S(1)} custom-call(s32[2,3]{1,0:T(2,128)S(1)} %stack.203.place_ref, s32[4,16,3072]{2,1,0:T(8,128)S(1)} %all-to-all-done.refs_0_, f32[48,3328]{1,0:T(8,128)S(1)} %collective-permute-done.3.refs_0_.refs_1_, f32[48,3328]{1,0:T(8,128)S(1)} %collective-permute-done.1.refs_0_.refs_2_, ...), custom_call_target="tpu_custom_call" | custom-call | flops 1000000 | bytes 1000000 | tf_op jit(solution)/shard_map/pallas_call | solution.py:213
  87.0 19.5 %collective-permute-done.6.refs_1_ = f32[544,512]{1,0:T(8,128)S(1)} collective-permute-done((f32[544,512]{1,0:T(8,128)S(1)}, f32[544,512]{1,0:T(8,128)S(1)}, u32[]{:S(2)}, u32[]{:S(2)}) %collective-permute-start.6) | collective-permute-done | bytes 1114144 | tf_op jit(solution)/shard_map/ppermute | solution.py:232
  106.5 1.6 %collective-permute-start.7 = (f32[32,128]{1,0:T(8,128)S(1)}, f32[32,128]{1,0:T(8,128)S(1)}, u32[]{:S(2)}, u32[]{:S(2)}) collective-permute-start(f32[32,128]{1,0:T(8,128)S(1)} %pad_maximum_fusion), channel_id=1, source_target_pairs={{0,1},{1,0},{2,3},{3,2},{4,5},{5,4},{6,7},{7,6},{8,9},{9,8},{10,11... | collective-permute-start | bytes 49160 | tf_op jit(solution)/shard_map/ppermute | solution.py:232
  108.1 2.1 %shard_map.102 = f32[8,8,128]{2,1,0:T(8,128)} custom-call(f32[544,512]{1,0:T(8,128)S(1)} %collective-permute-done.5.refs_0_, f32[544,512]{1,0:T(8,128)S(1)} %collective-permute-done.6.refs_1_, f32[544,512]{1,0:T(8,128)S(1)} %shard_map.101.refs_2_), custom_call_target="tpu_custom_call" | custom-call | flops 1000000 | bytes 1000000 | tf_op jit(solution)/shard_map/pallas_call | solution.py:368
  110.2 6.3 %all-to-all-start.1 = ((f32[8,8,128]{2,1,0:T(8,128)}), f32[8,8,128]{2,1,0:T(8,128)S(1)}, u32[]{:S(2)}, u32[]{:S(2)}) async-start(f32[8,8,128]{2,1,0:T(8,128)} %shard_map.102), calls=%async_computation.1 | async-start | bytes 65536 | tf_op jit(solution)/shard_map/all_to_all | solution.py:378
  117.8 5.4 %all-to-all-done.1 = f32[8,8,128]{2,1,0:T(8,128)S(1)} async-done(((f32[8,8,128]{2,1,0:T(8,128)}), f32[8,8,128]{2,1,0:T(8,128)S(1)}, u32[]{:S(2)}, u32[]{:S(2)}) %all-to-all-start.1) | async-done | bytes 32800 | tf_op jit(solution)/shard_map/all_to_all | solution.py:378
  (67 shorter events, 12.6 us)
Async XLA Ops:
  0.6 1.6 %copy-start.19 = (s32[8]{0:T(128)S(1)}, s32[8]{0:T(128)}, u32[]{:S(2)}) copy-start(s32[8]{0:T(128)} %param.11) | copy-start | bytes 100
  0.6 1.6 %copy-start.17 = (s32[8]{0:T(128)S(1)}, s32[8]{0:T(128)}, u32[]{:S(2)}) copy-start(s32[8]{0:T(128)} %param.13) | copy-start | bytes 100
  0.7 1.6 %copy-start.18 = (s32[8]{0:T(128)S(1)}, s32[8]{0:T(128)}, u32[]{:S(2)}) copy-start(s32[8]{0:T(128)} %param.12) | copy-start | bytes 100
  0.7 2.0 %copy-start.14 = (s32[3072]{0:T(1024)S(1)}, s32[3072]{0:T(1024)}, u32[]{:S(2)}) copy-start(s32[3072]{0:T(1024)} %param.9) | copy-start | bytes 36868
  0.7 2.0 %copy-start = (s32[3072,128]{1,0:T(8,128)S(1)}, s32[3072,128]{1,0:T(8,128)}, u32[]{:S(2)}) copy-start(s32[3072,128]{1,0:T(8,128)} %codes_ref.1) | copy-start | bytes 4718596
  7.9 32.4 %collective-permute-start.1 = (f32[48,3328]{1,0:T(8,128)}, f32[48,3328]{1,0:T(8,128)S(1)}, u32[]{:S(2)}, u32[]{:S(2)}) collective-permute-start(f32[48,3328]{1,0:T(8,128)} %get-tuple-element.28), channel_id=1, source_target_pairs={{0,16},{2,18},{4,20},{6,22},{8,24},{10,26},{12,28},{14,30},{16,0},... | collective-permute-start | bytes 1916936 | tf_op jit(solution)/shard_map/ppermute | solution.py:232
  12.0 36.3 %collective-permute-start.3 = (f32[48,3328]{1,0:T(8,128)S(1)}, f32[48,3328]{1,0:T(8,128)S(1)}, u32[]{:S(2)}, u32[]{:S(2)}) collective-permute-start(f32[48,3328]{1,0:T(8,128)S(1)} %get-tuple-element.30), channel_id=1, source_target_pairs={{0,8},{2,10},{4,12},{6,14},{8,0},{10,2},{12,4},{14,6},{16,24},{18,... | collective-permute-start | bytes 1916936 | tf_op jit(solution)/shard_map/ppermute | solution.py:232
  20.8 1.0 copy-start.3
  23.8 1.0 copy-start.11
  41.1 18.7 %collective-permute-start.2 = (f32[32,3328]{1,0:T(8,128)}, f32[32,3328]{1,0:T(8,128)S(1)}, u32[]{:S(2)}, u32[]{:S(2)}) collective-permute-start(f32[32,3328]{1,0:T(8,128)} %slice.30), channel_id=1, source_target_pairs={{0,8},{2,10},{4,12},{6,14},{8,0},{10,2},{12,4},{14,6},{16,24},{18,... | collective-permute-start | bytes 1277960 | tf_op jit(solution)/shard_map/ppermute | solution.py:232
  41.9 17.9 %collective-permute-start = (s32[16,3072]{1,0:T(8,128)}, s32[16,3072]{1,0:T(8,128)S(1)}, u32[]{:S(2)}, u32[]{:S(2)}) collective-permute-start(s32[16,3072]{1,0:T(8,128)} %get-tuple-element.23), channel_id=1, source_target_pairs={{0,24},{2,26},{4,28},{6,30},{8,16},{10,18},{12,20},{14,22},{16,8},... | collective-permute-start | bytes 589832 | tf_op jit(solution)/shard_map/ppermute | solution.py:232
  44.6 28.0 %all-to-all-start = ((s32[4,16,3072]{2,1,0:T(8,128)}), s32[4,16,3072]{2,1,0:T(8,128)S(1)}, u32[]{:S(2)}, u32[]{:S(2)}) async-start(s32[4,16,3072]{2,1,0:T(8,128)} %bitcast.78), calls=%async_computation | async-start | bytes 1572864 | tf_op jit(solution)/shard_map/all_to_all | solution.py:344
  48.3 1.2 %copy-start.10 = (f32[544,512]{1,0:T(8,128)S(1)}, f32[544,512]{1,0:T(8,128)}, u32[]{:S(2)}) copy-start(f32[544,512]{1,0:T(8,128)} %copy-done.9) | copy-start | bytes 3342340
  49.5 1.2 %copy-start.12 = (f32[544,512]{1,0:T(8,128)S(1)}, f32[544,512]{1,0:T(8,128)}, u32[]{:S(2)}) copy-start(f32[544,512]{1,0:T(8,128)} %copy-done.11) | copy-start | bytes 3342340
  62.2 2.8 %collective-permute-start.4 = (f32[544,512]{1,0:T(8,128)S(1)}, f32[544,512]{1,0:T(8,128)S(1)}, u32[]{:S(2)}, u32[]{:S(2)}) collective-permute-start(f32[544,512]{1,0:T(8,128)S(1)} %shard_map.98), channel_id=1, source_target_pairs={{0,2},{2,0},{4,6},{6,4},{8,10},{10,8},{12,14},{14,12},{16,18},{18,... | collective-permute-start | bytes 3342344 | tf_op jit(solution)/shard_map/ppermute | solution.py:232
  72.6 1.2 %copy-start.6 = (f32[544,512]{1,0:T(8,128)S(1)}, f32[544,512]{1,0:T(8,128)}, u32[]{:S(2)}) copy-start(f32[544,512]{1,0:T(8,128)} %copy-done.5) | copy-start | bytes 3342340
  73.8 5.7 %copy-start.8 = (f32[544,512]{1,0:T(8,128)S(1)}, f32[544,512]{1,0:T(8,128)}, u32[]{:S(2)}) copy-start(f32[544,512]{1,0:T(8,128)} %copy-done.7) | copy-start | bytes 3342340
  73.8 7.3 %copy-start.4 = (f32[544,512]{1,0:T(8,128)S(1)}, f32[544,512]{1,0:T(8,128)}, u32[]{:S(2)}) copy-start(f32[544,512]{1,0:T(8,128)} %copy-done.3) | copy-start | bytes 3342340
  79.4 7.5 %collective-permute-start.5 = (f32[544,512]{1,0:T(8,128)S(1)}, f32[544,512]{1,0:T(8,128)S(1)}, u32[]{:S(2)}, u32[]{:S(2)}) collective-permute-start(f32[544,512]{1,0:T(8,128)S(1)} %shard_map.100), channel_id=1, source_target_pairs={{0,2},{2,0},{4,6},{6,4},{8,10},{10,8},{12,14},{14,12},{16,18},{18,... | collective-permute-start | bytes 3342344 | tf_op jit(solution)/shard_map/ppermute | solution.py:232
  79.5 27.0 %collective-permute-start.6 = (f32[544,512]{1,0:T(8,128)S(1)}, f32[544,512]{1,0:T(8,128)S(1)}, u32[]{:S(2)}, u32[]{:S(2)}) collective-permute-start(f32[544,512]{1,0:T(8,128)S(1)} %copy-done.8), channel_id=1, source_target_pairs={{0,4},{2,6},{4,0},{6,2},{8,12},{10,14},{12,8},{14,10},{16,20},{18,... | collective-permute-start | bytes 3342344 | tf_op jit(solution)/shard_map/ppermute | solution.py:232
  106.5 10.1 %copy-start.2 = (f32[3072,32]{0,1:T(8,128)S(1)}, f32[3072,32]{0,1:T(8,128)}, u32[]{:S(2)}) copy-start(f32[3072,32]{0,1:T(8,128)} %param.7) | copy-start | bytes 1179652
  106.5 9.9 %collective-permute-start.7 = (f32[32,128]{1,0:T(8,128)S(1)}, f32[32,128]{1,0:T(8,128)S(1)}, u32[]{:S(2)}, u32[]{:S(2)}) collective-permute-start(f32[32,128]{1,0:T(8,128)S(1)} %pad_maximum_fusion), channel_id=1, source_target_pairs={{0,1},{1,0},{2,3},{3,2},{4,5},{5,4},{6,7},{7,6},{8,9},{9,8},{10,11... | collective-permute-start | bytes 49160 | tf_op jit(solution)/shard_map/ppermute | solution.py:232
  110.2 13.0 %all-to-all-start.1 = ((f32[8,8,128]{2,1,0:T(8,128)}), f32[8,8,128]{2,1,0:T(8,128)S(1)}, u32[]{:S(2)}, u32[]{:S(2)}) async-start(f32[8,8,128]{2,1,0:T(8,128)} %shard_map.102), calls=%async_computation.1 | async-start | bytes 65536 | tf_op jit(solution)/shard_map/all_to_all | solution.py:378
  116.6 7.1 %copy-start.16 = (f32[8,2,32]{2,1,0:T(2,128)}, f32[8,2,32]{2,1,0:T(2,128)S(1)}, u32[]{:S(2)}) copy-start(f32[8,2,32]{2,1,0:T(2,128)S(1)} %fusion.4) | copy-start | bytes 6148
  (6 other events, 5.6 us)

commit v5 on v4

--- a/solution.py
+++ b/solution.py
@@ -42,22 +42,35 @@
     return jnp.where((below | missing) & same, 1.0, 0.0).astype(jnp.bfloat16)
 
 
-def read_info(info, rows):
-    chunks = rows // LANES
-    prob = info[:, :rows]
-    labels = info[:, rows : rows + LANES]
-    nodes = info[:, rows + LANES : rows + 2 * LANES]
-    label = jnp.concatenate([labels[i : i + 1] for i in range(chunks)], axis=1)
-    node = jnp.concatenate([nodes[i : i + 1] for i in range(chunks)], axis=1)
+def half_width(rows):
+    return rows // 2 + 2 * LANES
+
+
+def read_info(halves, rows):
+    half = rows // 2
+    chunks = half // LANES
+    prob = jnp.concatenate([info[:, :half] for info in halves], axis=1)
+    label, node = (
+        jnp.concatenate(
+            [info[i : i + 1, low : low + LANES] for info in halves for i in range(chunks)], axis=1
+        )
+        for low in (half, half + LANES)
+    )
     return prob, label, node
+
+
+def child_sums(info, rows, node_count):
+    return info[-node_count:, rows // 2 : rows // 2 + LANES]
 
 
 def prep_kernel(
     own, blocks, starts_ref, split_ref, logits_ref, labels_ref, nodes_ref, codes_ref, *refs
 ):
-    outs, flag_ref, turned = refs[: len(blocks)], refs[-2], refs[-1]
+    info_ref, half_ref, flag_ref = refs[:3]
+    outs, turned = refs[3:-1], refs[-1]
     classes, rows = logits_ref.shape
-    chunks = rows // LANES
+    half, width = rows // 2, half_width(rows)
+    chunks = half // LANES
     turned[...] = codes_ref[...].T
     for (with_info, pieces), out_ref in zip(blocks, outs):
         base = classes if with_info else 0
@@ -66,13 +79,13 @@
             low = base + i * own
             out_ref[low : low + own, :rows] = turned[pl.ds(start, own), :].astype(out_ref.dtype)
             if with_info:
-                out_ref[low : low + own, rows:] = jnp.zeros((own, 2 * LANES), out_ref.dtype)
+                out_ref[low : low + own, rows:] = jnp.zeros((own, 2 * width - rows), out_ref.dtype)
     expo_vals = jnp.exp(logits_ref[...])
     prob = expo_vals / jnp.sum(expo_vals, axis=0, keepdims=True)
     labels = labels_ref[...].astype(jnp.float32)
     nodes = nodes_ref[...].astype(jnp.float32)
-    label = jnp.concatenate([labels[i : i + 1] for i in range(chunks)], axis=1)
-    node = jnp.concatenate([nodes[i : i + 1] for i in range(chunks)], axis=1)
+    label = jnp.concatenate([labels[i : i + 1] for i in range(2 * chunks)], axis=1)
+    node = jnp.concatenate([nodes[i : i + 1] for i in range(2 * chunks)], axis=1)
 
     feats = turned.shape[0]
     node_count = split_ref.shape[1]
@@ -101,19 +114,21 @@
         preferred_element_type=jnp.float32,
     )
     sums = jnp.concatenate([sums[:node_count], sums[node_count:]], axis=1)
+    pad = jnp.zeros((classes - chunks - node_count, LANES), jnp.float32)
+    long_pad = jnp.zeros((classes - chunks, LANES), jnp.float32)
+    for h in range(2):
+        some = slice(h * chunks, (h + 1) * chunks)
+        info_ref[:, h * width : h * width + half] = prob[:, h * half : (h + 1) * half]
+        info_ref[:, h * width + half : h * width + half + LANES] = jnp.concatenate(
+            [labels[some], pad, sums], axis=0
+        )
+        info_ref[:, h * width + half + LANES : (h + 1) * width] = jnp.concatenate(
+            [nodes[some], long_pad], axis=0
+        )
+    half_ref[...] = jnp.where(split_ref[3, 0] == 0, info_ref[:, :width], info_ref[:, width:])
     for (with_info, _), out_ref in zip(blocks, outs):
         if with_info:
-            out_ref[:classes, :rows] = prob
-            out_ref[:chunks, rows : rows + LANES] = labels
-            out_ref[:chunks, rows + LANES :] = nodes
-            if chunks < classes - node_count:
-                out_ref[chunks : classes - node_count, rows : rows + LANES] = jnp.zeros(
-                    (classes - node_count - chunks, LANES), jnp.float32
-                )
-            out_ref[classes - node_count : classes, rows : rows + LANES] = sums
-            out_ref[chunks:classes, rows + LANES :] = jnp.zeros(
-                (classes - chunks, LANES), jnp.float32
-            )
+            out_ref[:classes, :] = info_ref[...]
 
 
 def gradients(prob, label):
@@ -122,8 +137,8 @@
     return jnp.concatenate([prob - target, prob * (1.0 - prob)], axis=0)
 
 
-def masked_gradients(info, rows, node_count):
-    prob, label, node = read_info(info, rows)
+def masked_gradients(halves, rows, node_count):
+    prob, label, node = read_info(halves, rows)
     grad_hess = gradients(prob, label)
     return jnp.concatenate(
         [jnp.where(node == float(n), grad_hess, 0.0).astype(jnp.bfloat16) for n in range(node_count)],
@@ -174,18 +189,27 @@
 
 def add_kernel(classes, node_count, own, plan, place_ref, *refs):
     outs = len(plan[0][2])
-    arrays = 1 + max(max(c, i) for c, i, _ in plan)
+    arrays = 1 + max(max((c,) + i) for c, i, _ in plan)
     out_refs = refs[-outs:]
     held_refs = refs[arrays:-outs]
     pairs = 2 * classes * node_count
     for s, (codes_at, info_at, firsts) in enumerate(plan):
-        codes_ref, info_ref = refs[codes_at], refs[info_at]
-        rows = info_ref.shape[1] - 2 * LANES
+        codes_ref = refs[codes_at]
         if len(codes_ref.shape) == 3:
             codes_ref = codes_ref.at[place_ref[0, s]]
-        info = info_ref[:classes, :]
-        masked = masked_gradients(info, rows, node_count)
-        sums = info[classes - node_count :, rows : rows + LANES]
+        if len(info_at) == 1:
+            width = refs[info_at[0]].shape[1] // 2
+            low, high = (refs[info_at[0]][:classes, h * width : (h + 1) * width] for h in range(2))
+            sums_from = low
+        else:
+            width = refs[info_at[0]].shape[1]
+            near, far = (refs[i][...] for i in info_at)
+            low = jnp.where(place_ref[2, s] == 0, near, far)
+            high = jnp.where(place_ref[2, s] == 0, far, near)
+            sums_from = near
+        rows = 2 * (width - 2 * LANES)
+        masked = masked_gradients((low, high), rows, node_count)
+        sums = child_sums(sums_from, rows, node_count)
         for i, first in enumerate(firsts):
             out_ref = out_refs[i]
             product = lax.dot_general(
@@ -216,7 +240,7 @@
         + [whole] * (len(arrays) + len(held) * outs),
         out_specs=[whole] * outs,
         out_shape=[jax.ShapeDtypeStruct(shape, jnp.float32)] * outs,
-        compiler_params=pltpu.CompilerParams(vmem_limit_bytes=32 * 1024 * 1024),
+        compiler_params=pltpu.CompilerParams(vmem_limit_bytes=20 * 1024 * 1024),
         cost_estimate=SMALL_COST,
     )(places, *arrays, *[hist for hists in held for hist in hists])
 
@@ -246,19 +270,23 @@
     own = 8
     whole = pl.BlockSpec(memory_space=pltpu.VMEM)
     scalars = pl.BlockSpec(memory_space=pltpu.SMEM)
-    shapes = []
+    width = half_width(rows_dev)
+    shapes = [
+        jax.ShapeDtypeStruct((classes, 2 * width), jnp.float32),
+        jax.ShapeDtypeStruct((classes, width), jnp.float32),
+        jax.ShapeDtypeStruct((1, rows_dev), jnp.float32),
+    ]
     for with_info, pieces in blocks:
         codes = len(pieces) * own
         if with_info:
-            shape = (classes + codes, rows_dev + 2 * LANES)
-            shapes.append(jax.ShapeDtypeStruct(shape, jnp.float32))
+            shapes.append(jax.ShapeDtypeStruct((classes + codes, 2 * width), jnp.float32))
         else:
             shapes.append(jax.ShapeDtypeStruct((codes, rows_dev), jnp.int32))
     return pl.pallas_call(
         functools.partial(prep_kernel, own, blocks),
         in_specs=[scalars, scalars] + [whole] * 4,
-        out_specs=[whole] * (len(blocks) + 1),
-        out_shape=shapes + [jax.ShapeDtypeStruct((1, rows_dev), jnp.float32)],
+        out_specs=[whole] * len(shapes),
+        out_shape=shapes,
         scratch_shapes=[pltpu.VMEM((feats_dev, rows_dev), jnp.int32)],
         compiler_params=pltpu.CompilerParams(vmem_limit_bytes=20 * 1024 * 1024),
         cost_estimate=SMALL_COST,
@@ -270,10 +298,6 @@
         node_ids.reshape(-1, LANES),
         bin_codes,
     )
-
-
-def child_sums(info, rows_dev, classes, node_count):
-    return info[classes - node_count : classes, rows_dev : rows_dev + LANES]
 
 
 def finish(logits_t, node_ids, side_count, sums, node_count):
@@ -304,10 +328,17 @@
     own = 8
     row_index = lax.axis_index("rows")
     feat_index = lax.axis_index("feat")
-    splits = jnp.stack([split_feature - feat_index * feats_dev, split_bin, split_missing])
+    splits = jnp.stack(
+        [
+            split_feature - feat_index * feats_dev,
+            split_bin,
+            split_missing,
+            jnp.zeros_like(split_bin) + feat_index,
+        ]
+    )
     logits_t = logits.T
     add = functools.partial(add_rows, classes, node_count, own)
-    if feats_dev != own * n_rows or n_rows != 16:
+    if feats_dev != own * n_rows or n_rows != 16 or lax.axis_size("feat") != 2:
         return by_groups(
             logits_t, labels, node_ids, bin_codes, splits, row_index, per_node, pairs_dev
         )
@@ -318,53 +349,53 @@
         starts.append(jnp.stack([t % per_node * pairs_dev + t // per_node * own for t in takers]))
     starts = jnp.stack(starts)
     blocks = (
-        (True, ((0, 0), (0, 1), (0, 2), (0, 3))),
+        (False, ((0, 0), (0, 1), (0, 2), (0, 3))),
         (True, ((1, 0), (1, 1))),
-        (True, ((2, 0), (2, 1))),
+        (False, ((2, 0), (2, 1))),
         (False, ((3, 0), (3, 1))),
         (False, tuple((4 + z, quarter) for z in range(4) for quarter in (2, 3))),
     )
-    rows_0, rows_4, rows_8, codes_12, codes_late, flags = prepare(
+    info, half, flags, codes_0, rows_4, codes_8, codes_12, codes_late = prepare(
         blocks, starts, logits_t, labels, node_ids, bin_codes, splits
     )
 
     def place(*lines):
         line = jnp.stack([row_index // 4 ^ m // 4 for m in lines])
-        return jnp.stack([line, jnp.zeros_like(line) + row_index % 4])
-
-    first, second, third, fourth = [classes + i * own for i in range(4)]
-    rows_8 = swap(rows_8, "rows", 8)
+        return jnp.stack([line, row_index % 4 + 0 * line, feat_index + 0 * line])
+
+    near_8 = swap(half, "rows", 8)
     rows_4 = swap(rows_4, "rows", 4)
+    codes_8 = swap(codes_8, "rows", 8)
     codes_12 = swap(codes_12, "rows", 12)
-    hist_a, hist_b, hist_c, hist_d = add(((0, 0, (first, second, third, fourth)),), place(0), [rows_0])
-    hist_a, hist_b, codes_late, rows_8 = lax.optimization_barrier(
-        (hist_a, hist_b, codes_late, rows_8)
-    )
+    near_12 = swap(near_8, "rows", 4)
+    far_8 = swap(near_8, "feat", 1)
+    far_12 = swap(near_12, "feat", 1)
+    hist_a, hist_b, hist_c, hist_d = add(
+        ((0, (1,), (0, own, 2 * own, 3 * own)),), place(0), [codes_0, info]
+    )
+    near_8, codes_late = lax.optimization_barrier((near_8, codes_late))
     lines = [[4 * z + low for z in range(4)] for low in range(4)]
     codes_late = lax.all_to_all(
         codes_late.reshape(4, 2 * own, rows_dev), "rows", 0, 0, tiled=True, axis_index_groups=lines
     )
-    info_12 = swap(rows_8[:classes], "rows", 4)
-    hists = add(((0, 0, (first, second)),), place(4), [rows_4], [hist_a, hist_b])
-    hist_a, hist_b = add(((0, 0, (first, second)),), place(8), [rows_8], hists)
-    (to_core,) = add(((0, 1, (0,)),), place(12), [codes_12, info_12], [hist_a])
+    hists = add(((0, (0,), (classes, classes + own)),), place(4), [rows_4], [hist_a, hist_b])
+    hist_a, hist_b = add(((0, (1, 2), (0, own)),), place(8), [codes_8, near_8, far_8], hists)
+    (to_core,) = add(((0, (1, 2), (0,)),), place(12), [codes_12, near_12, far_12], [hist_a])
     from_core = swap(to_core, "rows", 1)
-    (to_plane,) = add(((0, 1, (own,)),), place(12), [codes_12, info_12], [hist_b], [from_core])
+    (to_plane,) = add(
+        ((0, (1, 2), (own,)),), place(12), [codes_12, near_12, far_12], [hist_b], [from_core]
+    )
     to_plane, codes_late = lax.optimization_barrier((to_plane, codes_late))
     from_plane = swap(to_plane, "rows", 2)
-    late = [codes_late, rows_4, rows_8, info_12]
-    (to_core,) = add(tuple((0, i, (0,)) for i in (1, 2, 3)), place(4, 8, 12), late, [hist_c])
-    from_core = swap(to_core, "rows", 1)
-    (kept,) = add(tuple((0, i, (own,)) for i in (1, 2, 3)), place(4, 8, 12), late, [hist_d])
+    late = [codes_late, rows_4, near_8, far_8, near_12, far_12]
+    to_core, kept = add(
+        tuple((0, i, (0, own)) for i in ((1,), (2, 3), (4, 5))), place(4, 8, 12), late, [hist_c, hist_d]
+    )
+    middle = to_core.shape[0] // 2
+    from_core = [swap(part, "rows", 1) for part in (to_core[:middle], to_core[middle:])]
+    from_core = jnp.concatenate(from_core, axis=0)
 
     pairs = node_count * width
-    parts = from_core[pairs:] + from_plane[pairs:] + kept[pairs:]
-    sums = jnp.sum(parts.reshape(4, node_count, -1, LANES), axis=(0, 2))
-    children = jnp.concatenate([sums, flags.reshape(-1, LANES)], axis=0)
-    children = sum_over(children, "feat")
-    side_count = children[node_count:].reshape(1, rows_dev)
-    new_logits, leaves = finish(logits_t, node_ids, side_count, children[:node_count], node_count)
-
     gains = pl.pallas_call(
         functools.partial(gain_kernel, classes, node_count),
         in_specs=[pl.BlockSpec(memory_space=pltpu.VMEM)] * 3,
@@ -374,6 +405,14 @@
         compiler_params=pltpu.CompilerParams(vmem_limit_bytes=16 * 1024 * 1024),
         cost_estimate=SMALL_COST,
     )(from_core, from_plane, kept)
+    gains, from_plane = lax.optimization_barrier((gains, from_plane))
+    parts = from_core[pairs:] + from_plane[pairs:] + kept[pairs:]
+    sums = jnp.sum(parts.reshape(4, node_count, -1, LANES), axis=(0, 2))
+    children = jnp.concatenate([sums, flags.reshape(-1, LANES)], axis=0)
+    children = sum_over(children, "feat")
+    side_count = children[node_count:].reshape(1, rows_dev)
+    new_logits, leaves = finish(logits_t, node_ids, side_count, children[:node_count], node_count)
+
     halves = [[h + n * per_node for n in range(node_count)] for h in range(per_node)]
     gain_rows = lax.all_to_all(gains, "rows", 0, 0, tiled=True, axis_index_groups=halves)
     return (new_logits, gain_rows.reshape(1, pairs_dev, 2 * BINS), leaves)
@@ -390,7 +429,7 @@
     group_count = n_rows // group
     starts = jnp.arange(group, dtype=jnp.int32)[:, None] * own
     blocks = tuple((True, ((r, 0),)) for r in range(group))
-    *rows_out, flags = prepare(blocks, starts, logits_t, labels, node_ids, bin_codes, splits)
+    info, _, flags, *rows_out = prepare(blocks, starts, logits_t, labels, node_ids, bin_codes, splits)
     members = [[g * group + r for r in range(group)] for g in range(group_count)]
     rows_in = lax.all_to_all(
         jnp.stack(rows_out), "rows", 0, 0, tiled=True, axis_index_groups=members
@@ -400,9 +439,9 @@
         held = [hists] if hists else []
         nowhere = jnp.full((2, 1), -1, jnp.int32) * jnp.array([[1], [0]], jnp.int32)
         hists = add_rows(
-            classes, node_count, own, ((0, 0, (classes,)),), nowhere, [rows_in[r]], *held
+            classes, node_count, own, ((0, (0,), (classes,)),), nowhere, [rows_in[r]], *held
         )
-    sums = lax.psum(child_sums(rows_out[0], rows_dev, classes, node_count), ("rows", "feat"))
+    sums = lax.psum(child_sums(info[:, : half_width(rows_dev)], rows_dev, node_count), ("rows", "feat"))
     side_count = lax.psum(flags, "feat")
     new_logits, leaves = finish(logits_t, node_ids, side_count, sums, node_count)
 

time: 124 us -> 120 us (0.968)
  waiting for transfers between devices: 48.3 us -> 43 us
  local copies, waits for them, and re-layouts: 12.9 us -> 8.93 us
  starting transfers between devices: 22.3 us -> 25.7 us
  Pallas kernels: 36.1 us -> 37.5 us
    all_to_all x1, waiting for transfers between devices: 4.21 us -> 0.01 us  [local(): lax.all_to_all(codes_late.reshape(4, 2 * own, rows_dev), 'rows', 0, 0, ti...]
    unnamed x41 -> x33, local copies, waits for them, and re-layouts: 12 us -> 8.15 us
    ppermute x8 -> x12, starting transfers between devices: 12.4 us -> 15.9 us  [swap(): return lax.ppermute(x, axis, [(i, i ^ bit) for i in range(size)])]
    pallas_call x7 -> x6, Pallas kernels: 31.4 us -> 32.6 us  [add_rows(): pl.pallas_call(functools.partial(add_kernel, classes, node_count, own, pl...]
    ppermute x8 -> x12, waiting for transfers between devices: 38.7 us -> 37.6 us  [swap(): return lax.ppermute(x, axis, [(i, i ^ bit) for i in range(size)])]
  transfers between devices with their start and end apart: 10 -> 14, of which waited for: 6 -> 7; matrix products, arithmetic and copies ran while one was open for 2% -> 2% of each run, Pallas kernels for 23% -> 27%
where the time goes in v5:
time: 120 us
  waiting for transfers between devices  43 us (36%)
  Pallas kernels  37.5 us (31%)
  starting transfers between devices  25.7 us (21%)
  local copies, waits for them, and re-layouts  8.93 us (7%)
  between operations  2.39 us (2%)
    ppermute x12, waiting for transfers between devices, swap(): return lax.ppermute(x, axis, [(i, i ^ bit) for i in range(size)])  37.6 us
    pallas_call x6, Pallas kernels, add_rows(): pl.pallas_call(functools.partial(add_kernel, classes, node_count, own, pl...  32.6 us
    ppermute x12, starting transfers between devices, swap(): return lax.ppermute(x, axis, [(i, i ^ bit) for i in range(size)])  15.9 us
    unnamed x33, local copies, waits for them, and re-layouts  8.15 us
    all_to_all x1, starting transfers between devices, local(): lax.all_to_all(gains, 'rows', 0, 0, tiled=True, axis_index_groups=halves)  6.05 us
    all_to_all x1, waiting for transfers between devices, local(): lax.all_to_all(gains, 'rows', 0, 0, tiled=True, axis_index_groups=halves)  5.36 us
    all_to_all x1, starting transfers between devices, local(): lax.all_to_all(codes_late.reshape(4, 2 * own, rows_dev), 'rows', 0, 0, ti...  3.77 us
    pallas_call x1, Pallas kernels, prepare(): pl.pallas_call(functools.partial(prep_kernel, own, blocks), in_specs=[sca...  2.78 us
  transfers between devices with their start and end apart: 14, of which 7 were waited for; matrix products, arithmetic and copies ran while one was open for 2% of the time, Pallas kernels for 27%

profile of v5, /device:TPU:0, one launch (start us, length us, event | category | flops | bytes accessed | tf_op | source)
XLA Modules:
  0.0 119.7 jit_solution(8088685146190047483)
XLA Ops:
  4.4 2.8 %shard_map.94 = (f32[32,3584]{1,0:T(8,128)S(1)}, f32[32,1792]{1,0:T(8,128)S(1)}, f32[1,3072]{1,0:T(1,128)S(1)}, s32[32,3072]{1,0:T(8,128)S(1)}, f32[48,3584]{1,0...) custom-call(s32[8,4]{1,0:T(8,128)S(1)} %stack.256.starts_ref, ...), custom_call_target="tpu_custom_call" | custom-call | flops 1000000 | bytes 1000000 | tf_op jit(solution)/shard_map/pallas_call | solution.py:285
  8.7 4.0 %collective-permute-start.1 = (f32[32,1792]{1,0:T(8,128)S(1)}, f32[32,1792]{1,0:T(8,128)}, u32[]{:S(2)}, u32[]{:S(2)}) collective-permute-start(f32[32,1792]{1,0:T(8,128)S(1)} %get-tuple-element.28), channel_id=1, source_target_pairs={{0,16},{2,18},{4,20},{6,22},{8,24},{10,26},{12,28},{14,30},{16,0},... | collective-permute-start | bytes 688136 | tf_op jit(solution)/shard_map/ppermute | solution.py:256
  12.8 1.6 %collective-permute-start.6 = (f32[48,3584]{1,0:T(8,128)}, f32[48,3584]{1,0:T(8,128)S(1)}, u32[]{:S(2)}, u32[]{:S(2)}) collective-permute-start(f32[48,3584]{1,0:T(8,128)} %get-tuple-element.32), channel_id=1, source_target_pairs={{0,8},{2,10},{4,12},{6,14},{8,0},{10,2},{12,4},{14,6},{16,24},{18,... | collective-permute-start | bytes 2064392 | tf_op jit(solution)/shard_map/ppermute | solution.py:256
  14.3 9.1 %collective-permute-done.1.refs_1_.refs_2_ = f32[32,1792]{1,0:T(8,128)} collective-permute-done((f32[32,1792]{1,0:T(8,128)S(1)}, f32[32,1792]{1,0:T(8,128)}, u32[]{:S(2)}, u32[]{:S(2)}) %collective-permute-start.1) | collective-permute-done | bytes 229408 | tf_op jit(solution)/shard_map/ppermute | solution.py:256
  24.0 3.5 %collective-permute-start.4 = (s32[16,3072]{1,0:T(8,128)}, s32[16,3072]{1,0:T(8,128)}, u32[]{:S(2)}, u32[]{:S(2)}) collective-permute-start(s32[16,3072]{1,0:T(8,128)} %get-tuple-element.29), channel_id=1, source_target_pairs={{0,16},{2,18},{4,20},{6,22},{8,24},{10,26},{12,28},{14,30},{16,0},... | collective-permute-start | bytes 589832 | tf_op jit(solution)/shard_map/ppermute | solution.py:256
  27.9 1.5 %collective-permute-start.5 = (f32[32,1792]{1,0:T(8,128)}, f32[32,1792]{1,0:T(8,128)}, u32[]{:S(2)}, u32[]{:S(2)}) collective-permute-start(f32[32,1792]{1,0:T(8,128)} %collective-permute-done.1.refs_1_.refs_2_), channel_id=1, source_target_pairs={{0,1},{1,0},{2,3},{3,2},{4,5},{5,4},{6,7},{7,6},{8,9},{9,8},{10,11... | collective-permute-start | bytes 688136 | tf_op jit(solution)/shard_map/ppermute | solution.py:256
  29.5 13.7 %collective-permute-done.2.refs_1_.refs_4_ = f32[32,1792]{1,0:T(8,128)S(1)} collective-permute-done((f32[32,1792]{1,0:T(8,128)}, f32[32,1792]{1,0:T(8,128)S(1)}, u32[]{:S(2)}, u32[]{:S(2)}) %collective-permute-start.2) | collective-permute-done | bytes 229408 | tf_op jit(solution)/shard_map/ppermute | solution.py:256
  43.2 1.6 %collective-permute-start.3 = (f32[32,1792]{1,0:T(8,128)S(1)}, f32[32,1792]{1,0:T(8,128)S(1)}, u32[]{:S(2)}, u32[]{:S(2)}) collective-permute-start(f32[32,1792]{1,0:T(8,128)S(1)} %collective-permute-done.2.refs_1_.refs_4_), channel_id=1, source_target_pairs={{0,1},{1,0},{2,3},{3,2},{4,5},{5,4},{6,7},{7,6},{8,9},{9,8},{10,11... | collective-permute-start | bytes 688136 | tf_op jit(solution)/shard_map/ppermute | solution.py:256
  45.3 3.8 %all-to-all-start = ((s32[4,16,3072]{2,1,0:T(8,128)}), s32[4,16,3072]{2,1,0:T(8,128)S(1)}, u32[]{:S(2)}, u32[]{:S(2)}) async-start(s32[4,16,3072]{2,1,0:T(8,128)} %bitcast.56), calls=%async_computation | async-start | bytes 1572864 | tf_op jit(solution)/shard_map/all_to_all | solution.py:378
  50.2 7.2 %shard_map.95 = (f32[544,512]{1,0:T(8,128)S(1)}, f32[544,512]{1,0:T(8,128)S(1)}, f32[544,512]{1,0:T(8,128)S(1)}, f32[544,512]{1,0:T(8,128)S(1)}) custom-call(s32[3,1]{1,0:T(4,128)S(1)} %copy.10.place_ref, s32[32,3072]{1,0:T(8,128)S(1)} %copy-done.9, f32[32,3584]{1,0:T(8,128)S(1)} %copy-done.7), custom_call_target="tpu_custom_call" | custom-call | flops 1000000 | bytes 1000000 | tf_op jit(solution)/shard_map/pallas_call | solution.py:237
  58.5 4.0 %shard_map.96 = (f32[544,512]{1,0:T(8,128)S(1)}, f32[544,512]{1,0:T(8,128)S(1)}) custom-call(s32[3,1]{1,0:T(4,128)S(1)} %copy.11.place_ref, f32[48,3584]{1,0:T(8,128)S(1)} %collective-permute-done.6.refs_0_.refs_1_, f32[544,512]{1,0:T(8,128)S(1)} %get-tuple-element.35.refs_1_, f32[544,512]{1,0:T(8,128)S(1)} %get-tuple-element.36.refs_2_), custom_call_target="tpu_custom_call" | custom-call | flops 1000000 | bytes 1000000 | tf_op jit(solution)/shard_map/pallas_call | solution.py:237
  62.5 4.6 %shard_map.97 = (f32[544,512]{1,0:T(8,128)S(1)}, f32[544,512]{1,0:T(8,128)S(1)}) custom-call(s32[3,1]{1,0:T(4,128)S(1)} %copy.12.place_ref, s32[16,3072]{1,0:T(8,128)} %collective-permute-done.4.refs_0_, f32[32,1792]{1,0:T(8,128)} %collective-permute-done.1.refs_1_.refs_2_, f32[32,1792]{1,0:T(8,128)} %collective-permute-done.5.refs_2_.refs_3_, ...), custom_call_target="tpu_custom_call" | custom-call | flops 1000000 | bytes 1000000 | tf_op jit(solution)/shard_map/pallas_call | solution.py:237
  67.2 2.8 %shard_map.98 = f32[544,512]{1,0:T(8,128)S(1)} custom-call(s32[3,1]{1,0:T(4,128)S(1)} %copy.14.place_ref, s32[16,3072]{1,0:T(8,128)} %collective-permute-done.refs_0_, f32[32,1792]{1,0:T(8,128)S(1)} %collective-permute-done.2.refs_1_.refs_4_, f32[32,1792]{1,0:T(8,128)S(1)} %collective-permute-done.3.refs_2_.refs_5_, f32[544,512]{1,0:T(8,128)S(1)} %get-tuple-element.40.refs_3_), custom_call_target="tpu_custom_call" | custom-call | flops 1000000 | bytes 1000000 | tf_op jit(solution)/shard_map/pallas_call | solution.py:237
  70.2 2.5 %collective-permute-done.7.refs_4_ = f32[544,512]{1,0:T(8,128)S(1)} collective-permute-done((f32[544,512]{1,0:T(8,128)S(1)}, f32[544,512]{1,0:T(8,128)S(1)}, u32[]{:S(2)}, u32[]{:S(2)}) %collective-permute-start.7) | collective-permute-done | bytes 1114144 | tf_op jit(solution)/shard_map/ppermute | solution.py:256
  72.8 3.0 %shard_map.99 = f32[544,512]{1,0:T(8,128)S(1)} custom-call(s32[3,1]{1,0:T(4,128)S(1)} %copy.14.place_ref, s32[16,3072]{1,0:T(8,128)} %collective-permute-done.refs_0_, f32[32,1792]{1,0:T(8,128)S(1)} %collective-permute-done.2.refs_1_.refs_4_, f32[32,1792]{1,0:T(8,128)S(1)} %collective-permute-done.3.refs_2_.refs_5_, ...), custom_call_target="tpu_custom_call" | custom-call | flops 1000000 | bytes 1000000 | tf_op jit(solution)/shard_map/pallas_call | solution.py:237
  76.8 1.5 %collective-permute-start.10 = (f32[544,512]{1,0:T(8,128)}, f32[544,512]{1,0:T(8,128)S(1)}, u32[]{:S(2)}, u32[]{:S(2)}) collective-permute-start(f32[544,512]{1,0:T(8,128)} %copy-done.5), channel_id=1, source_target_pairs={{0,4},{2,6},{4,0},{6,2},{8,12},{10,14},{12,8},{14,10},{16,20},{18,... | collective-permute-start | bytes 3342344 | tf_op jit(solution)/shard_map/ppermute | solution.py:256
  78.4 1.2 %copy-done.4 = f32[544,512]{1,0:T(8,128)S(1)} copy-done((f32[544,512]{1,0:T(8,128)S(1)}, f32[544,512]{1,0:T(8,128)}, u32[]{:S(2)}) %copy-start.4) | copy-done | bytes 1114136
  79.6 11.0 %shard_map.100 = (f32[544,512]{1,0:T(8,128)S(1)}, f32[544,512]{1,0:T(8,128)S(1)}) custom-call(s32[3,3]{1,0:T(4,128)S(1)} %add_add_fusion.place_ref, s32[4,16,3072]{2,1,0:T(8,128)S(1)} %all-to-all-done.refs_0_, f32[48,3584]{1,0:T(8,128)S(1)} %collective-permute-done.6.refs_0_.refs_1_, f32[32,1792]{1,0:T(8,128)} %collective-permute-done.1.refs_1_.refs_2_, ...), custom_call_target="tpu_custom_call" | custom-call | flops 1000000 | bytes 1000000 | tf_op jit(solution)/shard_map/pallas_call | solution.py:237
  91.3 1.4 %collective-permute-done.8 = f32[272,512]{1,0:T(8,128)S(1)} collective-permute-done((f32[272,512]{1,0:T(8,128)S(1)}, f32[272,512]{1,0:T(8,128)S(1)}, u32[]{:S(2)}, u32[]{:S(2)}) %collective-permute-start.8) | collective-permute-done | bytes 557088 | tf_op jit(solution)/shard_map/ppermute | solution.py:256
  93.6 10.0 %collective-permute-done.10.refs_1_ = f32[544,512]{1,0:T(8,128)S(1)} collective-permute-done((f32[544,512]{1,0:T(8,128)}, f32[544,512]{1,0:T(8,128)S(1)}, u32[]{:S(2)}, u32[]{:S(2)}) %collective-permute-start.10) | collective-permute-done | bytes 1114144 | tf_op jit(solution)/shard_map/ppermute | solution.py:256
  103.6 2.1 %shard_map.101 = f32[8,8,128]{2,1,0:T(8,128)} custom-call(f32[544,512]{1,0:T(8,128)S(1)} %pad_maximum_fusion.refs_0_, f32[544,512]{1,0:T(8,128)S(1)} %collective-permute-done.10.refs_1_, f32[544,512]{1,0:T(8,128)S(1)} %get-tuple-element.47.refs_2_), custom_call_target="tpu_custom_call" | custom-call | flops 1000000 | bytes 1000000 | tf_op jit(solution)/shard_map/pallas_call | solution.py:399
  106.3 6.1 %all-to-all-start.1 = ((f32[8,8,128]{2,1,0:T(8,128)}), f32[8,8,128]{2,1,0:T(8,128)S(1)}, u32[]{:S(2)}, u32[]{:S(2)}) async-start(f32[8,8,128]{2,1,0:T(8,128)} %shard_map.101), calls=%async_computation.1 | async-start | bytes 65536 | tf_op jit(solution)/shard_map/all_to_all | solution.py:417
  112.6 1.1 fusion
  113.7 5.4 %all-to-all-done.1 = f32[8,8,128]{2,1,0:T(8,128)S(1)} async-done(((f32[8,8,128]{2,1,0:T(8,128)}), f32[8,8,128]{2,1,0:T(8,128)S(1)}, u32[]{:S(2)}, u32[]{:S(2)}) %all-to-all-start.1) | async-done | bytes 32800 | tf_op jit(solution)/shard_map/all_to_all | solution.py:417
  (75 shorter events, 11.6 us)
Async XLA Ops:
  0.6 1.6 %copy-start.15 = (s32[8]{0:T(128)S(1)}, s32[8]{0:T(128)}, u32[]{:S(2)}) copy-start(s32[8]{0:T(128)} %param.11) | copy-start | bytes 100
  0.6 1.6 %copy-start.14 = (s32[8]{0:T(128)S(1)}, s32[8]{0:T(128)}, u32[]{:S(2)}) copy-start(s32[8]{0:T(128)} %param.12) | copy-start | bytes 100
  0.7 1.6 %copy-start.13 = (s32[8]{0:T(128)S(1)}, s32[8]{0:T(128)}, u32[]{:S(2)}) copy-start(s32[8]{0:T(128)} %param.13) | copy-start | bytes 100
  0.7 2.0 %copy-start.10 = (s32[3072]{0:T(1024)S(1)}, s32[3072]{0:T(1024)}, u32[]{:S(2)}) copy-start(s32[3072]{0:T(1024)} %param.9) | copy-start | bytes 36868
  0.7 2.0 %copy-start = (s32[3072,128]{1,0:T(8,128)S(1)}, s32[3072,128]{1,0:T(8,128)}, u32[]{:S(2)}) copy-start(s32[3072,128]{1,0:T(8,128)} %codes_ref.1) | copy-start | bytes 4718596
  8.7 40.5 %copy-start.9 = (s32[32,3072]{1,0:T(8,128)S(1)}, s32[32,3072]{1,0:T(8,128)}, u32[]{:S(2)}) copy-start(s32[32,3072]{1,0:T(8,128)} %copy-done.8) | copy-start | bytes 1179652
  8.7 14.8 %collective-permute-start.1 = (f32[32,1792]{1,0:T(8,128)S(1)}, f32[32,1792]{1,0:T(8,128)}, u32[]{:S(2)}, u32[]{:S(2)}) collective-permute-start(f32[32,1792]{1,0:T(8,128)S(1)} %get-tuple-element.28), channel_id=1, source_target_pairs={{0,16},{2,18},{4,20},{6,22},{8,24},{10,26},{12,28},{14,30},{16,0},... | collective-permute-start | bytes 688136 | tf_op jit(solution)/shard_map/ppermute | solution.py:256
  12.8 45.7 %collective-permute-start.6 = (f32[48,3584]{1,0:T(8,128)}, f32[48,3584]{1,0:T(8,128)S(1)}, u32[]{:S(2)}, u32[]{:S(2)}) collective-permute-start(f32[48,3584]{1,0:T(8,128)} %get-tuple-element.32), channel_id=1, source_target_pairs={{0,8},{2,10},{4,12},{6,14},{8,0},{10,2},{12,4},{14,6},{16,24},{18,... | collective-permute-start | bytes 2064392 | tf_op jit(solution)/shard_map/ppermute | solution.py:256
  23.5 19.7 %collective-permute-start.2 = (f32[32,1792]{1,0:T(8,128)}, f32[32,1792]{1,0:T(8,128)S(1)}, u32[]{:S(2)}, u32[]{:S(2)}) collective-permute-start(f32[32,1792]{1,0:T(8,128)} %collective-permute-done.1.refs_1_.refs_2_), channel_id=1, source_target_pairs={{0,8},{2,10},{4,12},{6,14},{8,0},{10,2},{12,4},{14,6},{16,24},{18,... | collective-permute-start | bytes 688136 | tf_op jit(solution)/shard_map/ppermute | solution.py:256
  24.0 38.5 %collective-permute-start.4 = (s32[16,3072]{1,0:T(8,128)}, s32[16,3072]{1,0:T(8,128)}, u32[]{:S(2)}, u32[]{:S(2)}) collective-permute-start(s32[16,3072]{1,0:T(8,128)} %get-tuple-element.29), channel_id=1, source_target_pairs={{0,16},{2,18},{4,20},{6,22},{8,24},{10,26},{12,28},{14,30},{16,0},... | collective-permute-start | bytes 589832 | tf_op jit(solution)/shard_map/ppermute | solution.py:256
  27.6 39.6 %collective-permute-start = (s32[16,3072]{1,0:T(8,128)}, s32[16,3072]{1,0:T(8,128)}, u32[]{:S(2)}, u32[]{:S(2)}) collective-permute-start(s32[16,3072]{1,0:T(8,128)} %get-tuple-element.27), channel_id=1, source_target_pairs={{0,24},{2,26},{4,28},{6,30},{8,16},{10,18},{12,20},{14,22},{16,8},... | collective-permute-start | bytes 589832 | tf_op jit(solution)/shard_map/ppermute | solution.py:256
  27.9 34.6 %collective-permute-start.5 = (f32[32,1792]{1,0:T(8,128)}, f32[32,1792]{1,0:T(8,128)}, u32[]{:S(2)}, u32[]{:S(2)}) collective-permute-start(f32[32,1792]{1,0:T(8,128)} %collective-permute-done.1.refs_1_.refs_2_), channel_id=1, source_target_pairs={{0,1},{1,0},{2,3},{3,2},{4,5},{5,4},{6,7},{7,6},{8,9},{9,8},{10,11... | collective-permute-start | bytes 688136 | tf_op jit(solution)/shard_map/ppermute | solution.py:256
  43.2 23.9 %collective-permute-start.3 = (f32[32,1792]{1,0:T(8,128)S(1)}, f32[32,1792]{1,0:T(8,128)S(1)}, u32[]{:S(2)}, u32[]{:S(2)}) collective-permute-start(f32[32,1792]{1,0:T(8,128)S(1)} %collective-permute-done.2.refs_1_.refs_4_), channel_id=1, source_target_pairs={{0,1},{1,0},{2,3},{3,2},{4,5},{5,4},{6,7},{7,6},{8,9},{9,8},{10,11... | collective-permute-start | bytes 688136 | tf_op jit(solution)/shard_map/ppermute | solution.py:256
  45.3 31.5 %all-to-all-start = ((s32[4,16,3072]{2,1,0:T(8,128)}), s32[4,16,3072]{2,1,0:T(8,128)S(1)}, u32[]{:S(2)}, u32[]{:S(2)}) async-start(s32[4,16,3072]{2,1,0:T(8,128)} %bitcast.56), calls=%async_computation | async-start | bytes 1572864 | tf_op jit(solution)/shard_map/all_to_all | solution.py:378
  69.9 2.8 %collective-permute-start.7 = (f32[544,512]{1,0:T(8,128)S(1)}, f32[544,512]{1,0:T(8,128)S(1)}, u32[]{:S(2)}, u32[]{:S(2)}) collective-permute-start(f32[544,512]{1,0:T(8,128)S(1)} %shard_map.98), channel_id=1, source_target_pairs={{0,2},{2,0},{4,6},{6,4},{8,10},{10,8},{12,14},{14,12},{16,18},{18,... | collective-permute-start | bytes 3342344 | tf_op jit(solution)/shard_map/ppermute | solution.py:256
  75.8 1.0 copy-start.5
  76.8 26.8 %collective-permute-start.10 = (f32[544,512]{1,0:T(8,128)}, f32[544,512]{1,0:T(8,128)S(1)}, u32[]{:S(2)}, u32[]{:S(2)}) collective-permute-start(f32[544,512]{1,0:T(8,128)} %copy-done.5), channel_id=1, source_target_pairs={{0,4},{2,6},{4,0},{6,2},{8,12},{10,14},{12,8},{14,10},{16,20},{18,... | collective-permute-start | bytes 3342344 | tf_op jit(solution)/shard_map/ppermute | solution.py:256
  78.4 1.2 %copy-start.4 = (f32[544,512]{1,0:T(8,128)S(1)}, f32[544,512]{1,0:T(8,128)}, u32[]{:S(2)}) copy-start(f32[544,512]{1,0:T(8,128)} %copy-done.3) | copy-start | bytes 3342340
  90.7 2.0 %collective-permute-start.8 = (f32[272,512]{1,0:T(8,128)S(1)}, f32[272,512]{1,0:T(8,128)S(1)}, u32[]{:S(2)}, u32[]{:S(2)}) collective-permute-start(f32[272,512]{1,0:T(8,128)S(1)} %get-tuple-element.52), channel_id=1, source_target_pairs={{0,2},{2,0},{4,6},{6,4},{8,10},{10,8},{12,14},{14,12},{16,18},{18,... | collective-permute-start | bytes 1671176 | tf_op jit(solution)/shard_map/ppermute | solution.py:256
  90.8 2.7 %collective-permute-start.9 = (f32[272,512]{1,0:T(8,128)S(1)}, f32[272,512]{1,0:T(8,128)S(1)}, u32[]{:S(2)}, u32[]{:S(2)}) collective-permute-start(f32[272,512]{1,0:T(8,128)S(1)} %get-tuple-element.51), channel_id=1, source_target_pairs={{0,2},{2,0},{4,6},{6,4},{8,10},{10,8},{12,14},{14,12},{16,18},{18,... | collective-permute-start | bytes 1671176 | tf_op jit(solution)/shard_map/ppermute | solution.py:256
  103.6 9.0 %copy-start.2 = (f32[3072,32]{0,1:T(8,128)S(1)}, f32[3072,32]{0,1:T(8,128)}, u32[]{:S(2)}) copy-start(f32[3072,32]{0,1:T(8,128)} %param.7) | copy-start | bytes 1179652
  105.7 6.7 %collective-permute-start.11 = (f32[32,128]{1,0:T(8,128)S(1)}, f32[32,128]{1,0:T(8,128)S(1)}, u32[]{:S(2)}, u32[]{:S(2)}) collective-permute-start(f32[32,128]{1,0:T(8,128)S(1)} %pad_maximum_fusion.1), channel_id=1, source_target_pairs={{0,1},{1,0},{2,3},{3,2},{4,5},{5,4},{6,7},{7,6},{8,9},{9,8},{10,11... | collective-permute-start | bytes 49160 | tf_op jit(solution)/shard_map/ppermute | solution.py:256
  106.3 12.7 %all-to-all-start.1 = ((f32[8,8,128]{2,1,0:T(8,128)}), f32[8,8,128]{2,1,0:T(8,128)S(1)}, u32[]{:S(2)}, u32[]{:S(2)}) async-start(f32[8,8,128]{2,1,0:T(8,128)} %shard_map.101), calls=%async_computation.1 | async-start | bytes 65536 | tf_op jit(solution)/shard_map/all_to_all | solution.py:417
  112.6 7.1 %copy-start.12 = (f32[8,2,32]{2,1,0:T(2,128)}, f32[8,2,32]{2,1,0:T(2,128)S(1)}, u32[]{:S(2)}) copy-start(f32[8,2,32]{2,1,0:T(2,128)S(1)} %fusion.5) | copy-start | bytes 6148
  (6 other events, 5.3 us)

commit v6 on v5

--- a/solution.py
+++ b/solution.py
@@ -9,6 +9,7 @@
 
 BINS = 64
 LANES = 128
+VMEM_BYTES = 12 * 1024 * 1024
 SMALL_COST = pl.CostEstimate(flops=1000000, bytes_accessed=1000000, transcendentals=0)
 
 
@@ -64,7 +65,17 @@
 
 
 def prep_kernel(
-    own, blocks, starts_ref, split_ref, logits_ref, labels_ref, nodes_ref, codes_ref, *refs
+    own,
+    blocks,
+    ids_ref,
+    feature_ref,
+    bin_ref,
+    missing_ref,
+    logits_ref,
+    labels_ref,
+    nodes_ref,
+    codes_ref,
+    *refs,
 ):
     info_ref, half_ref, flag_ref = refs[:3]
     outs, turned = refs[3:-1], refs[-1]
@@ -72,14 +83,18 @@
     half, width = rows // 2, half_width(rows)
     chunks = half // LANES
     turned[...] = codes_ref[...].T
-    for (with_info, pieces), out_ref in zip(blocks, outs):
-        base = classes if with_info else 0
-        for i, (taker, quarter) in enumerate(pieces):
-            start = pl.multiple_of(starts_ref[taker, quarter], own)
-            low = base + i * own
-            out_ref[low : low + own, :rows] = turned[pl.ds(start, own), :].astype(out_ref.dtype)
-            if with_info:
-                out_ref[low : low + own, rows:] = jnp.zeros((own, 2 * width - rows), out_ref.dtype)
+    for (infos, pieces), out_ref in zip(blocks, outs):
+        for i, start_of in enumerate(pieces):
+            start = pl.multiple_of(start_of(ids_ref[0]), own)
+            if infos == 0:
+                out_ref[i * own : (i + 1) * own, :] = turned[pl.ds(start, own), :]
+                continue
+            cut = rows * infos // 2
+            for h in range(2 // infos):
+                low = classes + (h * len(pieces) + i) * own
+                part = turned[pl.ds(start, own), h * cut : (h + 1) * cut]
+                out_ref[low : low + own, :cut] = part.astype(out_ref.dtype)
+                out_ref[low : low + own, cut:] = jnp.zeros((own, infos * width - cut), out_ref.dtype)
     expo_vals = jnp.exp(logits_ref[...])
     prob = expo_vals / jnp.sum(expo_vals, axis=0, keepdims=True)
     labels = labels_ref[...].astype(jnp.float32)
@@ -88,14 +103,14 @@
     node = jnp.concatenate([nodes[i : i + 1] for i in range(2 * chunks)], axis=1)
 
     feats = turned.shape[0]
-    node_count = split_ref.shape[1]
+    node_count = feature_ref.shape[0]
     side = jnp.zeros((1, rows), jnp.float32)
     for n in range(node_count):
-        col = split_ref[0, n]
+        col = feature_ref[n] - ids_ref[1] * feats
         held = (col >= 0) & (col < feats)
         code = turned[pl.ds(jnp.clip(col, 0, feats - 1), 1), :]
-        threshold = jnp.where(held, split_ref[1, n], -1)
-        missing = jnp.where(held & (split_ref[2, n] == 1), BINS - 1, -1)
+        threshold = jnp.where(held, bin_ref[n], -1)
+        missing = jnp.where(held & (missing_ref[n] == 1), BINS - 1, -1)
         left = (code < threshold) | (code == missing)
         value = jnp.where(left, 1.0, jnp.where(held, 2.0, 0.0))
         side = jnp.where(node == float(n), value, side)
@@ -125,10 +140,10 @@
         info_ref[:, h * width + half + LANES : (h + 1) * width] = jnp.concatenate(
             [nodes[some], long_pad], axis=0
         )
-    half_ref[...] = jnp.where(split_ref[3, 0] == 0, info_ref[:, :width], info_ref[:, width:])
-    for (with_info, _), out_ref in zip(blocks, outs):
-        if with_info:
-            out_ref[:classes, :] = info_ref[...]
+    half_ref[...] = jnp.where(ids_ref[1] == 0, info_ref[:, :width], info_ref[:, width:])
+    for (infos, _), out_ref in zip(blocks, outs):
+        if infos > 0:
+            out_ref[:classes, :] = half_ref[...] if infos == 1 else info_ref[...]
 
 
 def gradients(prob, label):
@@ -187,34 +202,42 @@
             gain_ref[n, 2 * pair + 1 : 2 * pair + 2, :] = gain[:, 2 * BINS :]
 
 
-def add_kernel(classes, node_count, own, plan, place_ref, *refs):
-    outs = len(plan[0][2])
-    arrays = 1 + max(max((c,) + i) for c, i, _ in plan)
+def add_kernel(classes, node_count, own, plan, carry, ids_ref, *refs):
+    outs = len(plan[0][3])
+    arrays = 1 + max(max((c,) + i) for _, c, i, _ in plan)
     out_refs = refs[-outs:]
     held_refs = refs[arrays:-outs]
     pairs = 2 * classes * node_count
-    for s, (codes_at, info_at, firsts) in enumerate(plan):
+    for s, (m, codes_at, info_at, firsts) in enumerate(plan):
         codes_ref = refs[codes_at]
+        line = (ids_ref[0] >> 2) ^ (m >> 2)
         if len(codes_ref.shape) == 3:
-            codes_ref = codes_ref.at[place_ref[0, s]]
+            codes_ref = codes_ref.at[line]
         if len(info_at) == 1:
             width = refs[info_at[0]].shape[1] // 2
             low, high = (refs[info_at[0]][:classes, h * width : (h + 1) * width] for h in range(2))
             sums_from = low
         else:
             width = refs[info_at[0]].shape[1]
-            near, far = (refs[i][...] for i in info_at)
-            low = jnp.where(place_ref[2, s] == 0, near, far)
-            high = jnp.where(place_ref[2, s] == 0, far, near)
+            near, far = (refs[i][:classes, :] for i in info_at)
+            low = jnp.where(ids_ref[1] == 0, near, far)
+            high = jnp.where(ids_ref[1] == 0, far, near)
             sums_from = near
         rows = 2 * (width - 2 * LANES)
         masked = masked_gradients((low, high), rows, node_count)
         sums = child_sums(sums_from, rows, node_count)
         for i, first in enumerate(firsts):
             out_ref = out_refs[i]
+            if codes_ref.shape[1] < rows:
+                second = first + (codes_ref.shape[0] - classes) // 2
+                codes = jnp.concatenate(
+                    [codes_ref[low : low + own, : rows // 2] for low in (first, second)], axis=1
+                )
+            else:
+                codes = codes_ref[first : first + own, :rows]
             product = lax.dot_general(
                 masked,
-                one_hot(codes_ref[first : first + own, :rows]),
+                one_hot(codes),
                 (((1,), (1,)), ((), ())),
                 preferred_element_type=jnp.float32,
             )
@@ -224,25 +247,28 @@
                 else:
                     out_ref[...] = jnp.zeros(out_ref.shape, out_ref.dtype)
             out_ref[:pairs, :] += product
-            for line in range(out_ref.shape[1] // LANES):
-                here = jnp.where(place_ref[0, s] == line, 1.0, 0.0)
-                band = pl.ds(pl.multiple_of(pairs + place_ref[1, s] * node_count, node_count), node_count)
-                out_ref[band, line * LANES : (line + 1) * LANES] += here * sums
-
-
-def add_rows(classes, node_count, own, plan, places, arrays, *held):
+            if not carry:
+                continue
+            low_row = pairs + (ids_ref[0] & 3) * node_count
+            band = pl.ds(pl.multiple_of(low_row, node_count), node_count)
+            for i in range(out_ref.shape[1] // LANES):
+                here = jnp.where(line == i, 1.0, 0.0)
+                out_ref[band, i * LANES : (i + 1) * LANES] += here * sums
+
+
+def add_rows(classes, node_count, own, carry, ids, plan, arrays, *held):
     shape = (2 * classes * node_count + 4 * node_count, own * BINS)
     whole = pl.BlockSpec(memory_space=pltpu.VMEM)
-    outs = len(plan[0][2])
+    outs = len(plan[0][3])
     return pl.pallas_call(
-        functools.partial(add_kernel, classes, node_count, own, plan),
+        functools.partial(add_kernel, classes, node_count, own, plan, carry),
         in_specs=[pl.BlockSpec(memory_space=pltpu.SMEM)]
         + [whole] * (len(arrays) + len(held) * outs),
         out_specs=[whole] * outs,
         out_shape=[jax.ShapeDtypeStruct(shape, jnp.float32)] * outs,
-        compiler_params=pltpu.CompilerParams(vmem_limit_bytes=20 * 1024 * 1024),
+        compiler_params=pltpu.CompilerParams(vmem_limit_bytes=VMEM_BYTES),
         cost_estimate=SMALL_COST,
-    )(places, *arrays, *[hist for hists in held for hist in hists])
+    )(ids, *arrays, *[hist for hists in held for hist in hists])
 
 
 def gain_kernel(classes, node_count, *refs):
@@ -264,7 +290,7 @@
     return x
 
 
-def prepare(blocks, starts, logits_t, labels, node_ids, bin_codes, splits):
+def prepare(blocks, ids, splits, logits_t, labels, node_ids, bin_codes):
     classes, rows_dev = logits_t.shape
     feats_dev = bin_codes.shape[1]
     own = 8
@@ -276,23 +302,24 @@
         jax.ShapeDtypeStruct((classes, width), jnp.float32),
         jax.ShapeDtypeStruct((1, rows_dev), jnp.float32),
     ]
-    for with_info, pieces in blocks:
+    for infos, pieces in blocks:
         codes = len(pieces) * own
-        if with_info:
-            shapes.append(jax.ShapeDtypeStruct((classes + codes, 2 * width), jnp.float32))
+        if infos == 0:
+            shapes.append(jax.ShapeDtypeStruct((codes, rows_dev), jnp.int32))
         else:
-            shapes.append(jax.ShapeDtypeStruct((codes, rows_dev), jnp.int32))
+            shape = (classes + codes * 2 // infos, infos * width)
+            shapes.append(jax.ShapeDtypeStruct(shape, jnp.float32))
     return pl.pallas_call(
         functools.partial(prep_kernel, own, blocks),
-        in_specs=[scalars, scalars] + [whole] * 4,
+        in_specs=[scalars] * 4 + [whole] * 4,
         out_specs=[whole] * len(shapes),
         out_shape=shapes,
         scratch_shapes=[pltpu.VMEM((feats_dev, rows_dev), jnp.int32)],
-        compiler_params=pltpu.CompilerParams(vmem_limit_bytes=20 * 1024 * 1024),
+        compiler_params=pltpu.CompilerParams(vmem_limit_bytes=VMEM_BYTES),
         cost_estimate=SMALL_COST,
     )(
-        starts,
-        splits,
+        ids,
+        *splits,
         logits_t,
         labels.reshape(-1, LANES),
         node_ids.reshape(-1, LANES),
@@ -328,68 +355,66 @@
     own = 8
     row_index = lax.axis_index("rows")
     feat_index = lax.axis_index("feat")
-    splits = jnp.stack(
-        [
-            split_feature - feat_index * feats_dev,
-            split_bin,
-            split_missing,
-            jnp.zeros_like(split_bin) + feat_index,
-        ]
-    )
+    ids = jnp.stack([row_index, feat_index]).astype(jnp.int32)
+    splits = (split_feature, split_bin, split_missing)
     logits_t = logits.T
-    add = functools.partial(add_rows, classes, node_count, own)
     if feats_dev != own * n_rows or n_rows != 16 or lax.axis_size("feat") != 2:
-        return by_groups(
-            logits_t, labels, node_ids, bin_codes, splits, row_index, per_node, pairs_dev
+        return by_groups(logits_t, labels, node_ids, bin_codes, splits, ids, per_node, pairs_dev)
+    add = functools.partial(add_rows, classes, node_count, own, True, ids)
+
+    def start(taker):
+        return (taker & 1) * pairs_dev + (taker >> 1) * own
+
+    def quarters(m, which):
+        return tuple(lambda row, low=m ^ 3 ^ q: start(row ^ low) for q in which)
+
+    def line_quarters(which):
+        return tuple(
+            lambda row, z=z, low=3 ^ q: start((z * 4 + (row & 3)) ^ low) for z in range(4) for q in which
         )
 
-    starts = []
-    for taker in [row_index ^ m for m in (0, 4, 8, 12)] + [z * 4 + row_index % 4 for z in range(4)]:
-        takers = [taker ^ low for low in (3, 2, 1, 0)]
-        starts.append(jnp.stack([t % per_node * pairs_dev + t // per_node * own for t in takers]))
-    starts = jnp.stack(starts)
     blocks = (
-        (False, ((0, 0), (0, 1), (0, 2), (0, 3))),
-        (True, ((1, 0), (1, 1))),
-        (False, ((2, 0), (2, 1))),
-        (False, ((3, 0), (3, 1))),
-        (False, tuple((4 + z, quarter) for z in range(4) for quarter in (2, 3))),
+        (0, quarters(0, (0, 1, 2, 3))),
+        (1, quarters(4, (0, 1))),
+        (0, quarters(8, (0, 1))),
+        (0, quarters(12, (0, 1))),
+        (0, line_quarters((2, 3))),
     )
     info, half, flags, codes_0, rows_4, codes_8, codes_12, codes_late = prepare(
-        blocks, starts, logits_t, labels, node_ids, bin_codes, splits
-    )
-
-    def place(*lines):
-        line = jnp.stack([row_index // 4 ^ m // 4 for m in lines])
-        return jnp.stack([line, row_index % 4 + 0 * line, feat_index + 0 * line])
+        blocks, ids, splits, logits_t, labels, node_ids, bin_codes
+    )
 
     near_8 = swap(half, "rows", 8)
     rows_4 = swap(rows_4, "rows", 4)
     codes_8 = swap(codes_8, "rows", 8)
     codes_12 = swap(codes_12, "rows", 12)
+    hist_a, hist_b, hist_c, hist_d = add(
+        ((0, 0, (1,), (0, own, 2 * own, 3 * own)),), [codes_0, info]
+    )
+    near_8, hist_a, codes_late = lax.optimization_barrier((near_8, hist_a, codes_late))
     near_12 = swap(near_8, "rows", 4)
     far_8 = swap(near_8, "feat", 1)
-    far_12 = swap(near_12, "feat", 1)
-    hist_a, hist_b, hist_c, hist_d = add(
-        ((0, (1,), (0, own, 2 * own, 3 * own)),), place(0), [codes_0, info]
-    )
-    near_8, codes_late = lax.optimization_barrier((near_8, codes_late))
+    far_4 = swap(rows_4[:classes], "feat", 1)
     lines = [[4 * z + low for z in range(4)] for low in range(4)]
     codes_late = lax.all_to_all(
         codes_late.reshape(4, 2 * own, rows_dev), "rows", 0, 0, tiled=True, axis_index_groups=lines
     )
-    hists = add(((0, (0,), (classes, classes + own)),), place(4), [rows_4], [hist_a, hist_b])
-    hist_a, hist_b = add(((0, (1, 2), (0, own)),), place(8), [codes_8, near_8, far_8], hists)
-    (to_core,) = add(((0, (1, 2), (0,)),), place(12), [codes_12, near_12, far_12], [hist_a])
+    hist_a, hist_b = add(
+        ((4, 0, (0, 1), (classes, classes + own)),), [rows_4, far_4], [hist_a, hist_b]
+    )
+    near_12, codes_8, codes_12, hist_a = lax.optimization_barrier((near_12, codes_8, codes_12, hist_a))
+    far_12 = swap(near_12, "feat", 1)
+    hist_a, hist_b = add(((8, 0, (1, 2), (0, own)),), [codes_8, near_8, far_8], [hist_a, hist_b])
+    (to_core,) = add(((12, 0, (1, 2), (0,)),), [codes_12, near_12, far_12], [hist_a])
     from_core = swap(to_core, "rows", 1)
-    (to_plane,) = add(
-        ((0, (1, 2), (own,)),), place(12), [codes_12, near_12, far_12], [hist_b], [from_core]
-    )
+    (to_plane,) = add(((12, 0, (1, 2), (own,)),), [codes_12, near_12, far_12], [hist_b], [from_core])
     to_plane, codes_late = lax.optimization_barrier((to_plane, codes_late))
     from_plane = swap(to_plane, "rows", 2)
-    late = [codes_late, rows_4, near_8, far_8, near_12, far_12]
+    late = [codes_late, rows_4, far_4, near_8, far_8, near_12, far_12]
     to_core, kept = add(
-        tuple((0, i, (0, own)) for i in ((1,), (2, 3), (4, 5))), place(4, 8, 12), late, [hist_c, hist_d]
+        tuple((m, 0, i, (0, own)) for m, i in ((4, (1, 2)), (8, (3, 4)), (12, (5, 6)))),
+        late,
+        [hist_c, hist_d],
     )
     middle = to_core.shape[0] // 2
     from_core = [swap(part, "rows", 1) for part in (to_core[:middle], to_core[middle:])]
@@ -402,7 +427,7 @@
         out_specs=pl.BlockSpec(memory_space=pltpu.VMEM),
         out_shape=jax.ShapeDtypeStruct((node_count, own, 2 * BINS), jnp.float32),
         scratch_shapes=[pltpu.VMEM((pairs, own * BINS), jnp.float32)],
-        compiler_params=pltpu.CompilerParams(vmem_limit_bytes=16 * 1024 * 1024),
+        compiler_params=pltpu.CompilerParams(vmem_limit_bytes=VMEM_BYTES),
         cost_estimate=SMALL_COST,
     )(from_core, from_plane, kept)
     gains, from_plane = lax.optimization_barrier((gains, from_plane))
@@ -418,18 +443,17 @@
     return (new_logits, gain_rows.reshape(1, pairs_dev, 2 * BINS), leaves)
 
 
-def by_groups(logits_t, labels, node_ids, bin_codes, splits, row_index, per_node, pairs_dev):
+def by_groups(logits_t, labels, node_ids, bin_codes, splits, ids, per_node, pairs_dev):
     classes, rows_dev = logits_t.shape
     feats_dev = bin_codes.shape[1]
-    node_count = splits.shape[1]
+    node_count = splits[0].shape[0]
     n_rows = lax.axis_size("rows")
     width = 2 * classes
     own = 8
     group = feats_dev // own
     group_count = n_rows // group
-    starts = jnp.arange(group, dtype=jnp.int32)[:, None] * own
-    blocks = tuple((True, ((r, 0),)) for r in range(group))
-    info, _, flags, *rows_out = prepare(blocks, starts, logits_t, labels, node_ids, bin_codes, splits)
+    blocks = tuple((2, (lambda row, r=r: r * own,)) for r in range(group))
+    info, _, flags, *rows_out = prepare(blocks, ids, splits, logits_t, labels, node_ids, bin_codes)
     members = [[g * group + r for r in range(group)] for g in range(group_count)]
     rows_in = lax.all_to_all(
         jnp.stack(rows_out), "rows", 0, 0, tiled=True, axis_index_groups=members
@@ -437,9 +461,8 @@
     hists = []
     for r in range(group):
         held = [hists] if hists else []
-        nowhere = jnp.full((2, 1), -1, jnp.int32) * jnp.array([[1], [0]], jnp.int32)
         hists = add_rows(
-            classes, node_count, own, ((0, (0,), (classes,)),), nowhere, [rows_in[r]], *held
+            classes, node_count, own, False, ids, ((0, 0, (0,), (classes,)),), [rows_in[r]], *held
         )
     sums = lax.psum(child_sums(info[:, : half_width(rows_dev)], rows_dev, node_count), ("rows", "feat"))
     side_count = lax.psum(flags, "feat")

time: 120 us -> 114 us (0.950)
  waiting for transfers between devices: 43 us -> 32.8 us
  local copies, waits for them, and re-layouts: 8.93 us -> 17.5 us
  Pallas kernels: 37.5 us -> 34.4 us
  between operations: 2.39 us -> 0.85 us
    ppermute x12 -> x13, waiting for transfers between devices: 37.6 us -> 25.7 us  [swap(): return lax.ppermute(x, axis, [(i, i ^ bit) for i in range(size)])]
    unnamed x33 -> x45, local copies, waits for them, and re-layouts: 8.15 us -> 17.4 us
    pallas_call x6, Pallas kernels: 32.6 us -> 30.6 us  [add_rows(): pl.pallas_call(functools.partial(add_kernel, classes, node_count, own, pl...]
    ppermute x12 -> x13, starting transfers between devices: 15.9 us -> 17.7 us  [swap(): return lax.ppermute(x, axis, [(i, i ^ bit) for i in range(size)])]
    all_to_all x1, waiting for transfers between devices: 0.01 us -> 1.75 us  [local(): lax.all_to_all(codes_late.reshape(4, 2 * own, rows_dev), 'rows', 0, 0, ti...]
  transfers between devices with their start and end apart: 14 -> 15, of which waited for: 7 -> 9; matrix products, arithmetic and copies ran while one was open for 2% -> 1% of each run, Pallas kernels for 27% -> 27%
where the time goes in v6:
time: 114 us; the launch traced here: 113 us
  Pallas kernels  34.4 us (30%)
  waiting for transfers between devices  32.8 us (29%)
  starting transfers between devices  26.5 us (23%)
  local copies, waits for them, and re-layouts  17.5 us (15%)
    pallas_call x6, Pallas kernels, add_rows(): pl.pallas_call(functools.partial(add_kernel, classes, node_count, own, pl...  30.6 us
    ppermute x13, waiting for transfers between devices, swap(): return lax.ppermute(x, axis, [(i, i ^ bit) for i in range(size)])  25.7 us
    ppermute x13, starting transfers between devices, swap(): return lax.ppermute(x, axis, [(i, i ^ bit) for i in range(size)])  17.7 us
    unnamed x45, local copies, waits for them, and re-layouts  17.4 us
    all_to_all x1, waiting for transfers between devices, local(): lax.all_to_all(gains, 'rows', 0, 0, tiled=True, axis_index_groups=halves)  5.36 us
    all_to_all x1, starting transfers between devices, local(): lax.all_to_all(gains, 'rows', 0, 0, tiled=True, axis_index_groups=halves)  5.13 us
    all_to_all x1, starting transfers between devices, local(): lax.all_to_all(codes_late.reshape(4, 2 * own, rows_dev), 'rows', 0, 0, ti...  3.67 us
  transfers between devices with their start and end apart: 15, of which 9 were waited for; matrix products, arithmetic and copies ran while one was open for 1% of the time, Pallas kernels for 27%

profile of v6, /device:TPU:0, one launch (start us, length us, event | category | flops | bytes accessed | tf_op | source)
XLA Modules:
  0.0 113.5 jit_solution(7430249699790953561)
XLA Ops:
  0.7 1.4 %copy-done = s32[3072,128]{1,0:T(8,128)S(1)} copy-done((s32[3072,128]{1,0:T(8,128)S(1)}, s32[3072,128]{1,0:T(8,128)}, u32[]{:S(2)}) %copy-start) | copy-done | bytes 1572888
  6.5 1.7 %shard_map.94 = (f32[32,3584]{1,0:T(8,128)S(1)}, f32[32,1792]{1,0:T(8,128)S(1)}, f32[1,3072]{1,0:T(1,128)S(1)}, s32[32,3072]{1,0:T(8,128)S(1)}, f32[64,1792]{1,0...) custom-call(s32[2]{0:T(128)S(1)} %pad_add_fusion.ids_ref, s32[8]{0:T(128)S(1)} %copy-done.18, ...), custom_call_target="tpu_custom_call" | custom-call | flops 1000000 | bytes 1000000 | tf_op jit(solution)/shard_map/pallas_call | solution.py:312
  9.1 3.0 %collective-permute-start.4 = (f32[64,1792]{1,0:T(8,128)S(1)}, f32[64,1792]{1,0:T(8,128)S(1)}, u32[]{:S(2)}, u32[]{:S(2)}) collective-permute-start(f32[64,1792]{1,0:T(8,128)S(1)} %get-tuple-element.40), channel_id=1, source_target_pairs={{0,8},{2,10},{4,12},{6,14},{8,0},{10,2},{12,4},{14,6},{16,24},{18,... | collective-permute-start | bytes 1376264 | tf_op jit(solution)/shard_map/ppermute | solution.py:282
  12.1 2.6 %collective-permute-start = (f32[32,1792]{1,0:T(8,128)S(1)}, f32[32,1792]{1,0:T(8,128)S(1)}, u32[]{:S(2)}, u32[]{:S(2)}) collective-permute-start(f32[32,1792]{1,0:T(8,128)S(1)} %get-tuple-element.32), channel_id=1, source_target_pairs={{0,16},{2,18},{4,20},{6,22},{8,24},{10,26},{12,28},{14,30},{16,0},... | collective-permute-start | bytes 688136 | tf_op jit(solution)/shard_map/ppermute | solution.py:282
  14.7 7.2 %shard_map.95 = (f32[544,512]{1,0:T(8,128)S(1)}, f32[544,512]{1,0:T(8,128)S(1)}, f32[544,512]{1,0:T(8,128)S(1)}, f32[544,512]{1,0:T(8,128)S(1)}) custom-call(s32[2]{0:T(128)S(1)} %pad_add_fusion.ids_ref, s32[32,3072]{1,0:T(8,128)S(1)} %get-tuple-element.33.refs_0_, f32[32,3584]{1,0:T(8,128)S(1)} %get-tuple-element.34.refs_1_), custom_call_target="tpu_custom_call" | custom-call | flops 1000000 | bytes 1000000 | tf_op jit(solution)/shard_map/pallas_call | solution.py:263
  23.0 4.6 %collective-permute-done.4.refs_0_.refs_1_ = f32[64,1792]{1,0:T(8,128)S(1)} collective-permute-done((f32[64,1792]{1,0:T(8,128)S(1)}, f32[64,1792]{1,0:T(8,128)S(1)}, u32[]{:S(2)}, u32[]{:S(2)}) %collective-permute-start.4) | collective-permute-done | bytes 458784 | tf_op jit(solution)/shard_map/ppermute | solution.py:282
  27.6 1.7 %collective-permute-start.5 = (f32[32,1792]{1,0:T(8,128)S(1)}, f32[32,1792]{1,0:T(8,128)S(1)}, u32[]{:S(2)}, u32[]{:S(2)}) collective-permute-start(f32[32,1792]{1,0:T(8,128)S(1)} %slice.47), channel_id=1, source_target_pairs={{0,1},{1,0},{2,3},{3,2},{4,5},{5,4},{6,7},{7,6},{8,9},{9,8},{10,11... | collective-permute-start | bytes 688136 | tf_op jit(solution)/shard_map/ppermute | solution.py:282
  30.3 3.2 %collective-permute-start.2 = (s32[16,3072]{1,0:T(8,128)S(1)}, s32[16,3072]{1,0:T(8,128)S(1)}, u32[]{:S(2)}, u32[]{:S(2)}) collective-permute-start(s32[16,3072]{1,0:T(8,128)S(1)} %get-tuple-element.38), channel_id=1, source_target_pairs={{0,16},{2,18},{4,20},{6,22},{8,24},{10,26},{12,28},{14,30},{16,0},... | collective-permute-start | bytes 589832 | tf_op jit(solution)/shard_map/ppermute | solution.py:282
  34.6 4.0 %shard_map.96 = (f32[544,512]{1,0:T(8,128)S(1)}, f32[544,512]{1,0:T(8,128)S(1)}) custom-call(s32[2]{0:T(128)S(1)} %pad_add_fusion.ids_ref, f32[64,1792]{1,0:T(8,128)S(1)} %collective-permute-done.4.refs_0_.refs_1_, f32[32,1792]{1,0:T(8,128)S(1)} %collective-permute-done.5.refs_1_.refs_2_, f32[544,512]{1,0:T(8,128)S(1)} %get-tuple-element.41.refs_2_, ...), custom_call_target="tpu_custom_call" | custom-call | flops 1000000 | bytes 1000000 | tf_op jit(solution)/shard_map/pallas_call | solution.py:263
  40.6 6.9 %collective-permute-done.2.refs_0_ = s32[16,3072]{1,0:T(8,128)S(1)} collective-permute-done((s32[16,3072]{1,0:T(8,128)S(1)}, s32[16,3072]{1,0:T(8,128)S(1)}, u32[]{:S(2)}, u32[]{:S(2)}) %collective-permute-start.2) | collective-permute-done | bytes 196640 | tf_op jit(solution)/shard_map/ppermute | solution.py:282
  50.1 3.7 %all-to-all-start = ((s32[4,16,3072]{2,1,0:T(8,128)}), s32[4,16,3072]{2,1,0:T(8,128)S(1)}, u32[]{:S(2)}, u32[]{:S(2)}) async-start(s32[4,16,3072]{2,1,0:T(8,128)} %bitcast.18), calls=%async_computation | async-start | bytes 1572864 | tf_op jit(solution)/shard_map/all_to_all | solution.py:399
  57.3 4.0 %shard_map.97 = (f32[544,512]{1,0:T(8,128)S(1)}, f32[544,512]{1,0:T(8,128)S(1)}) custom-call(s32[2]{0:T(128)S(1)} %pad_add_fusion.ids_ref, s32[16,3072]{1,0:T(8,128)S(1)} %copy-done.14, f32[32,1792]{1,0:T(8,128)S(1)} %collective-permute-done.refs_1_.refs_3_, f32[32,1792]{1,0:T(8,128)S(1)} %collective-permute-done.7.refs_2_.refs_4_, ...), custom_call_target="tpu_custom_call" | custom-call | flops 1000000 | bytes 1000000 | tf_op jit(solution)/shard_map/pallas_call | solution.py:263
  61.3 2.4 %shard_map.98 = f32[544,512]{1,0:T(8,128)S(1)} custom-call(s32[2]{0:T(128)S(1)} %pad_add_fusion.ids_ref, s32[16,3072]{1,0:T(8,128)S(1)} %copy-done.11, f32[32,1792]{1,0:T(8,128)S(1)} %collective-permute-done.1.refs_1_.refs_5_, f32[32,1792]{1,0:T(8,128)S(1)} %collective-permute-done.6.refs_2_.refs_6_, f32[544,512]{1,0:T(8,128)S(1)} %get-tuple-element.50.refs_3_), custom_call_target="tpu_custom_call" | custom-call | flops 1000000 | bytes 1000000 | tf_op jit(solution)/shard_map/pallas_call | solution.py:263
  63.7 2.7 %collective-permute-done.8.refs_4_ = f32[544,512]{1,0:T(8,128)S(1)} collective-permute-done((f32[544,512]{1,0:T(8,128)S(1)}, f32[544,512]{1,0:T(8,128)S(1)}, u32[]{:S(2)}, u32[]{:S(2)}) %collective-permute-start.8) | collective-permute-done | bytes 1114144 | tf_op jit(solution)/shard_map/ppermute | solution.py:282
  66.5 2.4 %shard_map.99 = f32[544,512]{1,0:T(8,128)S(1)} custom-call(s32[2]{0:T(128)S(1)} %pad_add_fusion.ids_ref, s32[16,3072]{1,0:T(8,128)S(1)} %copy-done.11, f32[32,1792]{1,0:T(8,128)S(1)} %collective-permute-done.1.refs_1_.refs_5_, f32[32,1792]{1,0:T(8,128)S(1)} %collective-permute-done.6.refs_2_.refs_6_, f32[544,512]{1,0:T(8,128)S(1)} %get-tuple-element.49.refs_3_, ...), custom_call_target="tpu_custom_call" | custom-call | flops 1000000 | bytes 1000000 | tf_op jit(solution)/shard_map/pallas_call | solution.py:263
  69.8 1.7 %all-to-all-done.refs_0_ = s32[4,16,3072]{2,1,0:T(8,128)S(1)} async-done(((s32[4,16,3072]{2,1,0:T(8,128)}), s32[4,16,3072]{2,1,0:T(8,128)S(1)}, u32[]{:S(2)}, u32[]{:S(2)}) %all-to-all-start) | async-done | bytes 786464 | tf_op jit(solution)/shard_map/all_to_all | solution.py:399
  71.6 1.6 %collective-permute-start.11 = (f32[544,512]{1,0:T(8,128)}, f32[544,512]{1,0:T(8,128)S(1)}, u32[]{:S(2)}, u32[]{:S(2)}) collective-permute-start(f32[544,512]{1,0:T(8,128)} %copy-done.5), channel_id=1, source_target_pairs={{0,4},{2,6},{4,0},{6,2},{8,12},{10,14},{12,8},{14,10},{16,20},{18,... | collective-permute-start | bytes 3342344 | tf_op jit(solution)/shard_map/ppermute | solution.py:282
  74.4 10.7 %shard_map.100 = (f32[544,512]{1,0:T(8,128)S(1)}, f32[544,512]{1,0:T(8,128)S(1)}) custom-call(s32[2]{0:T(128)S(1)} %pad_add_fusion.ids_ref, s32[4,16,3072]{2,1,0:T(8,128)S(1)} %all-to-all-done.refs_0_, f32[64,1792]{1,0:T(8,128)S(1)} %collective-permute-done.4.refs_0_.refs_1_, f32[32,1792]{1,0:T(8,128)S(1)} %collective-permute-done.5.refs_1_.refs_2_, ...), custom_call_target="tpu_custom_call" | custom-call | flops 1000000 | bytes 1000000 | tf_op jit(solution)/shard_map/pallas_call | solution.py:263
  85.8 1.4 %collective-permute-done.10 = f32[272,512]{1,0:T(8,128)S(1)} collective-permute-done((f32[272,512]{1,0:T(8,128)S(1)}, f32[272,512]{1,0:T(8,128)S(1)}, u32[]{:S(2)}, u32[]{:S(2)}) %collective-permute-start.10) | collective-permute-done | bytes 557088 | tf_op jit(solution)/shard_map/ppermute | solution.py:282
  88.1 8.8 %collective-permute-done.11.refs_1_ = f32[544,512]{1,0:T(8,128)S(1)} collective-permute-done((f32[544,512]{1,0:T(8,128)}, f32[544,512]{1,0:T(8,128)S(1)}, u32[]{:S(2)}, u32[]{:S(2)}) %collective-permute-start.11) | collective-permute-done | bytes 1114144 | tf_op jit(solution)/shard_map/ppermute | solution.py:282
  96.9 2.1 %shard_map.101 = f32[8,8,128]{2,1,0:T(8,128)} custom-call(f32[544,512]{1,0:T(8,128)S(1)} %pad_maximum_fusion.refs_0_, f32[544,512]{1,0:T(8,128)S(1)} %collective-permute-done.11.refs_1_, f32[544,512]{1,0:T(8,128)S(1)} %get-tuple-element.57.refs_2_), custom_call_target="tpu_custom_call" | custom-call | flops 1000000 | bytes 1000000 | tf_op jit(solution)/shard_map/pallas_call | solution.py:424
  99.0 2.1 %collective-permute-start.12 = (f32[32,128]{1,0:T(8,128)S(1)}, f32[32,128]{1,0:T(8,128)S(1)}, u32[]{:S(2)}, u32[]{:S(2)}) collective-permute-start(f32[32,128]{1,0:T(8,128)S(1)} %pad_maximum_fusion.1), channel_id=1, source_target_pairs={{0,1},{1,0},{2,3},{3,2},{4,5},{5,4},{6,7},{7,6},{8,9},{9,8},{10,11... | collective-permute-start | bytes 49160 | tf_op jit(solution)/shard_map/ppermute | solution.py:282
  101.1 5.1 %all-to-all-start.1 = ((f32[8,8,128]{2,1,0:T(8,128)}), f32[8,8,128]{2,1,0:T(8,128)S(1)}, u32[]{:S(2)}, u32[]{:S(2)}) async-start(f32[8,8,128]{2,1,0:T(8,128)} %shard_map.101), calls=%async_computation.1 | async-start | bytes 65536 | tf_op jit(solution)/shard_map/all_to_all | solution.py:442
  107.5 5.4 %all-to-all-done.1 = f32[8,8,128]{2,1,0:T(8,128)S(1)} async-done(((f32[8,8,128]{2,1,0:T(8,128)}), f32[8,8,128]{2,1,0:T(8,128)S(1)}, u32[]{:S(2)}, u32[]{:S(2)}) %all-to-all-start.1) | async-done | bytes 32800 | tf_op jit(solution)/shard_map/all_to_all | solution.py:442
  (71 shorter events, 22.3 us)
Async XLA Ops:
  0.7 1.4 %copy-start = (s32[3072,128]{1,0:T(8,128)S(1)}, s32[3072,128]{1,0:T(8,128)}, u32[]{:S(2)}) copy-start(s32[3072,128]{1,0:T(8,128)} %codes_ref.1) | copy-start | bytes 4718596
  9.1 18.5 %collective-permute-start.4 = (f32[64,1792]{1,0:T(8,128)S(1)}, f32[64,1792]{1,0:T(8,128)S(1)}, u32[]{:S(2)}, u32[]{:S(2)}) collective-permute-start(f32[64,1792]{1,0:T(8,128)S(1)} %get-tuple-element.40), channel_id=1, source_target_pairs={{0,8},{2,10},{4,12},{6,14},{8,0},{10,2},{12,4},{14,6},{16,24},{18,... | collective-permute-start | bytes 1376264 | tf_op jit(solution)/shard_map/ppermute | solution.py:282
  12.1 17.2 %collective-permute-start = (f32[32,1792]{1,0:T(8,128)S(1)}, f32[32,1792]{1,0:T(8,128)S(1)}, u32[]{:S(2)}, u32[]{:S(2)}) collective-permute-start(f32[32,1792]{1,0:T(8,128)S(1)} %get-tuple-element.32), channel_id=1, source_target_pairs={{0,16},{2,18},{4,20},{6,22},{8,24},{10,26},{12,28},{14,30},{16,0},... | collective-permute-start | bytes 688136 | tf_op jit(solution)/shard_map/ppermute | solution.py:282
  22.0 1.0 copy-start.3
  27.6 7.0 %collective-permute-start.5 = (f32[32,1792]{1,0:T(8,128)S(1)}, f32[32,1792]{1,0:T(8,128)S(1)}, u32[]{:S(2)}, u32[]{:S(2)}) collective-permute-start(f32[32,1792]{1,0:T(8,128)S(1)} %slice.47), channel_id=1, source_target_pairs={{0,1},{1,0},{2,3},{3,2},{4,5},{5,4},{6,7},{7,6},{8,9},{9,8},{10,11... | collective-permute-start | bytes 688136 | tf_op jit(solution)/shard_map/ppermute | solution.py:282
  29.3 19.6 %collective-permute-start.1 = (f32[32,1792]{1,0:T(8,128)S(1)}, f32[32,1792]{1,0:T(8,128)S(1)}, u32[]{:S(2)}, u32[]{:S(2)}) collective-permute-start(f32[32,1792]{1,0:T(8,128)S(1)} %collective-permute-done.refs_1_.refs_3_), channel_id=1, source_target_pairs={{0,8},{2,10},{4,12},{6,14},{8,0},{10,2},{12,4},{14,6},{16,24},{18,... | collective-permute-start | bytes 688136 | tf_op jit(solution)/shard_map/ppermute | solution.py:282
  30.3 17.2 %collective-permute-start.2 = (s32[16,3072]{1,0:T(8,128)S(1)}, s32[16,3072]{1,0:T(8,128)S(1)}, u32[]{:S(2)}, u32[]{:S(2)}) collective-permute-start(s32[16,3072]{1,0:T(8,128)S(1)} %get-tuple-element.38), channel_id=1, source_target_pairs={{0,16},{2,18},{4,20},{6,22},{8,24},{10,26},{12,28},{14,30},{16,0},... | collective-permute-start | bytes 589832 | tf_op jit(solution)/shard_map/ppermute | solution.py:282
  33.5 14.7 %collective-permute-start.3 = (s32[16,3072]{1,0:T(8,128)S(1)}, s32[16,3072]{1,0:T(8,128)S(1)}, u32[]{:S(2)}, u32[]{:S(2)}) collective-permute-start(s32[16,3072]{1,0:T(8,128)S(1)} %get-tuple-element.39), channel_id=1, source_target_pairs={{0,24},{2,26},{4,28},{6,30},{8,16},{10,18},{12,20},{14,22},{16,8},... | collective-permute-start | bytes 589832 | tf_op jit(solution)/shard_map/ppermute | solution.py:282
  33.7 20.1 %collective-permute-start.7 = (f32[32,1792]{1,0:T(8,128)S(1)}, f32[32,1792]{1,0:T(8,128)S(1)}, u32[]{:S(2)}, u32[]{:S(2)}) collective-permute-start(f32[32,1792]{1,0:T(8,128)S(1)} %collective-permute-done.refs_1_.refs_3_), channel_id=1, source_target_pairs={{0,1},{1,0},{2,3},{3,2},{4,5},{5,4},{6,7},{7,6},{8,9},{9,8},{10,11... | collective-permute-start | bytes 688136 | tf_op jit(solution)/shard_map/ppermute | solution.py:282
  48.9 12.3 %collective-permute-start.6 = (f32[32,1792]{1,0:T(8,128)S(1)}, f32[32,1792]{1,0:T(8,128)S(1)}, u32[]{:S(2)}, u32[]{:S(2)}) collective-permute-start(f32[32,1792]{1,0:T(8,128)S(1)} %collective-permute-done.1.refs_1_.refs_5_), channel_id=1, source_target_pairs={{0,1},{1,0},{2,3},{3,2},{4,5},{5,4},{6,7},{7,6},{8,9},{9,8},{10,11... | collective-permute-start | bytes 688136 | tf_op jit(solution)/shard_map/ppermute | solution.py:282
  50.1 21.4 %all-to-all-start = ((s32[4,16,3072]{2,1,0:T(8,128)}), s32[4,16,3072]{2,1,0:T(8,128)S(1)}, u32[]{:S(2)}, u32[]{:S(2)}) async-start(s32[4,16,3072]{2,1,0:T(8,128)} %bitcast.18), calls=%async_computation | async-start | bytes 1572864 | tf_op jit(solution)/shard_map/all_to_all | solution.py:399
  53.8 1.2 %copy-start.7 = (f32[544,512]{1,0:T(8,128)S(1)}, f32[544,512]{1,0:T(8,128)}, u32[]{:S(2)}) copy-start(f32[544,512]{1,0:T(8,128)} %copy-done.6) | copy-start | bytes 3342340
  55.1 1.2 %copy-start.9 = (f32[544,512]{1,0:T(8,128)S(1)}, f32[544,512]{1,0:T(8,128)}, u32[]{:S(2)}) copy-start(f32[544,512]{1,0:T(8,128)} %copy-done.8) | copy-start | bytes 3342340
  57.3 4.0 %copy-start.11 = (s32[16,3072]{1,0:T(8,128)S(1)}, s32[16,3072]{1,0:T(8,128)}, u32[]{:S(2)}) copy-start(s32[16,3072]{1,0:T(8,128)} %copy-done.10) | copy-start | bytes 589828
  63.6 2.8 %collective-permute-start.8 = (f32[544,512]{1,0:T(8,128)S(1)}, f32[544,512]{1,0:T(8,128)S(1)}, u32[]{:S(2)}, u32[]{:S(2)}) collective-permute-start(f32[544,512]{1,0:T(8,128)S(1)} %shard_map.98), channel_id=1, source_target_pairs={{0,2},{2,0},{4,6},{6,4},{8,10},{10,8},{12,14},{14,12},{16,18},{18,... | collective-permute-start | bytes 3342344 | tf_op jit(solution)/shard_map/ppermute | solution.py:282
  71.6 25.3 %collective-permute-start.11 = (f32[544,512]{1,0:T(8,128)}, f32[544,512]{1,0:T(8,128)S(1)}, u32[]{:S(2)}, u32[]{:S(2)}) collective-permute-start(f32[544,512]{1,0:T(8,128)} %copy-done.5), channel_id=1, source_target_pairs={{0,4},{2,6},{4,0},{6,2},{8,12},{10,14},{12,8},{14,10},{16,20},{18,... | collective-permute-start | bytes 3342344 | tf_op jit(solution)/shard_map/ppermute | solution.py:282
  73.1 1.2 %copy-start.4 = (f32[544,512]{1,0:T(8,128)S(1)}, f32[544,512]{1,0:T(8,128)}, u32[]{:S(2)}) copy-start(f32[544,512]{1,0:T(8,128)} %copy-done.3) | copy-start | bytes 3342340
  85.2 2.0 %collective-permute-start.10 = (f32[272,512]{1,0:T(8,128)S(1)}, f32[272,512]{1,0:T(8,128)S(1)}, u32[]{:S(2)}, u32[]{:S(2)}) collective-permute-start(f32[272,512]{1,0:T(8,128)S(1)} %get-tuple-element.61), channel_id=1, source_target_pairs={{0,2},{2,0},{4,6},{6,4},{8,10},{10,8},{12,14},{14,12},{16,18},{18,... | collective-permute-start | bytes 1671176 | tf_op jit(solution)/shard_map/ppermute | solution.py:282
  85.3 2.7 %collective-permute-start.9 = (f32[272,512]{1,0:T(8,128)S(1)}, f32[272,512]{1,0:T(8,128)S(1)}, u32[]{:S(2)}, u32[]{:S(2)}) collective-permute-start(f32[272,512]{1,0:T(8,128)S(1)} %get-tuple-element.62), channel_id=1, source_target_pairs={{0,2},{2,0},{4,6},{6,4},{8,10},{10,8},{12,14},{14,12},{16,18},{18,... | collective-permute-start | bytes 1671176 | tf_op jit(solution)/shard_map/ppermute | solution.py:282
  96.9 9.4 %copy-start.16 = (s32[3072]{0:T(1024)S(1)}, s32[3072]{0:T(1024)}, u32[]{:S(2)}) copy-start(s32[3072]{0:T(1024)} %param.9) | copy-start | bytes 36868
  96.9 9.5 %copy-start.2 = (f32[3072,32]{0,1:T(8,128)S(1)}, f32[3072,32]{0,1:T(8,128)}, u32[]{:S(2)}) copy-start(f32[3072,32]{0,1:T(8,128)} %param.7) | copy-start | bytes 1179652
  99.0 7.2 %collective-permute-start.12 = (f32[32,128]{1,0:T(8,128)S(1)}, f32[32,128]{1,0:T(8,128)S(1)}, u32[]{:S(2)}, u32[]{:S(2)}) collective-permute-start(f32[32,128]{1,0:T(8,128)S(1)} %pad_maximum_fusion.1), channel_id=1, source_target_pairs={{0,1},{1,0},{2,3},{3,2},{4,5},{5,4},{6,7},{7,6},{8,9},{9,8},{10,11... | collective-permute-start | bytes 49160 | tf_op jit(solution)/shard_map/ppermute | solution.py:282
  101.1 11.8 %all-to-all-start.1 = ((f32[8,8,128]{2,1,0:T(8,128)}), f32[8,8,128]{2,1,0:T(8,128)S(1)}, u32[]{:S(2)}, u32[]{:S(2)}) async-start(f32[8,8,128]{2,1,0:T(8,128)} %shard_map.101), calls=%async_computation.1 | async-start | bytes 65536 | tf_op jit(solution)/shard_map/all_to_all | solution.py:442
  106.4 7.1 %copy-start.21 = (f32[8,2,32]{2,1,0:T(2,128)}, f32[8,2,32]{2,1,0:T(2,128)S(1)}, u32[]{:S(2)}) copy-start(f32[8,2,32]{2,1,0:T(2,128)S(1)} %fusion.5) | copy-start | bytes 6148
  (13 other events, 10.6 us)

commit v7 on v6

--- a/solution.py
+++ b/solution.py
@@ -10,6 +10,7 @@
 BINS = 64
 LANES = 128
 VMEM_BYTES = 12 * 1024 * 1024
+PREP_VMEM_BYTES = 60 * 1024 * 1024
 SMALL_COST = pl.CostEstimate(flops=1000000, bytes_accessed=1000000, transcendentals=0)
 
 
@@ -67,25 +68,29 @@
 def prep_kernel(
     own,
     blocks,
-    ids_ref,
-    feature_ref,
-    bin_ref,
-    missing_ref,
-    logits_ref,
-    labels_ref,
-    nodes_ref,
-    codes_ref,
     *refs,
 ):
-    info_ref, half_ref, flag_ref = refs[:3]
-    outs, turned = refs[3:-1], refs[-1]
+    operands, rest = refs[:7], refs[7:]
+    info_ref, half_ref, flag_ref = rest[:3]
+    outs = rest[3 : 3 + len(blocks)]
+    turned, *buffers, sems = rest[3 + len(blocks) :]
+    copies = [
+        pltpu.make_async_copy(operand, buffer, sems.at[i])
+        for i, (operand, buffer) in enumerate(zip(operands, buffers))
+    ]
+    for copy in copies:
+        copy.start()
+    for copy in copies:
+        copy.wait()
+    codes_ref, logits_ref, labels_ref, nodes_ref, feature_ref, bin_ref, missing_ref = buffers
+    row_index, feat_index = lax.axis_index("rows"), lax.axis_index("feat")
     classes, rows = logits_ref.shape
     half, width = rows // 2, half_width(rows)
     chunks = half // LANES
     turned[...] = codes_ref[...].T
     for (infos, pieces), out_ref in zip(blocks, outs):
         for i, start_of in enumerate(pieces):
-            start = pl.multiple_of(start_of(ids_ref[0]), own)
+            start = pl.multiple_of(start_of(row_index), own)
             if infos == 0:
                 out_ref[i * own : (i + 1) * own, :] = turned[pl.ds(start, own), :]
                 continue
@@ -106,7 +111,7 @@
     node_count = feature_ref.shape[0]
     side = jnp.zeros((1, rows), jnp.float32)
     for n in range(node_count):
-        col = feature_ref[n] - ids_ref[1] * feats
+        col = feature_ref[n] - feat_index * feats
         held = (col >= 0) & (col < feats)
         code = turned[pl.ds(jnp.clip(col, 0, feats - 1), 1), :]
         threshold = jnp.where(held, bin_ref[n], -1)
@@ -140,7 +145,7 @@
         info_ref[:, h * width + half + LANES : (h + 1) * width] = jnp.concatenate(
             [nodes[some], long_pad], axis=0
         )
-    half_ref[...] = jnp.where(ids_ref[1] == 0, info_ref[:, :width], info_ref[:, width:])
+    half_ref[...] = jnp.where(feat_index == 0, info_ref[:, :width], info_ref[:, width:])
     for (infos, _), out_ref in zip(blocks, outs):
         if infos > 0:
             out_ref[:classes, :] = half_ref[...] if infos == 1 else info_ref[...]
@@ -202,17 +207,16 @@
             gain_ref[n, 2 * pair + 1 : 2 * pair + 2, :] = gain[:, 2 * BINS :]
 
 
-def add_kernel(classes, node_count, own, plan, carry, ids_ref, *refs):
+def add_kernel(classes, node_count, own, plan, carry, *refs):
     outs = len(plan[0][3])
     arrays = 1 + max(max((c,) + i) for _, c, i, _ in plan)
     out_refs = refs[-outs:]
     held_refs = refs[arrays:-outs]
     pairs = 2 * classes * node_count
+    row_index, feat_index = lax.axis_index("rows"), lax.axis_index("feat")
     for s, (m, codes_at, info_at, firsts) in enumerate(plan):
         codes_ref = refs[codes_at]
-        line = (ids_ref[0] >> 2) ^ (m >> 2)
-        if len(codes_ref.shape) == 3:
-            codes_ref = codes_ref.at[line]
+        line = (row_index >> 2) ^ (m >> 2)
         if len(info_at) == 1:
             width = refs[info_at[0]].shape[1] // 2
             low, high = (refs[info_at[0]][:classes, h * width : (h + 1) * width] for h in range(2))
@@ -220,8 +224,8 @@
         else:
             width = refs[info_at[0]].shape[1]
             near, far = (refs[i][:classes, :] for i in info_at)
-            low = jnp.where(ids_ref[1] == 0, near, far)
-            high = jnp.where(ids_ref[1] == 0, far, near)
+            low = jnp.where(feat_index == 0, near, far)
+            high = jnp.where(feat_index == 0, far, near)
             sums_from = near
         rows = 2 * (width - 2 * LANES)
         masked = masked_gradients((low, high), rows, node_count)
@@ -249,26 +253,25 @@
             out_ref[:pairs, :] += product
             if not carry:
                 continue
-            low_row = pairs + (ids_ref[0] & 3) * node_count
+            low_row = pairs + (row_index & 3) * node_count
             band = pl.ds(pl.multiple_of(low_row, node_count), node_count)
             for i in range(out_ref.shape[1] // LANES):
                 here = jnp.where(line == i, 1.0, 0.0)
                 out_ref[band, i * LANES : (i + 1) * LANES] += here * sums
 
 
-def add_rows(classes, node_count, own, carry, ids, plan, arrays, *held):
+def add_rows(classes, node_count, own, carry, plan, arrays, *held):
     shape = (2 * classes * node_count + 4 * node_count, own * BINS)
     whole = pl.BlockSpec(memory_space=pltpu.VMEM)
     outs = len(plan[0][3])
     return pl.pallas_call(
         functools.partial(add_kernel, classes, node_count, own, plan, carry),
-        in_specs=[pl.BlockSpec(memory_space=pltpu.SMEM)]
-        + [whole] * (len(arrays) + len(held) * outs),
+        in_specs=[whole] * (len(arrays) + len(held) * outs),
         out_specs=[whole] * outs,
         out_shape=[jax.ShapeDtypeStruct(shape, jnp.float32)] * outs,
         compiler_params=pltpu.CompilerParams(vmem_limit_bytes=VMEM_BYTES),
         cost_estimate=SMALL_COST,
-    )(ids, *arrays, *[hist for hists in held for hist in hists])
+    )(*arrays, *[hist for hists in held for hist in hists])
 
 
 def gain_kernel(classes, node_count, *refs):
@@ -290,12 +293,11 @@
     return x
 
 
-def prepare(blocks, ids, splits, logits_t, labels, node_ids, bin_codes):
+def prepare(blocks, splits, logits_t, labels, node_ids, bin_codes):
     classes, rows_dev = logits_t.shape
     feats_dev = bin_codes.shape[1]
     own = 8
     whole = pl.BlockSpec(memory_space=pltpu.VMEM)
-    scalars = pl.BlockSpec(memory_space=pltpu.SMEM)
     width = half_width(rows_dev)
     shapes = [
         jax.ShapeDtypeStruct((classes, 2 * width), jnp.float32),
@@ -309,22 +311,25 @@
         else:
             shape = (classes + codes * 2 // infos, infos * width)
             shapes.append(jax.ShapeDtypeStruct(shape, jnp.float32))
-    return pl.pallas_call(
-        functools.partial(prep_kernel, own, blocks),
-        in_specs=[scalars] * 4 + [whole] * 4,
-        out_specs=[whole] * len(shapes),
-        out_shape=shapes,
-        scratch_shapes=[pltpu.VMEM((feats_dev, rows_dev), jnp.int32)],
-        compiler_params=pltpu.CompilerParams(vmem_limit_bytes=VMEM_BYTES),
-        cost_estimate=SMALL_COST,
-    )(
-        ids,
-        *splits,
+    operands = (
+        bin_codes,
         logits_t,
         labels.reshape(-1, LANES),
         node_ids.reshape(-1, LANES),
-        bin_codes,
-    )
+        *splits,
+    )
+    spaces = [pltpu.VMEM] * 4 + [pltpu.SMEM] * 3
+    return pl.pallas_call(
+        functools.partial(prep_kernel, own, blocks),
+        in_specs=[pl.BlockSpec(memory_space=pltpu.HBM)] * len(operands),
+        out_specs=[whole] * len(shapes),
+        out_shape=shapes,
+        scratch_shapes=[pltpu.VMEM((feats_dev, rows_dev), jnp.int32)]
+        + [space(x.shape, x.dtype) for space, x in zip(spaces, operands)]
+        + [pltpu.SemaphoreType.DMA((len(operands),))],
+        compiler_params=pltpu.CompilerParams(vmem_limit_bytes=PREP_VMEM_BYTES),
+        cost_estimate=SMALL_COST,
+    )(*operands)
 
 
 def finish(logits_t, node_ids, side_count, sums, node_count):
@@ -353,35 +358,28 @@
     pairs_dev = feats_dev // per_node
     width = 2 * classes
     own = 8
-    row_index = lax.axis_index("rows")
-    feat_index = lax.axis_index("feat")
-    ids = jnp.stack([row_index, feat_index]).astype(jnp.int32)
     splits = (split_feature, split_bin, split_missing)
     logits_t = logits.T
     if feats_dev != own * n_rows or n_rows != 16 or lax.axis_size("feat") != 2:
-        return by_groups(logits_t, labels, node_ids, bin_codes, splits, ids, per_node, pairs_dev)
-    add = functools.partial(add_rows, classes, node_count, own, True, ids)
+        return by_groups(logits_t, labels, node_ids, bin_codes, splits, per_node, pairs_dev)
+    add = functools.partial(add_rows, classes, node_count, own, True)
 
     def start(taker):
         return (taker & 1) * pairs_dev + (taker >> 1) * own
 
     def quarters(m, which):
         return tuple(lambda row, low=m ^ 3 ^ q: start(row ^ low) for q in which)
-
-    def line_quarters(which):
-        return tuple(
-            lambda row, z=z, low=3 ^ q: start((z * 4 + (row & 3)) ^ low) for z in range(4) for q in which
-        )
 
     blocks = (
         (0, quarters(0, (0, 1, 2, 3))),
         (1, quarters(4, (0, 1))),
-        (0, quarters(8, (0, 1))),
+        (0, quarters(8, (0, 1, 2, 3))),
         (0, quarters(12, (0, 1))),
-        (0, line_quarters((2, 3))),
-    )
-    info, half, flags, codes_0, rows_4, codes_8, codes_12, codes_late = prepare(
-        blocks, ids, splits, logits_t, labels, node_ids, bin_codes
+        (0, quarters(4, (2, 3))),
+        (0, quarters(12, (2, 3))),
+    )
+    info, half, flags, codes_0, rows_4, codes_8, codes_12, late_4, late_12 = prepare(
+        blocks, splits, logits_t, labels, node_ids, bin_codes
     )
 
     near_8 = swap(half, "rows", 8)
@@ -391,14 +389,12 @@
     hist_a, hist_b, hist_c, hist_d = add(
         ((0, 0, (1,), (0, own, 2 * own, 3 * own)),), [codes_0, info]
     )
-    near_8, hist_a, codes_late = lax.optimization_barrier((near_8, hist_a, codes_late))
+    near_8, rows_4, hist_a = lax.optimization_barrier((near_8, rows_4, hist_a))
     near_12 = swap(near_8, "rows", 4)
     far_8 = swap(near_8, "feat", 1)
     far_4 = swap(rows_4[:classes], "feat", 1)
-    lines = [[4 * z + low for z in range(4)] for low in range(4)]
-    codes_late = lax.all_to_all(
-        codes_late.reshape(4, 2 * own, rows_dev), "rows", 0, 0, tiled=True, axis_index_groups=lines
-    )
+    late_4 = swap(late_4, "rows", 4)
+    late_12 = swap(late_12, "rows", 12)
     hist_a, hist_b = add(
         ((4, 0, (0, 1), (classes, classes + own)),), [rows_4, far_4], [hist_a, hist_b]
     )
@@ -408,11 +404,15 @@
     (to_core,) = add(((12, 0, (1, 2), (0,)),), [codes_12, near_12, far_12], [hist_a])
     from_core = swap(to_core, "rows", 1)
     (to_plane,) = add(((12, 0, (1, 2), (own,)),), [codes_12, near_12, far_12], [hist_b], [from_core])
-    to_plane, codes_late = lax.optimization_barrier((to_plane, codes_late))
     from_plane = swap(to_plane, "rows", 2)
-    late = [codes_late, rows_4, far_4, near_8, far_8, near_12, far_12]
+    _, codes_8 = lax.optimization_barrier((to_plane, codes_8))
+    late = [late_4, codes_8, late_12, rows_4, far_4, near_8, far_8, near_12, far_12]
     to_core, kept = add(
-        tuple((m, 0, i, (0, own)) for m, i in ((4, (1, 2)), (8, (3, 4)), (12, (5, 6)))),
+        (
+            (8, 1, (5, 6), (2 * own, 3 * own)),
+            (4, 0, (3, 4), (0, own)),
+            (12, 2, (7, 8), (0, own)),
+        ),
         late,
         [hist_c, hist_d],
     )
@@ -430,20 +430,23 @@
         compiler_params=pltpu.CompilerParams(vmem_limit_bytes=VMEM_BYTES),
         cost_estimate=SMALL_COST,
     )(from_core, from_plane, kept)
+    def gather(parts):
+        return jnp.sum(parts.reshape(4, node_count, -1, LANES), axis=(0, 2))
+
     gains, from_plane = lax.optimization_barrier((gains, from_plane))
-    parts = from_core[pairs:] + from_plane[pairs:] + kept[pairs:]
-    sums = jnp.sum(parts.reshape(4, node_count, -1, LANES), axis=(0, 2))
+    sums = gather(from_core[pairs:] + from_plane[pairs:] + kept[pairs:])
     children = jnp.concatenate([sums, flags.reshape(-1, LANES)], axis=0)
     children = sum_over(children, "feat")
     side_count = children[node_count:].reshape(1, rows_dev)
-    new_logits, leaves = finish(logits_t, node_ids, side_count, children[:node_count], node_count)
+    sums = children[:node_count]
+    new_logits, leaves = finish(logits_t, node_ids, side_count, sums, node_count)
 
     halves = [[h + n * per_node for n in range(node_count)] for h in range(per_node)]
     gain_rows = lax.all_to_all(gains, "rows", 0, 0, tiled=True, axis_index_groups=halves)
     return (new_logits, gain_rows.reshape(1, pairs_dev, 2 * BINS), leaves)
 
 
-def by_groups(logits_t, labels, node_ids, bin_codes, splits, ids, per_node, pairs_dev):
+def by_groups(logits_t, labels, node_ids, bin_codes, splits, per_node, pairs_dev):
     classes, rows_dev = logits_t.shape
     feats_dev = bin_codes.shape[1]
     node_count = splits[0].shape[0]
@@ -453,7 +456,7 @@
     group = feats_dev // own
     group_count = n_rows // group
     blocks = tuple((2, (lambda row, r=r: r * own,)) for r in range(group))
-    info, _, flags, *rows_out = prepare(blocks, ids, splits, logits_t, labels, node_ids, bin_codes)
+    info, _, flags, *rows_out = prepare(blocks, splits, logits_t, labels, node_ids, bin_codes)
     members = [[g * group + r for r in range(group)] for g in range(group_count)]
     rows_in = lax.all_to_all(
         jnp.stack(rows_out), "rows", 0, 0, tiled=True, axis_index_groups=members
@@ -462,7 +465,7 @@
     for r in range(group):
         held = [hists] if hists else []
         hists = add_rows(
-            classes, node_count, own, False, ids, ((0, 0, (0,), (classes,)),), [rows_in[r]], *held
+            classes, node_count, own, False, ((0, 0, (0,), (classes,)),), [rows_in[r]], *held
         )
     sums = lax.psum(child_sums(info[:, : half_width(rows_dev)], rows_dev, node_count), ("rows", "feat"))
     side_count = lax.psum(flags, "feat")

time: 114 us -> 101 us (0.89)
  local copies, waits for them, and re-layouts: 17.5 us -> 2.82 us
  waiting for transfers between devices: 32.8 us -> 37.5 us
  starting transfers between devices: 26.5 us -> 24.7 us
    unnamed x45 -> x19, local copies, waits for them, and re-layouts: 17.4 us -> 2.66 us
    ppermute x13 -> x15, waiting for transfers between devices: 25.7 us -> 32.2 us  [swap(): return lax.ppermute(x, axis, [(i, i ^ bit) for i in range(size)])]
    all_to_all x1 -> x0, starting transfers between devices: 3.67 us -> none  [local(): lax.all_to_all(codes_late.reshape(4, 2 * own, rows_dev), 'rows', 0, 0, ti...]
    ppermute x13 -> x15, starting transfers between devices: 17.7 us -> 21 us  [swap(): return lax.ppermute(x, axis, [(i, i ^ bit) for i in range(size)])]
    pallas_call x6, Pallas kernels: 30.6 us -> 27.4 us  [add_rows(): pl.pallas_call(functools.partial(add_kernel, classes, node_count, own, pl...]
    pallas_call x1, Pallas kernels: 1.71 us -> 3.89 us  [prepare(): pl.pallas_call(functools.partial(prep_kernel, own, blocks), in_specs=[pl....]
    all_to_all x1 -> x0, waiting for transfers between devices: 1.75 us -> none  [local(): lax.all_to_all(codes_late.reshape(4, 2 * own, rows_dev), 'rows', 0, 0, ti...]
    all_to_all x1, starting transfers between devices: 5.13 us -> 3.68 us  [local(): lax.all_to_all(gains, 'rows', 0, 0, tiled=True, axis_index_groups=halves)]
  transfers between devices with their start and end apart: 15 -> 16, of which waited for: 9 -> 12; matrix products, arithmetic and copies ran while one was open for 1% -> 1% of each run, Pallas kernels for 27% -> 25%
where the time goes in v7:
time: 101 us; the launch traced here: 100 us
  waiting for transfers between devices  37.5 us (37%)
  Pallas kernels  33.3 us (33%)
  starting transfers between devices  24.7 us (24%)
  local copies, waits for them, and re-layouts  2.82 us (3%)
  matrix products  1.1 us (1%)
    ppermute x15, waiting for transfers between devices, swap(): return lax.ppermute(x, axis, [(i, i ^ bit) for i in range(size)])  32.2 us
    pallas_call x6, Pallas kernels, add_rows(): pl.pallas_call(functools.partial(add_kernel, classes, node_count, own, pl...  27.4 us
    ppermute x15, starting transfers between devices, swap(): return lax.ppermute(x, axis, [(i, i ^ bit) for i in range(size)])  21 us
    all_to_all x1, waiting for transfers between devices, local(): lax.all_to_all(gains, 'rows', 0, 0, tiled=True, axis_index_groups=halves)  5.36 us
    pallas_call x1, Pallas kernels, prepare(): pl.pallas_call(functools.partial(prep_kernel, own, blocks), in_specs=[pl....  3.89 us
    all_to_all x1, starting transfers between devices, local(): lax.all_to_all(gains, 'rows', 0, 0, tiled=True, axis_index_groups=halves)  3.68 us
    unnamed x19, local copies, waits for them, and re-layouts  2.66 us
    pallas_call x1, Pallas kernels, local(): pl.pallas_call(functools.partial(gain_kernel, classes, node_count), in_sp...  2.07 us
  transfers between devices with their start and end apart: 16, of which 12 were waited for; matrix products, arithmetic and copies ran while one was open for 1% of the time, Pallas kernels for 25%

profile of v7, /device:TPU:0, one launch (start us, length us, event | category | flops | bytes accessed | tf_op | source)
XLA Modules:
  0.0 100.4 jit_solution(16166143999157941880)
XLA Ops:
  0.6 3.9 %shard_map.94 = (f32[32,3584]{1,0:T(8,128)}, f32[32,1792]{1,0:T(8,128)}, f32[1,3072]{1,0:T(1,128)}, s32[32,3072]{1,0:T(8,128)}, f32[64,1792]{1,0:T(8,128)}, /*in...) custom-call(s32[3072,128]{1,0:T(8,128)} %refs_0_.1, f32[32,3072]{1,0:T(8,128)} %bitcast.14, ...), custom_call_target="tpu_custom_call" | custom-call | flops 1000000 | bytes 1000000 | tf_op jit(solution)/shard_map/pallas_call | solution.py:322
  4.5 3.1 %collective-permute-start.2 = (f32[64,1792]{1,0:T(8,128)}, f32[64,1792]{1,0:T(8,128)S(1)}, u32[]{:S(2)}, u32[]{:S(2)}) collective-permute-start(f32[64,1792]{1,0:T(8,128)} %get-tuple-element.34), channel_id=1, source_target_pairs={{0,8},{2,10},{4,12},{6,14},{8,0},{10,2},{12,4},{14,6},{16,24},{18,... | collective-permute-start | bytes 1376264 | tf_op jit(solution)/shard_map/ppermute | solution.py:285
  7.6 2.6 %collective-permute-start.1 = (f32[32,1792]{1,0:T(8,128)}, f32[32,1792]{1,0:T(8,128)S(1)}, u32[]{:S(2)}, u32[]{:S(2)}) collective-permute-start(f32[32,1792]{1,0:T(8,128)} %get-tuple-element.33), channel_id=1, source_target_pairs={{0,16},{2,18},{4,20},{6,22},{8,24},{10,26},{12,28},{14,30},{16,0},... | collective-permute-start | bytes 688136 | tf_op jit(solution)/shard_map/ppermute | solution.py:285
  12.6 6.7 %shard_map.95 = (f32[544,512]{1,0:T(8,128)S(1)}, f32[544,512]{1,0:T(8,128)S(1)}, f32[544,512]{1,0:T(8,128)S(1)}, f32[544,512]{1,0:T(8,128)S(1)}) custom-call(s32[32,3072]{1,0:T(8,128)S(1)} %copy-done.1, f32[32,3584]{1,0:T(8,128)S(1)} %copy-done), custom_call_target="tpu_custom_call" | custom-call | flops 1000000 | bytes 1000000 | tf_op jit(solution)/shard_map/pallas_call | solution.py:267
  19.2 4.6 %collective-permute-done.1.refs_1_.refs_5_ = f32[32,1792]{1,0:T(8,128)S(1)} collective-permute-done((f32[32,1792]{1,0:T(8,128)}, f32[32,1792]{1,0:T(8,128)S(1)}, u32[]{:S(2)}, u32[]{:S(2)}) %collective-permute-start.1) | collective-permute-done | bytes 229408 | tf_op jit(solution)/shard_map/ppermute | solution.py:285
  23.8 4.2 %collective-permute-done.2.refs_0_.refs_3_ = f32[64,1792]{1,0:T(8,128)S(1)} collective-permute-done((f32[64,1792]{1,0:T(8,128)}, f32[64,1792]{1,0:T(8,128)S(1)}, u32[]{:S(2)}, u32[]{:S(2)}) %collective-permute-start.2) | collective-permute-done | bytes 458784 | tf_op jit(solution)/shard_map/ppermute | solution.py:285
  28.1 1.7 %collective-permute-start.6 = (f32[32,1792]{1,0:T(8,128)S(1)}, f32[32,1792]{1,0:T(8,128)S(1)}, u32[]{:S(2)}, u32[]{:S(2)}) collective-permute-start(f32[32,1792]{1,0:T(8,128)S(1)} %slice.36), channel_id=1, source_target_pairs={{0,1},{1,0},{2,3},{3,2},{4,5},{5,4},{6,7},{7,6},{8,9},{9,8},{10,11... | collective-permute-start | bytes 688136 | tf_op jit(solution)/shard_map/ppermute | solution.py:285
  29.8 2.5 %collective-permute-start.5 = (s32[16,3072]{1,0:T(8,128)S(1)}, s32[16,3072]{1,0:T(8,128)S(1)}, u32[]{:S(2)}, u32[]{:S(2)}) collective-permute-start(s32[16,3072]{1,0:T(8,128)S(1)} %copy-done.8), channel_id=1, source_target_pairs={{0,24},{2,26},{4,28},{6,30},{8,16},{10,18},{12,20},{14,22},{16,8},... | collective-permute-start | bytes 589832 | tf_op jit(solution)/shard_map/ppermute | solution.py:285
  32.8 3.7 %collective-permute-done.6.refs_1_.refs_4_ = f32[32,1792]{1,0:T(8,128)S(1)} collective-permute-done((f32[32,1792]{1,0:T(8,128)S(1)}, f32[32,1792]{1,0:T(8,128)S(1)}, u32[]{:S(2)}, u32[]{:S(2)}) %collective-permute-start.6) | collective-permute-done | bytes 229408 | tf_op jit(solution)/shard_map/ppermute | solution.py:285
  36.5 3.4 %shard_map.96 = (f32[544,512]{1,0:T(8,128)S(1)}, f32[544,512]{1,0:T(8,128)S(1)}) custom-call(f32[64,1792]{1,0:T(8,128)S(1)} %collective-permute-done.2.refs_0_.refs_3_, f32[32,1792]{1,0:T(8,128)S(1)} %collective-permute-done.6.refs_1_.refs_4_, f32[544,512]{1,0:T(8,128)S(1)} %get-tuple-element.42.refs_2_, f32[544,512]{1,0:T(8,128)S(1)} %get-tuple-element.43.refs_3_), custom_call_target="tpu_custom_call" | custom-call | flops 1000000 | bytes 1000000 | tf_op jit(solution)/shard_map/pallas_call | solution.py:267
  40.0 3.2 %collective-permute-done.5.refs_0_ = s32[16,3072]{1,0:T(8,128)S(1)} collective-permute-done((s32[16,3072]{1,0:T(8,128)S(1)}, s32[16,3072]{1,0:T(8,128)S(1)}, u32[]{:S(2)}, u32[]{:S(2)}) %collective-permute-start.5) | collective-permute-done | bytes 196640 | tf_op jit(solution)/shard_map/ppermute | solution.py:285
  44.8 3.4 %shard_map.97 = (f32[544,512]{1,0:T(8,128)S(1)}, f32[544,512]{1,0:T(8,128)S(1)}) custom-call(s32[32,3072]{1,0:T(8,128)S(1)} %collective-permute-done.4.refs_0_.refs_1_, f32[32,1792]{1,0:T(8,128)S(1)} %collective-permute-done.1.refs_1_.refs_5_, f32[32,1792]{1,0:T(8,128)S(1)} %collective-permute-done.8.refs_2_.refs_6_, ...), custom_call_target="tpu_custom_call" | custom-call | flops 1000000 | bytes 1000000 | tf_op jit(solution)/shard_map/pallas_call | solution.py:267
  48.2 1.6 %collective-permute-done.7.refs_2_.refs_8_ = f32[32,1792]{1,0:T(8,128)S(1)} collective-permute-done((f32[32,1792]{1,0:T(8,128)S(1)}, f32[32,1792]{1,0:T(8,128)S(1)}, u32[]{:S(2)}, u32[]{:S(2)}) %collective-permute-start.7) | collective-permute-done | bytes 229408 | tf_op jit(solution)/shard_map/ppermute | solution.py:285
  49.9 2.0 %shard_map.98 = f32[544,512]{1,0:T(8,128)S(1)} custom-call(s32[16,3072]{1,0:T(8,128)S(1)} %collective-permute-done.5.refs_0_, f32[32,1792]{1,0:T(8,128)S(1)} %collective-permute-done.3.refs_1_.refs_7_, f32[32,1792]{1,0:T(8,128)S(1)} %collective-permute-done.7.refs_2_.refs_8_, f32[544,512]{1,0:T(8,128)S(1)} %get-tuple-element.51.refs_3_), custom_call_target="tpu_custom_call" | custom-call | flops 1000000 | bytes 1000000 | tf_op jit(solution)/shard_map/pallas_call | solution.py:267
  52.0 3.1 %collective-permute-start = (s32[16,3072]{1,0:T(8,128)S(1)}, s32[16,3072]{1,0:T(8,128)S(1)}, u32[]{:S(2)}, u32[]{:S(2)}) collective-permute-start(s32[16,3072]{1,0:T(8,128)S(1)} %copy-done.7), channel_id=1, source_target_pairs={{0,8},{2,10},{4,12},{6,14},{8,0},{10,2},{12,4},{14,6},{16,24},{18,... | collective-permute-start | bytes 589832 | tf_op jit(solution)/shard_map/ppermute | solution.py:285
  55.0 2.5 %collective-permute-start.10 = (s32[16,3072]{1,0:T(8,128)S(1)}, s32[16,3072]{1,0:T(8,128)S(1)}, u32[]{:S(2)}, u32[]{:S(2)}) collective-permute-start(s32[16,3072]{1,0:T(8,128)S(1)} %copy-done.6), channel_id=1, source_target_pairs={{0,24},{2,26},{4,28},{6,30},{8,16},{10,18},{12,20},{14,22},{16,8},... | collective-permute-start | bytes 589832 | tf_op jit(solution)/shard_map/ppermute | solution.py:285
  57.5 1.8 %shard_map.99 = f32[544,512]{1,0:T(8,128)S(1)} custom-call(s32[16,3072]{1,0:T(8,128)S(1)} %collective-permute-done.5.refs_0_, f32[32,1792]{1,0:T(8,128)S(1)} %collective-permute-done.3.refs_1_.refs_7_, f32[32,1792]{1,0:T(8,128)S(1)} %collective-permute-done.7.refs_2_.refs_8_, f32[544,512]{1,0:T(8,128)S(1)} %get-tuple-element.50.refs_3_, ...), custom_call_target="tpu_custom_call" | custom-call | flops 1000000 | bytes 1000000 | tf_op jit(solution)/shard_map/pallas_call | solution.py:267
  59.3 1.6 %collective-permute-start.13 = (f32[544,512]{1,0:T(8,128)S(1)}, f32[544,512]{1,0:T(8,128)S(1)}, u32[]{:S(2)}, u32[]{:S(2)}) collective-permute-start(f32[544,512]{1,0:T(8,128)S(1)} %shard_map.99), channel_id=1, source_target_pairs={{0,4},{2,6},{4,0},{6,2},{8,12},{10,14},{12,8},{14,10},{16,20},{18,... | collective-permute-start | bytes 3342344 | tf_op jit(solution)/shard_map/ppermute | solution.py:285
  60.9 6.0 %collective-permute-done.10.refs_2_ = s32[16,3072]{1,0:T(8,128)S(1)} collective-permute-done((s32[16,3072]{1,0:T(8,128)S(1)}, s32[16,3072]{1,0:T(8,128)S(1)}, u32[]{:S(2)}, u32[]{:S(2)}) %collective-permute-start.10) | collective-permute-done | bytes 196640 | tf_op jit(solution)/shard_map/ppermute | solution.py:285
  66.9 9.9 %shard_map.100 = (f32[544,512]{1,0:T(8,128)S(1)}, f32[544,512]{1,0:T(8,128)S(1)}) custom-call(s32[16,3072]{1,0:T(8,128)S(1)} %collective-permute-done.refs_0_, s32[32,3072]{1,0:T(8,128)S(1)} %collective-permute-done.4.refs_0_.refs_1_, s32[16,3072]{1,0:T(8,128)S(1)} %collective-permute-done.10.refs_2_, f32[64,1792]{1,0:T(8,128)S(1)} %collective-permute-done.2.refs_0_.refs_3_, ...), custom_call_target="tpu_custom_call" | custom-call | flops 1000000 | bytes 1000000 | tf_op jit(solution)/shard_map/pallas_call | solution.py:267
  79.9 5.9 %collective-permute-done.13.refs_1_ = f32[544,512]{1,0:T(8,128)S(1)} collective-permute-done((f32[544,512]{1,0:T(8,128)S(1)}, f32[544,512]{1,0:T(8,128)S(1)}, u32[]{:S(2)}, u32[]{:S(2)}) %collective-permute-start.13) | collective-permute-done | bytes 1114144 | tf_op jit(solution)/shard_map/ppermute | solution.py:285
  85.8 2.1 %shard_map.101 = f32[8,8,128]{2,1,0:T(8,128)} custom-call(f32[544,512]{1,0:T(8,128)S(1)} %pad_maximum_fusion.refs_0_, f32[544,512]{1,0:T(8,128)S(1)} %collective-permute-done.13.refs_1_, f32[544,512]{1,0:T(8,128)S(1)} %get-tuple-element.57.refs_2_), custom_call_target="tpu_custom_call" | custom-call | flops 1000000 | bytes 1000000 | tf_op jit(solution)/shard_map/pallas_call | solution.py:424
  89.4 3.7 %all-to-all-start = ((f32[8,8,128]{2,1,0:T(8,128)}), f32[8,8,128]{2,1,0:T(8,128)S(1)}, u32[]{:S(2)}, u32[]{:S(2)}) async-start(f32[8,8,128]{2,1,0:T(8,128)} %shard_map.101), calls=%async_computation | async-start | bytes 65536 | tf_op jit(solution)/shard_map/all_to_all | solution.py:445
  94.4 5.4 %all-to-all-done = f32[8,8,128]{2,1,0:T(8,128)S(1)} async-done(((f32[8,8,128]{2,1,0:T(8,128)}), f32[8,8,128]{2,1,0:T(8,128)S(1)}, u32[]{:S(2)}, u32[]{:S(2)}) %all-to-all-start) | async-done | bytes 32800 | tf_op jit(solution)/shard_map/all_to_all | solution.py:445
  (46 shorter events, 11.0 us)
Async XLA Ops:
  4.5 23.5 %collective-permute-start.2 = (f32[64,1792]{1,0:T(8,128)}, f32[64,1792]{1,0:T(8,128)S(1)}, u32[]{:S(2)}, u32[]{:S(2)}) collective-permute-start(f32[64,1792]{1,0:T(8,128)} %get-tuple-element.34), channel_id=1, source_target_pairs={{0,8},{2,10},{4,12},{6,14},{8,0},{10,2},{12,4},{14,6},{16,24},{18,... | collective-permute-start | bytes 1376264 | tf_op jit(solution)/shard_map/ppermute | solution.py:285
  7.6 16.2 %collective-permute-start.1 = (f32[32,1792]{1,0:T(8,128)}, f32[32,1792]{1,0:T(8,128)S(1)}, u32[]{:S(2)}, u32[]{:S(2)}) collective-permute-start(f32[32,1792]{1,0:T(8,128)} %get-tuple-element.33), channel_id=1, source_target_pairs={{0,16},{2,18},{4,20},{6,22},{8,24},{10,26},{12,28},{14,30},{16,0},... | collective-permute-start | bytes 688136 | tf_op jit(solution)/shard_map/ppermute | solution.py:285
  10.2 33.1 %collective-permute-start.4 = (s32[32,3072]{1,0:T(8,128)}, s32[32,3072]{1,0:T(8,128)S(1)}, u32[]{:S(2)}, u32[]{:S(2)}) collective-permute-start(s32[32,3072]{1,0:T(8,128)} %get-tuple-element.39), channel_id=1, source_target_pairs={{0,16},{2,18},{4,20},{6,22},{8,24},{10,26},{12,28},{14,30},{16,0},... | collective-permute-start | bytes 1179656 | tf_op jit(solution)/shard_map/ppermute | solution.py:285
  10.5 1.0 %copy-start = (f32[32,3584]{1,0:T(8,128)S(1)}, f32[32,3584]{1,0:T(8,128)}, u32[]{:S(2)}) copy-start(f32[32,3584]{1,0:T(8,128)} %get-tuple-element.36.refs_1_) | copy-start | bytes 1376260
  12.6 17.2 %copy-start.8 = (s32[16,3072]{1,0:T(8,128)S(1)}, s32[16,3072]{1,0:T(8,128)}, u32[]{:S(2)}) copy-start(s32[16,3072]{1,0:T(8,128)} %get-tuple-element.40) | copy-start | bytes 589828
  28.1 8.4 %collective-permute-start.6 = (f32[32,1792]{1,0:T(8,128)S(1)}, f32[32,1792]{1,0:T(8,128)S(1)}, u32[]{:S(2)}, u32[]{:S(2)}) collective-permute-start(f32[32,1792]{1,0:T(8,128)S(1)} %slice.36), channel_id=1, source_target_pairs={{0,1},{1,0},{2,3},{3,2},{4,5},{5,4},{6,7},{7,6},{8,9},{9,8},{10,11... | collective-permute-start | bytes 688136 | tf_op jit(solution)/shard_map/ppermute | solution.py:285
  29.8 14.0 %collective-permute-start.3 = (f32[32,1792]{1,0:T(8,128)S(1)}, f32[32,1792]{1,0:T(8,128)S(1)}, u32[]{:S(2)}, u32[]{:S(2)}) collective-permute-start(f32[32,1792]{1,0:T(8,128)S(1)} %collective-permute-done.1.refs_1_.refs_5_), channel_id=1, source_target_pairs={{0,8},{2,10},{4,12},{6,14},{8,0},{10,2},{12,4},{14,6},{16,24},{18,... | collective-permute-start | bytes 688136 | tf_op jit(solution)/shard_map/ppermute | solution.py:285
  29.8 13.4 %collective-permute-start.5 = (s32[16,3072]{1,0:T(8,128)S(1)}, s32[16,3072]{1,0:T(8,128)S(1)}, u32[]{:S(2)}, u32[]{:S(2)}) collective-permute-start(s32[16,3072]{1,0:T(8,128)S(1)} %copy-done.8), channel_id=1, source_target_pairs={{0,24},{2,26},{4,28},{6,30},{8,16},{10,18},{12,20},{14,22},{16,8},... | collective-permute-start | bytes 589832 | tf_op jit(solution)/shard_map/ppermute | solution.py:285
  32.3 12.5 %collective-permute-start.8 = (f32[32,1792]{1,0:T(8,128)S(1)}, f32[32,1792]{1,0:T(8,128)S(1)}, u32[]{:S(2)}, u32[]{:S(2)}) collective-permute-start(f32[32,1792]{1,0:T(8,128)S(1)} %collective-permute-done.1.refs_1_.refs_5_), channel_id=1, source_target_pairs={{0,1},{1,0},{2,3},{3,2},{4,5},{5,4},{6,7},{7,6},{8,9},{9,8},{10,11... | collective-permute-start | bytes 688136 | tf_op jit(solution)/shard_map/ppermute | solution.py:285
  43.8 6.0 %collective-permute-start.7 = (f32[32,1792]{1,0:T(8,128)S(1)}, f32[32,1792]{1,0:T(8,128)S(1)}, u32[]{:S(2)}, u32[]{:S(2)}) collective-permute-start(f32[32,1792]{1,0:T(8,128)S(1)} %collective-permute-done.3.refs_1_.refs_7_), channel_id=1, source_target_pairs={{0,1},{1,0},{2,3},{3,2},{4,5},{5,4},{6,7},{7,6},{8,9},{9,8},{10,11... | collective-permute-start | bytes 688136 | tf_op jit(solution)/shard_map/ppermute | solution.py:285
  49.9 2.1 %copy-start.7 = (s32[16,3072]{1,0:T(8,128)S(1)}, s32[16,3072]{1,0:T(8,128)}, u32[]{:S(2)}) copy-start(s32[16,3072]{1,0:T(8,128)} %get-tuple-element.32) | copy-start | bytes 589828
  49.9 5.2 %copy-start.6 = (s32[16,3072]{1,0:T(8,128)S(1)}, s32[16,3072]{1,0:T(8,128)}, u32[]{:S(2)}) copy-start(s32[16,3072]{1,0:T(8,128)} %get-tuple-element.53) | copy-start | bytes 589828
  51.9 5.6 %collective-permute-start.9 = (f32[544,512]{1,0:T(8,128)S(1)}, f32[544,512]{1,0:T(8,128)S(1)}, u32[]{:S(2)}, u32[]{:S(2)}) collective-permute-start(f32[544,512]{1,0:T(8,128)S(1)} %shard_map.98), channel_id=1, source_target_pairs={{0,2},{2,0},{4,6},{6,4},{8,10},{10,8},{12,14},{14,12},{16,18},{18,... | collective-permute-start | bytes 3342344 | tf_op jit(solution)/shard_map/ppermute | solution.py:285
  52.0 8.9 %collective-permute-start = (s32[16,3072]{1,0:T(8,128)S(1)}, s32[16,3072]{1,0:T(8,128)S(1)}, u32[]{:S(2)}, u32[]{:S(2)}) collective-permute-start(s32[16,3072]{1,0:T(8,128)S(1)} %copy-done.7), channel_id=1, source_target_pairs={{0,8},{2,10},{4,12},{6,14},{8,0},{10,2},{12,4},{14,6},{16,24},{18,... | collective-permute-start | bytes 589832 | tf_op jit(solution)/shard_map/ppermute | solution.py:285
  55.0 11.9 %collective-permute-start.10 = (s32[16,3072]{1,0:T(8,128)S(1)}, s32[16,3072]{1,0:T(8,128)S(1)}, u32[]{:S(2)}, u32[]{:S(2)}) collective-permute-start(s32[16,3072]{1,0:T(8,128)S(1)} %copy-done.6), channel_id=1, source_target_pairs={{0,24},{2,26},{4,28},{6,30},{8,16},{10,18},{12,20},{14,22},{16,8},... | collective-permute-start | bytes 589832 | tf_op jit(solution)/shard_map/ppermute | solution.py:285
  59.3 26.4 %collective-permute-start.13 = (f32[544,512]{1,0:T(8,128)S(1)}, f32[544,512]{1,0:T(8,128)S(1)}, u32[]{:S(2)}, u32[]{:S(2)}) collective-permute-start(f32[544,512]{1,0:T(8,128)S(1)} %shard_map.99), channel_id=1, source_target_pairs={{0,4},{2,6},{4,0},{6,2},{8,12},{10,14},{12,8},{14,10},{16,20},{18,... | collective-permute-start | bytes 3342344 | tf_op jit(solution)/shard_map/ppermute | solution.py:285
  77.0 2.0 %collective-permute-start.12 = (f32[272,512]{1,0:T(8,128)S(1)}, f32[272,512]{1,0:T(8,128)S(1)}, u32[]{:S(2)}, u32[]{:S(2)}) collective-permute-start(f32[272,512]{1,0:T(8,128)S(1)} %get-tuple-element.61), channel_id=1, source_target_pairs={{0,2},{2,0},{4,6},{6,4},{8,10},{10,8},{12,14},{14,12},{16,18},{18,... | collective-permute-start | bytes 1671176 | tf_op jit(solution)/shard_map/ppermute | solution.py:285
  77.0 2.7 %collective-permute-start.11 = (f32[272,512]{1,0:T(8,128)S(1)}, f32[272,512]{1,0:T(8,128)S(1)}, u32[]{:S(2)}, u32[]{:S(2)}) collective-permute-start(f32[272,512]{1,0:T(8,128)S(1)} %get-tuple-element.62), channel_id=1, source_target_pairs={{0,2},{2,0},{4,6},{6,4},{8,10},{10,8},{12,14},{14,12},{16,18},{18,... | collective-permute-start | bytes 1671176 | tf_op jit(solution)/shard_map/ppermute | solution.py:285
  85.8 2.1 %copy-start.4 = (f32[1,3072]{1,0:T(1,128)S(1)}, f32[1,3072]{1,0:T(1,128)}, u32[]{:S(2)}) copy-start(f32[1,3072]{1,0:T(1,128)} %get-tuple-element.59) | copy-start | bytes 36868
  85.8 7.5 %copy-start.3 = (s32[3072]{0:T(1024)S(1)}, s32[3072]{0:T(1024)}, u32[]{:S(2)}) copy-start(s32[3072]{0:T(1024)} %param.9) | copy-start | bytes 36868
  85.8 7.6 %copy-start.2 = (f32[3072,32]{0,1:T(8,128)S(1)}, f32[3072,32]{0,1:T(8,128)}, u32[]{:S(2)}) copy-start(f32[3072,32]{0,1:T(8,128)} %param.7) | copy-start | bytes 1179652
  87.9 5.2 %collective-permute-start.14 = (f32[32,128]{1,0:T(8,128)S(1)}, f32[32,128]{1,0:T(8,128)S(1)}, u32[]{:S(2)}, u32[]{:S(2)}) collective-permute-start(f32[32,128]{1,0:T(8,128)S(1)} %pad_maximum_fusion.1), channel_id=1, source_target_pairs={{0,1},{1,0},{2,3},{3,2},{4,5},{5,4},{6,7},{7,6},{8,9},{9,8},{10,11... | collective-permute-start | bytes 49160 | tf_op jit(solution)/shard_map/ppermute | solution.py:285
  89.4 10.4 %all-to-all-start = ((f32[8,8,128]{2,1,0:T(8,128)}), f32[8,8,128]{2,1,0:T(8,128)S(1)}, u32[]{:S(2)}, u32[]{:S(2)}) async-start(f32[8,8,128]{2,1,0:T(8,128)} %shard_map.101), calls=%async_computation | async-start | bytes 65536 | tf_op jit(solution)/shard_map/all_to_all | solution.py:445
  93.3 7.1 %copy-start.5 = (f32[8,2,32]{2,1,0:T(2,128)}, f32[8,2,32]{2,1,0:T(2,128)S(1)}, u32[]{:S(2)}) copy-start(f32[8,2,32]{2,1,0:T(2,128)S(1)} %fusion.5) | copy-start | bytes 6148
  (1 other events, 1.0 us)

commit v8 on v7

--- a/solution.py
+++ b/solution.py
@@ -373,12 +373,13 @@
     blocks = (
         (0, quarters(0, (0, 1, 2, 3))),
         (1, quarters(4, (0, 1))),
-        (0, quarters(8, (0, 1, 2, 3))),
+        (0, quarters(8, (0, 1))),
         (0, quarters(12, (0, 1))),
         (0, quarters(4, (2, 3))),
+        (0, quarters(8, (2, 3))),
         (0, quarters(12, (2, 3))),
     )
-    info, half, flags, codes_0, rows_4, codes_8, codes_12, late_4, late_12 = prepare(
+    info, half, flags, codes_0, rows_4, codes_8, codes_12, late_4, late_8, late_12 = prepare(
         blocks, splits, logits_t, labels, node_ids, bin_codes
     )
 
@@ -394,6 +395,7 @@
     far_8 = swap(near_8, "feat", 1)
     far_4 = swap(rows_4[:classes], "feat", 1)
     late_4 = swap(late_4, "rows", 4)
+    late_8 = swap(late_8, "rows", 8)
     late_12 = swap(late_12, "rows", 12)
     hist_a, hist_b = add(
         ((4, 0, (0, 1), (classes, classes + own)),), [rows_4, far_4], [hist_a, hist_b]
@@ -405,16 +407,12 @@
     from_core = swap(to_core, "rows", 1)
     (to_plane,) = add(((12, 0, (1, 2), (own,)),), [codes_12, near_12, far_12], [hist_b], [from_core])
     from_plane = swap(to_plane, "rows", 2)
-    _, codes_8 = lax.optimization_barrier((to_plane, codes_8))
-    late = [late_4, codes_8, late_12, rows_4, far_4, near_8, far_8, near_12, far_12]
+    _, late_4 = lax.optimization_barrier((to_plane, late_4))
+    hists = add(((4, 0, (1, 2), (0, own)),), [late_4, rows_4, far_4], [hist_c, hist_d])
     to_core, kept = add(
-        (
-            (8, 1, (5, 6), (2 * own, 3 * own)),
-            (4, 0, (3, 4), (0, own)),
-            (12, 2, (7, 8), (0, own)),
-        ),
-        late,
-        [hist_c, hist_d],
+        ((8, 0, (2, 3), (0, own)), (12, 1, (4, 5), (0, own))),
+        [late_8, late_12, near_8, far_8, near_12, far_12],
+        hists,
     )
     middle = to_core.shape[0] // 2
     from_core = [swap(part, "rows", 1) for part in (to_core[:middle], to_core[middle:])]

time: 101 us -> 99.9 us (0.989)
  waiting for transfers between devices: 37.5 us -> 35.8 us
    ppermute x15 -> x16, waiting for transfers between devices: 32.2 us -> 30.5 us  [swap(): return lax.ppermute(x, axis, [(i, i ^ bit) for i in range(size)])]
    ppermute x15 -> x16, starting transfers between devices: 21 us -> 21.6 us  [swap(): return lax.ppermute(x, axis, [(i, i ^ bit) for i in range(size)])]
    pallas_call x6 -> x7, Pallas kernels: 27.4 us -> 27.5 us  [add_rows(): pl.pallas_call(functools.partial(add_kernel, classes, node_count, own, pl...]
    unnamed x19 -> x23, local copies, waits for them, and re-layouts: 2.66 us -> 2.66 us
  transfers between devices with their start and end apart: 16 -> 17, of which waited for: 12 -> 10; matrix products, arithmetic and copies ran while one was open for 1% -> 1% of each run, Pallas kernels for 25% -> 26%
where the time goes in v8:
time: 99.9 us; the launch traced here: 99.6 us
  waiting for transfers between devices  35.8 us (36%)
  Pallas kernels  33.5 us (34%)
  starting transfers between devices  25.3 us (25%)
  local copies, waits for them, and re-layouts  2.83 us (3%)
  matrix products  1.1 us (1%)
    ppermute x16, waiting for transfers between devices, swap(): return lax.ppermute(x, axis, [(i, i ^ bit) for i in range(size)])  30.5 us
    pallas_call x7, Pallas kernels, add_rows(): pl.pallas_call(functools.partial(add_kernel, classes, node_count, own, pl...  27.5 us
    ppermute x16, starting transfers between devices, swap(): return lax.ppermute(x, axis, [(i, i ^ bit) for i in range(size)])  21.6 us
    all_to_all x1, waiting for transfers between devices, local(): lax.all_to_all(gains, 'rows', 0, 0, tiled=True, axis_index_groups=halves)  5.36 us
    pallas_call x1, Pallas kernels, prepare(): pl.pallas_call(functools.partial(prep_kernel, own, blocks), in_specs=[pl....  3.93 us
    all_to_all x1, starting transfers between devices, local(): lax.all_to_all(gains, 'rows', 0, 0, tiled=True, axis_index_groups=halves)  3.69 us
    unnamed x23, local copies, waits for them, and re-layouts  2.66 us
    pallas_call x1, Pallas kernels, local(): pl.pallas_call(functools.partial(gain_kernel, classes, node_count), in_sp...  2.07 us
  transfers between devices with their start and end apart: 17, of which 10 were waited for; matrix products, arithmetic and copies ran while one was open for 1% of the time, Pallas kernels for 26%

profile of v8, /device:TPU:0, one launch (start us, length us, event | category | flops | bytes accessed | tf_op | source)
XLA Modules:
  0.0 99.6 jit_solution(756736811767731401)
XLA Ops:
  0.6 3.9 %shard_map.94 = (f32[32,3584]{1,0:T(8,128)}, f32[32,1792]{1,0:T(8,128)}, f32[1,3072]{1,0:T(1,128)}, s32[32,3072]{1,0:T(8,128)}, f32[64,1792]{1,0:T(8,128)}, /*in...) custom-call(s32[3072,128]{1,0:T(8,128)} %refs_0_.1, ...), custom_call_target="tpu_custom_call" | custom-call | flops 1000000 | bytes 1000000 | tf_op jit(solution)/shard_map/pallas_call | solution.py:322
  4.6 3.1 %collective-permute-start.3 = (f32[64,1792]{1,0:T(8,128)}, f32[64,1792]{1,0:T(8,128)S(1)}, u32[]{:S(2)}, u32[]{:S(2)}) collective-permute-start(f32[64,1792]{1,0:T(8,128)} %get-tuple-element.38), channel_id=1, source_target_pairs={{0,8},{2,10},{4,12},{6,14},{8,0},{10,2},{12,4},{14,6},{16,24},{18,... | collective-permute-start | bytes 1376264 | tf_op jit(solution)/shard_map/ppermute | solution.py:285
  7.7 2.6 %collective-permute-start.2 = (f32[32,1792]{1,0:T(8,128)}, f32[32,1792]{1,0:T(8,128)S(1)}, u32[]{:S(2)}, u32[]{:S(2)}) collective-permute-start(f32[32,1792]{1,0:T(8,128)} %get-tuple-element.37), channel_id=1, source_target_pairs={{0,16},{2,18},{4,20},{6,22},{8,24},{10,26},{12,28},{14,30},{16,0},... | collective-permute-start | bytes 688136 | tf_op jit(solution)/shard_map/ppermute | solution.py:285
  12.3 6.7 %shard_map.95 = (f32[544,512]{1,0:T(8,128)S(1)}, f32[544,512]{1,0:T(8,128)S(1)}, f32[544,512]{1,0:T(8,128)S(1)}, f32[544,512]{1,0:T(8,128)S(1)}) custom-call(s32[32,3072]{1,0:T(8,128)S(1)} %copy-done.1, f32[32,3584]{1,0:T(8,128)S(1)} %copy-done), custom_call_target="tpu_custom_call" | custom-call | flops 1000000 | bytes 1000000 | tf_op jit(solution)/shard_map/pallas_call | solution.py:267
  19.0 3.7 %collective-permute-done.2.refs_1_.refs_2_ = f32[32,1792]{1,0:T(8,128)S(1)} collective-permute-done((f32[32,1792]{1,0:T(8,128)}, f32[32,1792]{1,0:T(8,128)S(1)}, u32[]{:S(2)}, u32[]{:S(2)}) %collective-permute-start.2) | collective-permute-done | bytes 229408 | tf_op jit(solution)/shard_map/ppermute | solution.py:285
  23.3 1.7 %collective-permute-start.8 = (f32[32,1792]{1,0:T(8,128)S(1)}, f32[32,1792]{1,0:T(8,128)S(1)}, u32[]{:S(2)}, u32[]{:S(2)}) collective-permute-start(f32[32,1792]{1,0:T(8,128)S(1)} %slice.36), channel_id=1, source_target_pairs={{0,1},{1,0},{2,3},{3,2},{4,5},{5,4},{6,7},{7,6},{8,9},{9,8},{10,11... | collective-permute-start | bytes 688136 | tf_op jit(solution)/shard_map/ppermute | solution.py:285
  25.0 2.6 %collective-permute-start.5 = (f32[32,1792]{1,0:T(8,128)S(1)}, f32[32,1792]{1,0:T(8,128)S(1)}, u32[]{:S(2)}, u32[]{:S(2)}) collective-permute-start(f32[32,1792]{1,0:T(8,128)S(1)} %collective-permute-done.2.refs_1_.refs_2_), channel_id=1, source_target_pairs={{0,8},{2,10},{4,12},{6,14},{8,0},{10,2},{12,4},{14,6},{16,24},{18,... | collective-permute-start | bytes 688136 | tf_op jit(solution)/shard_map/ppermute | solution.py:285
  30.5 3.4 %shard_map.96 = (f32[544,512]{1,0:T(8,128)S(1)}, f32[544,512]{1,0:T(8,128)S(1)}) custom-call(f32[64,1792]{1,0:T(8,128)S(1)} %collective-permute-done.3.refs_0_.refs_1_, f32[32,1792]{1,0:T(8,128)S(1)} %collective-permute-done.8.refs_1_.refs_2_, f32[544,512]{1,0:T(8,128)S(1)} %get-tuple-element.46.refs_2_, f32[544,512]{1,0:T(8,128)S(1)} %get-tuple-element.47.refs_3_), custom_call_target="tpu_custom_call" | custom-call | flops 1000000 | bytes 1000000 | tf_op jit(solution)/shard_map/pallas_call | solution.py:267
  34.0 10.2 %collective-permute-done.6.refs_0_ = s32[16,3072]{1,0:T(8,128)S(1)} collective-permute-done((s32[16,3072]{1,0:T(8,128)S(1)}, s32[16,3072]{1,0:T(8,128)S(1)}, u32[]{:S(2)}, u32[]{:S(2)}) %collective-permute-start.6) | collective-permute-done | bytes 196640 | tf_op jit(solution)/shard_map/ppermute | solution.py:285
  44.7 3.4 %shard_map.97 = (f32[544,512]{1,0:T(8,128)S(1)}, f32[544,512]{1,0:T(8,128)S(1)}) custom-call(s32[16,3072]{1,0:T(8,128)S(1)} %collective-permute-done.6.refs_0_, f32[32,1792]{1,0:T(8,128)S(1)} %collective-permute-done.2.refs_1_.refs_2_, f32[32,1792]{1,0:T(8,128)S(1)} %collective-permute-done.4.refs_2_.refs_3_, f32[544,512]{1,0:T(8,128)S(1)} %get-tuple-element.52.refs_3_, ...), custom_call_target="tpu_custom_call" | custom-call | flops 1000000 | bytes 1000000 | tf_op jit(solution)/shard_map/pallas_call | solution.py:267
  48.2 2.0 %collective-permute-done.9.refs_2_.refs_5_ = f32[32,1792]{1,0:T(8,128)S(1)} collective-permute-done((f32[32,1792]{1,0:T(8,128)S(1)}, f32[32,1792]{1,0:T(8,128)S(1)}, u32[]{:S(2)}, u32[]{:S(2)}) %collective-permute-start.9) | collective-permute-done | bytes 229408 | tf_op jit(solution)/shard_map/ppermute | solution.py:285
  50.2 2.0 %shard_map.98 = f32[544,512]{1,0:T(8,128)S(1)} custom-call(s32[16,3072]{1,0:T(8,128)S(1)} %collective-permute-done.7.refs_0_, f32[32,1792]{1,0:T(8,128)S(1)} %collective-permute-done.5.refs_1_.refs_4_, f32[32,1792]{1,0:T(8,128)S(1)} %collective-permute-done.9.refs_2_.refs_5_, f32[544,512]{1,0:T(8,128)S(1)} %get-tuple-element.55.refs_3_), custom_call_target="tpu_custom_call" | custom-call | flops 1000000 | bytes 1000000 | tf_op jit(solution)/shard_map/pallas_call | solution.py:267
  52.3 2.9 %collective-permute-start.11 = (s32[16,3072]{1,0:T(8,128)S(1)}, s32[16,3072]{1,0:T(8,128)S(1)}, u32[]{:S(2)}, u32[]{:S(2)}) collective-permute-start(s32[16,3072]{1,0:T(8,128)S(1)} %copy-done.8), channel_id=1, source_target_pairs={{0,8},{2,10},{4,12},{6,14},{8,0},{10,2},{12,4},{14,6},{16,24},{18,... | collective-permute-start | bytes 589832 | tf_op jit(solution)/shard_map/ppermute | solution.py:285
  55.2 2.4 %collective-permute-start.1 = (s32[16,3072]{1,0:T(8,128)S(1)}, s32[16,3072]{1,0:T(8,128)S(1)}, u32[]{:S(2)}, u32[]{:S(2)}) collective-permute-start(s32[16,3072]{1,0:T(8,128)S(1)} %copy-done.6), channel_id=1, source_target_pairs={{0,24},{2,26},{4,28},{6,30},{8,16},{10,18},{12,20},{14,22},{16,8},... | collective-permute-start | bytes 589832 | tf_op jit(solution)/shard_map/ppermute | solution.py:285
  57.7 1.8 %shard_map.99 = f32[544,512]{1,0:T(8,128)S(1)} custom-call(s32[16,3072]{1,0:T(8,128)S(1)} %collective-permute-done.7.refs_0_, f32[32,1792]{1,0:T(8,128)S(1)} %collective-permute-done.5.refs_1_.refs_4_, f32[32,1792]{1,0:T(8,128)S(1)} %collective-permute-done.9.refs_2_.refs_5_, f32[544,512]{1,0:T(8,128)S(1)} %get-tuple-element.54.refs_3_, ...), custom_call_target="tpu_custom_call" | custom-call | flops 1000000 | bytes 1000000 | tf_op jit(solution)/shard_map/pallas_call | solution.py:267
  59.5 1.6 %collective-permute-start.14 = (f32[544,512]{1,0:T(8,128)S(1)}, f32[544,512]{1,0:T(8,128)S(1)}, u32[]{:S(2)}, u32[]{:S(2)}) collective-permute-start(f32[544,512]{1,0:T(8,128)S(1)} %shard_map.99), channel_id=1, source_target_pairs={{0,4},{2,6},{4,0},{6,2},{8,12},{10,14},{12,8},{14,10},{16,20},{18,... | collective-permute-start | bytes 3342344 | tf_op jit(solution)/shard_map/ppermute | solution.py:285
  61.1 2.6 %collective-permute-done.11.refs_0_ = s32[16,3072]{1,0:T(8,128)S(1)} collective-permute-done((s32[16,3072]{1,0:T(8,128)S(1)}, s32[16,3072]{1,0:T(8,128)S(1)}, u32[]{:S(2)}, u32[]{:S(2)}) %collective-permute-start.11) | collective-permute-done | bytes 196640 | tf_op jit(solution)/shard_map/ppermute | solution.py:285
  63.7 3.4 %shard_map.100 = (f32[544,512]{1,0:T(8,128)S(1)}, f32[544,512]{1,0:T(8,128)S(1)}) custom-call(s32[16,3072]{1,0:T(8,128)S(1)} %collective-permute-done.11.refs_0_, f32[64,1792]{1,0:T(8,128)S(1)} %collective-permute-done.3.refs_0_.refs_1_, f32[32,1792]{1,0:T(8,128)S(1)} %collective-permute-done.8.refs_1_.refs_2_, f32[544,512]{1,0:T(8,128)S(1)} %get-tuple-element.58.refs_3_, ...), custom_call_target="tpu_custom_call" | custom-call | flops 1000000 | bytes 1000000 | tf_op jit(solution)/shard_map/pallas_call | solution.py:267
  67.1 5.2 %collective-permute-done.refs_0_ = s32[16,3072]{1,0:T(8,128)S(1)} collective-permute-done((s32[16,3072]{1,0:T(8,128)S(1)}, s32[16,3072]{1,0:T(8,128)S(1)}, u32[]{:S(2)}, u32[]{:S(2)}) %collective-permute-start) | collective-permute-done | bytes 196640 | tf_op jit(solution)/shard_map/ppermute | solution.py:285
  72.3 6.7 %shard_map.101 = (f32[544,512]{1,0:T(8,128)S(1)}, f32[544,512]{1,0:T(8,128)S(1)}) custom-call(s32[16,3072]{1,0:T(8,128)S(1)} %collective-permute-done.refs_0_, s32[16,3072]{1,0:T(8,128)S(1)} %collective-permute-done.1.refs_1_, f32[32,1792]{1,0:T(8,128)S(1)} %collective-permute-done.2.refs_1_.refs_2_, f32[32,1792]{1,0:T(8,128)S(1)} %collective-permute-done.4.refs_2_.refs_3_, ...), custom_call_target="tpu_custom_call" | custom-call | flops 1000000 | bytes 1000000 | tf_op jit(solution)/shard_map/pallas_call | solution.py:267
  82.0 3.9 %collective-permute-done.14.refs_1_ = f32[544,512]{1,0:T(8,128)S(1)} collective-permute-done((f32[544,512]{1,0:T(8,128)S(1)}, f32[544,512]{1,0:T(8,128)S(1)}, u32[]{:S(2)}, u32[]{:S(2)}) %collective-permute-start.14) | collective-permute-done | bytes 1114144 | tf_op jit(solution)/shard_map/ppermute | solution.py:285
  85.9 2.1 %shard_map.102 = f32[8,8,128]{2,1,0:T(8,128)} custom-call(f32[544,512]{1,0:T(8,128)S(1)} %pad_maximum_fusion.refs_0_, f32[544,512]{1,0:T(8,128)S(1)} %collective-permute-done.14.refs_1_, f32[544,512]{1,0:T(8,128)S(1)} %get-tuple-element.63.refs_2_), custom_call_target="tpu_custom_call" | custom-call | flops 1000000 | bytes 1000000 | tf_op jit(solution)/shard_map/pallas_call | solution.py:422
  88.6 3.7 %all-to-all-start = ((f32[8,8,128]{2,1,0:T(8,128)}), f32[8,8,128]{2,1,0:T(8,128)S(1)}, u32[]{:S(2)}, u32[]{:S(2)}) async-start(f32[8,8,128]{2,1,0:T(8,128)} %shard_map.102), calls=%async_computation | async-start | bytes 65536 | tf_op jit(solution)/shard_map/all_to_all | solution.py:443
  93.6 5.4 %all-to-all-done = f32[8,8,128]{2,1,0:T(8,128)S(1)} async-done(((f32[8,8,128]{2,1,0:T(8,128)}), f32[8,8,128]{2,1,0:T(8,128)S(1)}, u32[]{:S(2)}, u32[]{:S(2)}) %all-to-all-start) | async-done | bytes 32800 | tf_op jit(solution)/shard_map/all_to_all | solution.py:443
  (53 shorter events, 11.7 us)
Async XLA Ops:
  4.6 18.7 %collective-permute-start.3 = (f32[64,1792]{1,0:T(8,128)}, f32[64,1792]{1,0:T(8,128)S(1)}, u32[]{:S(2)}, u32[]{:S(2)}) collective-permute-start(f32[64,1792]{1,0:T(8,128)} %get-tuple-element.38), channel_id=1, source_target_pairs={{0,8},{2,10},{4,12},{6,14},{8,0},{10,2},{12,4},{14,6},{16,24},{18,... | collective-permute-start | bytes 1376264 | tf_op jit(solution)/shard_map/ppermute | solution.py:285
  7.7 15.0 %collective-permute-start.2 = (f32[32,1792]{1,0:T(8,128)}, f32[32,1792]{1,0:T(8,128)S(1)}, u32[]{:S(2)}, u32[]{:S(2)}) collective-permute-start(f32[32,1792]{1,0:T(8,128)} %get-tuple-element.37), channel_id=1, source_target_pairs={{0,16},{2,18},{4,20},{6,22},{8,24},{10,26},{12,28},{14,30},{16,0},... | collective-permute-start | bytes 688136 | tf_op jit(solution)/shard_map/ppermute | solution.py:285
  12.3 15.4 %copy-start.10 = (s32[16,3072]{1,0:T(8,128)S(1)}, s32[16,3072]{1,0:T(8,128)}, u32[]{:S(2)}) copy-start(s32[16,3072]{1,0:T(8,128)} %get-tuple-element.43) | copy-start | bytes 589828
  12.3 16.9 %copy-start.9 = (s32[16,3072]{1,0:T(8,128)S(1)}, s32[16,3072]{1,0:T(8,128)}, u32[]{:S(2)}) copy-start(s32[16,3072]{1,0:T(8,128)} %get-tuple-element.44) | copy-start | bytes 589828
  23.3 7.2 %collective-permute-start.8 = (f32[32,1792]{1,0:T(8,128)S(1)}, f32[32,1792]{1,0:T(8,128)S(1)}, u32[]{:S(2)}, u32[]{:S(2)}) collective-permute-start(f32[32,1792]{1,0:T(8,128)S(1)} %slice.36), channel_id=1, source_target_pairs={{0,1},{1,0},{2,3},{3,2},{4,5},{5,4},{6,7},{7,6},{8,9},{9,8},{10,11... | collective-permute-start | bytes 688136 | tf_op jit(solution)/shard_map/ppermute | solution.py:285
  25.0 19.1 %collective-permute-start.5 = (f32[32,1792]{1,0:T(8,128)S(1)}, f32[32,1792]{1,0:T(8,128)S(1)}, u32[]{:S(2)}, u32[]{:S(2)}) collective-permute-start(f32[32,1792]{1,0:T(8,128)S(1)} %collective-permute-done.2.refs_1_.refs_2_), channel_id=1, source_target_pairs={{0,8},{2,10},{4,12},{6,14},{8,0},{10,2},{12,4},{14,6},{16,24},{18,... | collective-permute-start | bytes 688136 | tf_op jit(solution)/shard_map/ppermute | solution.py:285
  27.6 16.5 %collective-permute-start.6 = (s32[16,3072]{1,0:T(8,128)S(1)}, s32[16,3072]{1,0:T(8,128)S(1)}, u32[]{:S(2)}, u32[]{:S(2)}) collective-permute-start(s32[16,3072]{1,0:T(8,128)S(1)} %copy-done.10), channel_id=1, source_target_pairs={{0,16},{2,18},{4,20},{6,22},{8,24},{10,26},{12,28},{14,30},{16,0},... | collective-permute-start | bytes 589832 | tf_op jit(solution)/shard_map/ppermute | solution.py:285
  29.2 14.9 %collective-permute-start.7 = (s32[16,3072]{1,0:T(8,128)S(1)}, s32[16,3072]{1,0:T(8,128)S(1)}, u32[]{:S(2)}, u32[]{:S(2)}) collective-permute-start(s32[16,3072]{1,0:T(8,128)S(1)} %copy-done.9), channel_id=1, source_target_pairs={{0,24},{2,26},{4,28},{6,30},{8,16},{10,18},{12,20},{14,22},{16,8},... | collective-permute-start | bytes 589832 | tf_op jit(solution)/shard_map/ppermute | solution.py:285
  30.0 14.7 %collective-permute-start.4 = (f32[32,1792]{1,0:T(8,128)S(1)}, f32[32,1792]{1,0:T(8,128)S(1)}, u32[]{:S(2)}, u32[]{:S(2)}) collective-permute-start(f32[32,1792]{1,0:T(8,128)S(1)} %collective-permute-done.2.refs_1_.refs_2_), channel_id=1, source_target_pairs={{0,1},{1,0},{2,3},{3,2},{4,5},{5,4},{6,7},{7,6},{8,9},{9,8},{10,11... | collective-permute-start | bytes 688136 | tf_op jit(solution)/shard_map/ppermute | solution.py:285
  44.2 6.0 %collective-permute-start.9 = (f32[32,1792]{1,0:T(8,128)S(1)}, f32[32,1792]{1,0:T(8,128)S(1)}, u32[]{:S(2)}, u32[]{:S(2)}) collective-permute-start(f32[32,1792]{1,0:T(8,128)S(1)} %collective-permute-done.5.refs_1_.refs_4_), channel_id=1, source_target_pairs={{0,1},{1,0},{2,3},{3,2},{4,5},{5,4},{6,7},{7,6},{8,9},{9,8},{10,11... | collective-permute-start | bytes 688136 | tf_op jit(solution)/shard_map/ppermute | solution.py:285
  50.2 5.0 %copy-start.7 = (s32[16,3072]{1,0:T(8,128)S(1)}, s32[16,3072]{1,0:T(8,128)}, u32[]{:S(2)}) copy-start(s32[16,3072]{1,0:T(8,128)} %get-tuple-element.35) | copy-start | bytes 589828
  50.2 5.0 %copy-start.6 = (s32[16,3072]{1,0:T(8,128)S(1)}, s32[16,3072]{1,0:T(8,128)}, u32[]{:S(2)}) copy-start(s32[16,3072]{1,0:T(8,128)} %get-tuple-element.36) | copy-start | bytes 589828
  52.2 5.5 %collective-permute-start.10 = (f32[544,512]{1,0:T(8,128)S(1)}, f32[544,512]{1,0:T(8,128)S(1)}, u32[]{:S(2)}, u32[]{:S(2)}) collective-permute-start(f32[544,512]{1,0:T(8,128)S(1)} %shard_map.98), channel_id=1, source_target_pairs={{0,2},{2,0},{4,6},{6,4},{8,10},{10,8},{12,14},{14,12},{16,18},{18,... | collective-permute-start | bytes 3342344 | tf_op jit(solution)/shard_map/ppermute | solution.py:285
  52.3 11.4 %collective-permute-start.11 = (s32[16,3072]{1,0:T(8,128)S(1)}, s32[16,3072]{1,0:T(8,128)S(1)}, u32[]{:S(2)}, u32[]{:S(2)}) collective-permute-start(s32[16,3072]{1,0:T(8,128)S(1)} %copy-done.8), channel_id=1, source_target_pairs={{0,8},{2,10},{4,12},{6,14},{8,0},{10,2},{12,4},{14,6},{16,24},{18,... | collective-permute-start | bytes 589832 | tf_op jit(solution)/shard_map/ppermute | solution.py:285
  55.2 17.1 %collective-permute-start = (s32[16,3072]{1,0:T(8,128)S(1)}, s32[16,3072]{1,0:T(8,128)S(1)}, u32[]{:S(2)}, u32[]{:S(2)}) collective-permute-start(s32[16,3072]{1,0:T(8,128)S(1)} %copy-done.7), channel_id=1, source_target_pairs={{0,16},{2,18},{4,20},{6,22},{8,24},{10,26},{12,28},{14,30},{16,0},... | collective-permute-start | bytes 589832 | tf_op jit(solution)/shard_map/ppermute | solution.py:285
  55.2 17.1 %collective-permute-start.1 = (s32[16,3072]{1,0:T(8,128)S(1)}, s32[16,3072]{1,0:T(8,128)S(1)}, u32[]{:S(2)}, u32[]{:S(2)}) collective-permute-start(s32[16,3072]{1,0:T(8,128)S(1)} %copy-done.6), channel_id=1, source_target_pairs={{0,24},{2,26},{4,28},{6,30},{8,16},{10,18},{12,20},{14,22},{16,8},... | collective-permute-start | bytes 589832 | tf_op jit(solution)/shard_map/ppermute | solution.py:285
  59.5 26.4 %collective-permute-start.14 = (f32[544,512]{1,0:T(8,128)S(1)}, f32[544,512]{1,0:T(8,128)S(1)}, u32[]{:S(2)}, u32[]{:S(2)}) collective-permute-start(f32[544,512]{1,0:T(8,128)S(1)} %shard_map.99), channel_id=1, source_target_pairs={{0,4},{2,6},{4,0},{6,2},{8,12},{10,14},{12,8},{14,10},{16,20},{18,... | collective-permute-start | bytes 3342344 | tf_op jit(solution)/shard_map/ppermute | solution.py:285
  79.1 2.0 %collective-permute-start.12 = (f32[272,512]{1,0:T(8,128)S(1)}, f32[272,512]{1,0:T(8,128)S(1)}, u32[]{:S(2)}, u32[]{:S(2)}) collective-permute-start(f32[272,512]{1,0:T(8,128)S(1)} %get-tuple-element.68), channel_id=1, source_target_pairs={{0,2},{2,0},{4,6},{6,4},{8,10},{10,8},{12,14},{14,12},{16,18},{18,... | collective-permute-start | bytes 1671176 | tf_op jit(solution)/shard_map/ppermute | solution.py:285
  79.2 2.7 %collective-permute-start.13 = (f32[272,512]{1,0:T(8,128)S(1)}, f32[272,512]{1,0:T(8,128)S(1)}, u32[]{:S(2)}, u32[]{:S(2)}) collective-permute-start(f32[272,512]{1,0:T(8,128)S(1)} %get-tuple-element.67), channel_id=1, source_target_pairs={{0,2},{2,0},{4,6},{6,4},{8,10},{10,8},{12,14},{14,12},{16,18},{18,... | collective-permute-start | bytes 1671176 | tf_op jit(solution)/shard_map/ppermute | solution.py:285
  85.9 6.5 %copy-start.3 = (s32[3072]{0:T(1024)S(1)}, s32[3072]{0:T(1024)}, u32[]{:S(2)}) copy-start(s32[3072]{0:T(1024)} %param.9) | copy-start | bytes 36868
  85.9 6.6 %copy-start.2 = (f32[3072,32]{0,1:T(8,128)S(1)}, f32[3072,32]{0,1:T(8,128)}, u32[]{:S(2)}) copy-start(f32[3072,32]{0,1:T(8,128)} %param.7) | copy-start | bytes 1179652
  88.0 4.3 %collective-permute-start.15 = (f32[32,128]{1,0:T(8,128)S(1)}, f32[32,128]{1,0:T(8,128)S(1)}, u32[]{:S(2)}, u32[]{:S(2)}) collective-permute-start(f32[32,128]{1,0:T(8,128)S(1)} %pad_maximum_fusion.1), channel_id=1, source_target_pairs={{0,1},{1,0},{2,3},{3,2},{4,5},{5,4},{6,7},{7,6},{8,9},{9,8},{10,11... | collective-permute-start | bytes 49160 | tf_op jit(solution)/shard_map/ppermute | solution.py:285
  88.6 10.4 %all-to-all-start = ((f32[8,8,128]{2,1,0:T(8,128)}), f32[8,8,128]{2,1,0:T(8,128)S(1)}, u32[]{:S(2)}, u32[]{:S(2)}) async-start(f32[8,8,128]{2,1,0:T(8,128)} %shard_map.102), calls=%async_computation | async-start | bytes 65536 | tf_op jit(solution)/shard_map/all_to_all | solution.py:443
  92.5 7.1 %copy-start.5 = (f32[8,2,32]{2,1,0:T(2,128)}, f32[8,2,32]{2,1,0:T(2,128)S(1)}, u32[]{:S(2)}) copy-start(f32[8,2,32]{2,1,0:T(2,128)S(1)} %fusion.5) | copy-start | bytes 6148
  (4 other events, 6.2 us)

commit v9 on v8

--- a/solution.py
+++ b/solution.py
@@ -45,7 +45,7 @@
 
 
 def half_width(rows):
-    return rows // 2 + 2 * LANES
+    return rows // 2 + LANES
 
 
 def read_info(halves, rows):
@@ -54,15 +54,15 @@
     prob = jnp.concatenate([info[:, :half] for info in halves], axis=1)
     label, node = (
         jnp.concatenate(
-            [info[i : i + 1, low : low + LANES] for info in halves for i in range(chunks)], axis=1
+            [info[i : i + 1, half:] for info in halves for i in range(low, low + chunks)], axis=1
         )
-        for low in (half, half + LANES)
+        for low in (0, chunks)
     )
     return prob, label, node
 
 
 def child_sums(info, rows, node_count):
-    return info[-node_count:, rows // 2 : rows // 2 + LANES]
+    return info[-node_count:, rows // 2 :]
 
 
 def prep_kernel(
@@ -88,11 +88,13 @@
     half, width = rows // 2, half_width(rows)
     chunks = half // LANES
     turned[...] = codes_ref[...].T
-    for (infos, pieces), out_ref in zip(blocks, outs):
+    for (infos, pieces, _), out_ref in zip(blocks, outs):
+        if infos == 0 and out_ref.shape[1] > rows:
+            out_ref[:, rows:] = jnp.zeros((out_ref.shape[0], out_ref.shape[1] - rows), out_ref.dtype)
         for i, start_of in enumerate(pieces):
             start = pl.multiple_of(start_of(row_index), own)
             if infos == 0:
-                out_ref[i * own : (i + 1) * own, :] = turned[pl.ds(start, own), :]
+                out_ref[i * own : (i + 1) * own, :rows] = turned[pl.ds(start, own), :]
                 continue
             cut = rows * infos // 2
             for h in range(2 // infos):
@@ -134,19 +136,16 @@
         preferred_element_type=jnp.float32,
     )
     sums = jnp.concatenate([sums[:node_count], sums[node_count:]], axis=1)
-    pad = jnp.zeros((classes - chunks - node_count, LANES), jnp.float32)
-    long_pad = jnp.zeros((classes - chunks, LANES), jnp.float32)
+    pad = [jnp.zeros((classes - 2 * chunks - node_count, LANES), jnp.float32)]
+    pad = pad if pad[0].shape[0] > 0 else []
     for h in range(2):
         some = slice(h * chunks, (h + 1) * chunks)
         info_ref[:, h * width : h * width + half] = prob[:, h * half : (h + 1) * half]
-        info_ref[:, h * width + half : h * width + half + LANES] = jnp.concatenate(
-            [labels[some], pad, sums], axis=0
-        )
-        info_ref[:, h * width + half + LANES : (h + 1) * width] = jnp.concatenate(
-            [nodes[some], long_pad], axis=0
+        info_ref[:, h * width + half : (h + 1) * width] = jnp.concatenate(
+            [labels[some], nodes[some]] + pad + [sums], axis=0
         )
     half_ref[...] = jnp.where(feat_index == 0, info_ref[:, :width], info_ref[:, width:])
-    for (infos, _), out_ref in zip(blocks, outs):
+    for (infos, _, _), out_ref in zip(blocks, outs):
         if infos > 0:
             out_ref[:classes, :] = half_ref[...] if infos == 1 else info_ref[...]
 
@@ -227,7 +226,7 @@
             low = jnp.where(feat_index == 0, near, far)
             high = jnp.where(feat_index == 0, far, near)
             sums_from = near
-        rows = 2 * (width - 2 * LANES)
+        rows = 2 * (width - LANES)
         masked = masked_gradients((low, high), rows, node_count)
         sums = child_sums(sums_from, rows, node_count)
         for i, first in enumerate(firsts):
@@ -304,10 +303,10 @@
         jax.ShapeDtypeStruct((classes, width), jnp.float32),
         jax.ShapeDtypeStruct((1, rows_dev), jnp.float32),
     ]
-    for infos, pieces in blocks:
+    for infos, pieces, spare in blocks:
         codes = len(pieces) * own
         if infos == 0:
-            shapes.append(jax.ShapeDtypeStruct((codes, rows_dev), jnp.int32))
+            shapes.append(jax.ShapeDtypeStruct((codes, rows_dev + spare), jnp.int32))
         else:
             shape = (classes + codes * 2 // infos, infos * width)
             shapes.append(jax.ShapeDtypeStruct(shape, jnp.float32))
@@ -371,13 +370,13 @@
         return tuple(lambda row, low=m ^ 3 ^ q: start(row ^ low) for q in which)
 
     blocks = (
-        (0, quarters(0, (0, 1, 2, 3))),
-        (1, quarters(4, (0, 1))),
-        (0, quarters(8, (0, 1))),
-        (0, quarters(12, (0, 1))),
-        (0, quarters(4, (2, 3))),
-        (0, quarters(8, (2, 3))),
-        (0, quarters(12, (2, 3))),
+        (0, quarters(0, (0, 1, 2, 3)), 0),
+        (1, quarters(4, (0, 1)), 0),
+        (0, quarters(8, (0, 1)), 4 * LANES),
+        (0, quarters(12, (0, 1)), 4 * LANES),
+        (0, quarters(4, (2, 3)), 0),
+        (0, quarters(8, (2, 3)), 0),
+        (0, quarters(12, (2, 3)), 0),
     )
     info, half, flags, codes_0, rows_4, codes_8, codes_12, late_4, late_8, late_12 = prepare(
         blocks, splits, logits_t, labels, node_ids, bin_codes
@@ -453,7 +452,7 @@
     own = 8
     group = feats_dev // own
     group_count = n_rows // group
-    blocks = tuple((2, (lambda row, r=r: r * own,)) for r in range(group))
+    blocks = tuple((2, (lambda row, r=r: r * own,), 0) for r in range(group))
     info, _, flags, *rows_out = prepare(blocks, splits, logits_t, labels, node_ids, bin_codes)
     members = [[g * group + r for r in range(group)] for g in range(group_count)]
     rows_in = lax.all_to_all(

time: 99.9 us -> 96.3 us (0.964)
  waiting for transfers between devices: 35.8 us -> 32.7 us
    ppermute x16, waiting for transfers between devices: 30.5 us -> 27.4 us  [swap(): return lax.ppermute(x, axis, [(i, i ^ bit) for i in range(size)])]
    ppermute x16, starting transfers between devices: 21.6 us -> 19.3 us  [swap(): return lax.ppermute(x, axis, [(i, i ^ bit) for i in range(size)])]
    all_to_all x1, starting transfers between devices: 3.69 us -> 5.49 us  [local(): lax.all_to_all(gains, 'rows', 0, 0, tiled=True, axis_index_groups=halves)]
    unnamed x23 -> x19, local copies, waits for them, and re-layouts: 2.66 us -> 2.65 us
  transfers between devices with their start and end apart: 17 -> 17, of which waited for: 10 -> 11; matrix products, arithmetic and copies ran while one was open for 1% -> 2% of each run, Pallas kernels for 26% -> 27%
where the time goes in v9:
time: 96.3 us; the launch traced here: 96 us
  Pallas kernels  33.5 us (35%)
  waiting for transfers between devices  32.7 us (34%)
  starting transfers between devices  24.8 us (26%)
  local copies, waits for them, and re-layouts  2.81 us (3%)
  matrix products  1.1 us (1%)
    pallas_call x7, Pallas kernels, add_rows(): pl.pallas_call(functools.partial(add_kernel, classes, node_count, own, pl...  27.5 us
    ppermute x16, waiting for transfers between devices, swap(): return lax.ppermute(x, axis, [(i, i ^ bit) for i in range(size)])  27.4 us
    ppermute x16, starting transfers between devices, swap(): return lax.ppermute(x, axis, [(i, i ^ bit) for i in range(size)])  19.3 us
    all_to_all x1, starting transfers between devices, local(): lax.all_to_all(gains, 'rows', 0, 0, tiled=True, axis_index_groups=halves)  5.49 us
    all_to_all x1, waiting for transfers between devices, local(): lax.all_to_all(gains, 'rows', 0, 0, tiled=True, axis_index_groups=halves)  5.36 us
    pallas_call x1, Pallas kernels, prepare(): pl.pallas_call(functools.partial(prep_kernel, own, blocks), in_specs=[pl....  3.9 us
    unnamed x19, local copies, waits for them, and re-layouts  2.65 us
    pallas_call x1, Pallas kernels, local(): pl.pallas_call(functools.partial(gain_kernel, classes, node_count), in_sp...  2.07 us
  transfers between devices with their start and end apart: 17, of which 11 were waited for; matrix products, arithmetic and copies ran while one was open for 2% of the time, Pallas kernels for 27%

profile of v9, /device:TPU:0, one launch (start us, length us, event | category | flops | bytes accessed | tf_op | source)
XLA Modules:
  0.0 96.0 jit_solution(10173038886923166103)
XLA Ops:
  0.6 3.9 %shard_map.94 = (f32[32,3328]{1,0:T(8,128)}, f32[32,1664]{1,0:T(8,128)}, f32[1,3072]{1,0:T(1,128)}, s32[32,3072]{1,0:T(8,128)}, f32[64,1664]{1,0:T(8,128)}, /*in...) custom-call(s32[3072,128]{1,0:T(8,128)} %refs_0_.1, ...), custom_call_target="tpu_custom_call" | custom-call | flops 1000000 | bytes 1000000 | tf_op jit(solution)/shard_map/pallas_call | solution.py:321
  4.5 3.1 %collective-permute-start.3 = (f32[64,1664]{1,0:T(8,128)}, f32[64,1664]{1,0:T(8,128)S(1)}, u32[]{:S(2)}, u32[]{:S(2)}) collective-permute-start(f32[64,1664]{1,0:T(8,128)} %get-tuple-element.38), channel_id=1, source_target_pairs={{0,8},{2,10},{4,12},{6,14},{8,0},{10,2},{12,4},{14,6},{16,24},{18,... | collective-permute-start | bytes 1277960 | tf_op jit(solution)/shard_map/ppermute | solution.py:284
  7.6 2.6 %collective-permute-start.2 = (f32[32,1664]{1,0:T(8,128)}, f32[32,1664]{1,0:T(8,128)S(1)}, u32[]{:S(2)}, u32[]{:S(2)}) collective-permute-start(f32[32,1664]{1,0:T(8,128)} %get-tuple-element.37), channel_id=1, source_target_pairs={{0,16},{2,18},{4,20},{6,22},{8,24},{10,26},{12,28},{14,30},{16,0},... | collective-permute-start | bytes 638984 | tf_op jit(solution)/shard_map/ppermute | solution.py:284
  10.6 2.5 %collective-permute-start.7 = (s32[16,3584]{1,0:T(8,128)}, s32[16,3584]{1,0:T(8,128)S(1)}, u32[]{:S(2)}, u32[]{:S(2)}) collective-permute-start(s32[16,3584]{1,0:T(8,128)} %get-tuple-element.44), channel_id=1, source_target_pairs={{0,24},{2,26},{4,28},{6,30},{8,16},{10,18},{12,20},{14,22},{16,8},... | collective-permute-start | bytes 688136 | tf_op jit(solution)/shard_map/ppermute | solution.py:284
  15.0 6.7 %shard_map.95 = (f32[544,512]{1,0:T(8,128)S(1)}, f32[544,512]{1,0:T(8,128)S(1)}, f32[544,512]{1,0:T(8,128)S(1)}, f32[544,512]{1,0:T(8,128)S(1)}) custom-call(s32[32,3072]{1,0:T(8,128)S(1)} %copy-done.1, f32[32,3328]{1,0:T(8,128)S(1)} %copy-done), custom_call_target="tpu_custom_call" | custom-call | flops 1000000 | bytes 1000000 | tf_op jit(solution)/shard_map/pallas_call | solution.py:266
  22.8 3.4 %collective-permute-done.3.refs_0_.refs_1_ = f32[64,1664]{1,0:T(8,128)S(1)} collective-permute-done((f32[64,1664]{1,0:T(8,128)}, f32[64,1664]{1,0:T(8,128)S(1)}, u32[]{:S(2)}, u32[]{:S(2)}) %collective-permute-start.3) | collective-permute-done | bytes 426016 | tf_op jit(solution)/shard_map/ppermute | solution.py:284
  26.2 1.7 %collective-permute-start.8 = (f32[32,1664]{1,0:T(8,128)S(1)}, f32[32,1664]{1,0:T(8,128)S(1)}, u32[]{:S(2)}, u32[]{:S(2)}) collective-permute-start(f32[32,1664]{1,0:T(8,128)S(1)} %slice.36), channel_id=1, source_target_pairs={{0,1},{1,0},{2,3},{3,2},{4,5},{5,4},{6,7},{7,6},{8,9},{9,8},{10,11... | collective-permute-start | bytes 638984 | tf_op jit(solution)/shard_map/ppermute | solution.py:284
  28.3 6.1 %collective-permute-done.8.refs_1_.refs_2_ = f32[32,1664]{1,0:T(8,128)S(1)} collective-permute-done((f32[32,1664]{1,0:T(8,128)S(1)}, f32[32,1664]{1,0:T(8,128)S(1)}, u32[]{:S(2)}, u32[]{:S(2)}) %collective-permute-start.8) | collective-permute-done | bytes 213024 | tf_op jit(solution)/shard_map/ppermute | solution.py:284
  34.5 3.4 %shard_map.96 = (f32[544,512]{1,0:T(8,128)S(1)}, f32[544,512]{1,0:T(8,128)S(1)}) custom-call(f32[64,1664]{1,0:T(8,128)S(1)} %collective-permute-done.3.refs_0_.refs_1_, f32[32,1664]{1,0:T(8,128)S(1)} %collective-permute-done.8.refs_1_.refs_2_, f32[544,512]{1,0:T(8,128)S(1)} %get-tuple-element.46.refs_2_, f32[544,512]{1,0:T(8,128)S(1)} %get-tuple-element.47.refs_3_), custom_call_target="tpu_custom_call" | custom-call | flops 1000000 | bytes 1000000 | tf_op jit(solution)/shard_map/pallas_call | solution.py:266
  40.3 3.4 %shard_map.97 = (f32[544,512]{1,0:T(8,128)S(1)}, f32[544,512]{1,0:T(8,128)S(1)}) custom-call(s32[16,3584]{1,0:T(8,128)S(1)} %collective-permute-done.6.refs_0_, f32[32,1664]{1,0:T(8,128)S(1)} %collective-permute-done.2.refs_1_.refs_2_, f32[32,1664]{1,0:T(8,128)S(1)} %collective-permute-done.4.refs_2_.refs_3_, f32[544,512]{1,0:T(8,128)S(1)} %get-tuple-element.52.refs_3_, ...), custom_call_target="tpu_custom_call" | custom-call | flops 1000000 | bytes 1000000 | tf_op jit(solution)/shard_map/pallas_call | solution.py:266
  43.7 1.9 %collective-permute-done.9.refs_2_.refs_5_ = f32[32,1664]{1,0:T(8,128)S(1)} collective-permute-done((f32[32,1664]{1,0:T(8,128)S(1)}, f32[32,1664]{1,0:T(8,128)S(1)}, u32[]{:S(2)}, u32[]{:S(2)}) %collective-permute-start.9) | collective-permute-done | bytes 213024 | tf_op jit(solution)/shard_map/ppermute | solution.py:284
  45.6 2.0 %shard_map.98 = f32[544,512]{1,0:T(8,128)S(1)} custom-call(s32[16,3584]{1,0:T(8,128)S(1)} %collective-permute-done.7.refs_0_, f32[32,1664]{1,0:T(8,128)S(1)} %collective-permute-done.5.refs_1_.refs_4_, f32[32,1664]{1,0:T(8,128)S(1)} %collective-permute-done.9.refs_2_.refs_5_, f32[544,512]{1,0:T(8,128)S(1)} %get-tuple-element.55.refs_3_), custom_call_target="tpu_custom_call" | custom-call | flops 1000000 | bytes 1000000 | tf_op jit(solution)/shard_map/pallas_call | solution.py:266
  48.4 3.4 %collective-permute-start = (s32[16,3072]{1,0:T(8,128)S(1)}, s32[16,3072]{1,0:T(8,128)S(1)}, u32[]{:S(2)}, u32[]{:S(2)}) collective-permute-start(s32[16,3072]{1,0:T(8,128)S(1)} %copy-done.7), channel_id=1, source_target_pairs={{0,16},{2,18},{4,20},{6,22},{8,24},{10,26},{12,28},{14,30},{16,0},... | collective-permute-start | bytes 589832 | tf_op jit(solution)/shard_map/ppermute | solution.py:284
  52.2 1.8 %shard_map.99 = f32[544,512]{1,0:T(8,128)S(1)} custom-call(s32[16,3584]{1,0:T(8,128)S(1)} %collective-permute-done.7.refs_0_, f32[32,1664]{1,0:T(8,128)S(1)} %collective-permute-done.5.refs_1_.refs_4_, f32[32,1664]{1,0:T(8,128)S(1)} %collective-permute-done.9.refs_2_.refs_5_, f32[544,512]{1,0:T(8,128)S(1)} %get-tuple-element.54.refs_3_, ...), custom_call_target="tpu_custom_call" | custom-call | flops 1000000 | bytes 1000000 | tf_op jit(solution)/shard_map/pallas_call | solution.py:266
  54.0 1.6 %collective-permute-start.14 = (f32[544,512]{1,0:T(8,128)S(1)}, f32[544,512]{1,0:T(8,128)S(1)}, u32[]{:S(2)}, u32[]{:S(2)}) collective-permute-start(f32[544,512]{1,0:T(8,128)S(1)} %shard_map.99), channel_id=1, source_target_pairs={{0,4},{2,6},{4,0},{6,2},{8,12},{10,14},{12,8},{14,10},{16,20},{18,... | collective-permute-start | bytes 3342344 | tf_op jit(solution)/shard_map/ppermute | solution.py:284
  55.6 3.3 %collective-permute-done.11.refs_0_ = s32[16,3072]{1,0:T(8,128)S(1)} collective-permute-done((s32[16,3072]{1,0:T(8,128)S(1)}, s32[16,3072]{1,0:T(8,128)S(1)}, u32[]{:S(2)}, u32[]{:S(2)}) %collective-permute-start.11) | collective-permute-done | bytes 196640 | tf_op jit(solution)/shard_map/ppermute | solution.py:284
  58.9 3.4 %shard_map.100 = (f32[544,512]{1,0:T(8,128)S(1)}, f32[544,512]{1,0:T(8,128)S(1)}) custom-call(s32[16,3072]{1,0:T(8,128)S(1)} %collective-permute-done.11.refs_0_, f32[64,1664]{1,0:T(8,128)S(1)} %collective-permute-done.3.refs_0_.refs_1_, f32[32,1664]{1,0:T(8,128)S(1)} %collective-permute-done.8.refs_1_.refs_2_, f32[544,512]{1,0:T(8,128)S(1)} %get-tuple-element.58.refs_3_, ...), custom_call_target="tpu_custom_call" | custom-call | flops 1000000 | bytes 1000000 | tf_op jit(solution)/shard_map/pallas_call | solution.py:266
  62.3 3.6 %collective-permute-done.refs_0_ = s32[16,3072]{1,0:T(8,128)S(1)} collective-permute-done((s32[16,3072]{1,0:T(8,128)S(1)}, s32[16,3072]{1,0:T(8,128)S(1)}, u32[]{:S(2)}, u32[]{:S(2)}) %collective-permute-start) | collective-permute-done | bytes 196640 | tf_op jit(solution)/shard_map/ppermute | solution.py:284
  65.9 6.7 %shard_map.101 = (f32[544,512]{1,0:T(8,128)S(1)}, f32[544,512]{1,0:T(8,128)S(1)}) custom-call(s32[16,3072]{1,0:T(8,128)S(1)} %collective-permute-done.refs_0_, s32[16,3072]{1,0:T(8,128)S(1)} %collective-permute-done.1.refs_1_, f32[32,1664]{1,0:T(8,128)S(1)} %collective-permute-done.2.refs_1_.refs_2_, f32[32,1664]{1,0:T(8,128)S(1)} %collective-permute-done.4.refs_2_.refs_3_, ...), custom_call_target="tpu_custom_call" | custom-call | flops 1000000 | bytes 1000000 | tf_op jit(solution)/shard_map/pallas_call | solution.py:266
  73.3 1.4 %collective-permute-done.12 = f32[272,512]{1,0:T(8,128)S(1)} collective-permute-done((f32[272,512]{1,0:T(8,128)S(1)}, f32[272,512]{1,0:T(8,128)S(1)}, u32[]{:S(2)}, u32[]{:S(2)}) %collective-permute-start.12) | collective-permute-done | bytes 557088 | tf_op jit(solution)/shard_map/ppermute | solution.py:284
  75.6 4.5 %collective-permute-done.14.refs_1_ = f32[544,512]{1,0:T(8,128)S(1)} collective-permute-done((f32[544,512]{1,0:T(8,128)S(1)}, f32[544,512]{1,0:T(8,128)S(1)}, u32[]{:S(2)}, u32[]{:S(2)}) %collective-permute-start.14) | collective-permute-done | bytes 1114144 | tf_op jit(solution)/shard_map/ppermute | solution.py:284
  80.1 2.1 %shard_map.102 = f32[8,8,128]{2,1,0:T(8,128)} custom-call(f32[544,512]{1,0:T(8,128)S(1)} %pad_maximum_fusion.refs_0_, f32[544,512]{1,0:T(8,128)S(1)} %collective-permute-done.14.refs_1_, f32[544,512]{1,0:T(8,128)S(1)} %get-tuple-element.63.refs_2_), custom_call_target="tpu_custom_call" | custom-call | flops 1000000 | bytes 1000000 | tf_op jit(solution)/shard_map/pallas_call | solution.py:421
  83.2 5.5 %all-to-all-start = ((f32[8,8,128]{2,1,0:T(8,128)}), f32[8,8,128]{2,1,0:T(8,128)S(1)}, u32[]{:S(2)}, u32[]{:S(2)}) async-start(f32[8,8,128]{2,1,0:T(8,128)} %shard_map.102), calls=%async_computation | async-start | bytes 65536 | tf_op jit(solution)/shard_map/all_to_all | solution.py:442
  90.0 5.4 %all-to-all-done = f32[8,8,128]{2,1,0:T(8,128)S(1)} async-done(((f32[8,8,128]{2,1,0:T(8,128)}), f32[8,8,128]{2,1,0:T(8,128)S(1)}, u32[]{:S(2)}, u32[]{:S(2)}) %all-to-all-start) | async-done | bytes 32800 | tf_op jit(solution)/shard_map/all_to_all | solution.py:442
  (49 shorter events, 11.7 us)
Async XLA Ops:
  4.5 21.7 %collective-permute-start.3 = (f32[64,1664]{1,0:T(8,128)}, f32[64,1664]{1,0:T(8,128)S(1)}, u32[]{:S(2)}, u32[]{:S(2)}) collective-permute-start(f32[64,1664]{1,0:T(8,128)} %get-tuple-element.38), channel_id=1, source_target_pairs={{0,8},{2,10},{4,12},{6,14},{8,0},{10,2},{12,4},{14,6},{16,24},{18,... | collective-permute-start | bytes 1277960 | tf_op jit(solution)/shard_map/ppermute | solution.py:284
  7.6 15.1 %collective-permute-start.2 = (f32[32,1664]{1,0:T(8,128)}, f32[32,1664]{1,0:T(8,128)S(1)}, u32[]{:S(2)}, u32[]{:S(2)}) collective-permute-start(f32[32,1664]{1,0:T(8,128)} %get-tuple-element.37), channel_id=1, source_target_pairs={{0,16},{2,18},{4,20},{6,22},{8,24},{10,26},{12,28},{14,30},{16,0},... | collective-permute-start | bytes 638984 | tf_op jit(solution)/shard_map/ppermute | solution.py:284
  10.2 27.7 %collective-permute-start.6 = (s32[16,3584]{1,0:T(8,128)}, s32[16,3584]{1,0:T(8,128)S(1)}, u32[]{:S(2)}, u32[]{:S(2)}) collective-permute-start(s32[16,3584]{1,0:T(8,128)} %get-tuple-element.43), channel_id=1, source_target_pairs={{0,16},{2,18},{4,20},{6,22},{8,24},{10,26},{12,28},{14,30},{16,0},... | collective-permute-start | bytes 688136 | tf_op jit(solution)/shard_map/ppermute | solution.py:284
  10.6 27.4 %collective-permute-start.7 = (s32[16,3584]{1,0:T(8,128)}, s32[16,3584]{1,0:T(8,128)S(1)}, u32[]{:S(2)}, u32[]{:S(2)}) collective-permute-start(s32[16,3584]{1,0:T(8,128)} %get-tuple-element.44), channel_id=1, source_target_pairs={{0,24},{2,26},{4,28},{6,30},{8,16},{10,18},{12,20},{14,22},{16,8},... | collective-permute-start | bytes 688136 | tf_op jit(solution)/shard_map/ppermute | solution.py:284
  26.2 8.3 %collective-permute-start.8 = (f32[32,1664]{1,0:T(8,128)S(1)}, f32[32,1664]{1,0:T(8,128)S(1)}, u32[]{:S(2)}, u32[]{:S(2)}) collective-permute-start(f32[32,1664]{1,0:T(8,128)S(1)} %slice.36), channel_id=1, source_target_pairs={{0,1},{1,0},{2,3},{3,2},{4,5},{5,4},{6,7},{7,6},{8,9},{9,8},{10,11... | collective-permute-start | bytes 638984 | tf_op jit(solution)/shard_map/ppermute | solution.py:284
  27.9 11.2 %collective-permute-start.5 = (f32[32,1664]{1,0:T(8,128)S(1)}, f32[32,1664]{1,0:T(8,128)S(1)}, u32[]{:S(2)}, u32[]{:S(2)}) collective-permute-start(f32[32,1664]{1,0:T(8,128)S(1)} %collective-permute-done.2.refs_1_.refs_2_), channel_id=1, source_target_pairs={{0,8},{2,10},{4,12},{6,14},{8,0},{10,2},{12,4},{14,6},{16,24},{18,... | collective-permute-start | bytes 638984 | tf_op jit(solution)/shard_map/ppermute | solution.py:284
  27.9 12.3 %collective-permute-start.4 = (f32[32,1664]{1,0:T(8,128)S(1)}, f32[32,1664]{1,0:T(8,128)S(1)}, u32[]{:S(2)}, u32[]{:S(2)}) collective-permute-start(f32[32,1664]{1,0:T(8,128)S(1)} %collective-permute-done.2.refs_1_.refs_2_), channel_id=1, source_target_pairs={{0,1},{1,0},{2,3},{3,2},{4,5},{5,4},{6,7},{7,6},{8,9},{9,8},{10,11... | collective-permute-start | bytes 638984 | tf_op jit(solution)/shard_map/ppermute | solution.py:284
  39.2 6.4 %collective-permute-start.9 = (f32[32,1664]{1,0:T(8,128)S(1)}, f32[32,1664]{1,0:T(8,128)S(1)}, u32[]{:S(2)}, u32[]{:S(2)}) collective-permute-start(f32[32,1664]{1,0:T(8,128)S(1)} %collective-permute-done.5.refs_1_.refs_4_), channel_id=1, source_target_pairs={{0,1},{1,0},{2,3},{3,2},{4,5},{5,4},{6,7},{7,6},{8,9},{9,8},{10,11... | collective-permute-start | bytes 638984 | tf_op jit(solution)/shard_map/ppermute | solution.py:284
  45.6 2.1 %copy-start.8 = (s32[16,3072]{1,0:T(8,128)S(1)}, s32[16,3072]{1,0:T(8,128)}, u32[]{:S(2)}) copy-start(s32[16,3072]{1,0:T(8,128)} %get-tuple-element.56) | copy-start | bytes 589828
  45.6 2.8 %copy-start.7 = (s32[16,3072]{1,0:T(8,128)S(1)}, s32[16,3072]{1,0:T(8,128)}, u32[]{:S(2)}) copy-start(s32[16,3072]{1,0:T(8,128)} %get-tuple-element.35) | copy-start | bytes 589828
  45.6 6.2 %copy-start.6 = (s32[16,3072]{1,0:T(8,128)S(1)}, s32[16,3072]{1,0:T(8,128)}, u32[]{:S(2)}) copy-start(s32[16,3072]{1,0:T(8,128)} %get-tuple-element.36) | copy-start | bytes 589828
  47.6 4.6 %collective-permute-start.10 = (f32[544,512]{1,0:T(8,128)S(1)}, f32[544,512]{1,0:T(8,128)S(1)}, u32[]{:S(2)}, u32[]{:S(2)}) collective-permute-start(f32[544,512]{1,0:T(8,128)S(1)} %shard_map.98), channel_id=1, source_target_pairs={{0,2},{2,0},{4,6},{6,4},{8,10},{10,8},{12,14},{14,12},{16,18},{18,... | collective-permute-start | bytes 3342344 | tf_op jit(solution)/shard_map/ppermute | solution.py:284
  47.7 11.2 %collective-permute-start.11 = (s32[16,3072]{1,0:T(8,128)S(1)}, s32[16,3072]{1,0:T(8,128)S(1)}, u32[]{:S(2)}, u32[]{:S(2)}) collective-permute-start(s32[16,3072]{1,0:T(8,128)S(1)} %copy-done.8), channel_id=1, source_target_pairs={{0,8},{2,10},{4,12},{6,14},{8,0},{10,2},{12,4},{14,6},{16,24},{18,... | collective-permute-start | bytes 589832 | tf_op jit(solution)/shard_map/ppermute | solution.py:284
  48.4 17.6 %collective-permute-start = (s32[16,3072]{1,0:T(8,128)S(1)}, s32[16,3072]{1,0:T(8,128)S(1)}, u32[]{:S(2)}, u32[]{:S(2)}) collective-permute-start(s32[16,3072]{1,0:T(8,128)S(1)} %copy-done.7), channel_id=1, source_target_pairs={{0,16},{2,18},{4,20},{6,22},{8,24},{10,26},{12,28},{14,30},{16,0},... | collective-permute-start | bytes 589832 | tf_op jit(solution)/shard_map/ppermute | solution.py:284
  51.8 14.2 %collective-permute-start.1 = (s32[16,3072]{1,0:T(8,128)S(1)}, s32[16,3072]{1,0:T(8,128)S(1)}, u32[]{:S(2)}, u32[]{:S(2)}) collective-permute-start(s32[16,3072]{1,0:T(8,128)S(1)} %copy-done.6), channel_id=1, source_target_pairs={{0,24},{2,26},{4,28},{6,30},{8,16},{10,18},{12,20},{14,22},{16,8},... | collective-permute-start | bytes 589832 | tf_op jit(solution)/shard_map/ppermute | solution.py:284
  54.0 26.1 %collective-permute-start.14 = (f32[544,512]{1,0:T(8,128)S(1)}, f32[544,512]{1,0:T(8,128)S(1)}, u32[]{:S(2)}, u32[]{:S(2)}) collective-permute-start(f32[544,512]{1,0:T(8,128)S(1)} %shard_map.99), channel_id=1, source_target_pairs={{0,4},{2,6},{4,0},{6,2},{8,12},{10,14},{12,8},{14,10},{16,20},{18,... | collective-permute-start | bytes 3342344 | tf_op jit(solution)/shard_map/ppermute | solution.py:284
  72.7 2.0 %collective-permute-start.12 = (f32[272,512]{1,0:T(8,128)S(1)}, f32[272,512]{1,0:T(8,128)S(1)}, u32[]{:S(2)}, u32[]{:S(2)}) collective-permute-start(f32[272,512]{1,0:T(8,128)S(1)} %get-tuple-element.68), channel_id=1, source_target_pairs={{0,2},{2,0},{4,6},{6,4},{8,10},{10,8},{12,14},{14,12},{16,18},{18,... | collective-permute-start | bytes 1671176 | tf_op jit(solution)/shard_map/ppermute | solution.py:284
  72.8 2.7 %collective-permute-start.13 = (f32[272,512]{1,0:T(8,128)S(1)}, f32[272,512]{1,0:T(8,128)S(1)}, u32[]{:S(2)}, u32[]{:S(2)}) collective-permute-start(f32[272,512]{1,0:T(8,128)S(1)} %get-tuple-element.67), channel_id=1, source_target_pairs={{0,2},{2,0},{4,6},{6,4},{8,10},{10,8},{12,14},{14,12},{16,18},{18,... | collective-permute-start | bytes 1671176 | tf_op jit(solution)/shard_map/ppermute | solution.py:284
  80.1 2.1 %copy-start.4 = (f32[1,3072]{1,0:T(1,128)S(1)}, f32[1,3072]{1,0:T(1,128)}, u32[]{:S(2)}) copy-start(f32[1,3072]{1,0:T(1,128)} %get-tuple-element.65) | copy-start | bytes 36868
  80.1 8.7 %copy-start.3 = (s32[3072]{0:T(1024)S(1)}, s32[3072]{0:T(1024)}, u32[]{:S(2)}) copy-start(s32[3072]{0:T(1024)} %param.9) | copy-start | bytes 36868
  80.1 8.8 %copy-start.2 = (f32[3072,32]{0,1:T(8,128)S(1)}, f32[3072,32]{0,1:T(8,128)}, u32[]{:S(2)}) copy-start(f32[3072,32]{0,1:T(8,128)} %param.7) | copy-start | bytes 1179652
  82.2 6.5 %collective-permute-start.15 = (f32[32,128]{1,0:T(8,128)S(1)}, f32[32,128]{1,0:T(8,128)S(1)}, u32[]{:S(2)}, u32[]{:S(2)}) collective-permute-start(f32[32,128]{1,0:T(8,128)S(1)} %pad_maximum_fusion.1), channel_id=1, source_target_pairs={{0,1},{1,0},{2,3},{3,2},{4,5},{5,4},{6,7},{7,6},{8,9},{9,8},{10,11... | collective-permute-start | bytes 49160 | tf_op jit(solution)/shard_map/ppermute | solution.py:284
  83.2 12.2 %all-to-all-start = ((f32[8,8,128]{2,1,0:T(8,128)}), f32[8,8,128]{2,1,0:T(8,128)S(1)}, u32[]{:S(2)}, u32[]{:S(2)}) async-start(f32[8,8,128]{2,1,0:T(8,128)} %shard_map.102), calls=%async_computation | async-start | bytes 65536 | tf_op jit(solution)/shard_map/all_to_all | solution.py:442
  88.9 7.1 %copy-start.5 = (f32[8,2,32]{2,1,0:T(2,128)}, f32[8,2,32]{2,1,0:T(2,128)S(1)}, u32[]{:S(2)}) copy-start(f32[8,2,32]{2,1,0:T(2,128)S(1)} %fusion.5) | copy-start | bytes 6148
  (2 other events, 2.0 us)

commit v10 on v9

--- a/solution.py
+++ b/solution.py
@@ -208,7 +208,7 @@
 
 def add_kernel(classes, node_count, own, plan, carry, *refs):
     outs = len(plan[0][3])
-    arrays = 1 + max(max((c,) + i) for _, c, i, _ in plan)
+    arrays = 1 + max(max((c,) + tuple(j for j in i if j is not None)) for _, c, i, _ in plan)
     out_refs = refs[-outs:]
     held_refs = refs[arrays:-outs]
     pairs = 2 * classes * node_count
@@ -216,22 +216,35 @@
     for s, (m, codes_at, info_at, firsts) in enumerate(plan):
         codes_ref = refs[codes_at]
         line = (row_index >> 2) ^ (m >> 2)
+        cut = None
         if len(info_at) == 1:
             width = refs[info_at[0]].shape[1] // 2
-            low, high = (refs[info_at[0]][:classes, h * width : (h + 1) * width] for h in range(2))
-            sums_from = low
+            halves = [refs[info_at[0]][:classes, h * width : (h + 1) * width] for h in range(2)]
+            sums_from = halves[0]
+        elif None in info_at:
+            near_only = info_at[1] is None
+            info_ref = refs[info_at[0] if near_only else info_at[1]]
+            width = info_ref.shape[1]
+            halves = [info_ref[:classes, :]]
+            sums_from = halves[0] if near_only else None
+            which = feat_index if near_only else 1 - feat_index
+            cut = pl.ds(pl.multiple_of(which * (width - LANES), LANES), width - LANES)
         else:
             width = refs[info_at[0]].shape[1]
             near, far = (refs[i][:classes, :] for i in info_at)
-            low = jnp.where(feat_index == 0, near, far)
-            high = jnp.where(feat_index == 0, far, near)
+            halves = [
+                jnp.where(feat_index == 0, near, far),
+                jnp.where(feat_index == 0, far, near),
+            ]
             sums_from = near
         rows = 2 * (width - LANES)
-        masked = masked_gradients((low, high), rows, node_count)
-        sums = child_sums(sums_from, rows, node_count)
+        masked = masked_gradients(halves, rows, node_count)
+        sums = None if sums_from is None else child_sums(sums_from, rows, node_count)
         for i, first in enumerate(firsts):
             out_ref = out_refs[i]
-            if codes_ref.shape[1] < rows:
+            if cut is not None:
+                codes = codes_ref[first : first + own, cut]
+            elif codes_ref.shape[1] < rows:
                 second = first + (codes_ref.shape[0] - classes) // 2
                 codes = jnp.concatenate(
                     [codes_ref[low : low + own, : rows // 2] for low in (first, second)], axis=1
@@ -250,7 +263,7 @@
                 else:
                     out_ref[...] = jnp.zeros(out_ref.shape, out_ref.dtype)
             out_ref[:pairs, :] += product
-            if not carry:
+            if not carry or sums is None:
                 continue
             low_row = pairs + (row_index & 3) * node_count
             band = pl.ds(pl.multiple_of(low_row, node_count), node_count)
@@ -275,8 +288,19 @@
 
 def gain_kernel(classes, node_count, *refs):
     gain_ref, hist_ref = refs[-2:]
-    hist_ref[...] = sum(ref[: hist_ref.shape[0], :] for ref in refs[:-2])
+    out_refs = refs[-2 - node_count : -2]
+    hist_ref[...] = sum(ref[: hist_ref.shape[0], :] for ref in refs[: -2 - node_count])
     write_gains(hist_ref, gain_ref, classes, node_count)
+    for i, out_ref in enumerate(out_refs):
+        out_ref[...] = gain_ref[(lax.axis_index("rows") >> 1) ^ i]
+
+
+def place_kernel(*refs):
+    out_ref = refs[-1]
+    own = refs[0].shape[0]
+    for i, ref in enumerate(refs[:-1]):
+        start = ((lax.axis_index("rows") >> 1) ^ i) * own
+        out_ref[0, pl.ds(pl.multiple_of(start, own), own), :] = ref[...]
 
 
 def swap(x, axis, bit):
@@ -402,28 +426,30 @@
     near_12, codes_8, codes_12, hist_a = lax.optimization_barrier((near_12, codes_8, codes_12, hist_a))
     far_12 = swap(near_12, "feat", 1)
     hist_a, hist_b = add(((8, 0, (1, 2), (0, own)),), [codes_8, near_8, far_8], [hist_a, hist_b])
-    (to_core,) = add(((12, 0, (1, 2), (0,)),), [codes_12, near_12, far_12], [hist_a])
+    hist_a, hist_b = add(((12, 0, (1, None), (0, own)),), [codes_12, near_12], [hist_a, hist_b])
+    (to_core,) = add(((12, 0, (None, 1), (0,)),), [codes_12, far_12], [hist_a])
     from_core = swap(to_core, "rows", 1)
-    (to_plane,) = add(((12, 0, (1, 2), (own,)),), [codes_12, near_12, far_12], [hist_b], [from_core])
+    (to_plane,) = add(((12, 0, (None, 1), (own,)),), [codes_12, far_12], [hist_b], [from_core])
     from_plane = swap(to_plane, "rows", 2)
     _, late_4 = lax.optimization_barrier((to_plane, late_4))
     hists = add(((4, 0, (1, 2), (0, own)),), [late_4, rows_4, far_4], [hist_c, hist_d])
-    to_core, kept = add(
-        ((8, 0, (2, 3), (0, own)), (12, 1, (4, 5), (0, own))),
-        [late_8, late_12, near_8, far_8, near_12, far_12],
-        hists,
-    )
+    hists = add(((8, 0, (1, 2), (0, own)),), [late_8, near_8, far_8], hists)
+    to_core, kept = add(((12, 0, (1, 2), (0, own)),), [late_12, near_12, far_12], hists)
     middle = to_core.shape[0] // 2
     from_core = [swap(part, "rows", 1) for part in (to_core[:middle], to_core[middle:])]
     from_core = jnp.concatenate(from_core, axis=0)
 
     pairs = node_count * width
+    whole = pl.BlockSpec(memory_space=pltpu.VMEM)
     gains = pl.pallas_call(
         functools.partial(gain_kernel, classes, node_count),
-        in_specs=[pl.BlockSpec(memory_space=pltpu.VMEM)] * 3,
-        out_specs=pl.BlockSpec(memory_space=pltpu.VMEM),
-        out_shape=jax.ShapeDtypeStruct((node_count, own, 2 * BINS), jnp.float32),
-        scratch_shapes=[pltpu.VMEM((pairs, own * BINS), jnp.float32)],
+        in_specs=[whole] * 3,
+        out_specs=[whole] * node_count,
+        out_shape=[jax.ShapeDtypeStruct((own, 2 * BINS), jnp.float32)] * node_count,
+        scratch_shapes=[
+            pltpu.VMEM((node_count, own, 2 * BINS), jnp.float32),
+            pltpu.VMEM((pairs, own * BINS), jnp.float32),
+        ],
         compiler_params=pltpu.CompilerParams(vmem_limit_bytes=VMEM_BYTES),
         cost_estimate=SMALL_COST,
     )(from_core, from_plane, kept)
@@ -438,9 +464,17 @@
     sums = children[:node_count]
     new_logits, leaves = finish(logits_t, node_ids, side_count, sums, node_count)
 
-    halves = [[h + n * per_node for n in range(node_count)] for h in range(per_node)]
-    gain_rows = lax.all_to_all(gains, "rows", 0, 0, tiled=True, axis_index_groups=halves)
-    return (new_logits, gain_rows.reshape(1, pairs_dev, 2 * BINS), leaves)
+    gains = [gains[0]] + [swap(gains[i], "rows", 2 * i) for i in range(1, node_count)]
+    gains, new_logits = lax.optimization_barrier((gains, new_logits))
+    gain_rows = pl.pallas_call(
+        place_kernel,
+        in_specs=[whole] * node_count,
+        out_specs=whole,
+        out_shape=jax.ShapeDtypeStruct((1, pairs_dev, 2 * BINS), jnp.float32),
+        compiler_params=pltpu.CompilerParams(vmem_limit_bytes=VMEM_BYTES),
+        cost_estimate=SMALL_COST,
+    )(*gains)
+    return (new_logits, gain_rows, leaves)
 
 
 def by_groups(logits_t, labels, node_ids, bin_codes, splits, per_node, pairs_dev):

time: 96.3 us -> 98.9 us (1.027)
  starting transfers between devices: 24.8 us -> 30.5 us
  waiting for transfers between devices: 32.7 us -> 29.8 us
    ppermute x16 -> x23, starting transfers between devices: 19.3 us -> 30.5 us  [swap(): return lax.ppermute(x, axis, [(i, i ^ bit) for i in range(size)])]
    all_to_all x1 -> x0, starting transfers between devices: 5.49 us -> none  [local(): lax.all_to_all(gains, 'rows', 0, 0, tiled=True, axis_index_groups=halves)]
    all_to_all x1 -> x0, waiting for transfers between devices: 5.36 us -> none  [local(): lax.all_to_all(gains, 'rows', 0, 0, tiled=True, axis_index_groups=halves)]
    ppermute x16 -> x23, waiting for transfers between devices: 27.4 us -> 29.8 us  [swap(): return lax.ppermute(x, axis, [(i, i ^ bit) for i in range(size)])]
    unnamed x19 -> x18, local copies, waits for them, and re-layouts: 2.65 us -> 2.03 us
    pallas_call x7 -> x9, Pallas kernels: 27.5 us -> 28 us  [add_rows(): pl.pallas_call(functools.partial(add_kernel, classes, node_count, own, pl...]
  transfers between devices with their start and end apart: 17 -> 23, of which waited for: 11 -> 11; matrix products, arithmetic and copies ran while one was open for 2% -> 1% of each run, Pallas kernels for 27% -> 27%
where the time goes in v10:
time: 98.9 us; the launch traced here: 98.7 us
  Pallas kernels  34 us (34%)
  starting transfers between devices  30.5 us (31%)
  waiting for transfers between devices  29.8 us (30%)
  local copies, waits for them, and re-layouts  2.2 us (2%)
  matrix products  1.1 us (1%)
    ppermute x23, starting transfers between devices, swap(): return lax.ppermute(x, axis, [(i, i ^ bit) for i in range(size)])  30.5 us
    ppermute x23, waiting for transfers between devices, swap(): return lax.ppermute(x, axis, [(i, i ^ bit) for i in range(size)])  29.8 us
    pallas_call x9, Pallas kernels, add_rows(): pl.pallas_call(functools.partial(add_kernel, classes, node_count, own, pl...  28 us
    pallas_call x1, Pallas kernels, prepare(): pl.pallas_call(functools.partial(prep_kernel, own, blocks), in_specs=[pl....  3.91 us
    unnamed x18, local copies, waits for them, and re-layouts  2.03 us
  transfers between devices with their start and end apart: 23, of which 11 were waited for; matrix products, arithmetic and copies ran while one was open for 1% of the time, Pallas kernels for 27%

profile of v10, /device:TPU:0, one launch (start us, length us, event | category | flops | bytes accessed | tf_op | source)
XLA Modules:
  0.0 98.7 jit_solution(10289877738786761184)
XLA Ops:
  0.6 3.9 %shard_map.94 = (f32[32,3328]{1,0:T(8,128)}, f32[32,1664]{1,0:T(8,128)}, f32[1,3072]{1,0:T(1,128)}, s32[32,3072]{1,0:T(8,128)}, f32[64,1664]{1,0:T(8,128)}, /*in...) custom-call(s32[3072,128]{1,0:T(8,128)} %refs_0_.1, ...), custom_call_target="tpu_custom_call" | custom-call | flops 1000000 | bytes 1000000 | tf_op jit(solution)/shard_map/pallas_call | solution.py:345
  4.6 3.1 %collective-permute-start.2 = (f32[64,1664]{1,0:T(8,128)}, f32[64,1664]{1,0:T(8,128)S(1)}, u32[]{:S(2)}, u32[]{:S(2)}) collective-permute-start(f32[64,1664]{1,0:T(8,128)} %get-tuple-element.65), channel_id=1, source_target_pairs={{0,8},{2,10},{4,12},{6,14},{8,0},{10,2},{12,4},{14,6},{16,24},{18,... | collective-permute-start | bytes 1277960 | tf_op jit(solution)/shard_map/ppermute | solution.py:308
  7.6 2.6 %collective-permute-start.1 = (f32[32,1664]{1,0:T(8,128)}, f32[32,1664]{1,0:T(8,128)S(1)}, u32[]{:S(2)}, u32[]{:S(2)}) collective-permute-start(f32[32,1664]{1,0:T(8,128)} %get-tuple-element.64), channel_id=1, source_target_pairs={{0,16},{2,18},{4,20},{6,22},{8,24},{10,26},{12,28},{14,30},{16,0},... | collective-permute-start | bytes 638984 | tf_op jit(solution)/shard_map/ppermute | solution.py:308
  10.6 2.5 %collective-permute-start.5 = (s32[16,3584]{1,0:T(8,128)}, s32[16,3584]{1,0:T(8,128)S(1)}, u32[]{:S(2)}, u32[]{:S(2)}) collective-permute-start(s32[16,3584]{1,0:T(8,128)} %get-tuple-element.71), channel_id=1, source_target_pairs={{0,24},{2,26},{4,28},{6,30},{8,16},{10,18},{12,20},{14,22},{16,8},... | collective-permute-start | bytes 688136 | tf_op jit(solution)/shard_map/ppermute | solution.py:308
  15.0 6.7 %shard_map.95 = (f32[544,512]{1,0:T(8,128)S(1)}, f32[544,512]{1,0:T(8,128)S(1)}, f32[544,512]{1,0:T(8,128)S(1)}, f32[544,512]{1,0:T(8,128)S(1)}) custom-call(s32[32,3072]{1,0:T(8,128)S(1)} %copy-done.1, f32[32,3328]{1,0:T(8,128)S(1)} %copy-done), custom_call_target="tpu_custom_call" | custom-call | flops 1000000 | bytes 1000000 | tf_op jit(solution)/shard_map/pallas_call | solution.py:279
  22.8 3.4 %collective-permute-done.2.refs_0_.refs_1_ = f32[64,1664]{1,0:T(8,128)S(1)} collective-permute-done((f32[64,1664]{1,0:T(8,128)}, f32[64,1664]{1,0:T(8,128)S(1)}, u32[]{:S(2)}, u32[]{:S(2)}) %collective-permute-start.2) | collective-permute-done | bytes 426016 | tf_op jit(solution)/shard_map/ppermute | solution.py:308
  26.2 1.7 %collective-permute-start.6 = (f32[32,1664]{1,0:T(8,128)S(1)}, f32[32,1664]{1,0:T(8,128)S(1)}, u32[]{:S(2)}, u32[]{:S(2)}) collective-permute-start(f32[32,1664]{1,0:T(8,128)S(1)} %slice.36), channel_id=1, source_target_pairs={{0,1},{1,0},{2,3},{3,2},{4,5},{5,4},{6,7},{7,6},{8,9},{9,8},{10,11... | collective-permute-start | bytes 638984 | tf_op jit(solution)/shard_map/ppermute | solution.py:308
  28.4 6.1 %collective-permute-done.6.refs_1_.refs_2_ = f32[32,1664]{1,0:T(8,128)S(1)} collective-permute-done((f32[32,1664]{1,0:T(8,128)S(1)}, f32[32,1664]{1,0:T(8,128)S(1)}, u32[]{:S(2)}, u32[]{:S(2)}) %collective-permute-start.6) | collective-permute-done | bytes 213024 | tf_op jit(solution)/shard_map/ppermute | solution.py:308
  34.5 3.4 %shard_map.96 = (f32[544,512]{1,0:T(8,128)S(1)}, f32[544,512]{1,0:T(8,128)S(1)}) custom-call(f32[64,1664]{1,0:T(8,128)S(1)} %collective-permute-done.2.refs_0_.refs_1_, f32[32,1664]{1,0:T(8,128)S(1)} %collective-permute-done.6.refs_1_.refs_2_, f32[544,512]{1,0:T(8,128)S(1)} %get-tuple-element.73.refs_2_, f32[544,512]{1,0:T(8,128)S(1)} %get-tuple-element.74.refs_3_), custom_call_target="tpu_custom_call" | custom-call | flops 1000000 | bytes 1000000 | tf_op jit(solution)/shard_map/pallas_call | solution.py:279
  40.3 3.4 %shard_map.97 = (f32[544,512]{1,0:T(8,128)S(1)}, f32[544,512]{1,0:T(8,128)S(1)}) custom-call(s32[16,3584]{1,0:T(8,128)S(1)} %collective-permute-done.4.refs_0_, f32[32,1664]{1,0:T(8,128)S(1)} %collective-permute-done.1.refs_1_, f32[32,1664]{1,0:T(8,128)S(1)} %collective-permute-done.9.refs_2_, f32[544,512]{1,0:T(8,128)S(1)} %get-tuple-element.80.refs_3_, ...), custom_call_target="tpu_custom_call" | custom-call | flops 1000000 | bytes 1000000 | tf_op jit(solution)/shard_map/pallas_call | solution.py:279
  43.7 2.0 %shard_map.98 = (f32[544,512]{1,0:T(8,128)S(1)}, f32[544,512]{1,0:T(8,128)S(1)}) custom-call(s32[16,3584]{1,0:T(8,128)S(1)} %collective-permute-done.5.refs_0_, f32[32,1664]{1,0:T(8,128)S(1)} %collective-permute-done.3.refs_1_, f32[544,512]{1,0:T(8,128)S(1)} %get-tuple-element.82.refs_2_, f32[544,512]{1,0:T(8,128)S(1)} %get-tuple-element.83.refs_3_), custom_call_target="tpu_custom_call" | custom-call | flops 1000000 | bytes 1000000 | tf_op jit(solution)/shard_map/pallas_call | solution.py:279
  46.9 1.6 %collective-permute-start.11 = (s32[16,3072]{1,0:T(8,128)S(1)}, s32[16,3072]{1,0:T(8,128)S(1)}, u32[]{:S(2)}, u32[]{:S(2)}) collective-permute-start(s32[16,3072]{1,0:T(8,128)S(1)} %copy-done.8), channel_id=1, source_target_pairs={{0,8},{2,10},{4,12},{6,14},{8,0},{10,2},{12,4},{14,6},{16,24},{18,... | collective-permute-start | bytes 589832 | tf_op jit(solution)/shard_map/ppermute | solution.py:308
  48.6 2.2 %collective-permute-start.8 = (s32[16,3072]{1,0:T(8,128)S(1)}, s32[16,3072]{1,0:T(8,128)S(1)}, u32[]{:S(2)}, u32[]{:S(2)}) collective-permute-start(s32[16,3072]{1,0:T(8,128)S(1)} %copy-done.7), channel_id=1, source_target_pairs={{0,16},{2,18},{4,20},{6,22},{8,24},{10,26},{12,28},{14,30},{16,0},... | collective-permute-start | bytes 589832 | tf_op jit(solution)/shard_map/ppermute | solution.py:308
  53.9 4.1 %collective-permute-done.11.refs_0_ = s32[16,3072]{1,0:T(8,128)S(1)} collective-permute-done((s32[16,3072]{1,0:T(8,128)S(1)}, s32[16,3072]{1,0:T(8,128)S(1)}, u32[]{:S(2)}, u32[]{:S(2)}) %collective-permute-start.11) | collective-permute-done | bytes 196640 | tf_op jit(solution)/shard_map/ppermute | solution.py:308
  58.0 3.4 %shard_map.101 = (f32[544,512]{1,0:T(8,128)S(1)}, f32[544,512]{1,0:T(8,128)S(1)}) custom-call(s32[16,3072]{1,0:T(8,128)S(1)} %collective-permute-done.11.refs_0_, f32[64,1664]{1,0:T(8,128)S(1)} %collective-permute-done.2.refs_0_.refs_1_, f32[32,1664]{1,0:T(8,128)S(1)} %collective-permute-done.6.refs_1_.refs_2_, f32[544,512]{1,0:T(8,128)S(1)} %get-tuple-element.88.refs_3_, ...), custom_call_target="tpu_custom_call" | custom-call | flops 1000000 | bytes 1000000 | tf_op jit(solution)/shard_map/pallas_call | solution.py:279
  61.5 4.2 %collective-permute-done.8.refs_0_ = s32[16,3072]{1,0:T(8,128)S(1)} collective-permute-done((s32[16,3072]{1,0:T(8,128)S(1)}, s32[16,3072]{1,0:T(8,128)S(1)}, u32[]{:S(2)}, u32[]{:S(2)}) %collective-permute-start.8) | collective-permute-done | bytes 196640 | tf_op jit(solution)/shard_map/ppermute | solution.py:308
  65.7 3.4 %shard_map.102 = (f32[544,512]{1,0:T(8,128)S(1)}, f32[544,512]{1,0:T(8,128)S(1)}) custom-call(s32[16,3072]{1,0:T(8,128)S(1)} %collective-permute-done.8.refs_0_, f32[32,1664]{1,0:T(8,128)S(1)} %collective-permute-done.1.refs_1_, f32[32,1664]{1,0:T(8,128)S(1)} %collective-permute-done.9.refs_2_, f32[544,512]{1,0:T(8,128)S(1)} %get-tuple-element.90.refs_3_, ...), custom_call_target="tpu_custom_call" | custom-call | flops 1000000 | bytes 1000000 | tf_op jit(solution)/shard_map/pallas_call | solution.py:279
  69.1 3.4 %shard_map.103 = (f32[544,512]{1,0:T(8,128)S(1)}, f32[544,512]{1,0:T(8,128)S(1)}) custom-call(s32[16,3072]{1,0:T(8,128)S(1)} %collective-permute-done.refs_0_, f32[32,1664]{1,0:T(8,128)S(1)} %collective-permute-done.3.refs_1_, f32[32,1664]{1,0:T(8,128)S(1)} %collective-permute-done.7.refs_1_.refs_2_, f32[544,512]{1,0:T(8,128)S(1)} %get-tuple-element.92.refs_3_, ...), custom_call_target="tpu_custom_call" | custom-call | flops 1000000 | bytes 1000000 | tf_op jit(solution)/shard_map/pallas_call | solution.py:279
  75.6 3.0 %collective-permute-done.14.refs_1_ = f32[544,512]{1,0:T(8,128)S(1)} collective-permute-done((f32[544,512]{1,0:T(8,128)S(1)}, f32[544,512]{1,0:T(8,128)S(1)}, u32[]{:S(2)}, u32[]{:S(2)}) %collective-permute-start.14) | collective-permute-done | bytes 1114144 | tf_op jit(solution)/shard_map/ppermute | solution.py:308
  82.9 1.7 %collective-permute-start.17 = (f32[8,128]{1,0:T(8,128)S(1)}, f32[8,128]{1,0:T(8,128)S(1)}, u32[]{:S(2)}, u32[]{:S(2)}) collective-permute-start(f32[8,128]{1,0:T(8,128)S(1)} %get-tuple-element.107), channel_id=1, source_target_pairs={{0,12},{2,14},{4,8},{6,10},{8,4},{10,6},{12,0},{14,2},{16,28},{18,... | collective-permute-start | bytes 12296 | tf_op jit(solution)/shard_map/ppermute | solution.py:308
  84.6 1.6 %collective-permute-start.18 = (f32[8,128]{1,0:T(8,128)S(1)}, f32[8,128]{1,0:T(8,128)S(1)}, u32[]{:S(2)}, u32[]{:S(2)}) collective-permute-start(f32[8,128]{1,0:T(8,128)S(1)} %get-tuple-element.108), channel_id=1, source_target_pairs={{0,16},{2,18},{4,20},{6,22},{8,24},{10,26},{12,28},{14,30},{16,0},... | collective-permute-start | bytes 12296 | tf_op jit(solution)/shard_map/ppermute | solution.py:308
  86.2 2.3 %collective-permute-start.19 = (f32[8,128]{1,0:T(8,128)S(1)}, f32[8,128]{1,0:T(8,128)S(1)}, u32[]{:S(2)}, u32[]{:S(2)}) collective-permute-start(f32[8,128]{1,0:T(8,128)S(1)} %get-tuple-element.109), channel_id=1, source_target_pairs={{0,20},{2,22},{4,16},{6,18},{8,28},{10,30},{12,24},{14,26},{16,4},... | collective-permute-start | bytes 12296 | tf_op jit(solution)/shard_map/ppermute | solution.py:308
  88.7 3.1 %collective-permute-start.20 = (f32[8,128]{1,0:T(8,128)S(1)}, f32[8,128]{1,0:T(8,128)S(1)}, u32[]{:S(2)}, u32[]{:S(2)}) collective-permute-start(f32[8,128]{1,0:T(8,128)S(1)} %get-tuple-element.110), channel_id=1, source_target_pairs={{0,24},{2,26},{4,28},{6,30},{8,16},{10,18},{12,20},{14,22},{16,8},... | collective-permute-start | bytes 12296 | tf_op jit(solution)/shard_map/ppermute | solution.py:308
  94.1 3.9 %collective-permute-done.21.refs_7_ = f32[8,128]{1,0:T(8,128)S(1)} collective-permute-done((f32[8,128]{1,0:T(8,128)S(1)}, f32[8,128]{1,0:T(8,128)S(1)}, u32[]{:S(2)}, u32[]{:S(2)}) %collective-permute-start.21) | collective-permute-done | bytes 4128 | tf_op jit(solution)/shard_map/ppermute | solution.py:308
  (63 shorter events, 20.8 us)
Async XLA Ops:
  4.6 21.7 %collective-permute-start.2 = (f32[64,1664]{1,0:T(8,128)}, f32[64,1664]{1,0:T(8,128)S(1)}, u32[]{:S(2)}, u32[]{:S(2)}) collective-permute-start(f32[64,1664]{1,0:T(8,128)} %get-tuple-element.65), channel_id=1, source_target_pairs={{0,8},{2,10},{4,12},{6,14},{8,0},{10,2},{12,4},{14,6},{16,24},{18,... | collective-permute-start | bytes 1277960 | tf_op jit(solution)/shard_map/ppermute | solution.py:308
  7.6 15.1 %collective-permute-start.1 = (f32[32,1664]{1,0:T(8,128)}, f32[32,1664]{1,0:T(8,128)S(1)}, u32[]{:S(2)}, u32[]{:S(2)}) collective-permute-start(f32[32,1664]{1,0:T(8,128)} %get-tuple-element.64), channel_id=1, source_target_pairs={{0,16},{2,18},{4,20},{6,22},{8,24},{10,26},{12,28},{14,30},{16,0},... | collective-permute-start | bytes 638984 | tf_op jit(solution)/shard_map/ppermute | solution.py:308
  10.2 27.7 %collective-permute-start.4 = (s32[16,3584]{1,0:T(8,128)}, s32[16,3584]{1,0:T(8,128)S(1)}, u32[]{:S(2)}, u32[]{:S(2)}) collective-permute-start(s32[16,3584]{1,0:T(8,128)} %get-tuple-element.70), channel_id=1, source_target_pairs={{0,16},{2,18},{4,20},{6,22},{8,24},{10,26},{12,28},{14,30},{16,0},... | collective-permute-start | bytes 688136 | tf_op jit(solution)/shard_map/ppermute | solution.py:308
  10.6 27.4 %collective-permute-start.5 = (s32[16,3584]{1,0:T(8,128)}, s32[16,3584]{1,0:T(8,128)S(1)}, u32[]{:S(2)}, u32[]{:S(2)}) collective-permute-start(s32[16,3584]{1,0:T(8,128)} %get-tuple-element.71), channel_id=1, source_target_pairs={{0,24},{2,26},{4,28},{6,30},{8,16},{10,18},{12,20},{14,22},{16,8},... | collective-permute-start | bytes 688136 | tf_op jit(solution)/shard_map/ppermute | solution.py:308
  26.2 8.3 %collective-permute-start.6 = (f32[32,1664]{1,0:T(8,128)S(1)}, f32[32,1664]{1,0:T(8,128)S(1)}, u32[]{:S(2)}, u32[]{:S(2)}) collective-permute-start(f32[32,1664]{1,0:T(8,128)S(1)} %slice.36), channel_id=1, source_target_pairs={{0,1},{1,0},{2,3},{3,2},{4,5},{5,4},{6,7},{7,6},{8,9},{9,8},{10,11... | collective-permute-start | bytes 638984 | tf_op jit(solution)/shard_map/ppermute | solution.py:308
  27.9 11.2 %collective-permute-start.3 = (f32[32,1664]{1,0:T(8,128)S(1)}, f32[32,1664]{1,0:T(8,128)S(1)}, u32[]{:S(2)}, u32[]{:S(2)}) collective-permute-start(f32[32,1664]{1,0:T(8,128)S(1)} %collective-permute-done.1.refs_1_), channel_id=1, source_target_pairs={{0,8},{2,10},{4,12},{6,14},{8,0},{10,2},{12,4},{14,6},{16,24},{18,... | collective-permute-start | bytes 638984 | tf_op jit(solution)/shard_map/ppermute | solution.py:308
  27.9 12.3 %collective-permute-start.9 = (f32[32,1664]{1,0:T(8,128)S(1)}, f32[32,1664]{1,0:T(8,128)S(1)}, u32[]{:S(2)}, u32[]{:S(2)}) collective-permute-start(f32[32,1664]{1,0:T(8,128)S(1)} %collective-permute-done.1.refs_1_), channel_id=1, source_target_pairs={{0,1},{1,0},{2,3},{3,2},{4,5},{5,4},{6,7},{7,6},{8,9},{9,8},{10,11... | collective-permute-start | bytes 638984 | tf_op jit(solution)/shard_map/ppermute | solution.py:308
  39.2 6.6 %collective-permute-start.7 = (f32[32,1664]{1,0:T(8,128)S(1)}, f32[32,1664]{1,0:T(8,128)S(1)}, u32[]{:S(2)}, u32[]{:S(2)}) collective-permute-start(f32[32,1664]{1,0:T(8,128)S(1)} %collective-permute-done.3.refs_1_), channel_id=1, source_target_pairs={{0,1},{1,0},{2,3},{3,2},{4,5},{5,4},{6,7},{7,6},{8,9},{9,8},{10,11... | collective-permute-start | bytes 638984 | tf_op jit(solution)/shard_map/ppermute | solution.py:308
  46.8 4.6 %collective-permute-start.10 = (f32[544,512]{1,0:T(8,128)S(1)}, f32[544,512]{1,0:T(8,128)S(1)}, u32[]{:S(2)}, u32[]{:S(2)}) collective-permute-start(f32[544,512]{1,0:T(8,128)S(1)} %shard_map.99), channel_id=1, source_target_pairs={{0,2},{2,0},{4,6},{6,4},{8,10},{10,8},{12,14},{14,12},{16,18},{18,... | collective-permute-start | bytes 3342344 | tf_op jit(solution)/shard_map/ppermute | solution.py:308
  46.9 11.1 %collective-permute-start.11 = (s32[16,3072]{1,0:T(8,128)S(1)}, s32[16,3072]{1,0:T(8,128)S(1)}, u32[]{:S(2)}, u32[]{:S(2)}) collective-permute-start(s32[16,3072]{1,0:T(8,128)S(1)} %copy-done.8), channel_id=1, source_target_pairs={{0,8},{2,10},{4,12},{6,14},{8,0},{10,2},{12,4},{14,6},{16,24},{18,... | collective-permute-start | bytes 589832 | tf_op jit(solution)/shard_map/ppermute | solution.py:308
  48.6 17.1 %collective-permute-start.8 = (s32[16,3072]{1,0:T(8,128)S(1)}, s32[16,3072]{1,0:T(8,128)S(1)}, u32[]{:S(2)}, u32[]{:S(2)}) collective-permute-start(s32[16,3072]{1,0:T(8,128)S(1)} %copy-done.7), channel_id=1, source_target_pairs={{0,16},{2,18},{4,20},{6,22},{8,24},{10,26},{12,28},{14,30},{16,0},... | collective-permute-start | bytes 589832 | tf_op jit(solution)/shard_map/ppermute | solution.py:308
  50.8 18.3 %collective-permute-start = (s32[16,3072]{1,0:T(8,128)S(1)}, s32[16,3072]{1,0:T(8,128)S(1)}, u32[]{:S(2)}, u32[]{:S(2)}) collective-permute-start(s32[16,3072]{1,0:T(8,128)S(1)} %copy-done.6), channel_id=1, source_target_pairs={{0,24},{2,26},{4,28},{6,30},{8,16},{10,18},{12,20},{14,22},{16,8},... | collective-permute-start | bytes 589832 | tf_op jit(solution)/shard_map/ppermute | solution.py:308
  52.4 26.1 %collective-permute-start.14 = (f32[544,512]{1,0:T(8,128)S(1)}, f32[544,512]{1,0:T(8,128)S(1)}, u32[]{:S(2)}, u32[]{:S(2)}) collective-permute-start(f32[544,512]{1,0:T(8,128)S(1)} %shard_map.100), channel_id=1, source_target_pairs={{0,4},{2,6},{4,0},{6,2},{8,12},{10,14},{12,8},{14,10},{16,20},{18,... | collective-permute-start | bytes 3342344 | tf_op jit(solution)/shard_map/ppermute | solution.py:308
  72.7 2.0 %collective-permute-start.12 = (f32[272,512]{1,0:T(8,128)S(1)}, f32[272,512]{1,0:T(8,128)S(1)}, u32[]{:S(2)}, u32[]{:S(2)}) collective-permute-start(f32[272,512]{1,0:T(8,128)S(1)} %get-tuple-element.123), channel_id=1, source_target_pairs={{0,2},{2,0},{4,6},{6,4},{8,10},{10,8},{12,14},{14,12},{16,18},{18,... | collective-permute-start | bytes 1671176 | tf_op jit(solution)/shard_map/ppermute | solution.py:308
  72.8 2.7 %collective-permute-start.13 = (f32[272,512]{1,0:T(8,128)S(1)}, f32[272,512]{1,0:T(8,128)S(1)}, u32[]{:S(2)}, u32[]{:S(2)}) collective-permute-start(f32[272,512]{1,0:T(8,128)S(1)} %get-tuple-element.124), channel_id=1, source_target_pairs={{0,2},{2,0},{4,6},{6,4},{8,10},{10,8},{12,14},{14,12},{16,18},{18,... | collective-permute-start | bytes 1671176 | tf_op jit(solution)/shard_map/ppermute | solution.py:308
  78.6 13.9 %copy-start.2 = (f32[3072,32]{0,1:T(8,128)S(1)}, f32[3072,32]{0,1:T(8,128)}, u32[]{:S(2)}) copy-start(f32[3072,32]{0,1:T(8,128)} %param.7) | copy-start | bytes 1179652
  80.1 6.1 %collective-permute-start.22 = (f32[32,128]{1,0:T(8,128)S(1)}, f32[32,128]{1,0:T(8,128)S(1)}, u32[]{:S(2)}, u32[]{:S(2)}) collective-permute-start(f32[32,128]{1,0:T(8,128)S(1)} %pad_maximum_fusion.1), channel_id=1, source_target_pairs={{0,1},{1,0},{2,3},{3,2},{4,5},{5,4},{6,7},{7,6},{8,9},{9,8},{10,11... | collective-permute-start | bytes 49160 | tf_op jit(solution)/shard_map/ppermute | solution.py:308
  81.1 7.6 %collective-permute-start.15 = (f32[8,128]{1,0:T(8,128)S(1)}, f32[8,128]{1,0:T(8,128)S(1)}, u32[]{:S(2)}, u32[]{:S(2)}) collective-permute-start(f32[8,128]{1,0:T(8,128)S(1)} %get-tuple-element.105), channel_id=1, source_target_pairs={{0,4},{2,6},{4,0},{6,2},{8,12},{10,14},{12,8},{14,10},{16,20},{18,... | collective-permute-start | bytes 12296 | tf_op jit(solution)/shard_map/ppermute | solution.py:308
  82.6 9.1 %collective-permute-start.16 = (f32[8,128]{1,0:T(8,128)S(1)}, f32[8,128]{1,0:T(8,128)S(1)}, u32[]{:S(2)}, u32[]{:S(2)}) collective-permute-start(f32[8,128]{1,0:T(8,128)S(1)} %get-tuple-element.106), channel_id=1, source_target_pairs={{0,8},{2,10},{4,12},{6,14},{8,0},{10,2},{12,4},{14,6},{16,24},{18,... | collective-permute-start | bytes 12296 | tf_op jit(solution)/shard_map/ppermute | solution.py:308
  82.9 10.7 %collective-permute-start.17 = (f32[8,128]{1,0:T(8,128)S(1)}, f32[8,128]{1,0:T(8,128)S(1)}, u32[]{:S(2)}, u32[]{:S(2)}) collective-permute-start(f32[8,128]{1,0:T(8,128)S(1)} %get-tuple-element.107), channel_id=1, source_target_pairs={{0,12},{2,14},{4,8},{6,10},{8,4},{10,6},{12,0},{14,2},{16,28},{18,... | collective-permute-start | bytes 12296 | tf_op jit(solution)/shard_map/ppermute | solution.py:308
  84.6 9.0 %collective-permute-start.18 = (f32[8,128]{1,0:T(8,128)S(1)}, f32[8,128]{1,0:T(8,128)S(1)}, u32[]{:S(2)}, u32[]{:S(2)}) collective-permute-start(f32[8,128]{1,0:T(8,128)S(1)} %get-tuple-element.108), channel_id=1, source_target_pairs={{0,16},{2,18},{4,20},{6,22},{8,24},{10,26},{12,28},{14,30},{16,0},... | collective-permute-start | bytes 12296 | tf_op jit(solution)/shard_map/ppermute | solution.py:308
  86.2 7.4 %collective-permute-start.19 = (f32[8,128]{1,0:T(8,128)S(1)}, f32[8,128]{1,0:T(8,128)S(1)}, u32[]{:S(2)}, u32[]{:S(2)}) collective-permute-start(f32[8,128]{1,0:T(8,128)S(1)} %get-tuple-element.109), channel_id=1, source_target_pairs={{0,20},{2,22},{4,16},{6,18},{8,28},{10,30},{12,24},{14,26},{16,4},... | collective-permute-start | bytes 12296 | tf_op jit(solution)/shard_map/ppermute | solution.py:308
  88.7 5.5 %collective-permute-start.20 = (f32[8,128]{1,0:T(8,128)S(1)}, f32[8,128]{1,0:T(8,128)S(1)}, u32[]{:S(2)}, u32[]{:S(2)}) collective-permute-start(f32[8,128]{1,0:T(8,128)S(1)} %get-tuple-element.110), channel_id=1, source_target_pairs={{0,24},{2,26},{4,28},{6,30},{8,16},{10,18},{12,20},{14,22},{16,8},... | collective-permute-start | bytes 12296 | tf_op jit(solution)/shard_map/ppermute | solution.py:308
  91.7 6.3 %collective-permute-start.21 = (f32[8,128]{1,0:T(8,128)S(1)}, f32[8,128]{1,0:T(8,128)S(1)}, u32[]{:S(2)}, u32[]{:S(2)}) collective-permute-start(f32[8,128]{1,0:T(8,128)S(1)} %get-tuple-element.111), channel_id=1, source_target_pairs={{0,28},{2,30},{4,24},{6,26},{8,20},{10,22},{12,16},{14,18},{16,12}... | collective-permute-start | bytes 12296 | tf_op jit(solution)/shard_map/ppermute | solution.py:308
  (8 other events, 32.4 us)

commit v11 on v10

--- a/solution.py
+++ b/solution.py
@@ -288,19 +288,8 @@
 
 def gain_kernel(classes, node_count, *refs):
     gain_ref, hist_ref = refs[-2:]
-    out_refs = refs[-2 - node_count : -2]
-    hist_ref[...] = sum(ref[: hist_ref.shape[0], :] for ref in refs[: -2 - node_count])
+    hist_ref[...] = sum(ref[: hist_ref.shape[0], :] for ref in refs[:-2])
     write_gains(hist_ref, gain_ref, classes, node_count)
-    for i, out_ref in enumerate(out_refs):
-        out_ref[...] = gain_ref[(lax.axis_index("rows") >> 1) ^ i]
-
-
-def place_kernel(*refs):
-    out_ref = refs[-1]
-    own = refs[0].shape[0]
-    for i, ref in enumerate(refs[:-1]):
-        start = ((lax.axis_index("rows") >> 1) ^ i) * own
-        out_ref[0, pl.ds(pl.multiple_of(start, own), own), :] = ref[...]
 
 
 def swap(x, axis, bit):
@@ -396,8 +385,8 @@
     blocks = (
         (0, quarters(0, (0, 1, 2, 3)), 0),
         (1, quarters(4, (0, 1)), 0),
-        (0, quarters(8, (0, 1)), 4 * LANES),
-        (0, quarters(12, (0, 1)), 4 * LANES),
+        (0, quarters(8, (0, 1)), 3 * LANES),
+        (0, quarters(12, (0, 1)), 3 * LANES),
         (0, quarters(4, (2, 3)), 0),
         (0, quarters(8, (2, 3)), 0),
         (0, quarters(12, (2, 3)), 0),
@@ -440,16 +429,12 @@
     from_core = jnp.concatenate(from_core, axis=0)
 
     pairs = node_count * width
-    whole = pl.BlockSpec(memory_space=pltpu.VMEM)
     gains = pl.pallas_call(
         functools.partial(gain_kernel, classes, node_count),
-        in_specs=[whole] * 3,
-        out_specs=[whole] * node_count,
-        out_shape=[jax.ShapeDtypeStruct((own, 2 * BINS), jnp.float32)] * node_count,
-        scratch_shapes=[
-            pltpu.VMEM((node_count, own, 2 * BINS), jnp.float32),
-            pltpu.VMEM((pairs, own * BINS), jnp.float32),
-        ],
+        in_specs=[pl.BlockSpec(memory_space=pltpu.VMEM)] * 3,
+        out_specs=pl.BlockSpec(memory_space=pltpu.VMEM),
+        out_shape=jax.ShapeDtypeStruct((node_count, own, 2 * BINS), jnp.float32),
+        scratch_shapes=[pltpu.VMEM((pairs, own * BINS), jnp.float32)],
         compiler_params=pltpu.CompilerParams(vmem_limit_bytes=VMEM_BYTES),
         cost_estimate=SMALL_COST,
     )(from_core, from_plane, kept)
@@ -464,17 +449,9 @@
     sums = children[:node_count]
     new_logits, leaves = finish(logits_t, node_ids, side_count, sums, node_count)
 
-    gains = [gains[0]] + [swap(gains[i], "rows", 2 * i) for i in range(1, node_count)]
-    gains, new_logits = lax.optimization_barrier((gains, new_logits))
-    gain_rows = pl.pallas_call(
-        place_kernel,
-        in_specs=[whole] * node_count,
-        out_specs=whole,
-        out_shape=jax.ShapeDtypeStruct((1, pairs_dev, 2 * BINS), jnp.float32),
-        compiler_params=pltpu.CompilerParams(vmem_limit_bytes=VMEM_BYTES),
-        cost_estimate=SMALL_COST,
-    )(*gains)
-    return (new_logits, gain_rows, leaves)
+    halves = [[h + n * per_node for n in range(node_count)] for h in range(per_node)]
+    gain_rows = lax.all_to_all(gains, "rows", 0, 0, tiled=True, axis_index_groups=halves)
+    return (new_logits, gain_rows.reshape(1, pairs_dev, 2 * BINS), leaves)
 
 
 def by_groups(logits_t, labels, node_ids, bin_codes, splits, per_node, pairs_dev):

time: 98.9 us -> 94.2 us (0.952)
  starting transfers between devices: 30.5 us -> 24.7 us
    ppermute x23 -> x16, starting transfers between devices: 30.5 us -> 19.4 us  [swap(): return lax.ppermute(x, axis, [(i, i ^ bit) for i in range(size)])]
    all_to_all x0 -> x1, waiting for transfers between devices: none -> 5.36 us  [local(): lax.all_to_all(gains, 'rows', 0, 0, tiled=True, axis_index_groups=halves)]
    all_to_all x0 -> x1, starting transfers between devices: none -> 5.29 us  [local(): lax.all_to_all(gains, 'rows', 0, 0, tiled=True, axis_index_groups=halves)]
    ppermute x23 -> x16, waiting for transfers between devices: 29.8 us -> 24.9 us  [swap(): return lax.ppermute(x, axis, [(i, i ^ bit) for i in range(size)])]
    unnamed x18 -> x19, local copies, waits for them, and re-layouts: 2.03 us -> 2.65 us
  transfers between devices with their start and end apart: 23 -> 17, of which waited for: 11 -> 10; matrix products, arithmetic and copies ran while one was open for 1% -> 2% of each run, Pallas kernels for 27% -> 29%
where the time goes in v11:
time: 94.2 us; the launch traced here: 93.9 us
  Pallas kernels  34 us (36%)
  waiting for transfers between devices  30.2 us (32%)
  starting transfers between devices  24.7 us (26%)
  local copies, waits for them, and re-layouts  2.81 us (3%)
  matrix products  1.11 us (1%)
    pallas_call x9, Pallas kernels, add_rows(): pl.pallas_call(functools.partial(add_kernel, classes, node_count, own, pl...  28 us
    ppermute x16, waiting for transfers between devices, swap(): return lax.ppermute(x, axis, [(i, i ^ bit) for i in range(size)])  24.9 us
    ppermute x16, starting transfers between devices, swap(): return lax.ppermute(x, axis, [(i, i ^ bit) for i in range(size)])  19.4 us
    all_to_all x1, waiting for transfers between devices, local(): lax.all_to_all(gains, 'rows', 0, 0, tiled=True, axis_index_groups=halves)  5.36 us
    all_to_all x1, starting transfers between devices, local(): lax.all_to_all(gains, 'rows', 0, 0, tiled=True, axis_index_groups=halves)  5.29 us
    pallas_call x1, Pallas kernels, prepare(): pl.pallas_call(functools.partial(prep_kernel, own, blocks), in_specs=[pl....  3.89 us
    unnamed x19, local copies, waits for them, and re-layouts  2.65 us
    pallas_call x1, Pallas kernels, local(): pl.pallas_call(functools.partial(gain_kernel, classes, node_count), in_sp...  2.08 us
  transfers between devices with their start and end apart: 17, of which 10 were waited for; matrix products, arithmetic and copies ran while one was open for 2% of the time, Pallas kernels for 29%

profile of v11, /device:TPU:0, one launch (start us, length us, event | category | flops | bytes accessed | tf_op | source)
XLA Modules:
  0.0 93.9 jit_solution(3397068816401469103)
XLA Ops:
  0.6 3.9 %shard_map.94 = (f32[32,3328]{1,0:T(8,128)}, f32[32,1664]{1,0:T(8,128)}, f32[1,3072]{1,0:T(1,128)}, s32[32,3072]{1,0:T(8,128)}, f32[64,1664]{1,0:T(8,128)}, /*in...) custom-call(s32[3072,128]{1,0:T(8,128)} %refs_0_.1, ...), custom_call_target="tpu_custom_call" | custom-call | flops 1000000 | bytes 1000000 | tf_op jit(solution)/shard_map/pallas_call | solution.py:334
  4.5 3.1 %collective-permute-start.2 = (f32[64,1664]{1,0:T(8,128)}, f32[64,1664]{1,0:T(8,128)S(1)}, u32[]{:S(2)}, u32[]{:S(2)}) collective-permute-start(f32[64,1664]{1,0:T(8,128)} %get-tuple-element.41), channel_id=1, source_target_pairs={{0,8},{2,10},{4,12},{6,14},{8,0},{10,2},{12,4},{14,6},{16,24},{18,... | collective-permute-start | bytes 1277960 | tf_op jit(solution)/shard_map/ppermute | solution.py:297
  7.6 2.6 %collective-permute-start.1 = (f32[32,1664]{1,0:T(8,128)}, f32[32,1664]{1,0:T(8,128)S(1)}, u32[]{:S(2)}, u32[]{:S(2)}) collective-permute-start(f32[32,1664]{1,0:T(8,128)} %get-tuple-element.40), channel_id=1, source_target_pairs={{0,16},{2,18},{4,20},{6,22},{8,24},{10,26},{12,28},{14,30},{16,0},... | collective-permute-start | bytes 638984 | tf_op jit(solution)/shard_map/ppermute | solution.py:297
  10.5 2.5 %collective-permute-start.5 = (s32[16,3456]{1,0:T(8,128)}, s32[16,3456]{1,0:T(8,128)S(1)}, u32[]{:S(2)}, u32[]{:S(2)}) collective-permute-start(s32[16,3456]{1,0:T(8,128)} %get-tuple-element.47), channel_id=1, source_target_pairs={{0,24},{2,26},{4,28},{6,30},{8,16},{10,18},{12,20},{14,22},{16,8},... | collective-permute-start | bytes 663560 | tf_op jit(solution)/shard_map/ppermute | solution.py:297
  15.0 6.7 %shard_map.95 = (f32[544,512]{1,0:T(8,128)S(1)}, f32[544,512]{1,0:T(8,128)S(1)}, f32[544,512]{1,0:T(8,128)S(1)}, f32[544,512]{1,0:T(8,128)S(1)}) custom-call(s32[32,3072]{1,0:T(8,128)S(1)} %copy-done.1, f32[32,3328]{1,0:T(8,128)S(1)} %copy-done), custom_call_target="tpu_custom_call" | custom-call | flops 1000000 | bytes 1000000 | tf_op jit(solution)/shard_map/pallas_call | solution.py:279
  22.8 3.3 %collective-permute-done.2.refs_0_.refs_1_ = f32[64,1664]{1,0:T(8,128)S(1)} collective-permute-done((f32[64,1664]{1,0:T(8,128)}, f32[64,1664]{1,0:T(8,128)S(1)}, u32[]{:S(2)}, u32[]{:S(2)}) %collective-permute-start.2) | collective-permute-done | bytes 426016 | tf_op jit(solution)/shard_map/ppermute | solution.py:297
  26.1 1.7 %collective-permute-start.6 = (f32[32,1664]{1,0:T(8,128)S(1)}, f32[32,1664]{1,0:T(8,128)S(1)}, u32[]{:S(2)}, u32[]{:S(2)}) collective-permute-start(f32[32,1664]{1,0:T(8,128)S(1)} %slice.36), channel_id=1, source_target_pairs={{0,1},{1,0},{2,3},{3,2},{4,5},{5,4},{6,7},{7,6},{8,9},{9,8},{10,11... | collective-permute-start | bytes 638984 | tf_op jit(solution)/shard_map/ppermute | solution.py:297
  28.3 6.0 %collective-permute-done.6.refs_1_.refs_2_ = f32[32,1664]{1,0:T(8,128)S(1)} collective-permute-done((f32[32,1664]{1,0:T(8,128)S(1)}, f32[32,1664]{1,0:T(8,128)S(1)}, u32[]{:S(2)}, u32[]{:S(2)}) %collective-permute-start.6) | collective-permute-done | bytes 213024 | tf_op jit(solution)/shard_map/ppermute | solution.py:297
  34.4 3.4 %shard_map.96 = (f32[544,512]{1,0:T(8,128)S(1)}, f32[544,512]{1,0:T(8,128)S(1)}) custom-call(f32[64,1664]{1,0:T(8,128)S(1)} %collective-permute-done.2.refs_0_.refs_1_, f32[32,1664]{1,0:T(8,128)S(1)} %collective-permute-done.6.refs_1_.refs_2_, f32[544,512]{1,0:T(8,128)S(1)} %get-tuple-element.49.refs_2_, f32[544,512]{1,0:T(8,128)S(1)} %get-tuple-element.50.refs_3_), custom_call_target="tpu_custom_call" | custom-call | flops 1000000 | bytes 1000000 | tf_op jit(solution)/shard_map/pallas_call | solution.py:279
  39.9 3.4 %shard_map.97 = (f32[544,512]{1,0:T(8,128)S(1)}, f32[544,512]{1,0:T(8,128)S(1)}) custom-call(s32[16,3456]{1,0:T(8,128)S(1)} %collective-permute-done.4.refs_0_, f32[32,1664]{1,0:T(8,128)S(1)} %collective-permute-done.1.refs_1_, f32[32,1664]{1,0:T(8,128)S(1)} %collective-permute-done.9.refs_2_, f32[544,512]{1,0:T(8,128)S(1)} %get-tuple-element.56.refs_3_, ...), custom_call_target="tpu_custom_call" | custom-call | flops 1000000 | bytes 1000000 | tf_op jit(solution)/shard_map/pallas_call | solution.py:279
  43.3 2.0 %shard_map.98 = (f32[544,512]{1,0:T(8,128)S(1)}, f32[544,512]{1,0:T(8,128)S(1)}) custom-call(s32[16,3456]{1,0:T(8,128)S(1)} %collective-permute-done.5.refs_0_, f32[32,1664]{1,0:T(8,128)S(1)} %collective-permute-done.3.refs_1_, f32[544,512]{1,0:T(8,128)S(1)} %get-tuple-element.58.refs_2_, f32[544,512]{1,0:T(8,128)S(1)} %get-tuple-element.59.refs_3_), custom_call_target="tpu_custom_call" | custom-call | flops 1000000 | bytes 1000000 | tf_op jit(solution)/shard_map/pallas_call | solution.py:279
  46.5 1.3 %collective-permute-start.11 = (s32[16,3072]{1,0:T(8,128)S(1)}, s32[16,3072]{1,0:T(8,128)S(1)}, u32[]{:S(2)}, u32[]{:S(2)}) collective-permute-start(s32[16,3072]{1,0:T(8,128)S(1)} %copy-done.8), channel_id=1, source_target_pairs={{0,8},{2,10},{4,12},{6,14},{8,0},{10,2},{12,4},{14,6},{16,24},{18,... | collective-permute-start | bytes 589832 | tf_op jit(solution)/shard_map/ppermute | solution.py:297
  47.8 2.4 %collective-permute-start.8 = (s32[16,3072]{1,0:T(8,128)S(1)}, s32[16,3072]{1,0:T(8,128)S(1)}, u32[]{:S(2)}, u32[]{:S(2)}) collective-permute-start(s32[16,3072]{1,0:T(8,128)S(1)} %copy-done.7), channel_id=1, source_target_pairs={{0,16},{2,18},{4,20},{6,22},{8,24},{10,26},{12,28},{14,30},{16,0},... | collective-permute-start | bytes 589832 | tf_op jit(solution)/shard_map/ppermute | solution.py:297
  52.0 1.5 %collective-permute-start.14 = (f32[544,512]{1,0:T(8,128)S(1)}, f32[544,512]{1,0:T(8,128)S(1)}, u32[]{:S(2)}, u32[]{:S(2)}) collective-permute-start(f32[544,512]{1,0:T(8,128)S(1)} %shard_map.100), channel_id=1, source_target_pairs={{0,4},{2,6},{4,0},{6,2},{8,12},{10,14},{12,8},{14,10},{16,20},{18,... | collective-permute-start | bytes 3342344 | tf_op jit(solution)/shard_map/ppermute | solution.py:297
  53.5 4.1 %collective-permute-done.11.refs_0_ = s32[16,3072]{1,0:T(8,128)S(1)} collective-permute-done((s32[16,3072]{1,0:T(8,128)S(1)}, s32[16,3072]{1,0:T(8,128)S(1)}, u32[]{:S(2)}, u32[]{:S(2)}) %collective-permute-start.11) | collective-permute-done | bytes 196640 | tf_op jit(solution)/shard_map/ppermute | solution.py:297
  57.6 3.4 %shard_map.101 = (f32[544,512]{1,0:T(8,128)S(1)}, f32[544,512]{1,0:T(8,128)S(1)}) custom-call(s32[16,3072]{1,0:T(8,128)S(1)} %collective-permute-done.11.refs_0_, f32[64,1664]{1,0:T(8,128)S(1)} %collective-permute-done.2.refs_0_.refs_1_, f32[32,1664]{1,0:T(8,128)S(1)} %collective-permute-done.6.refs_1_.refs_2_, f32[544,512]{1,0:T(8,128)S(1)} %get-tuple-element.64.refs_3_, ...), custom_call_target="tpu_custom_call" | custom-call | flops 1000000 | bytes 1000000 | tf_op jit(solution)/shard_map/pallas_call | solution.py:279
  61.0 3.9 %collective-permute-done.8.refs_0_ = s32[16,3072]{1,0:T(8,128)S(1)} collective-permute-done((s32[16,3072]{1,0:T(8,128)S(1)}, s32[16,3072]{1,0:T(8,128)S(1)}, u32[]{:S(2)}, u32[]{:S(2)}) %collective-permute-start.8) | collective-permute-done | bytes 196640 | tf_op jit(solution)/shard_map/ppermute | solution.py:297
  65.0 3.4 %shard_map.102 = (f32[544,512]{1,0:T(8,128)S(1)}, f32[544,512]{1,0:T(8,128)S(1)}) custom-call(s32[16,3072]{1,0:T(8,128)S(1)} %collective-permute-done.8.refs_0_, f32[32,1664]{1,0:T(8,128)S(1)} %collective-permute-done.1.refs_1_, f32[32,1664]{1,0:T(8,128)S(1)} %collective-permute-done.9.refs_2_, f32[544,512]{1,0:T(8,128)S(1)} %get-tuple-element.66.refs_3_, ...), custom_call_target="tpu_custom_call" | custom-call | flops 1000000 | bytes 1000000 | tf_op jit(solution)/shard_map/pallas_call | solution.py:279
  68.4 3.4 %shard_map.103 = (f32[544,512]{1,0:T(8,128)S(1)}, f32[544,512]{1,0:T(8,128)S(1)}) custom-call(s32[16,3072]{1,0:T(8,128)S(1)} %collective-permute-done.refs_0_, f32[32,1664]{1,0:T(8,128)S(1)} %collective-permute-done.3.refs_1_, f32[32,1664]{1,0:T(8,128)S(1)} %collective-permute-done.7.refs_1_.refs_2_, f32[544,512]{1,0:T(8,128)S(1)} %get-tuple-element.68.refs_3_, ...), custom_call_target="tpu_custom_call" | custom-call | flops 1000000 | bytes 1000000 | tf_op jit(solution)/shard_map/pallas_call | solution.py:279
  72.5 1.4 %collective-permute-done.13 = f32[272,512]{1,0:T(8,128)S(1)} collective-permute-done((f32[272,512]{1,0:T(8,128)S(1)}, f32[272,512]{1,0:T(8,128)S(1)}, u32[]{:S(2)}, u32[]{:S(2)}) %collective-permute-start.13) | collective-permute-done | bytes 557088 | tf_op jit(solution)/shard_map/ppermute | solution.py:297
  74.9 3.3 %collective-permute-done.14.refs_1_ = f32[544,512]{1,0:T(8,128)S(1)} collective-permute-done((f32[544,512]{1,0:T(8,128)S(1)}, f32[544,512]{1,0:T(8,128)S(1)}, u32[]{:S(2)}, u32[]{:S(2)}) %collective-permute-start.14) | collective-permute-done | bytes 1114144 | tf_op jit(solution)/shard_map/ppermute | solution.py:297
  78.2 2.1 %shard_map.104 = f32[8,8,128]{2,1,0:T(8,128)} custom-call(f32[544,512]{1,0:T(8,128)S(1)} %pad_maximum_fusion.refs_0_, f32[544,512]{1,0:T(8,128)S(1)} %collective-permute-done.14.refs_1_, f32[544,512]{1,0:T(8,128)S(1)} %get-tuple-element.71.refs_2_), custom_call_target="tpu_custom_call" | custom-call | flops 1000000 | bytes 1000000 | tf_op jit(solution)/shard_map/pallas_call | solution.py:432
  81.3 5.3 %all-to-all-start = ((f32[8,8,128]{2,1,0:T(8,128)}), f32[8,8,128]{2,1,0:T(8,128)S(1)}, u32[]{:S(2)}, u32[]{:S(2)}) async-start(f32[8,8,128]{2,1,0:T(8,128)} %shard_map.104), calls=%async_computation | async-start | bytes 65536 | tf_op jit(solution)/shard_map/all_to_all | solution.py:453
  87.9 5.4 %all-to-all-done = f32[8,8,128]{2,1,0:T(8,128)S(1)} async-done(((f32[8,8,128]{2,1,0:T(8,128)}), f32[8,8,128]{2,1,0:T(8,128)S(1)}, u32[]{:S(2)}, u32[]{:S(2)}) %all-to-all-start) | async-done | bytes 32800 | tf_op jit(solution)/shard_map/all_to_all | solution.py:453
  (51 shorter events, 13.3 us)
Async XLA Ops:
  4.5 21.6 %collective-permute-start.2 = (f32[64,1664]{1,0:T(8,128)}, f32[64,1664]{1,0:T(8,128)S(1)}, u32[]{:S(2)}, u32[]{:S(2)}) collective-permute-start(f32[64,1664]{1,0:T(8,128)} %get-tuple-element.41), channel_id=1, source_target_pairs={{0,8},{2,10},{4,12},{6,14},{8,0},{10,2},{12,4},{14,6},{16,24},{18,... | collective-permute-start | bytes 1277960 | tf_op jit(solution)/shard_map/ppermute | solution.py:297
  7.6 15.1 %collective-permute-start.1 = (f32[32,1664]{1,0:T(8,128)}, f32[32,1664]{1,0:T(8,128)S(1)}, u32[]{:S(2)}, u32[]{:S(2)}) collective-permute-start(f32[32,1664]{1,0:T(8,128)} %get-tuple-element.40), channel_id=1, source_target_pairs={{0,16},{2,18},{4,20},{6,22},{8,24},{10,26},{12,28},{14,30},{16,0},... | collective-permute-start | bytes 638984 | tf_op jit(solution)/shard_map/ppermute | solution.py:297
  10.2 27.6 %collective-permute-start.4 = (s32[16,3456]{1,0:T(8,128)}, s32[16,3456]{1,0:T(8,128)S(1)}, u32[]{:S(2)}, u32[]{:S(2)}) collective-permute-start(s32[16,3456]{1,0:T(8,128)} %get-tuple-element.46), channel_id=1, source_target_pairs={{0,16},{2,18},{4,20},{6,22},{8,24},{10,26},{12,28},{14,30},{16,0},... | collective-permute-start | bytes 663560 | tf_op jit(solution)/shard_map/ppermute | solution.py:297
  10.5 27.3 %collective-permute-start.5 = (s32[16,3456]{1,0:T(8,128)}, s32[16,3456]{1,0:T(8,128)S(1)}, u32[]{:S(2)}, u32[]{:S(2)}) collective-permute-start(s32[16,3456]{1,0:T(8,128)} %get-tuple-element.47), channel_id=1, source_target_pairs={{0,24},{2,26},{4,28},{6,30},{8,16},{10,18},{12,20},{14,22},{16,8},... | collective-permute-start | bytes 663560 | tf_op jit(solution)/shard_map/ppermute | solution.py:297
  26.1 8.3 %collective-permute-start.6 = (f32[32,1664]{1,0:T(8,128)S(1)}, f32[32,1664]{1,0:T(8,128)S(1)}, u32[]{:S(2)}, u32[]{:S(2)}) collective-permute-start(f32[32,1664]{1,0:T(8,128)S(1)} %slice.36), channel_id=1, source_target_pairs={{0,1},{1,0},{2,3},{3,2},{4,5},{5,4},{6,7},{7,6},{8,9},{9,8},{10,11... | collective-permute-start | bytes 638984 | tf_op jit(solution)/shard_map/ppermute | solution.py:297
  27.8 10.9 %collective-permute-start.3 = (f32[32,1664]{1,0:T(8,128)S(1)}, f32[32,1664]{1,0:T(8,128)S(1)}, u32[]{:S(2)}, u32[]{:S(2)}) collective-permute-start(f32[32,1664]{1,0:T(8,128)S(1)} %collective-permute-done.1.refs_1_), channel_id=1, source_target_pairs={{0,8},{2,10},{4,12},{6,14},{8,0},{10,2},{12,4},{14,6},{16,24},{18,... | collective-permute-start | bytes 638984 | tf_op jit(solution)/shard_map/ppermute | solution.py:297
  27.8 12.0 %collective-permute-start.9 = (f32[32,1664]{1,0:T(8,128)S(1)}, f32[32,1664]{1,0:T(8,128)S(1)}, u32[]{:S(2)}, u32[]{:S(2)}) collective-permute-start(f32[32,1664]{1,0:T(8,128)S(1)} %collective-permute-done.1.refs_1_), channel_id=1, source_target_pairs={{0,1},{1,0},{2,3},{3,2},{4,5},{5,4},{6,7},{7,6},{8,9},{9,8},{10,11... | collective-permute-start | bytes 638984 | tf_op jit(solution)/shard_map/ppermute | solution.py:297
  38.8 6.6 %collective-permute-start.7 = (f32[32,1664]{1,0:T(8,128)S(1)}, f32[32,1664]{1,0:T(8,128)S(1)}, u32[]{:S(2)}, u32[]{:S(2)}) collective-permute-start(f32[32,1664]{1,0:T(8,128)S(1)} %collective-permute-done.3.refs_1_), channel_id=1, source_target_pairs={{0,1},{1,0},{2,3},{3,2},{4,5},{5,4},{6,7},{7,6},{8,9},{9,8},{10,11... | collective-permute-start | bytes 638984 | tf_op jit(solution)/shard_map/ppermute | solution.py:297
  45.4 1.1 %copy-start.8 = (s32[16,3072]{1,0:T(8,128)S(1)}, s32[16,3072]{1,0:T(8,128)}, u32[]{:S(2)}) copy-start(s32[16,3072]{1,0:T(8,128)} %get-tuple-element.62) | copy-start | bytes 589828
  45.4 2.5 %copy-start.7 = (s32[16,3072]{1,0:T(8,128)S(1)}, s32[16,3072]{1,0:T(8,128)}, u32[]{:S(2)}) copy-start(s32[16,3072]{1,0:T(8,128)} %get-tuple-element.53) | copy-start | bytes 589828
  45.4 4.9 %copy-start.6 = (s32[16,3072]{1,0:T(8,128)S(1)}, s32[16,3072]{1,0:T(8,128)}, u32[]{:S(2)}) copy-start(s32[16,3072]{1,0:T(8,128)} %get-tuple-element.39) | copy-start | bytes 589828
  46.4 4.6 %collective-permute-start.10 = (f32[544,512]{1,0:T(8,128)S(1)}, f32[544,512]{1,0:T(8,128)S(1)}, u32[]{:S(2)}, u32[]{:S(2)}) collective-permute-start(f32[544,512]{1,0:T(8,128)S(1)} %shard_map.99), channel_id=1, source_target_pairs={{0,2},{2,0},{4,6},{6,4},{8,10},{10,8},{12,14},{14,12},{16,18},{18,... | collective-permute-start | bytes 3342344 | tf_op jit(solution)/shard_map/ppermute | solution.py:297
  46.5 11.1 %collective-permute-start.11 = (s32[16,3072]{1,0:T(8,128)S(1)}, s32[16,3072]{1,0:T(8,128)S(1)}, u32[]{:S(2)}, u32[]{:S(2)}) collective-permute-start(s32[16,3072]{1,0:T(8,128)S(1)} %copy-done.8), channel_id=1, source_target_pairs={{0,8},{2,10},{4,12},{6,14},{8,0},{10,2},{12,4},{14,6},{16,24},{18,... | collective-permute-start | bytes 589832 | tf_op jit(solution)/shard_map/ppermute | solution.py:297
  47.8 17.1 %collective-permute-start.8 = (s32[16,3072]{1,0:T(8,128)S(1)}, s32[16,3072]{1,0:T(8,128)S(1)}, u32[]{:S(2)}, u32[]{:S(2)}) collective-permute-start(s32[16,3072]{1,0:T(8,128)S(1)} %copy-done.7), channel_id=1, source_target_pairs={{0,16},{2,18},{4,20},{6,22},{8,24},{10,26},{12,28},{14,30},{16,0},... | collective-permute-start | bytes 589832 | tf_op jit(solution)/shard_map/ppermute | solution.py:297
  50.2 18.2 %collective-permute-start = (s32[16,3072]{1,0:T(8,128)S(1)}, s32[16,3072]{1,0:T(8,128)S(1)}, u32[]{:S(2)}, u32[]{:S(2)}) collective-permute-start(s32[16,3072]{1,0:T(8,128)S(1)} %copy-done.6), channel_id=1, source_target_pairs={{0,24},{2,26},{4,28},{6,30},{8,16},{10,18},{12,20},{14,22},{16,8},... | collective-permute-start | bytes 589832 | tf_op jit(solution)/shard_map/ppermute | solution.py:297
  52.0 26.1 %collective-permute-start.14 = (f32[544,512]{1,0:T(8,128)S(1)}, f32[544,512]{1,0:T(8,128)S(1)}, u32[]{:S(2)}, u32[]{:S(2)}) collective-permute-start(f32[544,512]{1,0:T(8,128)S(1)} %shard_map.100), channel_id=1, source_target_pairs={{0,4},{2,6},{4,0},{6,2},{8,12},{10,14},{12,8},{14,10},{16,20},{18,... | collective-permute-start | bytes 3342344 | tf_op jit(solution)/shard_map/ppermute | solution.py:297
  72.0 2.0 %collective-permute-start.13 = (f32[272,512]{1,0:T(8,128)S(1)}, f32[272,512]{1,0:T(8,128)S(1)}, u32[]{:S(2)}, u32[]{:S(2)}) collective-permute-start(f32[272,512]{1,0:T(8,128)S(1)} %get-tuple-element.75), channel_id=1, source_target_pairs={{0,2},{2,0},{4,6},{6,4},{8,10},{10,8},{12,14},{14,12},{16,18},{18,... | collective-permute-start | bytes 1671176 | tf_op jit(solution)/shard_map/ppermute | solution.py:297
  72.0 2.7 %collective-permute-start.12 = (f32[272,512]{1,0:T(8,128)S(1)}, f32[272,512]{1,0:T(8,128)S(1)}, u32[]{:S(2)}, u32[]{:S(2)}) collective-permute-start(f32[272,512]{1,0:T(8,128)S(1)} %get-tuple-element.76), channel_id=1, source_target_pairs={{0,2},{2,0},{4,6},{6,4},{8,10},{10,8},{12,14},{14,12},{16,18},{18,... | collective-permute-start | bytes 1671176 | tf_op jit(solution)/shard_map/ppermute | solution.py:297
  78.2 2.1 %copy-start.4 = (f32[1,3072]{1,0:T(1,128)S(1)}, f32[1,3072]{1,0:T(1,128)}, u32[]{:S(2)}) copy-start(f32[1,3072]{1,0:T(1,128)} %get-tuple-element.73) | copy-start | bytes 36868
  78.2 8.5 %copy-start.3 = (s32[3072]{0:T(1024)S(1)}, s32[3072]{0:T(1024)}, u32[]{:S(2)}) copy-start(s32[3072]{0:T(1024)} %param.9) | copy-start | bytes 36868
  78.2 8.6 %copy-start.2 = (f32[3072,32]{0,1:T(8,128)S(1)}, f32[3072,32]{0,1:T(8,128)}, u32[]{:S(2)}) copy-start(f32[3072,32]{0,1:T(8,128)} %param.7) | copy-start | bytes 1179652
  80.3 6.3 %collective-permute-start.15 = (f32[32,128]{1,0:T(8,128)S(1)}, f32[32,128]{1,0:T(8,128)S(1)}, u32[]{:S(2)}, u32[]{:S(2)}) collective-permute-start(f32[32,128]{1,0:T(8,128)S(1)} %pad_maximum_fusion.1), channel_id=1, source_target_pairs={{0,1},{1,0},{2,3},{3,2},{4,5},{5,4},{6,7},{7,6},{8,9},{9,8},{10,11... | collective-permute-start | bytes 49160 | tf_op jit(solution)/shard_map/ppermute | solution.py:297
  81.3 12.0 %all-to-all-start = ((f32[8,8,128]{2,1,0:T(8,128)}), f32[8,8,128]{2,1,0:T(8,128)S(1)}, u32[]{:S(2)}, u32[]{:S(2)}) async-start(f32[8,8,128]{2,1,0:T(8,128)} %shard_map.104), calls=%async_computation | async-start | bytes 65536 | tf_op jit(solution)/shard_map/all_to_all | solution.py:453
  86.8 7.1 %copy-start.5 = (f32[8,2,32]{2,1,0:T(2,128)}, f32[8,2,32]{2,1,0:T(2,128)S(1)}, u32[]{:S(2)}) copy-start(f32[8,2,32]{2,1,0:T(2,128)S(1)} %fusion.5) | copy-start | bytes 6148
  (2 other events, 2.0 us)

commit v12 on v11

--- a/solution.py
+++ b/solution.py
@@ -80,13 +80,18 @@
     ]
     for copy in copies:
         copy.start()
-    for copy in copies:
-        copy.wait()
     codes_ref, logits_ref, labels_ref, nodes_ref, feature_ref, bin_ref, missing_ref = buffers
     row_index, feat_index = lax.axis_index("rows"), lax.axis_index("feat")
     classes, rows = logits_ref.shape
     half, width = rows // 2, half_width(rows)
     chunks = half // LANES
+    for copy in copies[1:]:
+        copy.wait()
+    expo_vals = jnp.exp(logits_ref[...])
+    prob = expo_vals / jnp.sum(expo_vals, axis=0, keepdims=True)
+    for h in range(2):
+        info_ref[:, h * width : h * width + half] = prob[:, h * half : (h + 1) * half]
+    copies[0].wait()
     turned[...] = codes_ref[...].T
     for (infos, pieces, _), out_ref in zip(blocks, outs):
         if infos == 0 and out_ref.shape[1] > rows:
@@ -102,8 +107,6 @@
                 part = turned[pl.ds(start, own), h * cut : (h + 1) * cut]
                 out_ref[low : low + own, :cut] = part.astype(out_ref.dtype)
                 out_ref[low : low + own, cut:] = jnp.zeros((own, infos * width - cut), out_ref.dtype)
-    expo_vals = jnp.exp(logits_ref[...])
-    prob = expo_vals / jnp.sum(expo_vals, axis=0, keepdims=True)
     labels = labels_ref[...].astype(jnp.float32)
     nodes = nodes_ref[...].astype(jnp.float32)
     label = jnp.concatenate([labels[i : i + 1] for i in range(2 * chunks)], axis=1)
@@ -140,7 +143,6 @@
     pad = pad if pad[0].shape[0] > 0 else []
     for h in range(2):
         some = slice(h * chunks, (h + 1) * chunks)
-        info_ref[:, h * width : h * width + half] = prob[:, h * half : (h + 1) * half]
         info_ref[:, h * width + half : (h + 1) * width] = jnp.concatenate(
             [labels[some], nodes[some]] + pad + [sums], axis=0
         )
@@ -265,15 +267,15 @@
             out_ref[:pairs, :] += product
             if not carry or sums is None:
                 continue
-            low_row = pairs + (row_index & 3) * node_count
+            low_row = pairs + (line >> 1) * node_count
             band = pl.ds(pl.multiple_of(low_row, node_count), node_count)
             for i in range(out_ref.shape[1] // LANES):
-                here = jnp.where(line == i, 1.0, 0.0)
+                here = jnp.where((row_index & 3) == i, 1.0, 0.0)
                 out_ref[band, i * LANES : (i + 1) * LANES] += here * sums
 
 
 def add_rows(classes, node_count, own, carry, plan, arrays, *held):
-    shape = (2 * classes * node_count + 4 * node_count, own * BINS)
+    shape = (2 * classes * node_count + 2 * node_count, own * BINS)
     whole = pl.BlockSpec(memory_space=pltpu.VMEM)
     outs = len(plan[0][3])
     return pl.pallas_call(
@@ -439,7 +441,7 @@
         cost_estimate=SMALL_COST,
     )(from_core, from_plane, kept)
     def gather(parts):
-        return jnp.sum(parts.reshape(4, node_count, -1, LANES), axis=(0, 2))
+        return jnp.sum(parts.reshape(2, node_count, -1, LANES), axis=(0, 2))
 
     gains, from_plane = lax.optimization_barrier((gains, from_plane))
     sums = gather(from_core[pairs:] + from_plane[pairs:] + kept[pairs:])

time: 94.2 us -> 93.5 us (level)
  no operation moved by 1% of the time
where the time goes in v12:
time: 93.5 us; the launch traced here: 93.2 us
  Pallas kernels  34.1 us (36%)
  waiting for transfers between devices  29.5 us (32%)
  starting transfers between devices  24.7 us (26%)
  local copies, waits for them, and re-layouts  2.81 us (3%)
  matrix products  1.11 us (1%)
    pallas_call x9, Pallas kernels, add_rows(): pl.pallas_call(functools.partial(add_kernel, classes, node_count, own, pl...  28 us
    ppermute x16, waiting for transfers between devices, swap(): return lax.ppermute(x, axis, [(i, i ^ bit) for i in range(size)])  24.1 us
    ppermute x16, starting transfers between devices, swap(): return lax.ppermute(x, axis, [(i, i ^ bit) for i in range(size)])  19.4 us
    all_to_all x1, waiting for transfers between devices, local(): lax.all_to_all(gains, 'rows', 0, 0, tiled=True, axis_index_groups=halves)  5.35 us
    all_to_all x1, starting transfers between devices, local(): lax.all_to_all(gains, 'rows', 0, 0, tiled=True, axis_index_groups=halves)  5.29 us
    pallas_call x1, Pallas kernels, prepare(): pl.pallas_call(functools.partial(prep_kernel, own, blocks), in_specs=[pl....  3.97 us
    unnamed x19, local copies, waits for them, and re-layouts  2.65 us
    pallas_call x1, Pallas kernels, local(): pl.pallas_call(functools.partial(gain_kernel, classes, node_count), in_sp...  2.08 us
  transfers between devices with their start and end apart: 17, of which 10 were waited for; matrix products, arithmetic and copies ran while one was open for 2% of the time, Pallas kernels for 29%

profile of v12, /device:TPU:0, one launch (start us, length us, event | category | flops | bytes accessed | tf_op | source)
XLA Modules:
  0.0 93.2 jit_solution(14911600266847705862)
XLA Ops:
  0.6 4.0 %shard_map.94 = (f32[32,3328]{1,0:T(8,128)}, f32[32,1664]{1,0:T(8,128)}, f32[1,3072]{1,0:T(1,128)}, s32[32,3072]{1,0:T(8,128)}, f32[64,1664]{1,0:T(8,128)}, /*in...) custom-call(s32[3072,128]{1,0:T(8,128)} %refs_0_.1, ...), custom_call_target="tpu_custom_call" | custom-call | flops 1000000 | bytes 1000000 | tf_op jit(solution)/shard_map/pallas_call | solution.py:336
  4.6 3.1 %collective-permute-start.2 = (f32[64,1664]{1,0:T(8,128)}, f32[64,1664]{1,0:T(8,128)S(1)}, u32[]{:S(2)}, u32[]{:S(2)}) collective-permute-start(f32[64,1664]{1,0:T(8,128)} %get-tuple-element.41), channel_id=1, source_target_pairs={{0,8},{2,10},{4,12},{6,14},{8,0},{10,2},{12,4},{14,6},{16,24},{18,... | collective-permute-start | bytes 1277960 | tf_op jit(solution)/shard_map/ppermute | solution.py:299
  7.7 2.6 %collective-permute-start.1 = (f32[32,1664]{1,0:T(8,128)}, f32[32,1664]{1,0:T(8,128)S(1)}, u32[]{:S(2)}, u32[]{:S(2)}) collective-permute-start(f32[32,1664]{1,0:T(8,128)} %get-tuple-element.40), channel_id=1, source_target_pairs={{0,16},{2,18},{4,20},{6,22},{8,24},{10,26},{12,28},{14,30},{16,0},... | collective-permute-start | bytes 638984 | tf_op jit(solution)/shard_map/ppermute | solution.py:299
  10.6 2.5 %collective-permute-start.5 = (s32[16,3456]{1,0:T(8,128)}, s32[16,3456]{1,0:T(8,128)S(1)}, u32[]{:S(2)}, u32[]{:S(2)}) collective-permute-start(s32[16,3456]{1,0:T(8,128)} %get-tuple-element.47), channel_id=1, source_target_pairs={{0,24},{2,26},{4,28},{6,30},{8,16},{10,18},{12,20},{14,22},{16,8},... | collective-permute-start | bytes 663560 | tf_op jit(solution)/shard_map/ppermute | solution.py:299
  15.1 6.7 %shard_map.95 = (f32[528,512]{1,0:T(8,128)S(1)}, f32[528,512]{1,0:T(8,128)S(1)}, f32[528,512]{1,0:T(8,128)S(1)}, f32[528,512]{1,0:T(8,128)S(1)}) custom-call(s32[32,3072]{1,0:T(8,128)S(1)} %copy-done.1, f32[32,3328]{1,0:T(8,128)S(1)} %copy-done), custom_call_target="tpu_custom_call" | custom-call | flops 1000000 | bytes 1000000 | tf_op jit(solution)/shard_map/pallas_call | solution.py:281
  22.8 3.3 %collective-permute-done.2.refs_0_.refs_1_ = f32[64,1664]{1,0:T(8,128)S(1)} collective-permute-done((f32[64,1664]{1,0:T(8,128)}, f32[64,1664]{1,0:T(8,128)S(1)}, u32[]{:S(2)}, u32[]{:S(2)}) %collective-permute-start.2) | collective-permute-done | bytes 426016 | tf_op jit(solution)/shard_map/ppermute | solution.py:299
  26.2 1.7 %collective-permute-start.6 = (f32[32,1664]{1,0:T(8,128)S(1)}, f32[32,1664]{1,0:T(8,128)S(1)}, u32[]{:S(2)}, u32[]{:S(2)}) collective-permute-start(f32[32,1664]{1,0:T(8,128)S(1)} %slice.36), channel_id=1, source_target_pairs={{0,1},{1,0},{2,3},{3,2},{4,5},{5,4},{6,7},{7,6},{8,9},{9,8},{10,11... | collective-permute-start | bytes 638984 | tf_op jit(solution)/shard_map/ppermute | solution.py:299
  28.4 6.0 %collective-permute-done.6.refs_1_.refs_2_ = f32[32,1664]{1,0:T(8,128)S(1)} collective-permute-done((f32[32,1664]{1,0:T(8,128)S(1)}, f32[32,1664]{1,0:T(8,128)S(1)}, u32[]{:S(2)}, u32[]{:S(2)}) %collective-permute-start.6) | collective-permute-done | bytes 213024 | tf_op jit(solution)/shard_map/ppermute | solution.py:299
  34.4 3.5 %shard_map.96 = (f32[528,512]{1,0:T(8,128)S(1)}, f32[528,512]{1,0:T(8,128)S(1)}) custom-call(f32[64,1664]{1,0:T(8,128)S(1)} %collective-permute-done.2.refs_0_.refs_1_, f32[32,1664]{1,0:T(8,128)S(1)} %collective-permute-done.6.refs_1_.refs_2_, f32[528,512]{1,0:T(8,128)S(1)} %get-tuple-element.49.refs_2_, f32[528,512]{1,0:T(8,128)S(1)} %get-tuple-element.50.refs_3_), custom_call_target="tpu_custom_call" | custom-call | flops 1000000 | bytes 1000000 | tf_op jit(solution)/shard_map/pallas_call | solution.py:281
  39.9 3.4 %shard_map.97 = (f32[528,512]{1,0:T(8,128)S(1)}, f32[528,512]{1,0:T(8,128)S(1)}) custom-call(s32[16,3456]{1,0:T(8,128)S(1)} %collective-permute-done.4.refs_0_, f32[32,1664]{1,0:T(8,128)S(1)} %collective-permute-done.1.refs_1_, f32[32,1664]{1,0:T(8,128)S(1)} %collective-permute-done.9.refs_2_, f32[528,512]{1,0:T(8,128)S(1)} %get-tuple-element.56.refs_3_, ...), custom_call_target="tpu_custom_call" | custom-call | flops 1000000 | bytes 1000000 | tf_op jit(solution)/shard_map/pallas_call | solution.py:281
  43.4 2.0 %shard_map.98 = (f32[528,512]{1,0:T(8,128)S(1)}, f32[528,512]{1,0:T(8,128)S(1)}) custom-call(s32[16,3456]{1,0:T(8,128)S(1)} %collective-permute-done.5.refs_0_, f32[32,1664]{1,0:T(8,128)S(1)} %collective-permute-done.3.refs_1_, f32[528,512]{1,0:T(8,128)S(1)} %get-tuple-element.58.refs_2_, f32[528,512]{1,0:T(8,128)S(1)} %get-tuple-element.59.refs_3_), custom_call_target="tpu_custom_call" | custom-call | flops 1000000 | bytes 1000000 | tf_op jit(solution)/shard_map/pallas_call | solution.py:281
  46.6 1.3 %collective-permute-start.11 = (s32[16,3072]{1,0:T(8,128)S(1)}, s32[16,3072]{1,0:T(8,128)S(1)}, u32[]{:S(2)}, u32[]{:S(2)}) collective-permute-start(s32[16,3072]{1,0:T(8,128)S(1)} %copy-done.8), channel_id=1, source_target_pairs={{0,8},{2,10},{4,12},{6,14},{8,0},{10,2},{12,4},{14,6},{16,24},{18,... | collective-permute-start | bytes 589832 | tf_op jit(solution)/shard_map/ppermute | solution.py:299
  47.9 2.4 %collective-permute-start.8 = (s32[16,3072]{1,0:T(8,128)S(1)}, s32[16,3072]{1,0:T(8,128)S(1)}, u32[]{:S(2)}, u32[]{:S(2)}) collective-permute-start(s32[16,3072]{1,0:T(8,128)S(1)} %copy-done.7), channel_id=1, source_target_pairs={{0,16},{2,18},{4,20},{6,22},{8,24},{10,26},{12,28},{14,30},{16,0},... | collective-permute-start | bytes 589832 | tf_op jit(solution)/shard_map/ppermute | solution.py:299
  52.1 1.5 %collective-permute-start.14 = (f32[528,512]{1,0:T(8,128)S(1)}, f32[528,512]{1,0:T(8,128)S(1)}, u32[]{:S(2)}, u32[]{:S(2)}) collective-permute-start(f32[528,512]{1,0:T(8,128)S(1)} %shard_map.100), channel_id=1, source_target_pairs={{0,4},{2,6},{4,0},{6,2},{8,12},{10,14},{12,8},{14,10},{16,20},{18,... | collective-permute-start | bytes 3244040 | tf_op jit(solution)/shard_map/ppermute | solution.py:299
  53.6 4.1 %collective-permute-done.11.refs_0_ = s32[16,3072]{1,0:T(8,128)S(1)} collective-permute-done((s32[16,3072]{1,0:T(8,128)S(1)}, s32[16,3072]{1,0:T(8,128)S(1)}, u32[]{:S(2)}, u32[]{:S(2)}) %collective-permute-start.11) | collective-permute-done | bytes 196640 | tf_op jit(solution)/shard_map/ppermute | solution.py:299
  57.7 3.5 %shard_map.101 = (f32[528,512]{1,0:T(8,128)S(1)}, f32[528,512]{1,0:T(8,128)S(1)}) custom-call(s32[16,3072]{1,0:T(8,128)S(1)} %collective-permute-done.11.refs_0_, f32[64,1664]{1,0:T(8,128)S(1)} %collective-permute-done.2.refs_0_.refs_1_, f32[32,1664]{1,0:T(8,128)S(1)} %collective-permute-done.6.refs_1_.refs_2_, f32[528,512]{1,0:T(8,128)S(1)} %get-tuple-element.64.refs_3_, ...), custom_call_target="tpu_custom_call" | custom-call | flops 1000000 | bytes 1000000 | tf_op jit(solution)/shard_map/pallas_call | solution.py:281
  61.1 3.9 %collective-permute-done.8.refs_0_ = s32[16,3072]{1,0:T(8,128)S(1)} collective-permute-done((s32[16,3072]{1,0:T(8,128)S(1)}, s32[16,3072]{1,0:T(8,128)S(1)}, u32[]{:S(2)}, u32[]{:S(2)}) %collective-permute-start.8) | collective-permute-done | bytes 196640 | tf_op jit(solution)/shard_map/ppermute | solution.py:299
  65.0 3.4 %shard_map.102 = (f32[528,512]{1,0:T(8,128)S(1)}, f32[528,512]{1,0:T(8,128)S(1)}) custom-call(s32[16,3072]{1,0:T(8,128)S(1)} %collective-permute-done.8.refs_0_, f32[32,1664]{1,0:T(8,128)S(1)} %collective-permute-done.1.refs_1_, f32[32,1664]{1,0:T(8,128)S(1)} %collective-permute-done.9.refs_2_, f32[528,512]{1,0:T(8,128)S(1)} %get-tuple-element.66.refs_3_, ...), custom_call_target="tpu_custom_call" | custom-call | flops 1000000 | bytes 1000000 | tf_op jit(solution)/shard_map/pallas_call | solution.py:281
  68.5 3.5 %shard_map.103 = (f32[528,512]{1,0:T(8,128)S(1)}, f32[528,512]{1,0:T(8,128)S(1)}) custom-call(s32[16,3072]{1,0:T(8,128)S(1)} %collective-permute-done.refs_0_, f32[32,1664]{1,0:T(8,128)S(1)} %collective-permute-done.3.refs_1_, f32[32,1664]{1,0:T(8,128)S(1)} %collective-permute-done.7.refs_1_.refs_2_, f32[528,512]{1,0:T(8,128)S(1)} %get-tuple-element.68.refs_3_, ...), custom_call_target="tpu_custom_call" | custom-call | flops 1000000 | bytes 1000000 | tf_op jit(solution)/shard_map/pallas_call | solution.py:281
  72.6 1.4 %collective-permute-done.13 = f32[264,512]{1,0:T(8,128)S(1)} collective-permute-done((f32[264,512]{1,0:T(8,128)S(1)}, f32[264,512]{1,0:T(8,128)S(1)}, u32[]{:S(2)}, u32[]{:S(2)}) %collective-permute-start.13) | collective-permute-done | bytes 540704 | tf_op jit(solution)/shard_map/ppermute | solution.py:299
  74.9 2.6 %collective-permute-done.14.refs_1_ = f32[528,512]{1,0:T(8,128)S(1)} collective-permute-done((f32[528,512]{1,0:T(8,128)S(1)}, f32[528,512]{1,0:T(8,128)S(1)}, u32[]{:S(2)}, u32[]{:S(2)}) %collective-permute-start.14) | collective-permute-done | bytes 1081376 | tf_op jit(solution)/shard_map/ppermute | solution.py:299
  77.5 2.1 %shard_map.104 = f32[8,8,128]{2,1,0:T(8,128)} custom-call(f32[528,512]{1,0:T(8,128)S(1)} %pad_maximum_fusion.refs_0_, f32[528,512]{1,0:T(8,128)S(1)} %collective-permute-done.14.refs_1_, f32[528,512]{1,0:T(8,128)S(1)} %get-tuple-element.71.refs_2_), custom_call_target="tpu_custom_call" | custom-call | flops 1000000 | bytes 1000000 | tf_op jit(solution)/shard_map/pallas_call | solution.py:434
  80.7 5.3 %all-to-all-start = ((f32[8,8,128]{2,1,0:T(8,128)}), f32[8,8,128]{2,1,0:T(8,128)S(1)}, u32[]{:S(2)}, u32[]{:S(2)}) async-start(f32[8,8,128]{2,1,0:T(8,128)} %shard_map.104), calls=%async_computation | async-start | bytes 65536 | tf_op jit(solution)/shard_map/all_to_all | solution.py:455
  87.3 5.4 %all-to-all-done = f32[8,8,128]{2,1,0:T(8,128)S(1)} async-done(((f32[8,8,128]{2,1,0:T(8,128)}), f32[8,8,128]{2,1,0:T(8,128)S(1)}, u32[]{:S(2)}, u32[]{:S(2)}) %all-to-all-start) | async-done | bytes 32800 | tf_op jit(solution)/shard_map/all_to_all | solution.py:455
  (51 shorter events, 13.2 us)
Async XLA Ops:
  4.6 21.6 %collective-permute-start.2 = (f32[64,1664]{1,0:T(8,128)}, f32[64,1664]{1,0:T(8,128)S(1)}, u32[]{:S(2)}, u32[]{:S(2)}) collective-permute-start(f32[64,1664]{1,0:T(8,128)} %get-tuple-element.41), channel_id=1, source_target_pairs={{0,8},{2,10},{4,12},{6,14},{8,0},{10,2},{12,4},{14,6},{16,24},{18,... | collective-permute-start | bytes 1277960 | tf_op jit(solution)/shard_map/ppermute | solution.py:299
  7.7 15.1 %collective-permute-start.1 = (f32[32,1664]{1,0:T(8,128)}, f32[32,1664]{1,0:T(8,128)S(1)}, u32[]{:S(2)}, u32[]{:S(2)}) collective-permute-start(f32[32,1664]{1,0:T(8,128)} %get-tuple-element.40), channel_id=1, source_target_pairs={{0,16},{2,18},{4,20},{6,22},{8,24},{10,26},{12,28},{14,30},{16,0},... | collective-permute-start | bytes 638984 | tf_op jit(solution)/shard_map/ppermute | solution.py:299
  10.3 27.6 %collective-permute-start.4 = (s32[16,3456]{1,0:T(8,128)}, s32[16,3456]{1,0:T(8,128)S(1)}, u32[]{:S(2)}, u32[]{:S(2)}) collective-permute-start(s32[16,3456]{1,0:T(8,128)} %get-tuple-element.46), channel_id=1, source_target_pairs={{0,16},{2,18},{4,20},{6,22},{8,24},{10,26},{12,28},{14,30},{16,0},... | collective-permute-start | bytes 663560 | tf_op jit(solution)/shard_map/ppermute | solution.py:299
  10.6 27.3 %collective-permute-start.5 = (s32[16,3456]{1,0:T(8,128)}, s32[16,3456]{1,0:T(8,128)S(1)}, u32[]{:S(2)}, u32[]{:S(2)}) collective-permute-start(s32[16,3456]{1,0:T(8,128)} %get-tuple-element.47), channel_id=1, source_target_pairs={{0,24},{2,26},{4,28},{6,30},{8,16},{10,18},{12,20},{14,22},{16,8},... | collective-permute-start | bytes 663560 | tf_op jit(solution)/shard_map/ppermute | solution.py:299
  26.2 8.3 %collective-permute-start.6 = (f32[32,1664]{1,0:T(8,128)S(1)}, f32[32,1664]{1,0:T(8,128)S(1)}, u32[]{:S(2)}, u32[]{:S(2)}) collective-permute-start(f32[32,1664]{1,0:T(8,128)S(1)} %slice.36), channel_id=1, source_target_pairs={{0,1},{1,0},{2,3},{3,2},{4,5},{5,4},{6,7},{7,6},{8,9},{9,8},{10,11... | collective-permute-start | bytes 638984 | tf_op jit(solution)/shard_map/ppermute | solution.py:299
  27.9 10.9 %collective-permute-start.3 = (f32[32,1664]{1,0:T(8,128)S(1)}, f32[32,1664]{1,0:T(8,128)S(1)}, u32[]{:S(2)}, u32[]{:S(2)}) collective-permute-start(f32[32,1664]{1,0:T(8,128)S(1)} %collective-permute-done.1.refs_1_), channel_id=1, source_target_pairs={{0,8},{2,10},{4,12},{6,14},{8,0},{10,2},{12,4},{14,6},{16,24},{18,... | collective-permute-start | bytes 638984 | tf_op jit(solution)/shard_map/ppermute | solution.py:299
  27.9 12.0 %collective-permute-start.9 = (f32[32,1664]{1,0:T(8,128)S(1)}, f32[32,1664]{1,0:T(8,128)S(1)}, u32[]{:S(2)}, u32[]{:S(2)}) collective-permute-start(f32[32,1664]{1,0:T(8,128)S(1)} %collective-permute-done.1.refs_1_), channel_id=1, source_target_pairs={{0,1},{1,0},{2,3},{3,2},{4,5},{5,4},{6,7},{7,6},{8,9},{9,8},{10,11... | collective-permute-start | bytes 638984 | tf_op jit(solution)/shard_map/ppermute | solution.py:299
  38.8 6.6 %collective-permute-start.7 = (f32[32,1664]{1,0:T(8,128)S(1)}, f32[32,1664]{1,0:T(8,128)S(1)}, u32[]{:S(2)}, u32[]{:S(2)}) collective-permute-start(f32[32,1664]{1,0:T(8,128)S(1)} %collective-permute-done.3.refs_1_), channel_id=1, source_target_pairs={{0,1},{1,0},{2,3},{3,2},{4,5},{5,4},{6,7},{7,6},{8,9},{9,8},{10,11... | collective-permute-start | bytes 638984 | tf_op jit(solution)/shard_map/ppermute | solution.py:299
  45.4 1.1 %copy-start.8 = (s32[16,3072]{1,0:T(8,128)S(1)}, s32[16,3072]{1,0:T(8,128)}, u32[]{:S(2)}) copy-start(s32[16,3072]{1,0:T(8,128)} %get-tuple-element.62) | copy-start | bytes 589828
  45.4 2.5 %copy-start.7 = (s32[16,3072]{1,0:T(8,128)S(1)}, s32[16,3072]{1,0:T(8,128)}, u32[]{:S(2)}) copy-start(s32[16,3072]{1,0:T(8,128)} %get-tuple-element.53) | copy-start | bytes 589828
  45.4 4.9 %copy-start.6 = (s32[16,3072]{1,0:T(8,128)S(1)}, s32[16,3072]{1,0:T(8,128)}, u32[]{:S(2)}) copy-start(s32[16,3072]{1,0:T(8,128)} %get-tuple-element.39) | copy-start | bytes 589828
  46.5 4.6 %collective-permute-start.10 = (f32[528,512]{1,0:T(8,128)S(1)}, f32[528,512]{1,0:T(8,128)S(1)}, u32[]{:S(2)}, u32[]{:S(2)}) collective-permute-start(f32[528,512]{1,0:T(8,128)S(1)} %shard_map.99), channel_id=1, source_target_pairs={{0,2},{2,0},{4,6},{6,4},{8,10},{10,8},{12,14},{14,12},{16,18},{18,... | collective-permute-start | bytes 3244040 | tf_op jit(solution)/shard_map/ppermute | solution.py:299
  46.6 11.1 %collective-permute-start.11 = (s32[16,3072]{1,0:T(8,128)S(1)}, s32[16,3072]{1,0:T(8,128)S(1)}, u32[]{:S(2)}, u32[]{:S(2)}) collective-permute-start(s32[16,3072]{1,0:T(8,128)S(1)} %copy-done.8), channel_id=1, source_target_pairs={{0,8},{2,10},{4,12},{6,14},{8,0},{10,2},{12,4},{14,6},{16,24},{18,... | collective-permute-start | bytes 589832 | tf_op jit(solution)/shard_map/ppermute | solution.py:299
  47.9 17.1 %collective-permute-start.8 = (s32[16,3072]{1,0:T(8,128)S(1)}, s32[16,3072]{1,0:T(8,128)S(1)}, u32[]{:S(2)}, u32[]{:S(2)}) collective-permute-start(s32[16,3072]{1,0:T(8,128)S(1)} %copy-done.7), channel_id=1, source_target_pairs={{0,16},{2,18},{4,20},{6,22},{8,24},{10,26},{12,28},{14,30},{16,0},... | collective-permute-start | bytes 589832 | tf_op jit(solution)/shard_map/ppermute | solution.py:299
  50.3 18.2 %collective-permute-start = (s32[16,3072]{1,0:T(8,128)S(1)}, s32[16,3072]{1,0:T(8,128)S(1)}, u32[]{:S(2)}, u32[]{:S(2)}) collective-permute-start(s32[16,3072]{1,0:T(8,128)S(1)} %copy-done.6), channel_id=1, source_target_pairs={{0,24},{2,26},{4,28},{6,30},{8,16},{10,18},{12,20},{14,22},{16,8},... | collective-permute-start | bytes 589832 | tf_op jit(solution)/shard_map/ppermute | solution.py:299
  52.1 25.4 %collective-permute-start.14 = (f32[528,512]{1,0:T(8,128)S(1)}, f32[528,512]{1,0:T(8,128)S(1)}, u32[]{:S(2)}, u32[]{:S(2)}) collective-permute-start(f32[528,512]{1,0:T(8,128)S(1)} %shard_map.100), channel_id=1, source_target_pairs={{0,4},{2,6},{4,0},{6,2},{8,12},{10,14},{12,8},{14,10},{16,20},{18,... | collective-permute-start | bytes 3244040 | tf_op jit(solution)/shard_map/ppermute | solution.py:299
  72.0 2.0 %collective-permute-start.13 = (f32[264,512]{1,0:T(8,128)S(1)}, f32[264,512]{1,0:T(8,128)S(1)}, u32[]{:S(2)}, u32[]{:S(2)}) collective-permute-start(f32[264,512]{1,0:T(8,128)S(1)} %get-tuple-element.75), channel_id=1, source_target_pairs={{0,2},{2,0},{4,6},{6,4},{8,10},{10,8},{12,14},{14,12},{16,18},{18,... | collective-permute-start | bytes 1622024 | tf_op jit(solution)/shard_map/ppermute | solution.py:299
  72.1 2.7 %collective-permute-start.12 = (f32[264,512]{1,0:T(8,128)S(1)}, f32[264,512]{1,0:T(8,128)S(1)}, u32[]{:S(2)}, u32[]{:S(2)}) collective-permute-start(f32[264,512]{1,0:T(8,128)S(1)} %get-tuple-element.76), channel_id=1, source_target_pairs={{0,2},{2,0},{4,6},{6,4},{8,10},{10,8},{12,14},{14,12},{16,18},{18,... | collective-permute-start | bytes 1622024 | tf_op jit(solution)/shard_map/ppermute | solution.py:299
  77.5 2.1 %copy-start.4 = (f32[1,3072]{1,0:T(1,128)S(1)}, f32[1,3072]{1,0:T(1,128)}, u32[]{:S(2)}) copy-start(f32[1,3072]{1,0:T(1,128)} %get-tuple-element.73) | copy-start | bytes 36868
  77.5 8.5 %copy-start.3 = (s32[3072]{0:T(1024)S(1)}, s32[3072]{0:T(1024)}, u32[]{:S(2)}) copy-start(s32[3072]{0:T(1024)} %param.9) | copy-start | bytes 36868
  77.5 8.6 %copy-start.2 = (f32[3072,32]{0,1:T(8,128)S(1)}, f32[3072,32]{0,1:T(8,128)}, u32[]{:S(2)}) copy-start(f32[3072,32]{0,1:T(8,128)} %param.7) | copy-start | bytes 1179652
  79.6 6.3 %collective-permute-start.15 = (f32[32,128]{1,0:T(8,128)S(1)}, f32[32,128]{1,0:T(8,128)S(1)}, u32[]{:S(2)}, u32[]{:S(2)}) collective-permute-start(f32[32,128]{1,0:T(8,128)S(1)} %pad_maximum_fusion.1), channel_id=1, source_target_pairs={{0,1},{1,0},{2,3},{3,2},{4,5},{5,4},{6,7},{7,6},{8,9},{9,8},{10,11... | collective-permute-start | bytes 49160 | tf_op jit(solution)/shard_map/ppermute | solution.py:299
  80.7 12.0 %all-to-all-start = ((f32[8,8,128]{2,1,0:T(8,128)}), f32[8,8,128]{2,1,0:T(8,128)S(1)}, u32[]{:S(2)}, u32[]{:S(2)}) async-start(f32[8,8,128]{2,1,0:T(8,128)} %shard_map.104), calls=%async_computation | async-start | bytes 65536 | tf_op jit(solution)/shard_map/all_to_all | solution.py:455
  86.1 7.1 %copy-start.5 = (f32[8,2,32]{2,1,0:T(2,128)}, f32[8,2,32]{2,1,0:T(2,128)S(1)}, u32[]{:S(2)}) copy-start(f32[8,2,32]{2,1,0:T(2,128)S(1)} %fusion.5) | copy-start | bytes 6148
  (2 other events, 2.0 us)

commit v13 on v12

--- a/solution.py
+++ b/solution.py
@@ -244,7 +244,10 @@
         sums = None if sums_from is None else child_sums(sums_from, rows, node_count)
         for i, first in enumerate(firsts):
             out_ref = out_refs[i]
-            if cut is not None:
+            if cut is not None and codes_ref.shape[1] < rows:
+                low = first + which * ((codes_ref.shape[0] - classes) // 2)
+                codes = codes_ref[pl.ds(pl.multiple_of(low, own), own), : rows // 2]
+            elif cut is not None:
                 codes = codes_ref[first : first + own, cut]
             elif codes_ref.shape[1] < rows:
                 second = first + (codes_ref.shape[0] - classes) // 2
@@ -411,12 +414,13 @@
     late_4 = swap(late_4, "rows", 4)
     late_8 = swap(late_8, "rows", 8)
     late_12 = swap(late_12, "rows", 12)
-    hist_a, hist_b = add(
-        ((4, 0, (0, 1), (classes, classes + own)),), [rows_4, far_4], [hist_a, hist_b]
-    )
-    near_12, codes_8, codes_12, hist_a = lax.optimization_barrier((near_12, codes_8, codes_12, hist_a))
+    firsts = (classes, classes + own)
+    hists = add(((4, 0, (0, None), firsts),), [rows_4], [hist_a, hist_b])
+    hists = add(((4, 0, (None, 1), firsts),), [rows_4, far_4], hists)
+    hist_a, hist_b = add(((8, 0, (1, None), (0, own)),), [codes_8, near_8], hists)
+    near_12, codes_12, hist_a = lax.optimization_barrier((near_12, codes_12, hist_a))
     far_12 = swap(near_12, "feat", 1)
-    hist_a, hist_b = add(((8, 0, (1, 2), (0, own)),), [codes_8, near_8, far_8], [hist_a, hist_b])
+    hist_a, hist_b = add(((8, 0, (None, 1), (0, own)),), [codes_8, far_8], [hist_a, hist_b])
     hist_a, hist_b = add(((12, 0, (1, None), (0, own)),), [codes_12, near_12], [hist_a, hist_b])
     (to_core,) = add(((12, 0, (None, 1), (0,)),), [codes_12, far_12], [hist_a])
     from_core = swap(to_core, "rows", 1)

time: 93.5 us -> 93.5 us (level)
    pallas_call x9 -> x11, Pallas kernels: 28 us -> 28.5 us  [add_rows(): pl.pallas_call(functools.partial(add_kernel, classes, node_count, own, pl...]
  transfers between devices with their start and end apart: 17 -> 17, of which waited for: 10 -> 11; matrix products, arithmetic and copies ran while one was open for 2% -> 2% of each run, Pallas kernels for 29% -> 29%
where the time goes in v13:
time: 93.5 us; the launch traced here: 93.3 us
  Pallas kernels  34.5 us (37%)
  waiting for transfers between devices  28.9 us (31%)
  starting transfers between devices  24.9 us (27%)
  local copies, waits for them, and re-layouts  2.81 us (3%)
  matrix products  1.11 us (1%)
    pallas_call x11, Pallas kernels, add_rows(): pl.pallas_call(functools.partial(add_kernel, classes, node_count, own, pl...  28.5 us
    ppermute x16, waiting for transfers between devices, swap(): return lax.ppermute(x, axis, [(i, i ^ bit) for i in range(size)])  23.5 us
    ppermute x16, starting transfers between devices, swap(): return lax.ppermute(x, axis, [(i, i ^ bit) for i in range(size)])  19.4 us
    all_to_all x1, starting transfers between devices, local(): lax.all_to_all(gains, 'rows', 0, 0, tiled=True, axis_index_groups=halves)  5.54 us
    all_to_all x1, waiting for transfers between devices, local(): lax.all_to_all(gains, 'rows', 0, 0, tiled=True, axis_index_groups=halves)  5.35 us
    pallas_call x1, Pallas kernels, prepare(): pl.pallas_call(functools.partial(prep_kernel, own, blocks), in_specs=[pl....  3.98 us
    unnamed x19, local copies, waits for them, and re-layouts  2.65 us
    pallas_call x1, Pallas kernels, local(): pl.pallas_call(functools.partial(gain_kernel, classes, node_count), in_sp...  2.08 us
  transfers between devices with their start and end apart: 17, of which 11 were waited for; matrix products, arithmetic and copies ran while one was open for 2% of the time, Pallas kernels for 29%

profile of v13, /device:TPU:0, one launch (start us, length us, event | category | flops | bytes accessed | tf_op | source)
XLA Modules:
  0.0 93.3 jit_solution(14398869741541498017)
XLA Ops:
  0.6 4.0 %shard_map.94 = (f32[32,3328]{1,0:T(8,128)}, f32[32,1664]{1,0:T(8,128)}, f32[1,3072]{1,0:T(1,128)}, s32[32,3072]{1,0:T(8,128)}, f32[64,1664]{1,0:T(8,128)}, /*in...) custom-call(s32[3072,128]{1,0:T(8,128)} %refs_0_.1, ...), custom_call_target="tpu_custom_call" | custom-call | flops 1000000 | bytes 1000000 | tf_op jit(solution)/shard_map/pallas_call | solution.py:339
  4.6 3.1 %collective-permute-start.2 = (f32[64,1664]{1,0:T(8,128)}, f32[64,1664]{1,0:T(8,128)S(1)}, u32[]{:S(2)}, u32[]{:S(2)}) collective-permute-start(f32[64,1664]{1,0:T(8,128)} %get-tuple-element.44), channel_id=1, source_target_pairs={{0,8},{2,10},{4,12},{6,14},{8,0},{10,2},{12,4},{14,6},{16,24},{18,... | collective-permute-start | bytes 1277960 | tf_op jit(solution)/shard_map/ppermute | solution.py:302
  7.7 2.6 %collective-permute-start.1 = (f32[32,1664]{1,0:T(8,128)}, f32[32,1664]{1,0:T(8,128)S(1)}, u32[]{:S(2)}, u32[]{:S(2)}) collective-permute-start(f32[32,1664]{1,0:T(8,128)} %get-tuple-element.43), channel_id=1, source_target_pairs={{0,16},{2,18},{4,20},{6,22},{8,24},{10,26},{12,28},{14,30},{16,0},... | collective-permute-start | bytes 638984 | tf_op jit(solution)/shard_map/ppermute | solution.py:302
  10.6 2.5 %collective-permute-start.4 = (s32[16,3456]{1,0:T(8,128)}, s32[16,3456]{1,0:T(8,128)S(1)}, u32[]{:S(2)}, u32[]{:S(2)}) collective-permute-start(s32[16,3456]{1,0:T(8,128)} %get-tuple-element.49), channel_id=1, source_target_pairs={{0,24},{2,26},{4,28},{6,30},{8,16},{10,18},{12,20},{14,22},{16,8},... | collective-permute-start | bytes 663560 | tf_op jit(solution)/shard_map/ppermute | solution.py:302
  15.1 6.7 %shard_map.95 = (f32[528,512]{1,0:T(8,128)S(1)}, f32[528,512]{1,0:T(8,128)S(1)}, f32[528,512]{1,0:T(8,128)S(1)}, f32[528,512]{1,0:T(8,128)S(1)}) custom-call(s32[32,3072]{1,0:T(8,128)S(1)} %copy-done.1, f32[32,3328]{1,0:T(8,128)S(1)} %copy-done), custom_call_target="tpu_custom_call" | custom-call | flops 1000000 | bytes 1000000 | tf_op jit(solution)/shard_map/pallas_call | solution.py:284
  22.9 3.3 %collective-permute-done.2.refs_0_.refs_1_ = f32[64,1664]{1,0:T(8,128)S(1)} collective-permute-done((f32[64,1664]{1,0:T(8,128)}, f32[64,1664]{1,0:T(8,128)S(1)}, u32[]{:S(2)}, u32[]{:S(2)}) %collective-permute-start.2) | collective-permute-done | bytes 426016 | tf_op jit(solution)/shard_map/ppermute | solution.py:302
  26.2 1.7 %collective-permute-start.6 = (f32[32,1664]{1,0:T(8,128)S(1)}, f32[32,1664]{1,0:T(8,128)S(1)}, u32[]{:S(2)}, u32[]{:S(2)}) collective-permute-start(f32[32,1664]{1,0:T(8,128)S(1)} %slice.36), channel_id=1, source_target_pairs={{0,1},{1,0},{2,3},{3,2},{4,5},{5,4},{6,7},{7,6},{8,9},{9,8},{10,11... | collective-permute-start | bytes 638984 | tf_op jit(solution)/shard_map/ppermute | solution.py:302
  28.4 1.8 %shard_map.96 = (f32[528,512]{1,0:T(8,128)S(1)}, f32[528,512]{1,0:T(8,128)S(1)}) custom-call(f32[64,1664]{1,0:T(8,128)S(1)} %collective-permute-done.2.refs_0_.refs_1_, f32[528,512]{1,0:T(8,128)S(1)} %get-tuple-element.52.refs_1_, f32[528,512]{1,0:T(8,128)S(1)} %get-tuple-element.53.refs_2_), custom_call_target="tpu_custom_call" | custom-call | flops 1000000 | bytes 1000000 | tf_op jit(solution)/shard_map/pallas_call | solution.py:284
  30.3 4.2 %collective-permute-done.6.refs_1_.refs_2_ = f32[32,1664]{1,0:T(8,128)S(1)} collective-permute-done((f32[32,1664]{1,0:T(8,128)S(1)}, f32[32,1664]{1,0:T(8,128)S(1)}, u32[]{:S(2)}, u32[]{:S(2)}) %collective-permute-start.6) | collective-permute-done | bytes 213024 | tf_op jit(solution)/shard_map/ppermute | solution.py:302
  34.5 1.8 %shard_map.97 = (f32[528,512]{1,0:T(8,128)S(1)}, f32[528,512]{1,0:T(8,128)S(1)}) custom-call(f32[64,1664]{1,0:T(8,128)S(1)} %collective-permute-done.2.refs_0_.refs_1_, f32[32,1664]{1,0:T(8,128)S(1)} %collective-permute-done.6.refs_1_.refs_2_, f32[528,512]{1,0:T(8,128)S(1)} %get-tuple-element.54.refs_2_, f32[528,512]{1,0:T(8,128)S(1)} %get-tuple-element.55.refs_3_), custom_call_target="tpu_custom_call" | custom-call | flops 1000000 | bytes 1000000 | tf_op jit(solution)/shard_map/pallas_call | solution.py:284
  36.3 1.8 %shard_map.98 = (f32[528,512]{1,0:T(8,128)S(1)}, f32[528,512]{1,0:T(8,128)S(1)}) custom-call(s32[16,3456]{1,0:T(8,128)S(1)} %collective-permute-done.5.refs_0_, f32[32,1664]{1,0:T(8,128)S(1)} %collective-permute-done.1.refs_1_, f32[528,512]{1,0:T(8,128)S(1)} %get-tuple-element.56.refs_2_, f32[528,512]{1,0:T(8,128)S(1)} %get-tuple-element.57.refs_3_), custom_call_target="tpu_custom_call" | custom-call | flops 1000000 | bytes 1000000 | tf_op jit(solution)/shard_map/pallas_call | solution.py:284
  39.9 1.8 %shard_map.99 = (f32[528,512]{1,0:T(8,128)S(1)}, f32[528,512]{1,0:T(8,128)S(1)}) custom-call(s32[16,3456]{1,0:T(8,128)S(1)} %collective-permute-done.5.refs_0_, f32[32,1664]{1,0:T(8,128)S(1)} %collective-permute-done.9.refs_1_.refs_2_, f32[528,512]{1,0:T(8,128)S(1)} %get-tuple-element.62.refs_2_, f32[528,512]{1,0:T(8,128)S(1)} %get-tuple-element.63.refs_3_), custom_call_target="tpu_custom_call" | custom-call | flops 1000000 | bytes 1000000 | tf_op jit(solution)/shard_map/pallas_call | solution.py:284
  41.8 2.0 %shard_map.100 = (f32[528,512]{1,0:T(8,128)S(1)}, f32[528,512]{1,0:T(8,128)S(1)}) custom-call(s32[16,3456]{1,0:T(8,128)S(1)} %collective-permute-done.4.refs_0_, f32[32,1664]{1,0:T(8,128)S(1)} %collective-permute-done.3.refs_1_, f32[528,512]{1,0:T(8,128)S(1)} %get-tuple-element.64.refs_2_, f32[528,512]{1,0:T(8,128)S(1)} %get-tuple-element.65.refs_3_), custom_call_target="tpu_custom_call" | custom-call | flops 1000000 | bytes 1000000 | tf_op jit(solution)/shard_map/pallas_call | solution.py:284
  46.7 3.6 %collective-permute-start.8 = (s32[16,3072]{1,0:T(8,128)S(1)}, s32[16,3072]{1,0:T(8,128)S(1)}, u32[]{:S(2)}, u32[]{:S(2)}) collective-permute-start(s32[16,3072]{1,0:T(8,128)S(1)} %copy-done.7), channel_id=1, source_target_pairs={{0,16},{2,18},{4,20},{6,22},{8,24},{10,26},{12,28},{14,30},{16,0},... | collective-permute-start | bytes 589832 | tf_op jit(solution)/shard_map/ppermute | solution.py:302
  51.9 1.6 %collective-permute-start.14 = (f32[528,512]{1,0:T(8,128)S(1)}, f32[528,512]{1,0:T(8,128)S(1)}, u32[]{:S(2)}, u32[]{:S(2)}) collective-permute-start(f32[528,512]{1,0:T(8,128)S(1)} %shard_map.102), channel_id=1, source_target_pairs={{0,4},{2,6},{4,0},{6,2},{8,12},{10,14},{12,8},{14,10},{16,20},{18,... | collective-permute-start | bytes 3244040 | tf_op jit(solution)/shard_map/ppermute | solution.py:302
  53.5 4.1 %collective-permute-done.11.refs_0_ = s32[16,3072]{1,0:T(8,128)S(1)} collective-permute-done((s32[16,3072]{1,0:T(8,128)S(1)}, s32[16,3072]{1,0:T(8,128)S(1)}, u32[]{:S(2)}, u32[]{:S(2)}) %collective-permute-start.11) | collective-permute-done | bytes 196640 | tf_op jit(solution)/shard_map/ppermute | solution.py:302
  57.6 3.4 %shard_map.103 = (f32[528,512]{1,0:T(8,128)S(1)}, f32[528,512]{1,0:T(8,128)S(1)}) custom-call(s32[16,3072]{1,0:T(8,128)S(1)} %collective-permute-done.11.refs_0_, f32[64,1664]{1,0:T(8,128)S(1)} %collective-permute-done.2.refs_0_.refs_1_, f32[32,1664]{1,0:T(8,128)S(1)} %collective-permute-done.6.refs_1_.refs_2_, f32[528,512]{1,0:T(8,128)S(1)} %get-tuple-element.70.refs_3_, ...), custom_call_target="tpu_custom_call" | custom-call | flops 1000000 | bytes 1000000 | tf_op jit(solution)/shard_map/pallas_call | solution.py:284
  61.1 3.4 %collective-permute-done.8.refs_0_ = s32[16,3072]{1,0:T(8,128)S(1)} collective-permute-done((s32[16,3072]{1,0:T(8,128)S(1)}, s32[16,3072]{1,0:T(8,128)S(1)}, u32[]{:S(2)}, u32[]{:S(2)}) %collective-permute-start.8) | collective-permute-done | bytes 196640 | tf_op jit(solution)/shard_map/ppermute | solution.py:302
  64.5 3.5 %shard_map.104 = (f32[528,512]{1,0:T(8,128)S(1)}, f32[528,512]{1,0:T(8,128)S(1)}) custom-call(s32[16,3072]{1,0:T(8,128)S(1)} %collective-permute-done.8.refs_0_, f32[32,1664]{1,0:T(8,128)S(1)} %collective-permute-done.1.refs_1_, f32[32,1664]{1,0:T(8,128)S(1)} %collective-permute-done.9.refs_1_.refs_2_, f32[528,512]{1,0:T(8,128)S(1)} %get-tuple-element.72.refs_3_, ...), custom_call_target="tpu_custom_call" | custom-call | flops 1000000 | bytes 1000000 | tf_op jit(solution)/shard_map/pallas_call | solution.py:284
  68.0 3.5 %shard_map.105 = (f32[528,512]{1,0:T(8,128)S(1)}, f32[528,512]{1,0:T(8,128)S(1)}) custom-call(s32[16,3072]{1,0:T(8,128)S(1)} %collective-permute-done.refs_0_, f32[32,1664]{1,0:T(8,128)S(1)} %collective-permute-done.3.refs_1_, f32[32,1664]{1,0:T(8,128)S(1)} %collective-permute-done.7.refs_1_.refs_2_, f32[528,512]{1,0:T(8,128)S(1)} %get-tuple-element.74.refs_3_, ...), custom_call_target="tpu_custom_call" | custom-call | flops 1000000 | bytes 1000000 | tf_op jit(solution)/shard_map/pallas_call | solution.py:284
  74.3 3.0 %collective-permute-done.14.refs_1_ = f32[528,512]{1,0:T(8,128)S(1)} collective-permute-done((f32[528,512]{1,0:T(8,128)S(1)}, f32[528,512]{1,0:T(8,128)S(1)}, u32[]{:S(2)}, u32[]{:S(2)}) %collective-permute-start.14) | collective-permute-done | bytes 1081376 | tf_op jit(solution)/shard_map/ppermute | solution.py:302
  77.4 2.1 %shard_map.106 = f32[8,8,128]{2,1,0:T(8,128)} custom-call(f32[528,512]{1,0:T(8,128)S(1)} %pad_maximum_fusion.refs_0_, f32[528,512]{1,0:T(8,128)S(1)} %collective-permute-done.14.refs_1_, f32[528,512]{1,0:T(8,128)S(1)} %get-tuple-element.77.refs_2_), custom_call_target="tpu_custom_call" | custom-call | flops 1000000 | bytes 1000000 | tf_op jit(solution)/shard_map/pallas_call | solution.py:438
  80.4 5.5 %all-to-all-start = ((f32[8,8,128]{2,1,0:T(8,128)}), f32[8,8,128]{2,1,0:T(8,128)S(1)}, u32[]{:S(2)}, u32[]{:S(2)}) async-start(f32[8,8,128]{2,1,0:T(8,128)} %shard_map.106), calls=%async_computation | async-start | bytes 65536 | tf_op jit(solution)/shard_map/all_to_all | solution.py:459
  87.3 5.4 %all-to-all-done = f32[8,8,128]{2,1,0:T(8,128)S(1)} async-done(((f32[8,8,128]{2,1,0:T(8,128)}), f32[8,8,128]{2,1,0:T(8,128)S(1)}, u32[]{:S(2)}, u32[]{:S(2)}) %all-to-all-start) | async-done | bytes 32800 | tf_op jit(solution)/shard_map/all_to_all | solution.py:459
  (53 shorter events, 15.9 us)
Async XLA Ops:
  4.6 21.6 %collective-permute-start.2 = (f32[64,1664]{1,0:T(8,128)}, f32[64,1664]{1,0:T(8,128)S(1)}, u32[]{:S(2)}, u32[]{:S(2)}) collective-permute-start(f32[64,1664]{1,0:T(8,128)} %get-tuple-element.44), channel_id=1, source_target_pairs={{0,8},{2,10},{4,12},{6,14},{8,0},{10,2},{12,4},{14,6},{16,24},{18,... | collective-permute-start | bytes 1277960 | tf_op jit(solution)/shard_map/ppermute | solution.py:302
  7.7 15.1 %collective-permute-start.1 = (f32[32,1664]{1,0:T(8,128)}, f32[32,1664]{1,0:T(8,128)S(1)}, u32[]{:S(2)}, u32[]{:S(2)}) collective-permute-start(f32[32,1664]{1,0:T(8,128)} %get-tuple-element.43), channel_id=1, source_target_pairs={{0,16},{2,18},{4,20},{6,22},{8,24},{10,26},{12,28},{14,30},{16,0},... | collective-permute-start | bytes 638984 | tf_op jit(solution)/shard_map/ppermute | solution.py:302
  10.3 26.0 %collective-permute-start.5 = (s32[16,3456]{1,0:T(8,128)}, s32[16,3456]{1,0:T(8,128)S(1)}, u32[]{:S(2)}, u32[]{:S(2)}) collective-permute-start(s32[16,3456]{1,0:T(8,128)} %get-tuple-element.50), channel_id=1, source_target_pairs={{0,16},{2,18},{4,20},{6,22},{8,24},{10,26},{12,28},{14,30},{16,0},... | collective-permute-start | bytes 663560 | tf_op jit(solution)/shard_map/ppermute | solution.py:302
  10.6 27.5 %collective-permute-start.4 = (s32[16,3456]{1,0:T(8,128)}, s32[16,3456]{1,0:T(8,128)S(1)}, u32[]{:S(2)}, u32[]{:S(2)}) collective-permute-start(s32[16,3456]{1,0:T(8,128)} %get-tuple-element.49), channel_id=1, source_target_pairs={{0,24},{2,26},{4,28},{6,30},{8,16},{10,18},{12,20},{14,22},{16,8},... | collective-permute-start | bytes 663560 | tf_op jit(solution)/shard_map/ppermute | solution.py:302
  26.2 8.3 %collective-permute-start.6 = (f32[32,1664]{1,0:T(8,128)S(1)}, f32[32,1664]{1,0:T(8,128)S(1)}, u32[]{:S(2)}, u32[]{:S(2)}) collective-permute-start(f32[32,1664]{1,0:T(8,128)S(1)} %slice.36), channel_id=1, source_target_pairs={{0,1},{1,0},{2,3},{3,2},{4,5},{5,4},{6,7},{7,6},{8,9},{9,8},{10,11... | collective-permute-start | bytes 638984 | tf_op jit(solution)/shard_map/ppermute | solution.py:302
  27.9 10.9 %collective-permute-start.3 = (f32[32,1664]{1,0:T(8,128)S(1)}, f32[32,1664]{1,0:T(8,128)S(1)}, u32[]{:S(2)}, u32[]{:S(2)}) collective-permute-start(f32[32,1664]{1,0:T(8,128)S(1)} %collective-permute-done.1.refs_1_), channel_id=1, source_target_pairs={{0,8},{2,10},{4,12},{6,14},{8,0},{10,2},{12,4},{14,6},{16,24},{18,... | collective-permute-start | bytes 638984 | tf_op jit(solution)/shard_map/ppermute | solution.py:302
  27.9 12.0 %collective-permute-start.9 = (f32[32,1664]{1,0:T(8,128)S(1)}, f32[32,1664]{1,0:T(8,128)S(1)}, u32[]{:S(2)}, u32[]{:S(2)}) collective-permute-start(f32[32,1664]{1,0:T(8,128)S(1)} %collective-permute-done.1.refs_1_), channel_id=1, source_target_pairs={{0,1},{1,0},{2,3},{3,2},{4,5},{5,4},{6,7},{7,6},{8,9},{9,8},{10,11... | collective-permute-start | bytes 638984 | tf_op jit(solution)/shard_map/ppermute | solution.py:302
  38.8 6.5 %collective-permute-start.7 = (f32[32,1664]{1,0:T(8,128)S(1)}, f32[32,1664]{1,0:T(8,128)S(1)}, u32[]{:S(2)}, u32[]{:S(2)}) collective-permute-start(f32[32,1664]{1,0:T(8,128)S(1)} %collective-permute-done.3.refs_1_), channel_id=1, source_target_pairs={{0,1},{1,0},{2,3},{3,2},{4,5},{5,4},{6,7},{7,6},{8,9},{9,8},{10,11... | collective-permute-start | bytes 638984 | tf_op jit(solution)/shard_map/ppermute | solution.py:302
  45.3 1.1 %copy-start.8 = (s32[16,3072]{1,0:T(8,128)S(1)}, s32[16,3072]{1,0:T(8,128)}, u32[]{:S(2)}) copy-start(s32[16,3072]{1,0:T(8,128)} %get-tuple-element.68) | copy-start | bytes 589828
  45.3 1.4 %copy-start.7 = (s32[16,3072]{1,0:T(8,128)S(1)}, s32[16,3072]{1,0:T(8,128)}, u32[]{:S(2)}) copy-start(s32[16,3072]{1,0:T(8,128)} %get-tuple-element.60) | copy-start | bytes 589828
  45.3 5.0 %copy-start.6 = (s32[16,3072]{1,0:T(8,128)S(1)}, s32[16,3072]{1,0:T(8,128)}, u32[]{:S(2)}) copy-start(s32[16,3072]{1,0:T(8,128)} %get-tuple-element.42) | copy-start | bytes 589828
  46.3 4.6 %collective-permute-start.10 = (f32[528,512]{1,0:T(8,128)S(1)}, f32[528,512]{1,0:T(8,128)S(1)}, u32[]{:S(2)}, u32[]{:S(2)}) collective-permute-start(f32[528,512]{1,0:T(8,128)S(1)} %shard_map.101), channel_id=1, source_target_pairs={{0,2},{2,0},{4,6},{6,4},{8,10},{10,8},{12,14},{14,12},{16,18},{18,... | collective-permute-start | bytes 3244040 | tf_op jit(solution)/shard_map/ppermute | solution.py:302
  46.4 11.2 %collective-permute-start.11 = (s32[16,3072]{1,0:T(8,128)S(1)}, s32[16,3072]{1,0:T(8,128)S(1)}, u32[]{:S(2)}, u32[]{:S(2)}) collective-permute-start(s32[16,3072]{1,0:T(8,128)S(1)} %copy-done.8), channel_id=1, source_target_pairs={{0,8},{2,10},{4,12},{6,14},{8,0},{10,2},{12,4},{14,6},{16,24},{18,... | collective-permute-start | bytes 589832 | tf_op jit(solution)/shard_map/ppermute | solution.py:302
  46.7 17.7 %collective-permute-start.8 = (s32[16,3072]{1,0:T(8,128)S(1)}, s32[16,3072]{1,0:T(8,128)S(1)}, u32[]{:S(2)}, u32[]{:S(2)}) collective-permute-start(s32[16,3072]{1,0:T(8,128)S(1)} %copy-done.7), channel_id=1, source_target_pairs={{0,16},{2,18},{4,20},{6,22},{8,24},{10,26},{12,28},{14,30},{16,0},... | collective-permute-start | bytes 589832 | tf_op jit(solution)/shard_map/ppermute | solution.py:302
  50.3 17.6 %collective-permute-start = (s32[16,3072]{1,0:T(8,128)S(1)}, s32[16,3072]{1,0:T(8,128)S(1)}, u32[]{:S(2)}, u32[]{:S(2)}) collective-permute-start(s32[16,3072]{1,0:T(8,128)S(1)} %copy-done.6), channel_id=1, source_target_pairs={{0,24},{2,26},{4,28},{6,30},{8,16},{10,18},{12,20},{14,22},{16,8},... | collective-permute-start | bytes 589832 | tf_op jit(solution)/shard_map/ppermute | solution.py:302
  51.9 25.4 %collective-permute-start.14 = (f32[528,512]{1,0:T(8,128)S(1)}, f32[528,512]{1,0:T(8,128)S(1)}, u32[]{:S(2)}, u32[]{:S(2)}) collective-permute-start(f32[528,512]{1,0:T(8,128)S(1)} %shard_map.102), channel_id=1, source_target_pairs={{0,4},{2,6},{4,0},{6,2},{8,12},{10,14},{12,8},{14,10},{16,20},{18,... | collective-permute-start | bytes 3244040 | tf_op jit(solution)/shard_map/ppermute | solution.py:302
  71.5 2.0 %collective-permute-start.13 = (f32[264,512]{1,0:T(8,128)S(1)}, f32[264,512]{1,0:T(8,128)S(1)}, u32[]{:S(2)}, u32[]{:S(2)}) collective-permute-start(f32[264,512]{1,0:T(8,128)S(1)} %get-tuple-element.81), channel_id=1, source_target_pairs={{0,2},{2,0},{4,6},{6,4},{8,10},{10,8},{12,14},{14,12},{16,18},{18,... | collective-permute-start | bytes 1622024 | tf_op jit(solution)/shard_map/ppermute | solution.py:302
  71.6 2.7 %collective-permute-start.12 = (f32[264,512]{1,0:T(8,128)S(1)}, f32[264,512]{1,0:T(8,128)S(1)}, u32[]{:S(2)}, u32[]{:S(2)}) collective-permute-start(f32[264,512]{1,0:T(8,128)S(1)} %get-tuple-element.82), channel_id=1, source_target_pairs={{0,2},{2,0},{4,6},{6,4},{8,10},{10,8},{12,14},{14,12},{16,18},{18,... | collective-permute-start | bytes 1622024 | tf_op jit(solution)/shard_map/ppermute | solution.py:302
  77.4 2.1 %copy-start.4 = (f32[1,3072]{1,0:T(1,128)S(1)}, f32[1,3072]{1,0:T(1,128)}, u32[]{:S(2)}) copy-start(f32[1,3072]{1,0:T(1,128)} %get-tuple-element.79) | copy-start | bytes 36868
  77.4 8.7 %copy-start.3 = (s32[3072]{0:T(1024)S(1)}, s32[3072]{0:T(1024)}, u32[]{:S(2)}) copy-start(s32[3072]{0:T(1024)} %param.9) | copy-start | bytes 36868
  77.4 8.8 %copy-start.2 = (f32[3072,32]{0,1:T(8,128)S(1)}, f32[3072,32]{0,1:T(8,128)}, u32[]{:S(2)}) copy-start(f32[3072,32]{0,1:T(8,128)} %param.7) | copy-start | bytes 1179652
  79.5 6.5 %collective-permute-start.15 = (f32[32,128]{1,0:T(8,128)S(1)}, f32[32,128]{1,0:T(8,128)S(1)}, u32[]{:S(2)}, u32[]{:S(2)}) collective-permute-start(f32[32,128]{1,0:T(8,128)S(1)} %pad_maximum_fusion.1), channel_id=1, source_target_pairs={{0,1},{1,0},{2,3},{3,2},{4,5},{5,4},{6,7},{7,6},{8,9},{9,8},{10,11... | collective-permute-start | bytes 49160 | tf_op jit(solution)/shard_map/ppermute | solution.py:302
  80.4 12.2 %all-to-all-start = ((f32[8,8,128]{2,1,0:T(8,128)}), f32[8,8,128]{2,1,0:T(8,128)S(1)}, u32[]{:S(2)}, u32[]{:S(2)}) async-start(f32[8,8,128]{2,1,0:T(8,128)} %shard_map.106), calls=%async_computation | async-start | bytes 65536 | tf_op jit(solution)/shard_map/all_to_all | solution.py:459
  86.1 7.1 %copy-start.5 = (f32[8,2,32]{2,1,0:T(2,128)}, f32[8,2,32]{2,1,0:T(2,128)S(1)}, u32[]{:S(2)}) copy-start(f32[8,2,32]{2,1,0:T(2,128)S(1)} %fusion.5) | copy-start | bytes 6148
  (2 other events, 2.0 us)

commit v14 on v13

--- a/solution.py
+++ b/solution.py
@@ -73,7 +73,7 @@
     operands, rest = refs[:7], refs[7:]
     info_ref, half_ref, flag_ref = rest[:3]
     outs = rest[3 : 3 + len(blocks)]
-    turned, *buffers, sems = rest[3 + len(blocks) :]
+    turned, *buffers, sems, out_sems = rest[3 + len(blocks) :]
     copies = [
         pltpu.make_async_copy(operand, buffer, sems.at[i])
         for i, (operand, buffer) in enumerate(zip(operands, buffers))
@@ -93,13 +93,18 @@
         info_ref[:, h * width : h * width + half] = prob[:, h * half : (h + 1) * half]
     copies[0].wait()
     turned[...] = codes_ref[...].T
+    leaving = []
     for (infos, pieces, _), out_ref in zip(blocks, outs):
-        if infos == 0 and out_ref.shape[1] > rows:
-            out_ref[:, rows:] = jnp.zeros((out_ref.shape[0], out_ref.shape[1] - rows), out_ref.dtype)
         for i, start_of in enumerate(pieces):
             start = pl.multiple_of(start_of(row_index), own)
             if infos == 0:
-                out_ref[i * own : (i + 1) * own, :rows] = turned[pl.ds(start, own), :]
+                copy = pltpu.make_async_copy(
+                    turned.at[pl.ds(start, own), :],
+                    out_ref.at[i * own : (i + 1) * own, :rows],
+                    out_sems.at[len(leaving)],
+                )
+                copy.start()
+                leaving.append(copy)
                 continue
             cut = rows * infos // 2
             for h in range(2 // infos):
@@ -150,6 +155,8 @@
     for (infos, _, _), out_ref in zip(blocks, outs):
         if infos > 0:
             out_ref[:classes, :] = half_ref[...] if infos == 1 else info_ref[...]
+    for copy in leaving:
+        copy.wait()
 
 
 def gradients(prob, label):
@@ -336,14 +343,16 @@
         *splits,
     )
     spaces = [pltpu.VMEM] * 4 + [pltpu.SMEM] * 3
+    loose = sum(len(pieces) for infos, pieces, _ in blocks if infos == 0)
     return pl.pallas_call(
         functools.partial(prep_kernel, own, blocks),
         in_specs=[pl.BlockSpec(memory_space=pltpu.HBM)] * len(operands),
-        out_specs=[whole] * len(shapes),
+        out_specs=[whole] * 3
+        + [pl.BlockSpec(memory_space=pltpu.HBM) if infos == 0 else whole for infos, _, _ in blocks],
         out_shape=shapes,
         scratch_shapes=[pltpu.VMEM((feats_dev, rows_dev), jnp.int32)]
         + [space(x.shape, x.dtype) for space, x in zip(spaces, operands)]
-        + [pltpu.SemaphoreType.DMA((len(operands),))],
+        + [pltpu.SemaphoreType.DMA((len(operands),)), pltpu.SemaphoreType.DMA((max(1, loose),))],
         compiler_params=pltpu.CompilerParams(vmem_limit_bytes=PREP_VMEM_BYTES),
         cost_estimate=SMALL_COST,
     )(*operands)

time: 93.5 us -> 94.3 us (level)
  no operation moved by 1% of the time
where the time goes in v14:
time: 94.3 us; the launch traced here: 94 us
  Pallas kernels  35.3 us (37%)
  waiting for transfers between devices  28.8 us (31%)
  starting transfers between devices  24.9 us (26%)
  local copies, waits for them, and re-layouts  2.81 us (3%)
  matrix products  1.11 us (1%)
    pallas_call x11, Pallas kernels, add_rows(): pl.pallas_call(functools.partial(add_kernel, classes, node_count, own, pl...  28.5 us
    ppermute x16, waiting for transfers between devices, swap(): return lax.ppermute(x, axis, [(i, i ^ bit) for i in range(size)])  23.5 us
    ppermute x16, starting transfers between devices, swap(): return lax.ppermute(x, axis, [(i, i ^ bit) for i in range(size)])  19.4 us
    all_to_all x1, starting transfers between devices, local(): lax.all_to_all(gains, 'rows', 0, 0, tiled=True, axis_index_groups=halves)  5.54 us
    all_to_all x1, waiting for transfers between devices, local(): lax.all_to_all(gains, 'rows', 0, 0, tiled=True, axis_index_groups=halves)  5.35 us
    pallas_call x1, Pallas kernels, prepare(): pl.pallas_call(functools.partial(prep_kernel, own, blocks), in_specs=[pl....  4.71 us
    unnamed x19, local copies, waits for them, and re-layouts  2.65 us
    pallas_call x1, Pallas kernels, local(): pl.pallas_call(functools.partial(gain_kernel, classes, node_count), in_sp...  2.08 us
  transfers between devices with their start and end apart: 17, of which 11 were waited for; matrix products, arithmetic and copies ran while one was open for 2% of the time, Pallas kernels for 29%

profile of v14, /device:TPU:0, one launch (start us, length us, event | category | flops | bytes accessed | tf_op | source)
XLA Modules:
  0.0 94.0 jit_solution(15421322165934759468)
XLA Ops:
  0.6 4.7 %shard_map.94 = (f32[32,3328]{1,0:T(8,128)}, f32[32,1664]{1,0:T(8,128)}, f32[1,3072]{1,0:T(1,128)}, s32[32,3072]{1,0:T(8,128)}, f32[64,1664]{1,0:T(8,128)}, /*in...) custom-call(s32[3072,128]{1,0:T(8,128)} %refs_0_.1, ...), custom_call_target="tpu_custom_call" | custom-call | flops 1000000 | bytes 1000000 | tf_op jit(solution)/shard_map/pallas_call | solution.py:347
  5.3 3.1 %collective-permute-start.2 = (f32[64,1664]{1,0:T(8,128)}, f32[64,1664]{1,0:T(8,128)S(1)}, u32[]{:S(2)}, u32[]{:S(2)}) collective-permute-start(f32[64,1664]{1,0:T(8,128)} %get-tuple-element.44), channel_id=1, source_target_pairs={{0,8},{2,10},{4,12},{6,14},{8,0},{10,2},{12,4},{14,6},{16,24},{18,... | collective-permute-start | bytes 1277960 | tf_op jit(solution)/shard_map/ppermute | solution.py:309
  8.4 2.6 %collective-permute-start.1 = (f32[32,1664]{1,0:T(8,128)}, f32[32,1664]{1,0:T(8,128)S(1)}, u32[]{:S(2)}, u32[]{:S(2)}) collective-permute-start(f32[32,1664]{1,0:T(8,128)} %get-tuple-element.43), channel_id=1, source_target_pairs={{0,16},{2,18},{4,20},{6,22},{8,24},{10,26},{12,28},{14,30},{16,0},... | collective-permute-start | bytes 638984 | tf_op jit(solution)/shard_map/ppermute | solution.py:309
  11.4 2.5 %collective-permute-start.4 = (s32[16,3456]{1,0:T(8,128)}, s32[16,3456]{1,0:T(8,128)S(1)}, u32[]{:S(2)}, u32[]{:S(2)}) collective-permute-start(s32[16,3456]{1,0:T(8,128)} %get-tuple-element.49), channel_id=1, source_target_pairs={{0,24},{2,26},{4,28},{6,30},{8,16},{10,18},{12,20},{14,22},{16,8},... | collective-permute-start | bytes 663560 | tf_op jit(solution)/shard_map/ppermute | solution.py:309
  15.8 6.7 %shard_map.95 = (f32[528,512]{1,0:T(8,128)S(1)}, f32[528,512]{1,0:T(8,128)S(1)}, f32[528,512]{1,0:T(8,128)S(1)}, f32[528,512]{1,0:T(8,128)S(1)}) custom-call(s32[32,3072]{1,0:T(8,128)S(1)} %copy-done.1, f32[32,3328]{1,0:T(8,128)S(1)} %copy-done), custom_call_target="tpu_custom_call" | custom-call | flops 1000000 | bytes 1000000 | tf_op jit(solution)/shard_map/pallas_call | solution.py:291
  23.6 3.3 %collective-permute-done.2.refs_0_.refs_1_ = f32[64,1664]{1,0:T(8,128)S(1)} collective-permute-done((f32[64,1664]{1,0:T(8,128)}, f32[64,1664]{1,0:T(8,128)S(1)}, u32[]{:S(2)}, u32[]{:S(2)}) %collective-permute-start.2) | collective-permute-done | bytes 426016 | tf_op jit(solution)/shard_map/ppermute | solution.py:309
  26.9 1.7 %collective-permute-start.6 = (f32[32,1664]{1,0:T(8,128)S(1)}, f32[32,1664]{1,0:T(8,128)S(1)}, u32[]{:S(2)}, u32[]{:S(2)}) collective-permute-start(f32[32,1664]{1,0:T(8,128)S(1)} %slice.36), channel_id=1, source_target_pairs={{0,1},{1,0},{2,3},{3,2},{4,5},{5,4},{6,7},{7,6},{8,9},{9,8},{10,11... | collective-permute-start | bytes 638984 | tf_op jit(solution)/shard_map/ppermute | solution.py:309
  29.1 1.8 %shard_map.96 = (f32[528,512]{1,0:T(8,128)S(1)}, f32[528,512]{1,0:T(8,128)S(1)}) custom-call(f32[64,1664]{1,0:T(8,128)S(1)} %collective-permute-done.2.refs_0_.refs_1_, f32[528,512]{1,0:T(8,128)S(1)} %get-tuple-element.52.refs_1_, f32[528,512]{1,0:T(8,128)S(1)} %get-tuple-element.53.refs_2_), custom_call_target="tpu_custom_call" | custom-call | flops 1000000 | bytes 1000000 | tf_op jit(solution)/shard_map/pallas_call | solution.py:291
  31.0 4.2 %collective-permute-done.6.refs_1_.refs_2_ = f32[32,1664]{1,0:T(8,128)S(1)} collective-permute-done((f32[32,1664]{1,0:T(8,128)S(1)}, f32[32,1664]{1,0:T(8,128)S(1)}, u32[]{:S(2)}, u32[]{:S(2)}) %collective-permute-start.6) | collective-permute-done | bytes 213024 | tf_op jit(solution)/shard_map/ppermute | solution.py:309
  35.2 1.8 %shard_map.97 = (f32[528,512]{1,0:T(8,128)S(1)}, f32[528,512]{1,0:T(8,128)S(1)}) custom-call(f32[64,1664]{1,0:T(8,128)S(1)} %collective-permute-done.2.refs_0_.refs_1_, f32[32,1664]{1,0:T(8,128)S(1)} %collective-permute-done.6.refs_1_.refs_2_, f32[528,512]{1,0:T(8,128)S(1)} %get-tuple-element.54.refs_2_, f32[528,512]{1,0:T(8,128)S(1)} %get-tuple-element.55.refs_3_), custom_call_target="tpu_custom_call" | custom-call | flops 1000000 | bytes 1000000 | tf_op jit(solution)/shard_map/pallas_call | solution.py:291
  37.0 1.8 %shard_map.98 = (f32[528,512]{1,0:T(8,128)S(1)}, f32[528,512]{1,0:T(8,128)S(1)}) custom-call(s32[16,3456]{1,0:T(8,128)S(1)} %collective-permute-done.5.refs_0_, f32[32,1664]{1,0:T(8,128)S(1)} %collective-permute-done.1.refs_1_, f32[528,512]{1,0:T(8,128)S(1)} %get-tuple-element.56.refs_2_, f32[528,512]{1,0:T(8,128)S(1)} %get-tuple-element.57.refs_3_), custom_call_target="tpu_custom_call" | custom-call | flops 1000000 | bytes 1000000 | tf_op jit(solution)/shard_map/pallas_call | solution.py:291
  40.7 1.8 %shard_map.99 = (f32[528,512]{1,0:T(8,128)S(1)}, f32[528,512]{1,0:T(8,128)S(1)}) custom-call(s32[16,3456]{1,0:T(8,128)S(1)} %collective-permute-done.5.refs_0_, f32[32,1664]{1,0:T(8,128)S(1)} %collective-permute-done.9.refs_1_.refs_2_, f32[528,512]{1,0:T(8,128)S(1)} %get-tuple-element.62.refs_2_, f32[528,512]{1,0:T(8,128)S(1)} %get-tuple-element.63.refs_3_), custom_call_target="tpu_custom_call" | custom-call | flops 1000000 | bytes 1000000 | tf_op jit(solution)/shard_map/pallas_call | solution.py:291
  42.5 2.0 %shard_map.100 = (f32[528,512]{1,0:T(8,128)S(1)}, f32[528,512]{1,0:T(8,128)S(1)}) custom-call(s32[16,3456]{1,0:T(8,128)S(1)} %collective-permute-done.4.refs_0_, f32[32,1664]{1,0:T(8,128)S(1)} %collective-permute-done.3.refs_1_, f32[528,512]{1,0:T(8,128)S(1)} %get-tuple-element.64.refs_2_, f32[528,512]{1,0:T(8,128)S(1)} %get-tuple-element.65.refs_3_), custom_call_target="tpu_custom_call" | custom-call | flops 1000000 | bytes 1000000 | tf_op jit(solution)/shard_map/pallas_call | solution.py:291
  47.5 3.6 %collective-permute-start.8 = (s32[16,3072]{1,0:T(8,128)S(1)}, s32[16,3072]{1,0:T(8,128)S(1)}, u32[]{:S(2)}, u32[]{:S(2)}) collective-permute-start(s32[16,3072]{1,0:T(8,128)S(1)} %copy-done.7), channel_id=1, source_target_pairs={{0,16},{2,18},{4,20},{6,22},{8,24},{10,26},{12,28},{14,30},{16,0},... | collective-permute-start | bytes 589832 | tf_op jit(solution)/shard_map/ppermute | solution.py:309
  52.7 1.6 %collective-permute-start.14 = (f32[528,512]{1,0:T(8,128)S(1)}, f32[528,512]{1,0:T(8,128)S(1)}, u32[]{:S(2)}, u32[]{:S(2)}) collective-permute-start(f32[528,512]{1,0:T(8,128)S(1)} %shard_map.102), channel_id=1, source_target_pairs={{0,4},{2,6},{4,0},{6,2},{8,12},{10,14},{12,8},{14,10},{16,20},{18,... | collective-permute-start | bytes 3244040 | tf_op jit(solution)/shard_map/ppermute | solution.py:309
  54.3 4.1 %collective-permute-done.11.refs_0_ = s32[16,3072]{1,0:T(8,128)S(1)} collective-permute-done((s32[16,3072]{1,0:T(8,128)S(1)}, s32[16,3072]{1,0:T(8,128)S(1)}, u32[]{:S(2)}, u32[]{:S(2)}) %collective-permute-start.11) | collective-permute-done | bytes 196640 | tf_op jit(solution)/shard_map/ppermute | solution.py:309
  58.3 3.5 %shard_map.103 = (f32[528,512]{1,0:T(8,128)S(1)}, f32[528,512]{1,0:T(8,128)S(1)}) custom-call(s32[16,3072]{1,0:T(8,128)S(1)} %collective-permute-done.11.refs_0_, f32[64,1664]{1,0:T(8,128)S(1)} %collective-permute-done.2.refs_0_.refs_1_, f32[32,1664]{1,0:T(8,128)S(1)} %collective-permute-done.6.refs_1_.refs_2_, f32[528,512]{1,0:T(8,128)S(1)} %get-tuple-element.70.refs_3_, ...), custom_call_target="tpu_custom_call" | custom-call | flops 1000000 | bytes 1000000 | tf_op jit(solution)/shard_map/pallas_call | solution.py:291
  61.8 3.4 %collective-permute-done.8.refs_0_ = s32[16,3072]{1,0:T(8,128)S(1)} collective-permute-done((s32[16,3072]{1,0:T(8,128)S(1)}, s32[16,3072]{1,0:T(8,128)S(1)}, u32[]{:S(2)}, u32[]{:S(2)}) %collective-permute-start.8) | collective-permute-done | bytes 196640 | tf_op jit(solution)/shard_map/ppermute | solution.py:309
  65.2 3.4 %shard_map.104 = (f32[528,512]{1,0:T(8,128)S(1)}, f32[528,512]{1,0:T(8,128)S(1)}) custom-call(s32[16,3072]{1,0:T(8,128)S(1)} %collective-permute-done.8.refs_0_, f32[32,1664]{1,0:T(8,128)S(1)} %collective-permute-done.1.refs_1_, f32[32,1664]{1,0:T(8,128)S(1)} %collective-permute-done.9.refs_1_.refs_2_, f32[528,512]{1,0:T(8,128)S(1)} %get-tuple-element.72.refs_3_, ...), custom_call_target="tpu_custom_call" | custom-call | flops 1000000 | bytes 1000000 | tf_op jit(solution)/shard_map/pallas_call | solution.py:291
  68.7 3.5 %shard_map.105 = (f32[528,512]{1,0:T(8,128)S(1)}, f32[528,512]{1,0:T(8,128)S(1)}) custom-call(s32[16,3072]{1,0:T(8,128)S(1)} %collective-permute-done.refs_0_, f32[32,1664]{1,0:T(8,128)S(1)} %collective-permute-done.3.refs_1_, f32[32,1664]{1,0:T(8,128)S(1)} %collective-permute-done.7.refs_1_.refs_2_, f32[528,512]{1,0:T(8,128)S(1)} %get-tuple-element.74.refs_3_, ...), custom_call_target="tpu_custom_call" | custom-call | flops 1000000 | bytes 1000000 | tf_op jit(solution)/shard_map/pallas_call | solution.py:291
  75.1 3.0 %collective-permute-done.14.refs_1_ = f32[528,512]{1,0:T(8,128)S(1)} collective-permute-done((f32[528,512]{1,0:T(8,128)S(1)}, f32[528,512]{1,0:T(8,128)S(1)}, u32[]{:S(2)}, u32[]{:S(2)}) %collective-permute-start.14) | collective-permute-done | bytes 1081376 | tf_op jit(solution)/shard_map/ppermute | solution.py:309
  78.1 2.1 %shard_map.106 = f32[8,8,128]{2,1,0:T(8,128)} custom-call(f32[528,512]{1,0:T(8,128)S(1)} %pad_maximum_fusion.refs_0_, f32[528,512]{1,0:T(8,128)S(1)} %collective-permute-done.14.refs_1_, f32[528,512]{1,0:T(8,128)S(1)} %get-tuple-element.77.refs_2_), custom_call_target="tpu_custom_call" | custom-call | flops 1000000 | bytes 1000000 | tf_op jit(solution)/shard_map/pallas_call | solution.py:447
  81.1 5.5 %all-to-all-start = ((f32[8,8,128]{2,1,0:T(8,128)}), f32[8,8,128]{2,1,0:T(8,128)S(1)}, u32[]{:S(2)}, u32[]{:S(2)}) async-start(f32[8,8,128]{2,1,0:T(8,128)} %shard_map.106), calls=%async_computation | async-start | bytes 65536 | tf_op jit(solution)/shard_map/all_to_all | solution.py:468
  88.0 5.4 %all-to-all-done = f32[8,8,128]{2,1,0:T(8,128)S(1)} async-done(((f32[8,8,128]{2,1,0:T(8,128)}), f32[8,8,128]{2,1,0:T(8,128)S(1)}, u32[]{:S(2)}, u32[]{:S(2)}) %all-to-all-start) | async-done | bytes 32800 | tf_op jit(solution)/shard_map/all_to_all | solution.py:468
  (53 shorter events, 15.9 us)
Async XLA Ops:
  5.3 21.6 %collective-permute-start.2 = (f32[64,1664]{1,0:T(8,128)}, f32[64,1664]{1,0:T(8,128)S(1)}, u32[]{:S(2)}, u32[]{:S(2)}) collective-permute-start(f32[64,1664]{1,0:T(8,128)} %get-tuple-element.44), channel_id=1, source_target_pairs={{0,8},{2,10},{4,12},{6,14},{8,0},{10,2},{12,4},{14,6},{16,24},{18,... | collective-permute-start | bytes 1277960 | tf_op jit(solution)/shard_map/ppermute | solution.py:309
  8.4 15.1 %collective-permute-start.1 = (f32[32,1664]{1,0:T(8,128)}, f32[32,1664]{1,0:T(8,128)S(1)}, u32[]{:S(2)}, u32[]{:S(2)}) collective-permute-start(f32[32,1664]{1,0:T(8,128)} %get-tuple-element.43), channel_id=1, source_target_pairs={{0,16},{2,18},{4,20},{6,22},{8,24},{10,26},{12,28},{14,30},{16,0},... | collective-permute-start | bytes 638984 | tf_op jit(solution)/shard_map/ppermute | solution.py:309
  11.0 26.0 %collective-permute-start.5 = (s32[16,3456]{1,0:T(8,128)}, s32[16,3456]{1,0:T(8,128)S(1)}, u32[]{:S(2)}, u32[]{:S(2)}) collective-permute-start(s32[16,3456]{1,0:T(8,128)} %get-tuple-element.50), channel_id=1, source_target_pairs={{0,16},{2,18},{4,20},{6,22},{8,24},{10,26},{12,28},{14,30},{16,0},... | collective-permute-start | bytes 663560 | tf_op jit(solution)/shard_map/ppermute | solution.py:309
  11.4 27.5 %collective-permute-start.4 = (s32[16,3456]{1,0:T(8,128)}, s32[16,3456]{1,0:T(8,128)S(1)}, u32[]{:S(2)}, u32[]{:S(2)}) collective-permute-start(s32[16,3456]{1,0:T(8,128)} %get-tuple-element.49), channel_id=1, source_target_pairs={{0,24},{2,26},{4,28},{6,30},{8,16},{10,18},{12,20},{14,22},{16,8},... | collective-permute-start | bytes 663560 | tf_op jit(solution)/shard_map/ppermute | solution.py:309
  26.9 8.3 %collective-permute-start.6 = (f32[32,1664]{1,0:T(8,128)S(1)}, f32[32,1664]{1,0:T(8,128)S(1)}, u32[]{:S(2)}, u32[]{:S(2)}) collective-permute-start(f32[32,1664]{1,0:T(8,128)S(1)} %slice.36), channel_id=1, source_target_pairs={{0,1},{1,0},{2,3},{3,2},{4,5},{5,4},{6,7},{7,6},{8,9},{9,8},{10,11... | collective-permute-start | bytes 638984 | tf_op jit(solution)/shard_map/ppermute | solution.py:309
  28.7 10.9 %collective-permute-start.3 = (f32[32,1664]{1,0:T(8,128)S(1)}, f32[32,1664]{1,0:T(8,128)S(1)}, u32[]{:S(2)}, u32[]{:S(2)}) collective-permute-start(f32[32,1664]{1,0:T(8,128)S(1)} %collective-permute-done.1.refs_1_), channel_id=1, source_target_pairs={{0,8},{2,10},{4,12},{6,14},{8,0},{10,2},{12,4},{14,6},{16,24},{18,... | collective-permute-start | bytes 638984 | tf_op jit(solution)/shard_map/ppermute | solution.py:309
  28.7 12.0 %collective-permute-start.9 = (f32[32,1664]{1,0:T(8,128)S(1)}, f32[32,1664]{1,0:T(8,128)S(1)}, u32[]{:S(2)}, u32[]{:S(2)}) collective-permute-start(f32[32,1664]{1,0:T(8,128)S(1)} %collective-permute-done.1.refs_1_), channel_id=1, source_target_pairs={{0,1},{1,0},{2,3},{3,2},{4,5},{5,4},{6,7},{7,6},{8,9},{9,8},{10,11... | collective-permute-start | bytes 638984 | tf_op jit(solution)/shard_map/ppermute | solution.py:309
  39.6 6.5 %collective-permute-start.7 = (f32[32,1664]{1,0:T(8,128)S(1)}, f32[32,1664]{1,0:T(8,128)S(1)}, u32[]{:S(2)}, u32[]{:S(2)}) collective-permute-start(f32[32,1664]{1,0:T(8,128)S(1)} %collective-permute-done.3.refs_1_), channel_id=1, source_target_pairs={{0,1},{1,0},{2,3},{3,2},{4,5},{5,4},{6,7},{7,6},{8,9},{9,8},{10,11... | collective-permute-start | bytes 638984 | tf_op jit(solution)/shard_map/ppermute | solution.py:309
  46.0 1.1 %copy-start.8 = (s32[16,3072]{1,0:T(8,128)S(1)}, s32[16,3072]{1,0:T(8,128)}, u32[]{:S(2)}) copy-start(s32[16,3072]{1,0:T(8,128)} %get-tuple-element.68) | copy-start | bytes 589828
  46.0 1.4 %copy-start.7 = (s32[16,3072]{1,0:T(8,128)S(1)}, s32[16,3072]{1,0:T(8,128)}, u32[]{:S(2)}) copy-start(s32[16,3072]{1,0:T(8,128)} %get-tuple-element.60) | copy-start | bytes 589828
  46.1 5.0 %copy-start.6 = (s32[16,3072]{1,0:T(8,128)S(1)}, s32[16,3072]{1,0:T(8,128)}, u32[]{:S(2)}) copy-start(s32[16,3072]{1,0:T(8,128)} %get-tuple-element.42) | copy-start | bytes 589828
  47.1 4.6 %collective-permute-start.10 = (f32[528,512]{1,0:T(8,128)S(1)}, f32[528,512]{1,0:T(8,128)S(1)}, u32[]{:S(2)}, u32[]{:S(2)}) collective-permute-start(f32[528,512]{1,0:T(8,128)S(1)} %shard_map.101), channel_id=1, source_target_pairs={{0,2},{2,0},{4,6},{6,4},{8,10},{10,8},{12,14},{14,12},{16,18},{18,... | collective-permute-start | bytes 3244040 | tf_op jit(solution)/shard_map/ppermute | solution.py:309
  47.2 11.2 %collective-permute-start.11 = (s32[16,3072]{1,0:T(8,128)S(1)}, s32[16,3072]{1,0:T(8,128)S(1)}, u32[]{:S(2)}, u32[]{:S(2)}) collective-permute-start(s32[16,3072]{1,0:T(8,128)S(1)} %copy-done.8), channel_id=1, source_target_pairs={{0,8},{2,10},{4,12},{6,14},{8,0},{10,2},{12,4},{14,6},{16,24},{18,... | collective-permute-start | bytes 589832 | tf_op jit(solution)/shard_map/ppermute | solution.py:309
  47.5 17.7 %collective-permute-start.8 = (s32[16,3072]{1,0:T(8,128)S(1)}, s32[16,3072]{1,0:T(8,128)S(1)}, u32[]{:S(2)}, u32[]{:S(2)}) collective-permute-start(s32[16,3072]{1,0:T(8,128)S(1)} %copy-done.7), channel_id=1, source_target_pairs={{0,16},{2,18},{4,20},{6,22},{8,24},{10,26},{12,28},{14,30},{16,0},... | collective-permute-start | bytes 589832 | tf_op jit(solution)/shard_map/ppermute | solution.py:309
  51.1 17.6 %collective-permute-start = (s32[16,3072]{1,0:T(8,128)S(1)}, s32[16,3072]{1,0:T(8,128)S(1)}, u32[]{:S(2)}, u32[]{:S(2)}) collective-permute-start(s32[16,3072]{1,0:T(8,128)S(1)} %copy-done.6), channel_id=1, source_target_pairs={{0,24},{2,26},{4,28},{6,30},{8,16},{10,18},{12,20},{14,22},{16,8},... | collective-permute-start | bytes 589832 | tf_op jit(solution)/shard_map/ppermute | solution.py:309
  52.7 25.4 %collective-permute-start.14 = (f32[528,512]{1,0:T(8,128)S(1)}, f32[528,512]{1,0:T(8,128)S(1)}, u32[]{:S(2)}, u32[]{:S(2)}) collective-permute-start(f32[528,512]{1,0:T(8,128)S(1)} %shard_map.102), channel_id=1, source_target_pairs={{0,4},{2,6},{4,0},{6,2},{8,12},{10,14},{12,8},{14,10},{16,20},{18,... | collective-permute-start | bytes 3244040 | tf_op jit(solution)/shard_map/ppermute | solution.py:309
  72.2 2.0 %collective-permute-start.13 = (f32[264,512]{1,0:T(8,128)S(1)}, f32[264,512]{1,0:T(8,128)S(1)}, u32[]{:S(2)}, u32[]{:S(2)}) collective-permute-start(f32[264,512]{1,0:T(8,128)S(1)} %get-tuple-element.81), channel_id=1, source_target_pairs={{0,2},{2,0},{4,6},{6,4},{8,10},{10,8},{12,14},{14,12},{16,18},{18,... | collective-permute-start | bytes 1622024 | tf_op jit(solution)/shard_map/ppermute | solution.py:309
  72.3 2.7 %collective-permute-start.12 = (f32[264,512]{1,0:T(8,128)S(1)}, f32[264,512]{1,0:T(8,128)S(1)}, u32[]{:S(2)}, u32[]{:S(2)}) collective-permute-start(f32[264,512]{1,0:T(8,128)S(1)} %get-tuple-element.82), channel_id=1, source_target_pairs={{0,2},{2,0},{4,6},{6,4},{8,10},{10,8},{12,14},{14,12},{16,18},{18,... | collective-permute-start | bytes 1622024 | tf_op jit(solution)/shard_map/ppermute | solution.py:309
  78.1 2.1 %copy-start.4 = (f32[1,3072]{1,0:T(1,128)S(1)}, f32[1,3072]{1,0:T(1,128)}, u32[]{:S(2)}) copy-start(f32[1,3072]{1,0:T(1,128)} %get-tuple-element.79) | copy-start | bytes 36868
  78.1 8.7 %copy-start.3 = (s32[3072]{0:T(1024)S(1)}, s32[3072]{0:T(1024)}, u32[]{:S(2)}) copy-start(s32[3072]{0:T(1024)} %param.9) | copy-start | bytes 36868
  78.1 8.8 %copy-start.2 = (f32[3072,32]{0,1:T(8,128)S(1)}, f32[3072,32]{0,1:T(8,128)}, u32[]{:S(2)}) copy-start(f32[3072,32]{0,1:T(8,128)} %param.7) | copy-start | bytes 1179652
  80.2 6.5 %collective-permute-start.15 = (f32[32,128]{1,0:T(8,128)S(1)}, f32[32,128]{1,0:T(8,128)S(1)}, u32[]{:S(2)}, u32[]{:S(2)}) collective-permute-start(f32[32,128]{1,0:T(8,128)S(1)} %pad_maximum_fusion.1), channel_id=1, source_target_pairs={{0,1},{1,0},{2,3},{3,2},{4,5},{5,4},{6,7},{7,6},{8,9},{9,8},{10,11... | collective-permute-start | bytes 49160 | tf_op jit(solution)/shard_map/ppermute | solution.py:309
  81.1 12.2 %all-to-all-start = ((f32[8,8,128]{2,1,0:T(8,128)}), f32[8,8,128]{2,1,0:T(8,128)S(1)}, u32[]{:S(2)}, u32[]{:S(2)}) async-start(f32[8,8,128]{2,1,0:T(8,128)} %shard_map.106), calls=%async_computation | async-start | bytes 65536 | tf_op jit(solution)/shard_map/all_to_all | solution.py:468
  86.9 7.1 %copy-start.5 = (f32[8,2,32]{2,1,0:T(2,128)}, f32[8,2,32]{2,1,0:T(2,128)S(1)}, u32[]{:S(2)}) copy-start(f32[8,2,32]{2,1,0:T(2,128)S(1)} %fusion.5) | copy-start | bytes 6148
  (2 other events, 2.0 us)

commit v15 on v13

--- a/solution.py
+++ b/solution.py
@@ -208,11 +208,16 @@
             gain_ref[n, 2 * pair + 1 : 2 * pair + 2, :] = gain[:, 2 * BINS :]
 
 
-def add_kernel(classes, node_count, own, plan, carry, *refs):
+def add_kernel(classes, node_count, own, plan, carry, cuts, *refs):
     outs = len(plan[0][3])
     arrays = 1 + max(max((c,) + tuple(j for j in i if j is not None)) for _, c, i, _ in plan)
-    out_refs = refs[-outs:]
-    held_refs = refs[arrays:-outs]
+    if cuts is None:
+        piece_refs, out_refs = None, refs[-outs:]
+        held_refs = refs[arrays:-outs]
+    else:
+        out_refs = refs[-outs:]
+        piece_refs = refs[-outs - sum(cuts) : -outs]
+        held_refs = refs[arrays : -outs - sum(cuts)]
     pairs = 2 * classes * node_count
     row_index, feat_index = lax.axis_index("rows"), lax.axis_index("feat")
     for s, (m, codes_at, info_at, firsts) in enumerate(plan):
@@ -275,25 +280,42 @@
             for i in range(out_ref.shape[1] // LANES):
                 here = jnp.where((row_index & 3) == i, 1.0, 0.0)
                 out_ref[band, i * LANES : (i + 1) * LANES] += here * sums
-
-
-def add_rows(classes, node_count, own, carry, plan, arrays, *held):
+    if cuts is not None:
+        for out_ref, cut in zip(out_refs, cuts):
+            rows = out_ref.shape[0] // cut
+            for i in range(cut):
+                piece_refs[i][...] = out_ref[i * rows : (i + 1) * rows, :]
+            piece_refs = piece_refs[cut:]
+
+
+def add_rows(classes, node_count, own, carry, plan, arrays, *held, cuts=None):
     shape = (2 * classes * node_count + 2 * node_count, own * BINS)
     whole = pl.BlockSpec(memory_space=pltpu.VMEM)
     outs = len(plan[0][3])
+    heights = [shape[0]] * outs
+    if cuts is not None:
+        heights = [shape[0] // cut for cut in cuts for _ in range(cut)]
     return pl.pallas_call(
-        functools.partial(add_kernel, classes, node_count, own, plan, carry),
+        functools.partial(add_kernel, classes, node_count, own, plan, carry, cuts),
         in_specs=[whole] * (len(arrays) + len(held) * outs),
-        out_specs=[whole] * outs,
-        out_shape=[jax.ShapeDtypeStruct(shape, jnp.float32)] * outs,
+        out_specs=[whole] * len(heights),
+        out_shape=[jax.ShapeDtypeStruct((height, shape[1]), jnp.float32) for height in heights],
+        scratch_shapes=[] if cuts is None else [pltpu.VMEM(shape, jnp.float32)] * outs,
         compiler_params=pltpu.CompilerParams(vmem_limit_bytes=VMEM_BYTES),
         cost_estimate=SMALL_COST,
     )(*arrays, *[hist for hists in held for hist in hists])
 
 
-def gain_kernel(classes, node_count, *refs):
+def gain_kernel(classes, node_count, cuts, *refs):
     gain_ref, hist_ref = refs[-2:]
-    hist_ref[...] = sum(ref[: hist_ref.shape[0], :] for ref in refs[:-2])
+    pairs = hist_ref.shape[0]
+    for i, cut in enumerate(cuts):
+        pieces, refs = refs[:cut], refs[cut:]
+        rows = pieces[0].shape[0]
+        for j, piece in enumerate(pieces):
+            low, high = j * rows, min((j + 1) * rows, pairs)
+            part = piece[: high - low, :]
+            hist_ref[low:high, :] = part if i == 0 else hist_ref[low:high, :] + part
     write_gains(hist_ref, gain_ref, classes, node_count)
 
 
@@ -424,31 +446,34 @@
     hist_a, hist_b = add(((12, 0, (1, None), (0, own)),), [codes_12, near_12], [hist_a, hist_b])
     (to_core,) = add(((12, 0, (None, 1), (0,)),), [codes_12, far_12], [hist_a])
     from_core = swap(to_core, "rows", 1)
-    (to_plane,) = add(((12, 0, (None, 1), (own,)),), [codes_12, far_12], [hist_b], [from_core])
-    from_plane = swap(to_plane, "rows", 2)
+    to_plane = add(
+        ((12, 0, (None, 1), (own,)),), [codes_12, far_12], [hist_b], [from_core], cuts=(2,)
+    )
+    from_plane = [swap(piece, "rows", 2) for piece in to_plane]
     _, late_4 = lax.optimization_barrier((to_plane, late_4))
     hists = add(((4, 0, (1, 2), (0, own)),), [late_4, rows_4, far_4], [hist_c, hist_d])
     hists = add(((8, 0, (1, 2), (0, own)),), [late_8, near_8, far_8], hists)
-    to_core, kept = add(((12, 0, (1, 2), (0, own)),), [late_12, near_12, far_12], hists)
-    middle = to_core.shape[0] // 2
-    from_core = [swap(part, "rows", 1) for part in (to_core[:middle], to_core[middle:])]
-    from_core = jnp.concatenate(from_core, axis=0)
+    *to_core, kept = add(
+        ((12, 0, (1, 2), (0, own)),), [late_12, near_12, far_12], hists, cuts=(3, 1)
+    )
+    from_core = [swap(piece, "rows", 1) for piece in to_core]
 
     pairs = node_count * width
     gains = pl.pallas_call(
-        functools.partial(gain_kernel, classes, node_count),
-        in_specs=[pl.BlockSpec(memory_space=pltpu.VMEM)] * 3,
+        functools.partial(gain_kernel, classes, node_count, (1, len(from_core), len(from_plane))),
+        in_specs=[pl.BlockSpec(memory_space=pltpu.VMEM)] * (1 + len(from_core) + len(from_plane)),
         out_specs=pl.BlockSpec(memory_space=pltpu.VMEM),
         out_shape=jax.ShapeDtypeStruct((node_count, own, 2 * BINS), jnp.float32),
         scratch_shapes=[pltpu.VMEM((pairs, own * BINS), jnp.float32)],
         compiler_params=pltpu.CompilerParams(vmem_limit_bytes=VMEM_BYTES),
         cost_estimate=SMALL_COST,
-    )(from_core, from_plane, kept)
+    )(kept, *from_core, *from_plane)
     def gather(parts):
         return jnp.sum(parts.reshape(2, node_count, -1, LANES), axis=(0, 2))
 
     gains, from_plane = lax.optimization_barrier((gains, from_plane))
-    sums = gather(from_core[pairs:] + from_plane[pairs:] + kept[pairs:])
+    low = -2 * node_count
+    sums = gather(from_core[-1][low:] + from_plane[-1][low:] + kept[low:])
     children = jnp.concatenate([sums, flags.reshape(-1, LANES)], axis=0)
     children = sum_over(children, "feat")
     side_count = children[node_count:].reshape(1, rows_dev)

time: 93.5 us -> 93.5 us (level)
    ppermute x16 -> x18, starting transfers between devices: 19.4 us -> 20 us  [swap(): return lax.ppermute(x, axis, [(i, i ^ bit) for i in range(size)])]
    ppermute x16 -> x18, waiting for transfers between devices: 23.5 us -> 23 us  [swap(): return lax.ppermute(x, axis, [(i, i ^ bit) for i in range(size)])]
  transfers between devices with their start and end apart: 17 -> 19, of which waited for: 11 -> 12; matrix products, arithmetic and copies ran while one was open for 2% -> 1% of each run, Pallas kernels for 29% -> 30%
where the time goes in v15:
time: 93.5 us; the launch traced here: 93.2 us
  Pallas kernels  34.6 us (37%)
  waiting for transfers between devices  28.3 us (30%)
  starting transfers between devices  25.5 us (27%)
  local copies, waits for them, and re-layouts  2.73 us (3%)
  matrix products  1.11 us (1%)
    pallas_call x11, Pallas kernels, add_rows(): pl.pallas_call(functools.partial(add_kernel, classes, node_count, own, pl...  28.6 us
    ppermute x18, waiting for transfers between devices, swap(): return lax.ppermute(x, axis, [(i, i ^ bit) for i in range(size)])  23 us
    ppermute x18, starting transfers between devices, swap(): return lax.ppermute(x, axis, [(i, i ^ bit) for i in range(size)])  20 us
    all_to_all x1, starting transfers between devices, local(): lax.all_to_all(gains, 'rows', 0, 0, tiled=True, axis_index_groups=halves)  5.54 us
    all_to_all x1, waiting for transfers between devices, local(): lax.all_to_all(gains, 'rows', 0, 0, tiled=True, axis_index_groups=halves)  5.36 us
    pallas_call x1, Pallas kernels, prepare(): pl.pallas_call(functools.partial(prep_kernel, own, blocks), in_specs=[pl....  3.97 us
    unnamed x19, local copies, waits for them, and re-layouts  2.65 us
    pallas_call x1, Pallas kernels, local(): pl.pallas_call(functools.partial(gain_kernel, classes, node_count, (1, le...  2.08 us
  transfers between devices with their start and end apart: 19, of which 12 were waited for; matrix products, arithmetic and copies ran while one was open for 1% of the time, Pallas kernels for 30%

profile of v15, /device:TPU:0, one launch (start us, length us, event | category | flops | bytes accessed | tf_op | source)
XLA Modules:
  0.0 93.2 jit_solution(2352102215089250212)
XLA Ops:
  0.6 4.0 %shard_map.94 = (f32[32,3328]{1,0:T(8,128)}, f32[32,1664]{1,0:T(8,128)}, f32[1,3072]{1,0:T(1,128)}, s32[32,3072]{1,0:T(8,128)}, f32[64,1664]{1,0:T(8,128)}, /*in...) custom-call(s32[3072,128]{1,0:T(8,128)} %refs_0_.1, ...), custom_call_target="tpu_custom_call" | custom-call | flops 1000000 | bytes 1000000 | tf_op jit(solution)/shard_map/pallas_call | solution.py:361
  4.6 3.1 %collective-permute-start.2 = (f32[64,1664]{1,0:T(8,128)}, f32[64,1664]{1,0:T(8,128)S(1)}, u32[]{:S(2)}, u32[]{:S(2)}) collective-permute-start(f32[64,1664]{1,0:T(8,128)} %get-tuple-element.48), channel_id=1, source_target_pairs={{0,8},{2,10},{4,12},{6,14},{8,0},{10,2},{12,4},{14,6},{16,24},{18,... | collective-permute-start | bytes 1277960 | tf_op jit(solution)/shard_map/ppermute | solution.py:324
  7.7 2.6 %collective-permute-start.1 = (f32[32,1664]{1,0:T(8,128)}, f32[32,1664]{1,0:T(8,128)S(1)}, u32[]{:S(2)}, u32[]{:S(2)}) collective-permute-start(f32[32,1664]{1,0:T(8,128)} %get-tuple-element.47), channel_id=1, source_target_pairs={{0,16},{2,18},{4,20},{6,22},{8,24},{10,26},{12,28},{14,30},{16,0},... | collective-permute-start | bytes 638984 | tf_op jit(solution)/shard_map/ppermute | solution.py:324
  10.6 2.5 %collective-permute-start.4 = (s32[16,3456]{1,0:T(8,128)}, s32[16,3456]{1,0:T(8,128)S(1)}, u32[]{:S(2)}, u32[]{:S(2)}) collective-permute-start(s32[16,3456]{1,0:T(8,128)} %get-tuple-element.53), channel_id=1, source_target_pairs={{0,24},{2,26},{4,28},{6,30},{8,16},{10,18},{12,20},{14,22},{16,8},... | collective-permute-start | bytes 663560 | tf_op jit(solution)/shard_map/ppermute | solution.py:324
  15.1 6.7 %shard_map.95 = (f32[528,512]{1,0:T(8,128)S(1)}, f32[528,512]{1,0:T(8,128)S(1)}, f32[528,512]{1,0:T(8,128)S(1)}, f32[528,512]{1,0:T(8,128)S(1)}) custom-call(s32[32,3072]{1,0:T(8,128)S(1)} %copy-done.1, f32[32,3328]{1,0:T(8,128)S(1)} %copy-done), custom_call_target="tpu_custom_call" | custom-call | flops 1000000 | bytes 1000000 | tf_op jit(solution)/shard_map/pallas_call | solution.py:298
  22.8 3.3 %collective-permute-done.2.refs_0_.refs_1_ = f32[64,1664]{1,0:T(8,128)S(1)} collective-permute-done((f32[64,1664]{1,0:T(8,128)}, f32[64,1664]{1,0:T(8,128)S(1)}, u32[]{:S(2)}, u32[]{:S(2)}) %collective-permute-start.2) | collective-permute-done | bytes 426016 | tf_op jit(solution)/shard_map/ppermute | solution.py:324
  26.2 1.7 %collective-permute-start.6 = (f32[32,1664]{1,0:T(8,128)S(1)}, f32[32,1664]{1,0:T(8,128)S(1)}, u32[]{:S(2)}, u32[]{:S(2)}) collective-permute-start(f32[32,1664]{1,0:T(8,128)S(1)} %slice.30), channel_id=1, source_target_pairs={{0,1},{1,0},{2,3},{3,2},{4,5},{5,4},{6,7},{7,6},{8,9},{9,8},{10,11... | collective-permute-start | bytes 638984 | tf_op jit(solution)/shard_map/ppermute | solution.py:324
  28.4 1.8 %shard_map.96 = (f32[528,512]{1,0:T(8,128)S(1)}, f32[528,512]{1,0:T(8,128)S(1)}) custom-call(f32[64,1664]{1,0:T(8,128)S(1)} %collective-permute-done.2.refs_0_.refs_1_, f32[528,512]{1,0:T(8,128)S(1)} %get-tuple-element.56.refs_1_, f32[528,512]{1,0:T(8,128)S(1)} %get-tuple-element.57.refs_2_), custom_call_target="tpu_custom_call" | custom-call | flops 1000000 | bytes 1000000 | tf_op jit(solution)/shard_map/pallas_call | solution.py:298
  30.3 4.2 %collective-permute-done.6.refs_1_.refs_2_ = f32[32,1664]{1,0:T(8,128)S(1)} collective-permute-done((f32[32,1664]{1,0:T(8,128)S(1)}, f32[32,1664]{1,0:T(8,128)S(1)}, u32[]{:S(2)}, u32[]{:S(2)}) %collective-permute-start.6) | collective-permute-done | bytes 213024 | tf_op jit(solution)/shard_map/ppermute | solution.py:324
  34.5 1.8 %shard_map.97 = (f32[528,512]{1,0:T(8,128)S(1)}, f32[528,512]{1,0:T(8,128)S(1)}) custom-call(f32[64,1664]{1,0:T(8,128)S(1)} %collective-permute-done.2.refs_0_.refs_1_, f32[32,1664]{1,0:T(8,128)S(1)} %collective-permute-done.6.refs_1_.refs_2_, f32[528,512]{1,0:T(8,128)S(1)} %get-tuple-element.58.refs_2_, f32[528,512]{1,0:T(8,128)S(1)} %get-tuple-element.59.refs_3_), custom_call_target="tpu_custom_call" | custom-call | flops 1000000 | bytes 1000000 | tf_op jit(solution)/shard_map/pallas_call | solution.py:298
  36.3 1.8 %shard_map.98 = (f32[528,512]{1,0:T(8,128)S(1)}, f32[528,512]{1,0:T(8,128)S(1)}) custom-call(s32[16,3456]{1,0:T(8,128)S(1)} %collective-permute-done.5.refs_0_, f32[32,1664]{1,0:T(8,128)S(1)} %collective-permute-done.1.refs_1_, f32[528,512]{1,0:T(8,128)S(1)} %get-tuple-element.60.refs_2_, f32[528,512]{1,0:T(8,128)S(1)} %get-tuple-element.61.refs_3_), custom_call_target="tpu_custom_call" | custom-call | flops 1000000 | bytes 1000000 | tf_op jit(solution)/shard_map/pallas_call | solution.py:298
  39.9 1.8 %shard_map.99 = (f32[528,512]{1,0:T(8,128)S(1)}, f32[528,512]{1,0:T(8,128)S(1)}) custom-call(s32[16,3456]{1,0:T(8,128)S(1)} %collective-permute-done.5.refs_0_, f32[32,1664]{1,0:T(8,128)S(1)} %collective-permute-done.9.refs_1_.refs_2_, f32[528,512]{1,0:T(8,128)S(1)} %get-tuple-element.66.refs_2_, f32[528,512]{1,0:T(8,128)S(1)} %get-tuple-element.67.refs_3_), custom_call_target="tpu_custom_call" | custom-call | flops 1000000 | bytes 1000000 | tf_op jit(solution)/shard_map/pallas_call | solution.py:298
  41.8 2.0 %shard_map.100 = (f32[528,512]{1,0:T(8,128)S(1)}, f32[528,512]{1,0:T(8,128)S(1)}) custom-call(s32[16,3456]{1,0:T(8,128)S(1)} %collective-permute-done.4.refs_0_, f32[32,1664]{1,0:T(8,128)S(1)} %collective-permute-done.3.refs_1_, f32[528,512]{1,0:T(8,128)S(1)} %get-tuple-element.68.refs_2_, f32[528,512]{1,0:T(8,128)S(1)} %get-tuple-element.69.refs_3_), custom_call_target="tpu_custom_call" | custom-call | flops 1000000 | bytes 1000000 | tf_op jit(solution)/shard_map/pallas_call | solution.py:298
  46.7 3.6 %collective-permute-start.8 = (s32[16,3072]{1,0:T(8,128)S(1)}, s32[16,3072]{1,0:T(8,128)S(1)}, u32[]{:S(2)}, u32[]{:S(2)}) collective-permute-start(s32[16,3072]{1,0:T(8,128)S(1)} %copy-done.7), channel_id=1, source_target_pairs={{0,16},{2,18},{4,20},{6,22},{8,24},{10,26},{12,28},{14,30},{16,0},... | collective-permute-start | bytes 589832 | tf_op jit(solution)/shard_map/ppermute | solution.py:324
  51.9 1.6 %collective-permute-start.15 = (f32[264,512]{1,0:T(8,128)S(1)}, f32[264,512]{1,0:T(8,128)S(1)}, u32[]{:S(2)}, u32[]{:S(2)}) collective-permute-start(f32[264,512]{1,0:T(8,128)S(1)} %get-tuple-element.72), channel_id=1, source_target_pairs={{0,4},{2,6},{4,0},{6,2},{8,12},{10,14},{12,8},{14,10},{16,20},{18,... | collective-permute-start | bytes 1622024 | tf_op jit(solution)/shard_map/ppermute | solution.py:324
  54.0 3.6 %collective-permute-done.11.refs_0_ = s32[16,3072]{1,0:T(8,128)S(1)} collective-permute-done((s32[16,3072]{1,0:T(8,128)S(1)}, s32[16,3072]{1,0:T(8,128)S(1)}, u32[]{:S(2)}, u32[]{:S(2)}) %collective-permute-start.11) | collective-permute-done | bytes 196640 | tf_op jit(solution)/shard_map/ppermute | solution.py:324
  57.6 3.5 %shard_map.103 = (f32[528,512]{1,0:T(8,128)S(1)}, f32[528,512]{1,0:T(8,128)S(1)}) custom-call(s32[16,3072]{1,0:T(8,128)S(1)} %collective-permute-done.11.refs_0_, f32[64,1664]{1,0:T(8,128)S(1)} %collective-permute-done.2.refs_0_.refs_1_, f32[32,1664]{1,0:T(8,128)S(1)} %collective-permute-done.6.refs_1_.refs_2_, f32[528,512]{1,0:T(8,128)S(1)} %get-tuple-element.76.refs_3_, ...), custom_call_target="tpu_custom_call" | custom-call | flops 1000000 | bytes 1000000 | tf_op jit(solution)/shard_map/pallas_call | solution.py:298
  61.1 3.4 %collective-permute-done.8.refs_0_ = s32[16,3072]{1,0:T(8,128)S(1)} collective-permute-done((s32[16,3072]{1,0:T(8,128)S(1)}, s32[16,3072]{1,0:T(8,128)S(1)}, u32[]{:S(2)}, u32[]{:S(2)}) %collective-permute-start.8) | collective-permute-done | bytes 196640 | tf_op jit(solution)/shard_map/ppermute | solution.py:324
  64.5 3.4 %shard_map.104 = (f32[528,512]{1,0:T(8,128)S(1)}, f32[528,512]{1,0:T(8,128)S(1)}) custom-call(s32[16,3072]{1,0:T(8,128)S(1)} %collective-permute-done.8.refs_0_, f32[32,1664]{1,0:T(8,128)S(1)} %collective-permute-done.1.refs_1_, f32[32,1664]{1,0:T(8,128)S(1)} %collective-permute-done.9.refs_1_.refs_2_, f32[528,512]{1,0:T(8,128)S(1)} %get-tuple-element.78.refs_3_, ...), custom_call_target="tpu_custom_call" | custom-call | flops 1000000 | bytes 1000000 | tf_op jit(solution)/shard_map/pallas_call | solution.py:298
  67.9 3.6 %shard_map.105 = (f32[176,512]{1,0:T(8,128)S(1)}, f32[176,512]{1,0:T(8,128)S(1)}, f32[176,512]{1,0:T(8,128)S(1)}, f32[528,512]{1,0:T(8,128)S(1)}) custom-call(s32[16,3072]{1,0:T(8,128)S(1)} %collective-permute-done.refs_0_, f32[32,1664]{1,0:T(8,128)S(1)} %collective-permute-done.3.refs_1_, f32[32,1664]{1,0:T(8,128)S(1)} %collective-permute-done.7.refs_1_.refs_2_, ...), custom_call_target="tpu_custom_call" | custom-call | flops 1000000 | bytes 1000000 | tf_op jit(solution)/shard_map/pallas_call | solution.py:298
  74.3 3.1 %collective-permute-done.16.refs_5_ = f32[264,512]{1,0:T(8,128)S(1)} collective-permute-done((f32[264,512]{1,0:T(8,128)S(1)}, f32[264,512]{1,0:T(8,128)S(1)}, u32[]{:S(2)}, u32[]{:S(2)}) %collective-permute-start.16) | collective-permute-done | bytes 540704 | tf_op jit(solution)/shard_map/ppermute | solution.py:324
  77.4 2.1 %shard_map.106 = f32[8,8,128]{2,1,0:T(8,128)} custom-call(f32[528,512]{1,0:T(8,128)S(1)} %get-tuple-element.83.refs_0_, f32[176,512]{1,0:T(8,128)S(1)} %collective-permute-done.13.refs_1_, f32[176,512]{1,0:T(8,128)S(1)} %collective-permute-done.14.refs_2_, f32[176,512]{1,0:T(8,128)S(1)} %collective-permute-done.12.refs_3_, ...), custom_call_target="tpu_custom_call" | custom-call | flops 1000000 | bytes 1000000 | tf_op jit(solution)/shard_map/pallas_call | solution.py:462
  80.4 5.5 %all-to-all-start = ((f32[8,8,128]{2,1,0:T(8,128)}), f32[8,8,128]{2,1,0:T(8,128)S(1)}, u32[]{:S(2)}, u32[]{:S(2)}) async-start(f32[8,8,128]{2,1,0:T(8,128)} %shard_map.106), calls=%async_computation | async-start | bytes 65536 | tf_op jit(solution)/shard_map/all_to_all | solution.py:484
  87.3 5.4 %all-to-all-done = f32[8,8,128]{2,1,0:T(8,128)S(1)} async-done(((f32[8,8,128]{2,1,0:T(8,128)}), f32[8,8,128]{2,1,0:T(8,128)S(1)}, u32[]{:S(2)}, u32[]{:S(2)}) %all-to-all-start) | async-done | bytes 32800 | tf_op jit(solution)/shard_map/all_to_all | solution.py:484
  (55 shorter events, 16.3 us)
Async XLA Ops:
  4.6 21.6 %collective-permute-start.2 = (f32[64,1664]{1,0:T(8,128)}, f32[64,1664]{1,0:T(8,128)S(1)}, u32[]{:S(2)}, u32[]{:S(2)}) collective-permute-start(f32[64,1664]{1,0:T(8,128)} %get-tuple-element.48), channel_id=1, source_target_pairs={{0,8},{2,10},{4,12},{6,14},{8,0},{10,2},{12,4},{14,6},{16,24},{18,... | collective-permute-start | bytes 1277960 | tf_op jit(solution)/shard_map/ppermute | solution.py:324
  7.7 15.1 %collective-permute-start.1 = (f32[32,1664]{1,0:T(8,128)}, f32[32,1664]{1,0:T(8,128)S(1)}, u32[]{:S(2)}, u32[]{:S(2)}) collective-permute-start(f32[32,1664]{1,0:T(8,128)} %get-tuple-element.47), channel_id=1, source_target_pairs={{0,16},{2,18},{4,20},{6,22},{8,24},{10,26},{12,28},{14,30},{16,0},... | collective-permute-start | bytes 638984 | tf_op jit(solution)/shard_map/ppermute | solution.py:324
  10.3 26.0 %collective-permute-start.5 = (s32[16,3456]{1,0:T(8,128)}, s32[16,3456]{1,0:T(8,128)S(1)}, u32[]{:S(2)}, u32[]{:S(2)}) collective-permute-start(s32[16,3456]{1,0:T(8,128)} %get-tuple-element.54), channel_id=1, source_target_pairs={{0,16},{2,18},{4,20},{6,22},{8,24},{10,26},{12,28},{14,30},{16,0},... | collective-permute-start | bytes 663560 | tf_op jit(solution)/shard_map/ppermute | solution.py:324
  10.6 27.5 %collective-permute-start.4 = (s32[16,3456]{1,0:T(8,128)}, s32[16,3456]{1,0:T(8,128)S(1)}, u32[]{:S(2)}, u32[]{:S(2)}) collective-permute-start(s32[16,3456]{1,0:T(8,128)} %get-tuple-element.53), channel_id=1, source_target_pairs={{0,24},{2,26},{4,28},{6,30},{8,16},{10,18},{12,20},{14,22},{16,8},... | collective-permute-start | bytes 663560 | tf_op jit(solution)/shard_map/ppermute | solution.py:324
  26.2 8.3 %collective-permute-start.6 = (f32[32,1664]{1,0:T(8,128)S(1)}, f32[32,1664]{1,0:T(8,128)S(1)}, u32[]{:S(2)}, u32[]{:S(2)}) collective-permute-start(f32[32,1664]{1,0:T(8,128)S(1)} %slice.30), channel_id=1, source_target_pairs={{0,1},{1,0},{2,3},{3,2},{4,5},{5,4},{6,7},{7,6},{8,9},{9,8},{10,11... | collective-permute-start | bytes 638984 | tf_op jit(solution)/shard_map/ppermute | solution.py:324
  27.9 10.9 %collective-permute-start.3 = (f32[32,1664]{1,0:T(8,128)S(1)}, f32[32,1664]{1,0:T(8,128)S(1)}, u32[]{:S(2)}, u32[]{:S(2)}) collective-permute-start(f32[32,1664]{1,0:T(8,128)S(1)} %collective-permute-done.1.refs_1_), channel_id=1, source_target_pairs={{0,8},{2,10},{4,12},{6,14},{8,0},{10,2},{12,4},{14,6},{16,24},{18,... | collective-permute-start | bytes 638984 | tf_op jit(solution)/shard_map/ppermute | solution.py:324
  27.9 12.0 %collective-permute-start.9 = (f32[32,1664]{1,0:T(8,128)S(1)}, f32[32,1664]{1,0:T(8,128)S(1)}, u32[]{:S(2)}, u32[]{:S(2)}) collective-permute-start(f32[32,1664]{1,0:T(8,128)S(1)} %collective-permute-done.1.refs_1_), channel_id=1, source_target_pairs={{0,1},{1,0},{2,3},{3,2},{4,5},{5,4},{6,7},{7,6},{8,9},{9,8},{10,11... | collective-permute-start | bytes 638984 | tf_op jit(solution)/shard_map/ppermute | solution.py:324
  38.8 6.5 %collective-permute-start.7 = (f32[32,1664]{1,0:T(8,128)S(1)}, f32[32,1664]{1,0:T(8,128)S(1)}, u32[]{:S(2)}, u32[]{:S(2)}) collective-permute-start(f32[32,1664]{1,0:T(8,128)S(1)} %collective-permute-done.3.refs_1_), channel_id=1, source_target_pairs={{0,1},{1,0},{2,3},{3,2},{4,5},{5,4},{6,7},{7,6},{8,9},{9,8},{10,11... | collective-permute-start | bytes 638984 | tf_op jit(solution)/shard_map/ppermute | solution.py:324
  45.3 5.0 %copy-start.6 = (s32[16,3072]{1,0:T(8,128)S(1)}, s32[16,3072]{1,0:T(8,128)}, u32[]{:S(2)}) copy-start(s32[16,3072]{1,0:T(8,128)} %get-tuple-element.46) | copy-start | bytes 589828
  46.3 4.6 %collective-permute-start.10 = (f32[528,512]{1,0:T(8,128)S(1)}, f32[528,512]{1,0:T(8,128)S(1)}, u32[]{:S(2)}, u32[]{:S(2)}) collective-permute-start(f32[528,512]{1,0:T(8,128)S(1)} %shard_map.101), channel_id=1, source_target_pairs={{0,2},{2,0},{4,6},{6,4},{8,10},{10,8},{12,14},{14,12},{16,18},{18,... | collective-permute-start | bytes 3244040 | tf_op jit(solution)/shard_map/ppermute | solution.py:324
  46.4 11.2 %collective-permute-start.11 = (s32[16,3072]{1,0:T(8,128)S(1)}, s32[16,3072]{1,0:T(8,128)S(1)}, u32[]{:S(2)}, u32[]{:S(2)}) collective-permute-start(s32[16,3072]{1,0:T(8,128)S(1)} %copy-done.8), channel_id=1, source_target_pairs={{0,8},{2,10},{4,12},{6,14},{8,0},{10,2},{12,4},{14,6},{16,24},{18,... | collective-permute-start | bytes 589832 | tf_op jit(solution)/shard_map/ppermute | solution.py:324
  46.7 17.7 %collective-permute-start.8 = (s32[16,3072]{1,0:T(8,128)S(1)}, s32[16,3072]{1,0:T(8,128)S(1)}, u32[]{:S(2)}, u32[]{:S(2)}) collective-permute-start(s32[16,3072]{1,0:T(8,128)S(1)} %copy-done.7), channel_id=1, source_target_pairs={{0,16},{2,18},{4,20},{6,22},{8,24},{10,26},{12,28},{14,30},{16,0},... | collective-permute-start | bytes 589832 | tf_op jit(solution)/shard_map/ppermute | solution.py:324
  50.3 17.6 %collective-permute-start = (s32[16,3072]{1,0:T(8,128)S(1)}, s32[16,3072]{1,0:T(8,128)S(1)}, u32[]{:S(2)}, u32[]{:S(2)}) collective-permute-start(s32[16,3072]{1,0:T(8,128)S(1)} %copy-done.6), channel_id=1, source_target_pairs={{0,24},{2,26},{4,28},{6,30},{8,16},{10,18},{12,20},{14,22},{16,8},... | collective-permute-start | bytes 589832 | tf_op jit(solution)/shard_map/ppermute | solution.py:324
  51.9 22.4 %collective-permute-start.15 = (f32[264,512]{1,0:T(8,128)S(1)}, f32[264,512]{1,0:T(8,128)S(1)}, u32[]{:S(2)}, u32[]{:S(2)}) collective-permute-start(f32[264,512]{1,0:T(8,128)S(1)} %get-tuple-element.72), channel_id=1, source_target_pairs={{0,4},{2,6},{4,0},{6,2},{8,12},{10,14},{12,8},{14,10},{16,20},{18,... | collective-permute-start | bytes 1622024 | tf_op jit(solution)/shard_map/ppermute | solution.py:324
  53.5 23.8 %collective-permute-start.16 = (f32[264,512]{1,0:T(8,128)S(1)}, f32[264,512]{1,0:T(8,128)S(1)}, u32[]{:S(2)}, u32[]{:S(2)}) collective-permute-start(f32[264,512]{1,0:T(8,128)S(1)} %get-tuple-element.73), channel_id=1, source_target_pairs={{0,4},{2,6},{4,0},{6,2},{8,12},{10,14},{12,8},{14,10},{16,20},{18,... | collective-permute-start | bytes 1622024 | tf_op jit(solution)/shard_map/ppermute | solution.py:324
  71.5 1.7 %collective-permute-start.12 = (f32[176,512]{1,0:T(8,128)S(1)}, f32[176,512]{1,0:T(8,128)S(1)}, u32[]{:S(2)}, u32[]{:S(2)}) collective-permute-start(f32[176,512]{1,0:T(8,128)S(1)} %get-tuple-element.82), channel_id=1, source_target_pairs={{0,2},{2,0},{4,6},{6,4},{8,10},{10,8},{12,14},{14,12},{16,18},{18,... | collective-permute-start | bytes 1081352 | tf_op jit(solution)/shard_map/ppermute | solution.py:324
  71.6 2.2 %collective-permute-start.13 = (f32[176,512]{1,0:T(8,128)S(1)}, f32[176,512]{1,0:T(8,128)S(1)}, u32[]{:S(2)}, u32[]{:S(2)}) collective-permute-start(f32[176,512]{1,0:T(8,128)S(1)} %get-tuple-element.84), channel_id=1, source_target_pairs={{0,2},{2,0},{4,6},{6,4},{8,10},{10,8},{12,14},{14,12},{16,18},{18,... | collective-permute-start | bytes 1081352 | tf_op jit(solution)/shard_map/ppermute | solution.py:324
  72.1 2.2 %collective-permute-start.14 = (f32[176,512]{1,0:T(8,128)S(1)}, f32[176,512]{1,0:T(8,128)S(1)}, u32[]{:S(2)}, u32[]{:S(2)}) collective-permute-start(f32[176,512]{1,0:T(8,128)S(1)} %get-tuple-element.85), channel_id=1, source_target_pairs={{0,2},{2,0},{4,6},{6,4},{8,10},{10,8},{12,14},{14,12},{16,18},{18,... | collective-permute-start | bytes 1081352 | tf_op jit(solution)/shard_map/ppermute | solution.py:324
  77.4 2.1 %copy-start.4 = (f32[1,3072]{1,0:T(1,128)S(1)}, f32[1,3072]{1,0:T(1,128)}, u32[]{:S(2)}) copy-start(f32[1,3072]{1,0:T(1,128)} %get-tuple-element.87) | copy-start | bytes 36868
  77.4 8.7 %copy-start.3 = (s32[3072]{0:T(1024)S(1)}, s32[3072]{0:T(1024)}, u32[]{:S(2)}) copy-start(s32[3072]{0:T(1024)} %param.9) | copy-start | bytes 36868
  77.4 8.8 %copy-start.2 = (f32[3072,32]{0,1:T(8,128)S(1)}, f32[3072,32]{0,1:T(8,128)}, u32[]{:S(2)}) copy-start(f32[3072,32]{0,1:T(8,128)} %param.7) | copy-start | bytes 1179652
  79.5 6.5 %collective-permute-start.17 = (f32[32,128]{1,0:T(8,128)S(1)}, f32[32,128]{1,0:T(8,128)S(1)}, u32[]{:S(2)}, u32[]{:S(2)}) collective-permute-start(f32[32,128]{1,0:T(8,128)S(1)} %pad_maximum_fusion), channel_id=1, source_target_pairs={{0,1},{1,0},{2,3},{3,2},{4,5},{5,4},{6,7},{7,6},{8,9},{9,8},{10,11... | collective-permute-start | bytes 49160 | tf_op jit(solution)/shard_map/ppermute | solution.py:324
  80.4 12.2 %all-to-all-start = ((f32[8,8,128]{2,1,0:T(8,128)}), f32[8,8,128]{2,1,0:T(8,128)S(1)}, u32[]{:S(2)}, u32[]{:S(2)}) async-start(f32[8,8,128]{2,1,0:T(8,128)} %shard_map.106), calls=%async_computation | async-start | bytes 65536 | tf_op jit(solution)/shard_map/all_to_all | solution.py:484
  86.1 7.1 %copy-start.5 = (f32[8,2,32]{2,1,0:T(2,128)}, f32[8,2,32]{2,1,0:T(2,128)S(1)}, u32[]{:S(2)}) copy-start(f32[8,2,32]{2,1,0:T(2,128)S(1)} %fusion.5) | copy-start | bytes 6148
  (4 other events, 4.5 us)

commit v16 on v15

--- a/solution.py
+++ b/solution.py
@@ -216,8 +216,9 @@
         held_refs = refs[arrays:-outs]
     else:
         out_refs = refs[-outs:]
-        piece_refs = refs[-outs - sum(cuts) : -outs]
-        held_refs = refs[arrays : -outs - sum(cuts)]
+        count = sum(len(cut) for cut in cuts)
+        piece_refs = refs[-outs - count : -outs]
+        held_refs = refs[arrays : -outs - count]
     pairs = 2 * classes * node_count
     row_index, feat_index = lax.axis_index("rows"), lax.axis_index("feat")
     for s, (m, codes_at, info_at, firsts) in enumerate(plan):
@@ -282,10 +283,11 @@
                 out_ref[band, i * LANES : (i + 1) * LANES] += here * sums
     if cuts is not None:
         for out_ref, cut in zip(out_refs, cuts):
-            rows = out_ref.shape[0] // cut
-            for i in range(cut):
-                piece_refs[i][...] = out_ref[i * rows : (i + 1) * rows, :]
-            piece_refs = piece_refs[cut:]
+            low = 0
+            for i, height in enumerate(cut):
+                piece_refs[i][...] = out_ref[low : low + height, :]
+                low += height
+            piece_refs = piece_refs[len(cut) :]
 
 
 def add_rows(classes, node_count, own, carry, plan, arrays, *held, cuts=None):
@@ -294,7 +296,7 @@
     outs = len(plan[0][3])
     heights = [shape[0]] * outs
     if cuts is not None:
-        heights = [shape[0] // cut for cut in cuts for _ in range(cut)]
+        heights = [height for cut in cuts for height in cut]
     return pl.pallas_call(
         functools.partial(add_kernel, classes, node_count, own, plan, carry, cuts),
         in_specs=[whole] * (len(arrays) + len(held) * outs),
@@ -311,9 +313,9 @@
     pairs = hist_ref.shape[0]
     for i, cut in enumerate(cuts):
         pieces, refs = refs[:cut], refs[cut:]
-        rows = pieces[0].shape[0]
-        for j, piece in enumerate(pieces):
-            low, high = j * rows, min((j + 1) * rows, pairs)
+        high = 0
+        for piece in pieces:
+            low, high = high, min(high + piece.shape[0], pairs)
             part = piece[: high - low, :]
             hist_ref[low:high, :] = part if i == 0 else hist_ref[low:high, :] + part
     write_gains(hist_ref, gain_ref, classes, node_count)
@@ -415,8 +417,8 @@
         (0, quarters(8, (0, 1)), 3 * LANES),
         (0, quarters(12, (0, 1)), 3 * LANES),
         (0, quarters(4, (2, 3)), 0),
-        (0, quarters(8, (2, 3)), 0),
-        (0, quarters(12, (2, 3)), 0),
+        (0, quarters(8, (2, 3)), 1 * LANES),
+        (0, quarters(12, (2, 3)), 1 * LANES),
     )
     info, half, flags, codes_0, rows_4, codes_8, codes_12, late_4, late_8, late_12 = prepare(
         blocks, splits, logits_t, labels, node_ids, bin_codes
@@ -446,15 +448,13 @@
     hist_a, hist_b = add(((12, 0, (1, None), (0, own)),), [codes_12, near_12], [hist_a, hist_b])
     (to_core,) = add(((12, 0, (None, 1), (0,)),), [codes_12, far_12], [hist_a])
     from_core = swap(to_core, "rows", 1)
-    to_plane = add(
-        ((12, 0, (None, 1), (own,)),), [codes_12, far_12], [hist_b], [from_core], cuts=(2,)
-    )
-    from_plane = [swap(piece, "rows", 2) for piece in to_plane]
+    (to_plane,) = add(((12, 0, (None, 1), (own,)),), [codes_12, far_12], [hist_b], [from_core])
+    from_plane = [swap(to_plane, "rows", 2)]
     _, late_4 = lax.optimization_barrier((to_plane, late_4))
     hists = add(((4, 0, (1, 2), (0, own)),), [late_4, rows_4, far_4], [hist_c, hist_d])
     hists = add(((8, 0, (1, 2), (0, own)),), [late_8, near_8, far_8], hists)
     *to_core, kept = add(
-        ((12, 0, (1, 2), (0, own)),), [late_12, near_12, far_12], hists, cuts=(3, 1)
+        ((12, 0, (1, 2), (0, own)),), [late_12, near_12, far_12], hists, cuts=((176,176,176), (528,))
     )
     from_core = [swap(piece, "rows", 1) for piece in to_core]
 

time: 93.5 us -> 97.5 us (1.043)
  waiting for transfers between devices: 28.3 us -> 34.8 us
  starting transfers between devices: 25.5 us -> 22.9 us
    ppermute x18 -> x17, waiting for transfers between devices: 23 us -> 29.5 us  [swap(): return lax.ppermute(x, axis, [(i, i ^ bit) for i in range(size)])]
    ppermute x18 -> x17, starting transfers between devices: 20 us -> 18.6 us  [swap(): return lax.ppermute(x, axis, [(i, i ^ bit) for i in range(size)])]
    all_to_all x1, starting transfers between devices: 5.54 us -> 4.27 us  [local(): lax.all_to_all(gains, 'rows', 0, 0, tiled=True, axis_index_groups=halves)]
  transfers between devices with their start and end apart: 19 -> 18, of which waited for: 12 -> 11; matrix products, arithmetic and copies ran while one was open for 1% -> 1% of each run, Pallas kernels for 30% -> 27%
where the time goes in v16:
time: 97.5 us; the launch traced here: 97.2 us
  waiting for transfers between devices  34.8 us (36%)
  Pallas kernels  34.7 us (36%)
  starting transfers between devices  22.9 us (23%)
  local copies, waits for them, and re-layouts  2.73 us (3%)
  matrix products  1.1 us (1%)
    ppermute x17, waiting for transfers between devices, swap(): return lax.ppermute(x, axis, [(i, i ^ bit) for i in range(size)])  29.5 us
    pallas_call x11, Pallas kernels, add_rows(): pl.pallas_call(functools.partial(add_kernel, classes, node_count, own, pl...  28.6 us
    ppermute x17, starting transfers between devices, swap(): return lax.ppermute(x, axis, [(i, i ^ bit) for i in range(size)])  18.6 us
    all_to_all x1, waiting for transfers between devices, local(): lax.all_to_all(gains, 'rows', 0, 0, tiled=True, axis_index_groups=halves)  5.36 us
    all_to_all x1, starting transfers between devices, local(): lax.all_to_all(gains, 'rows', 0, 0, tiled=True, axis_index_groups=halves)  4.27 us
    pallas_call x1, Pallas kernels, prepare(): pl.pallas_call(functools.partial(prep_kernel, own, blocks), in_specs=[pl....  3.98 us
    unnamed x19, local copies, waits for them, and re-layouts  2.65 us
    pallas_call x1, Pallas kernels, local(): pl.pallas_call(functools.partial(gain_kernel, classes, node_count, (1, le...  2.1 us
  transfers between devices with their start and end apart: 18, of which 11 were waited for; matrix products, arithmetic and copies ran while one was open for 1% of the time, Pallas kernels for 27%

profile of v16, /device:TPU:0, one launch (start us, length us, event | category | flops | bytes accessed | tf_op | source)
XLA Modules:
  0.0 97.2 jit_solution(449759979899147447)
XLA Ops:
  0.6 4.0 %shard_map.94 = (f32[32,3328]{1,0:T(8,128)}, f32[32,1664]{1,0:T(8,128)}, f32[1,3072]{1,0:T(1,128)}, s32[32,3072]{1,0:T(8,128)}, f32[64,1664]{1,0:T(8,128)}, /*in...) custom-call(s32[3072,128]{1,0:T(8,128)} %refs_0_.1, ...), custom_call_target="tpu_custom_call" | custom-call | flops 1000000 | bytes 1000000 | tf_op jit(solution)/shard_map/pallas_call | solution.py:363
  4.6 3.1 %collective-permute-start.2 = (f32[64,1664]{1,0:T(8,128)}, f32[64,1664]{1,0:T(8,128)S(1)}, u32[]{:S(2)}, u32[]{:S(2)}) collective-permute-start(f32[64,1664]{1,0:T(8,128)} %get-tuple-element.46), channel_id=1, source_target_pairs={{0,8},{2,10},{4,12},{6,14},{8,0},{10,2},{12,4},{14,6},{16,24},{18,... | collective-permute-start | bytes 1277960 | tf_op jit(solution)/shard_map/ppermute | solution.py:326
  7.7 2.6 %collective-permute-start.1 = (f32[32,1664]{1,0:T(8,128)}, f32[32,1664]{1,0:T(8,128)S(1)}, u32[]{:S(2)}, u32[]{:S(2)}) collective-permute-start(f32[32,1664]{1,0:T(8,128)} %get-tuple-element.45), channel_id=1, source_target_pairs={{0,16},{2,18},{4,20},{6,22},{8,24},{10,26},{12,28},{14,30},{16,0},... | collective-permute-start | bytes 638984 | tf_op jit(solution)/shard_map/ppermute | solution.py:326
  10.6 2.5 %collective-permute-start.4 = (s32[16,3456]{1,0:T(8,128)}, s32[16,3456]{1,0:T(8,128)S(1)}, u32[]{:S(2)}, u32[]{:S(2)}) collective-permute-start(s32[16,3456]{1,0:T(8,128)} %get-tuple-element.51), channel_id=1, source_target_pairs={{0,24},{2,26},{4,28},{6,30},{8,16},{10,18},{12,20},{14,22},{16,8},... | collective-permute-start | bytes 663560 | tf_op jit(solution)/shard_map/ppermute | solution.py:326
  15.1 6.7 %shard_map.95 = (f32[528,512]{1,0:T(8,128)S(1)}, f32[528,512]{1,0:T(8,128)S(1)}, f32[528,512]{1,0:T(8,128)S(1)}, f32[528,512]{1,0:T(8,128)S(1)}) custom-call(s32[32,3072]{1,0:T(8,128)S(1)} %copy-done.1, f32[32,3328]{1,0:T(8,128)S(1)} %copy-done), custom_call_target="tpu_custom_call" | custom-call | flops 1000000 | bytes 1000000 | tf_op jit(solution)/shard_map/pallas_call | solution.py:300
  22.9 3.3 %collective-permute-done.2.refs_0_.refs_1_ = f32[64,1664]{1,0:T(8,128)S(1)} collective-permute-done((f32[64,1664]{1,0:T(8,128)}, f32[64,1664]{1,0:T(8,128)S(1)}, u32[]{:S(2)}, u32[]{:S(2)}) %collective-permute-start.2) | collective-permute-done | bytes 426016 | tf_op jit(solution)/shard_map/ppermute | solution.py:326
  26.2 1.7 %collective-permute-start.6 = (f32[32,1664]{1,0:T(8,128)S(1)}, f32[32,1664]{1,0:T(8,128)S(1)}, u32[]{:S(2)}, u32[]{:S(2)}) collective-permute-start(f32[32,1664]{1,0:T(8,128)S(1)} %slice.30), channel_id=1, source_target_pairs={{0,1},{1,0},{2,3},{3,2},{4,5},{5,4},{6,7},{7,6},{8,9},{9,8},{10,11... | collective-permute-start | bytes 638984 | tf_op jit(solution)/shard_map/ppermute | solution.py:326
  28.4 1.8 %shard_map.96 = (f32[528,512]{1,0:T(8,128)S(1)}, f32[528,512]{1,0:T(8,128)S(1)}) custom-call(f32[64,1664]{1,0:T(8,128)S(1)} %collective-permute-done.2.refs_0_.refs_1_, f32[528,512]{1,0:T(8,128)S(1)} %get-tuple-element.54.refs_1_, f32[528,512]{1,0:T(8,128)S(1)} %get-tuple-element.55.refs_2_), custom_call_target="tpu_custom_call" | custom-call | flops 1000000 | bytes 1000000 | tf_op jit(solution)/shard_map/pallas_call | solution.py:300
  30.3 4.2 %collective-permute-done.6.refs_1_.refs_2_ = f32[32,1664]{1,0:T(8,128)S(1)} collective-permute-done((f32[32,1664]{1,0:T(8,128)S(1)}, f32[32,1664]{1,0:T(8,128)S(1)}, u32[]{:S(2)}, u32[]{:S(2)}) %collective-permute-start.6) | collective-permute-done | bytes 213024 | tf_op jit(solution)/shard_map/ppermute | solution.py:326
  34.5 1.8 %shard_map.97 = (f32[528,512]{1,0:T(8,128)S(1)}, f32[528,512]{1,0:T(8,128)S(1)}) custom-call(f32[64,1664]{1,0:T(8,128)S(1)} %collective-permute-done.2.refs_0_.refs_1_, f32[32,1664]{1,0:T(8,128)S(1)} %collective-permute-done.6.refs_1_.refs_2_, f32[528,512]{1,0:T(8,128)S(1)} %get-tuple-element.56.refs_2_, f32[528,512]{1,0:T(8,128)S(1)} %get-tuple-element.57.refs_3_), custom_call_target="tpu_custom_call" | custom-call | flops 1000000 | bytes 1000000 | tf_op jit(solution)/shard_map/pallas_call | solution.py:300
  36.3 1.8 %shard_map.98 = (f32[528,512]{1,0:T(8,128)S(1)}, f32[528,512]{1,0:T(8,128)S(1)}) custom-call(s32[16,3456]{1,0:T(8,128)S(1)} %collective-permute-done.5.refs_0_, f32[32,1664]{1,0:T(8,128)S(1)} %collective-permute-done.1.refs_1_, f32[528,512]{1,0:T(8,128)S(1)} %get-tuple-element.58.refs_2_, f32[528,512]{1,0:T(8,128)S(1)} %get-tuple-element.59.refs_3_), custom_call_target="tpu_custom_call" | custom-call | flops 1000000 | bytes 1000000 | tf_op jit(solution)/shard_map/pallas_call | solution.py:300
  39.9 1.8 %shard_map.99 = (f32[528,512]{1,0:T(8,128)S(1)}, f32[528,512]{1,0:T(8,128)S(1)}) custom-call(s32[16,3456]{1,0:T(8,128)S(1)} %collective-permute-done.5.refs_0_, f32[32,1664]{1,0:T(8,128)S(1)} %collective-permute-done.9.refs_1_.refs_2_, f32[528,512]{1,0:T(8,128)S(1)} %get-tuple-element.64.refs_2_, f32[528,512]{1,0:T(8,128)S(1)} %get-tuple-element.65.refs_3_), custom_call_target="tpu_custom_call" | custom-call | flops 1000000 | bytes 1000000 | tf_op jit(solution)/shard_map/pallas_call | solution.py:300
  41.8 2.0 %shard_map.100 = (f32[528,512]{1,0:T(8,128)S(1)}, f32[528,512]{1,0:T(8,128)S(1)}) custom-call(s32[16,3456]{1,0:T(8,128)S(1)} %collective-permute-done.4.refs_0_, f32[32,1664]{1,0:T(8,128)S(1)} %collective-permute-done.3.refs_1_, f32[528,512]{1,0:T(8,128)S(1)} %get-tuple-element.66.refs_2_, f32[528,512]{1,0:T(8,128)S(1)} %get-tuple-element.67.refs_3_), custom_call_target="tpu_custom_call" | custom-call | flops 1000000 | bytes 1000000 | tf_op jit(solution)/shard_map/pallas_call | solution.py:300
  43.8 1.5 %collective-permute-done.7.refs_1_.refs_2_ = f32[32,1664]{1,0:T(8,128)S(1)} collective-permute-done((f32[32,1664]{1,0:T(8,128)S(1)}, f32[32,1664]{1,0:T(8,128)S(1)}, u32[]{:S(2)}, u32[]{:S(2)}) %collective-permute-start.7) | collective-permute-done | bytes 213024 | tf_op jit(solution)/shard_map/ppermute | solution.py:326
  46.4 2.7 %collective-permute-done.10.refs_3_ = f32[528,512]{1,0:T(8,128)S(1)} collective-permute-done((f32[528,512]{1,0:T(8,128)S(1)}, f32[528,512]{1,0:T(8,128)S(1)}, u32[]{:S(2)}, u32[]{:S(2)}) %collective-permute-start.10) | collective-permute-done | bytes 1081376 | tf_op jit(solution)/shard_map/ppermute | solution.py:326
  50.2 1.6 %collective-permute-start.15 = (f32[528,512]{1,0:T(8,128)S(1)}, f32[528,512]{1,0:T(8,128)S(1)}, u32[]{:S(2)}, u32[]{:S(2)}) collective-permute-start(f32[528,512]{1,0:T(8,128)S(1)} %shard_map.102), channel_id=1, source_target_pairs={{0,4},{2,6},{4,0},{6,2},{8,12},{10,14},{12,8},{14,10},{16,20},{18,... | collective-permute-start | bytes 3244040 | tf_op jit(solution)/shard_map/ppermute | solution.py:326
  53.1 2.0 %collective-permute-start = (s32[16,3200]{1,0:T(8,128)S(1)}, s32[16,3200]{1,0:T(8,128)S(1)}, u32[]{:S(2)}, u32[]{:S(2)}) collective-permute-start(s32[16,3200]{1,0:T(8,128)S(1)} %copy-done.6), channel_id=1, source_target_pairs={{0,24},{2,26},{4,28},{6,30},{8,16},{10,18},{12,20},{14,22},{16,8},... | collective-permute-start | bytes 614408 | tf_op jit(solution)/shard_map/ppermute | solution.py:326
  55.7 13.9 %collective-permute-done.11.refs_0_ = s32[16,3072]{1,0:T(8,128)S(1)} collective-permute-done((s32[16,3072]{1,0:T(8,128)S(1)}, s32[16,3072]{1,0:T(8,128)S(1)}, u32[]{:S(2)}, u32[]{:S(2)}) %collective-permute-start.11) | collective-permute-done | bytes 196640 | tf_op jit(solution)/shard_map/ppermute | solution.py:326
  69.5 3.5 %shard_map.103 = (f32[528,512]{1,0:T(8,128)S(1)}, f32[528,512]{1,0:T(8,128)S(1)}) custom-call(s32[16,3072]{1,0:T(8,128)S(1)} %collective-permute-done.11.refs_0_, f32[64,1664]{1,0:T(8,128)S(1)} %collective-permute-done.2.refs_0_.refs_1_, f32[32,1664]{1,0:T(8,128)S(1)} %collective-permute-done.6.refs_1_.refs_2_, f32[528,512]{1,0:T(8,128)S(1)} %get-tuple-element.72.refs_3_, ...), custom_call_target="tpu_custom_call" | custom-call | flops 1000000 | bytes 1000000 | tf_op jit(solution)/shard_map/pallas_call | solution.py:300
  73.0 3.4 %shard_map.104 = (f32[528,512]{1,0:T(8,128)S(1)}, f32[528,512]{1,0:T(8,128)S(1)}) custom-call(s32[16,3200]{1,0:T(8,128)S(1)} %collective-permute-done.8.refs_0_, f32[32,1664]{1,0:T(8,128)S(1)} %collective-permute-done.1.refs_1_, f32[32,1664]{1,0:T(8,128)S(1)} %collective-permute-done.9.refs_1_.refs_2_, f32[528,512]{1,0:T(8,128)S(1)} %get-tuple-element.74.refs_3_, ...), custom_call_target="tpu_custom_call" | custom-call | flops 1000000 | bytes 1000000 | tf_op jit(solution)/shard_map/pallas_call | solution.py:300
  76.5 3.6 %shard_map.105 = (f32[176,512]{1,0:T(8,128)S(1)}, f32[176,512]{1,0:T(8,128)S(1)}, f32[176,512]{1,0:T(8,128)S(1)}, f32[528,512]{1,0:T(8,128)S(1)}) custom-call(s32[16,3200]{1,0:T(8,128)S(1)} %collective-permute-done.refs_0_, f32[32,1664]{1,0:T(8,128)S(1)} %collective-permute-done.3.refs_1_, f32[32,1664]{1,0:T(8,128)S(1)} %collective-permute-done.7.refs_1_.refs_2_, ...), custom_call_target="tpu_custom_call" | custom-call | flops 1000000 | bytes 1000000 | tf_op jit(solution)/shard_map/pallas_call | solution.py:300
  82.8 2.1 %shard_map.106 = f32[8,8,128]{2,1,0:T(8,128)} custom-call(f32[528,512]{1,0:T(8,128)S(1)} %get-tuple-element.79.refs_0_, f32[176,512]{1,0:T(8,128)S(1)} %collective-permute-done.13.refs_1_, f32[176,512]{1,0:T(8,128)S(1)} %collective-permute-done.14.refs_2_, f32[176,512]{1,0:T(8,128)S(1)} %collective-permute-done.12.refs_3_, ...), custom_call_target="tpu_custom_call" | custom-call | flops 1000000 | bytes 1000000 | tf_op jit(solution)/shard_map/pallas_call | solution.py:462
  85.6 4.3 %all-to-all-start = ((f32[8,8,128]{2,1,0:T(8,128)}), f32[8,8,128]{2,1,0:T(8,128)S(1)}, u32[]{:S(2)}, u32[]{:S(2)}) async-start(f32[8,8,128]{2,1,0:T(8,128)} %shard_map.106), calls=%async_computation | async-start | bytes 65536 | tf_op jit(solution)/shard_map/all_to_all | solution.py:484
  91.2 5.4 %all-to-all-done = f32[8,8,128]{2,1,0:T(8,128)S(1)} async-done(((f32[8,8,128]{2,1,0:T(8,128)}), f32[8,8,128]{2,1,0:T(8,128)S(1)}, u32[]{:S(2)}, u32[]{:S(2)}) %all-to-all-start) | async-done | bytes 32800 | tf_op jit(solution)/shard_map/all_to_all | solution.py:484
  (53 shorter events, 15.1 us)
Async XLA Ops:
  4.6 21.6 %collective-permute-start.2 = (f32[64,1664]{1,0:T(8,128)}, f32[64,1664]{1,0:T(8,128)S(1)}, u32[]{:S(2)}, u32[]{:S(2)}) collective-permute-start(f32[64,1664]{1,0:T(8,128)} %get-tuple-element.46), channel_id=1, source_target_pairs={{0,8},{2,10},{4,12},{6,14},{8,0},{10,2},{12,4},{14,6},{16,24},{18,... | collective-permute-start | bytes 1277960 | tf_op jit(solution)/shard_map/ppermute | solution.py:326
  7.7 15.1 %collective-permute-start.1 = (f32[32,1664]{1,0:T(8,128)}, f32[32,1664]{1,0:T(8,128)S(1)}, u32[]{:S(2)}, u32[]{:S(2)}) collective-permute-start(f32[32,1664]{1,0:T(8,128)} %get-tuple-element.45), channel_id=1, source_target_pairs={{0,16},{2,18},{4,20},{6,22},{8,24},{10,26},{12,28},{14,30},{16,0},... | collective-permute-start | bytes 638984 | tf_op jit(solution)/shard_map/ppermute | solution.py:326
  10.3 26.0 %collective-permute-start.5 = (s32[16,3456]{1,0:T(8,128)}, s32[16,3456]{1,0:T(8,128)S(1)}, u32[]{:S(2)}, u32[]{:S(2)}) collective-permute-start(s32[16,3456]{1,0:T(8,128)} %get-tuple-element.52), channel_id=1, source_target_pairs={{0,16},{2,18},{4,20},{6,22},{8,24},{10,26},{12,28},{14,30},{16,0},... | collective-permute-start | bytes 663560 | tf_op jit(solution)/shard_map/ppermute | solution.py:326
  10.6 27.5 %collective-permute-start.4 = (s32[16,3456]{1,0:T(8,128)}, s32[16,3456]{1,0:T(8,128)S(1)}, u32[]{:S(2)}, u32[]{:S(2)}) collective-permute-start(s32[16,3456]{1,0:T(8,128)} %get-tuple-element.51), channel_id=1, source_target_pairs={{0,24},{2,26},{4,28},{6,30},{8,16},{10,18},{12,20},{14,22},{16,8},... | collective-permute-start | bytes 663560 | tf_op jit(solution)/shard_map/ppermute | solution.py:326
  26.2 8.3 %collective-permute-start.6 = (f32[32,1664]{1,0:T(8,128)S(1)}, f32[32,1664]{1,0:T(8,128)S(1)}, u32[]{:S(2)}, u32[]{:S(2)}) collective-permute-start(f32[32,1664]{1,0:T(8,128)S(1)} %slice.30), channel_id=1, source_target_pairs={{0,1},{1,0},{2,3},{3,2},{4,5},{5,4},{6,7},{7,6},{8,9},{9,8},{10,11... | collective-permute-start | bytes 638984 | tf_op jit(solution)/shard_map/ppermute | solution.py:326
  27.9 10.9 %collective-permute-start.3 = (f32[32,1664]{1,0:T(8,128)S(1)}, f32[32,1664]{1,0:T(8,128)S(1)}, u32[]{:S(2)}, u32[]{:S(2)}) collective-permute-start(f32[32,1664]{1,0:T(8,128)S(1)} %collective-permute-done.1.refs_1_), channel_id=1, source_target_pairs={{0,8},{2,10},{4,12},{6,14},{8,0},{10,2},{12,4},{14,6},{16,24},{18,... | collective-permute-start | bytes 638984 | tf_op jit(solution)/shard_map/ppermute | solution.py:326
  27.9 12.0 %collective-permute-start.9 = (f32[32,1664]{1,0:T(8,128)S(1)}, f32[32,1664]{1,0:T(8,128)S(1)}, u32[]{:S(2)}, u32[]{:S(2)}) collective-permute-start(f32[32,1664]{1,0:T(8,128)S(1)} %collective-permute-done.1.refs_1_), channel_id=1, source_target_pairs={{0,1},{1,0},{2,3},{3,2},{4,5},{5,4},{6,7},{7,6},{8,9},{9,8},{10,11... | collective-permute-start | bytes 638984 | tf_op jit(solution)/shard_map/ppermute | solution.py:326
  38.9 6.5 %collective-permute-start.7 = (f32[32,1664]{1,0:T(8,128)S(1)}, f32[32,1664]{1,0:T(8,128)S(1)}, u32[]{:S(2)}, u32[]{:S(2)}) collective-permute-start(f32[32,1664]{1,0:T(8,128)S(1)} %collective-permute-done.3.refs_1_), channel_id=1, source_target_pairs={{0,1},{1,0},{2,3},{3,2},{4,5},{5,4},{6,7},{7,6},{8,9},{9,8},{10,11... | collective-permute-start | bytes 638984 | tf_op jit(solution)/shard_map/ppermute | solution.py:326
  46.3 2.8 %collective-permute-start.10 = (f32[528,512]{1,0:T(8,128)S(1)}, f32[528,512]{1,0:T(8,128)S(1)}, u32[]{:S(2)}, u32[]{:S(2)}) collective-permute-start(f32[528,512]{1,0:T(8,128)S(1)} %shard_map.101), channel_id=1, source_target_pairs={{0,2},{2,0},{4,6},{6,4},{8,10},{10,8},{12,14},{14,12},{16,18},{18,... | collective-permute-start | bytes 3244040 | tf_op jit(solution)/shard_map/ppermute | solution.py:326
  49.1 2.6 %copy-start.7 = (s32[16,3200]{1,0:T(8,128)S(1)}, s32[16,3200]{1,0:T(8,128)}, u32[]{:S(2)}) copy-start(s32[16,3200]{1,0:T(8,128)} %get-tuple-element.62) | copy-start | bytes 614404
  49.1 4.0 %copy-start.6 = (s32[16,3200]{1,0:T(8,128)S(1)}, s32[16,3200]{1,0:T(8,128)}, u32[]{:S(2)}) copy-start(s32[16,3200]{1,0:T(8,128)} %get-tuple-element.44) | copy-start | bytes 614404
  49.1 6.0 %copy-start.8 = (s32[16,3072]{1,0:T(8,128)S(1)}, s32[16,3072]{1,0:T(8,128)}, u32[]{:S(2)}) copy-start(s32[16,3072]{1,0:T(8,128)} %get-tuple-element.70) | copy-start | bytes 589828
  50.2 32.7 %collective-permute-start.15 = (f32[528,512]{1,0:T(8,128)S(1)}, f32[528,512]{1,0:T(8,128)S(1)}, u32[]{:S(2)}, u32[]{:S(2)}) collective-permute-start(f32[528,512]{1,0:T(8,128)S(1)} %shard_map.102), channel_id=1, source_target_pairs={{0,4},{2,6},{4,0},{6,2},{8,12},{10,14},{12,8},{14,10},{16,20},{18,... | collective-permute-start | bytes 3244040 | tf_op jit(solution)/shard_map/ppermute | solution.py:326
  51.8 21.2 %collective-permute-start.8 = (s32[16,3200]{1,0:T(8,128)S(1)}, s32[16,3200]{1,0:T(8,128)S(1)}, u32[]{:S(2)}, u32[]{:S(2)}) collective-permute-start(s32[16,3200]{1,0:T(8,128)S(1)} %copy-done.7), channel_id=1, source_target_pairs={{0,16},{2,18},{4,20},{6,22},{8,24},{10,26},{12,28},{14,30},{16,0},... | collective-permute-start | bytes 614408 | tf_op jit(solution)/shard_map/ppermute | solution.py:326
  53.1 23.4 %collective-permute-start = (s32[16,3200]{1,0:T(8,128)S(1)}, s32[16,3200]{1,0:T(8,128)S(1)}, u32[]{:S(2)}, u32[]{:S(2)}) collective-permute-start(s32[16,3200]{1,0:T(8,128)S(1)} %copy-done.6), channel_id=1, source_target_pairs={{0,24},{2,26},{4,28},{6,30},{8,16},{10,18},{12,20},{14,22},{16,8},... | collective-permute-start | bytes 614408 | tf_op jit(solution)/shard_map/ppermute | solution.py:326
  55.1 14.4 %collective-permute-start.11 = (s32[16,3072]{1,0:T(8,128)S(1)}, s32[16,3072]{1,0:T(8,128)S(1)}, u32[]{:S(2)}, u32[]{:S(2)}) collective-permute-start(s32[16,3072]{1,0:T(8,128)S(1)} %copy-done.8), channel_id=1, source_target_pairs={{0,8},{2,10},{4,12},{6,14},{8,0},{10,2},{12,4},{14,6},{16,24},{18,... | collective-permute-start | bytes 589832 | tf_op jit(solution)/shard_map/ppermute | solution.py:326
  80.1 1.7 %collective-permute-start.12 = (f32[176,512]{1,0:T(8,128)S(1)}, f32[176,512]{1,0:T(8,128)S(1)}, u32[]{:S(2)}, u32[]{:S(2)}) collective-permute-start(f32[176,512]{1,0:T(8,128)S(1)} %get-tuple-element.78), channel_id=1, source_target_pairs={{0,2},{2,0},{4,6},{6,4},{8,10},{10,8},{12,14},{14,12},{16,18},{18,... | collective-permute-start | bytes 1081352 | tf_op jit(solution)/shard_map/ppermute | solution.py:326
  80.1 2.2 %collective-permute-start.13 = (f32[176,512]{1,0:T(8,128)S(1)}, f32[176,512]{1,0:T(8,128)S(1)}, u32[]{:S(2)}, u32[]{:S(2)}) collective-permute-start(f32[176,512]{1,0:T(8,128)S(1)} %get-tuple-element.80), channel_id=1, source_target_pairs={{0,2},{2,0},{4,6},{6,4},{8,10},{10,8},{12,14},{14,12},{16,18},{18,... | collective-permute-start | bytes 1081352 | tf_op jit(solution)/shard_map/ppermute | solution.py:326
  80.6 2.2 %collective-permute-start.14 = (f32[176,512]{1,0:T(8,128)S(1)}, f32[176,512]{1,0:T(8,128)S(1)}, u32[]{:S(2)}, u32[]{:S(2)}) collective-permute-start(f32[176,512]{1,0:T(8,128)S(1)} %get-tuple-element.81), channel_id=1, source_target_pairs={{0,2},{2,0},{4,6},{6,4},{8,10},{10,8},{12,14},{14,12},{16,18},{18,... | collective-permute-start | bytes 1081352 | tf_op jit(solution)/shard_map/ppermute | solution.py:326
  82.8 7.2 %copy-start.3 = (s32[3072]{0:T(1024)S(1)}, s32[3072]{0:T(1024)}, u32[]{:S(2)}) copy-start(s32[3072]{0:T(1024)} %param.9) | copy-start | bytes 36868
  82.8 7.3 %copy-start.2 = (f32[3072,32]{0,1:T(8,128)S(1)}, f32[3072,32]{0,1:T(8,128)}, u32[]{:S(2)}) copy-start(f32[3072,32]{0,1:T(8,128)} %param.7) | copy-start | bytes 1179652
  85.0 4.9 %collective-permute-start.16 = (f32[32,128]{1,0:T(8,128)S(1)}, f32[32,128]{1,0:T(8,128)S(1)}, u32[]{:S(2)}, u32[]{:S(2)}) collective-permute-start(f32[32,128]{1,0:T(8,128)S(1)} %pad_maximum_fusion), channel_id=1, source_target_pairs={{0,1},{1,0},{2,3},{3,2},{4,5},{5,4},{6,7},{7,6},{8,9},{9,8},{10,11... | collective-permute-start | bytes 49160 | tf_op jit(solution)/shard_map/ppermute | solution.py:326
  85.6 11.0 %all-to-all-start = ((f32[8,8,128]{2,1,0:T(8,128)}), f32[8,8,128]{2,1,0:T(8,128)S(1)}, u32[]{:S(2)}, u32[]{:S(2)}) async-start(f32[8,8,128]{2,1,0:T(8,128)} %shard_map.106), calls=%async_computation | async-start | bytes 65536 | tf_op jit(solution)/shard_map/all_to_all | solution.py:484
  90.1 7.1 %copy-start.5 = (f32[8,2,32]{2,1,0:T(2,128)}, f32[8,2,32]{2,1,0:T(2,128)S(1)}, u32[]{:S(2)}) copy-start(f32[8,2,32]{2,1,0:T(2,128)S(1)} %fusion.5) | copy-start | bytes 6148
  (3 other events, 4.1 us)

commit v17 on v13

--- a/solution.py
+++ b/solution.py
@@ -389,14 +389,13 @@
 
     blocks = (
         (0, quarters(0, (0, 1, 2, 3)), 0),
-        (1, quarters(4, (0, 1)), 0),
+        (1, quarters(4, (0, 1, 2, 3)), 0),
         (0, quarters(8, (0, 1)), 3 * LANES),
         (0, quarters(12, (0, 1)), 3 * LANES),
-        (0, quarters(4, (2, 3)), 0),
         (0, quarters(8, (2, 3)), 0),
         (0, quarters(12, (2, 3)), 0),
     )
-    info, half, flags, codes_0, rows_4, codes_8, codes_12, late_4, late_8, late_12 = prepare(
+    info, half, flags, codes_0, rows_4, codes_8, codes_12, late_8, late_12 = prepare(
         blocks, splits, logits_t, labels, node_ids, bin_codes
     )
 
@@ -411,7 +410,6 @@
     near_12 = swap(near_8, "rows", 4)
     far_8 = swap(near_8, "feat", 1)
     far_4 = swap(rows_4[:classes], "feat", 1)
-    late_4 = swap(late_4, "rows", 4)
     late_8 = swap(late_8, "rows", 8)
     late_12 = swap(late_12, "rows", 12)
     firsts = (classes, classes + own)
@@ -426,8 +424,9 @@
     from_core = swap(to_core, "rows", 1)
     (to_plane,) = add(((12, 0, (None, 1), (own,)),), [codes_12, far_12], [hist_b], [from_core])
     from_plane = swap(to_plane, "rows", 2)
-    _, late_4 = lax.optimization_barrier((to_plane, late_4))
-    hists = add(((4, 0, (1, 2), (0, own)),), [late_4, rows_4, far_4], [hist_c, hist_d])
+    _, hist_c = lax.optimization_barrier((to_plane, hist_c))
+    lasts = (classes + 2 * own, classes + 3 * own)
+    hists = add(((4, 0, (0, 1), lasts),), [rows_4, far_4], [hist_c, hist_d])
     hists = add(((8, 0, (1, 2), (0, own)),), [late_8, near_8, far_8], hists)
     to_core, kept = add(((12, 0, (1, 2), (0, own)),), [late_12, near_12, far_12], hists)
     middle = to_core.shape[0] // 2

time: 93.5 us -> 99 us (1.059)
  waiting for transfers between devices: 28.9 us -> 33.5 us
    ppermute x16 -> x15, waiting for transfers between devices: 23.5 us -> 28.2 us  [swap(): return lax.ppermute(x, axis, [(i, i ^ bit) for i in range(size)])]
    ppermute x16 -> x15, starting transfers between devices: 19.4 us -> 20.9 us  [swap(): return lax.ppermute(x, axis, [(i, i ^ bit) for i in range(size)])]
    unnamed x19 -> x17, local copies, waits for them, and re-layouts: 2.65 us -> 2.64 us
  transfers between devices with their start and end apart: 17 -> 16, of which waited for: 11 -> 9; matrix products, arithmetic and copies ran while one was open for 2% -> 1% of each run, Pallas kernels for 29% -> 28%
where the time goes in v17:
time: 99 us; the launch traced here: 98.7 us
  Pallas kernels  34.5 us (35%)
  waiting for transfers between devices  33.5 us (34%)
  starting transfers between devices  25.7 us (26%)
  local copies, waits for them, and re-layouts  2.8 us (3%)
  matrix products  1.1 us (1%)
    pallas_call x11, Pallas kernels, add_rows(): pl.pallas_call(functools.partial(add_kernel, classes, node_count, own, pl...  28.5 us
    ppermute x15, waiting for transfers between devices, swap(): return lax.ppermute(x, axis, [(i, i ^ bit) for i in range(size)])  28.2 us
    ppermute x15, starting transfers between devices, swap(): return lax.ppermute(x, axis, [(i, i ^ bit) for i in range(size)])  20.9 us
    all_to_all x1, waiting for transfers between devices, local(): lax.all_to_all(gains, 'rows', 0, 0, tiled=True, axis_index_groups=halves)  5.36 us
    all_to_all x1, starting transfers between devices, local(): lax.all_to_all(gains, 'rows', 0, 0, tiled=True, axis_index_groups=halves)  4.75 us
    pallas_call x1, Pallas kernels, prepare(): pl.pallas_call(functools.partial(prep_kernel, own, blocks), in_specs=[pl....  3.97 us
    unnamed x17, local copies, waits for them, and re-layouts  2.64 us
    pallas_call x1, Pallas kernels, local(): pl.pallas_call(functools.partial(gain_kernel, classes, node_count), in_sp...  2.08 us
  transfers between devices with their start and end apart: 16, of which 9 were waited for; matrix products, arithmetic and copies ran while one was open for 1% of the time, Pallas kernels for 28%

profile of v17, /device:TPU:0, one launch (start us, length us, event | category | flops | bytes accessed | tf_op | source)
XLA Modules:
  0.0 98.7 jit_solution(1085196554742019983)
XLA Ops:
  0.6 4.0 %shard_map.94 = (f32[32,3328]{1,0:T(8,128)}, f32[32,1664]{1,0:T(8,128)}, f32[1,3072]{1,0:T(1,128)}, s32[32,3072]{1,0:T(8,128)}, f32[96,1664]{1,0:T(8,128)}, /*in...) custom-call(s32[3072,128]{1,0:T(8,128)} %refs_0_.1, f32[32,3072]{1,0:T(8,128)} %bitcast.14, ...), custom_call_target="tpu_custom_call" | custom-call | flops 1000000 | bytes 1000000 | tf_op jit(solution)/shard_map/pallas_call | solution.py:339
  4.6 3.1 %collective-permute-start.2 = (f32[96,1664]{1,0:T(8,128)}, f32[96,1664]{1,0:T(8,128)S(1)}, u32[]{:S(2)}, u32[]{:S(2)}) collective-permute-start(f32[96,1664]{1,0:T(8,128)} %get-tuple-element.43), channel_id=1, source_target_pairs={{0,8},{2,10},{4,12},{6,14},{8,0},{10,2},{12,4},{14,6},{16,24},{18,... | collective-permute-start | bytes 1916936 | tf_op jit(solution)/shard_map/ppermute | solution.py:302
  7.7 2.6 %collective-permute-start.1 = (f32[32,1664]{1,0:T(8,128)}, f32[32,1664]{1,0:T(8,128)S(1)}, u32[]{:S(2)}, u32[]{:S(2)}) collective-permute-start(f32[32,1664]{1,0:T(8,128)} %get-tuple-element.42), channel_id=1, source_target_pairs={{0,16},{2,18},{4,20},{6,22},{8,24},{10,26},{12,28},{14,30},{16,0},... | collective-permute-start | bytes 638984 | tf_op jit(solution)/shard_map/ppermute | solution.py:302
  10.6 2.5 %collective-permute-start.4 = (s32[16,3456]{1,0:T(8,128)}, s32[16,3456]{1,0:T(8,128)S(1)}, u32[]{:S(2)}, u32[]{:S(2)}) collective-permute-start(s32[16,3456]{1,0:T(8,128)} %get-tuple-element.48), channel_id=1, source_target_pairs={{0,24},{2,26},{4,28},{6,30},{8,16},{10,18},{12,20},{14,22},{16,8},... | collective-permute-start | bytes 663560 | tf_op jit(solution)/shard_map/ppermute | solution.py:302
  15.1 6.7 %shard_map.95 = (f32[528,512]{1,0:T(8,128)S(1)}, f32[528,512]{1,0:T(8,128)S(1)}, f32[528,512]{1,0:T(8,128)S(1)}, f32[528,512]{1,0:T(8,128)S(1)}) custom-call(s32[32,3072]{1,0:T(8,128)S(1)} %copy-done.1, f32[32,3328]{1,0:T(8,128)S(1)} %copy-done), custom_call_target="tpu_custom_call" | custom-call | flops 1000000 | bytes 1000000 | tf_op jit(solution)/shard_map/pallas_call | solution.py:284
  21.8 5.6 %collective-permute-done.1.refs_1_ = f32[32,1664]{1,0:T(8,128)S(1)} collective-permute-done((f32[32,1664]{1,0:T(8,128)}, f32[32,1664]{1,0:T(8,128)S(1)}, u32[]{:S(2)}, u32[]{:S(2)}) %collective-permute-start.1) | collective-permute-done | bytes 213024 | tf_op jit(solution)/shard_map/ppermute | solution.py:302
  27.4 4.2 %collective-permute-done.2.refs_0_ = f32[96,1664]{1,0:T(8,128)S(1)} collective-permute-done((f32[96,1664]{1,0:T(8,128)}, f32[96,1664]{1,0:T(8,128)S(1)}, u32[]{:S(2)}, u32[]{:S(2)}) %collective-permute-start.2) | collective-permute-done | bytes 639008 | tf_op jit(solution)/shard_map/ppermute | solution.py:302
  31.6 1.7 %collective-permute-start.6 = (f32[32,1664]{1,0:T(8,128)S(1)}, f32[32,1664]{1,0:T(8,128)S(1)}, u32[]{:S(2)}, u32[]{:S(2)}) collective-permute-start(f32[32,1664]{1,0:T(8,128)S(1)} %slice.36), channel_id=1, source_target_pairs={{0,1},{1,0},{2,3},{3,2},{4,5},{5,4},{6,7},{7,6},{8,9},{9,8},{10,11... | collective-permute-start | bytes 638984 | tf_op jit(solution)/shard_map/ppermute | solution.py:302
  33.7 1.8 %shard_map.96 = (f32[528,512]{1,0:T(8,128)S(1)}, f32[528,512]{1,0:T(8,128)S(1)}) custom-call(f32[96,1664]{1,0:T(8,128)S(1)} %collective-permute-done.2.refs_0_, f32[528,512]{1,0:T(8,128)S(1)} %get-tuple-element.51.refs_1_, f32[528,512]{1,0:T(8,128)S(1)} %get-tuple-element.52.refs_2_), custom_call_target="tpu_custom_call" | custom-call | flops 1000000 | bytes 1000000 | tf_op jit(solution)/shard_map/pallas_call | solution.py:284
  35.6 4.3 %collective-permute-done.6.refs_1_ = f32[32,1664]{1,0:T(8,128)S(1)} collective-permute-done((f32[32,1664]{1,0:T(8,128)S(1)}, f32[32,1664]{1,0:T(8,128)S(1)}, u32[]{:S(2)}, u32[]{:S(2)}) %collective-permute-start.6) | collective-permute-done | bytes 213024 | tf_op jit(solution)/shard_map/ppermute | solution.py:302
  39.9 1.8 %shard_map.97 = (f32[528,512]{1,0:T(8,128)S(1)}, f32[528,512]{1,0:T(8,128)S(1)}) custom-call(f32[96,1664]{1,0:T(8,128)S(1)} %collective-permute-done.2.refs_0_, f32[32,1664]{1,0:T(8,128)S(1)} %collective-permute-done.6.refs_1_, f32[528,512]{1,0:T(8,128)S(1)} %get-tuple-element.53.refs_2_, f32[528,512]{1,0:T(8,128)S(1)} %get-tuple-element.54.refs_3_), custom_call_target="tpu_custom_call" | custom-call | flops 1000000 | bytes 1000000 | tf_op jit(solution)/shard_map/pallas_call | solution.py:284
  41.7 1.8 %shard_map.98 = (f32[528,512]{1,0:T(8,128)S(1)}, f32[528,512]{1,0:T(8,128)S(1)}) custom-call(s32[16,3456]{1,0:T(8,128)S(1)} %collective-permute-done.5.refs_0_, f32[32,1664]{1,0:T(8,128)S(1)} %collective-permute-done.1.refs_1_, f32[528,512]{1,0:T(8,128)S(1)} %get-tuple-element.55.refs_2_, f32[528,512]{1,0:T(8,128)S(1)} %get-tuple-element.56.refs_3_), custom_call_target="tpu_custom_call" | custom-call | flops 1000000 | bytes 1000000 | tf_op jit(solution)/shard_map/pallas_call | solution.py:284
  43.6 1.7 %collective-permute-start.7 = (f32[32,1664]{1,0:T(8,128)S(1)}, f32[32,1664]{1,0:T(8,128)S(1)}, u32[]{:S(2)}, u32[]{:S(2)}) collective-permute-start(f32[32,1664]{1,0:T(8,128)S(1)} %collective-permute-done.3.refs_1_), channel_id=1, source_target_pairs={{0,1},{1,0},{2,3},{3,2},{4,5},{5,4},{6,7},{7,6},{8,9},{9,8},{10,11... | collective-permute-start | bytes 638984 | tf_op jit(solution)/shard_map/ppermute | solution.py:302
  45.3 1.8 %shard_map.99 = (f32[528,512]{1,0:T(8,128)S(1)}, f32[528,512]{1,0:T(8,128)S(1)}) custom-call(s32[16,3456]{1,0:T(8,128)S(1)} %collective-permute-done.5.refs_0_, f32[32,1664]{1,0:T(8,128)S(1)} %collective-permute-done.9.refs_1_.refs_2_, f32[528,512]{1,0:T(8,128)S(1)} %get-tuple-element.61.refs_2_, f32[528,512]{1,0:T(8,128)S(1)} %get-tuple-element.62.refs_3_), custom_call_target="tpu_custom_call" | custom-call | flops 1000000 | bytes 1000000 | tf_op jit(solution)/shard_map/pallas_call | solution.py:284
  47.2 2.0 %shard_map.100 = (f32[528,512]{1,0:T(8,128)S(1)}, f32[528,512]{1,0:T(8,128)S(1)}) custom-call(s32[16,3456]{1,0:T(8,128)S(1)} %collective-permute-done.4.refs_0_, f32[32,1664]{1,0:T(8,128)S(1)} %collective-permute-done.3.refs_1_, f32[528,512]{1,0:T(8,128)S(1)} %get-tuple-element.63.refs_2_, f32[528,512]{1,0:T(8,128)S(1)} %get-tuple-element.64.refs_3_), custom_call_target="tpu_custom_call" | custom-call | flops 1000000 | bytes 1000000 | tf_op jit(solution)/shard_map/pallas_call | solution.py:284
  51.1 3.4 %collective-permute-start.8 = (s32[16,3072]{1,0:T(8,128)S(1)}, s32[16,3072]{1,0:T(8,128)S(1)}, u32[]{:S(2)}, u32[]{:S(2)}) collective-permute-start(s32[16,3072]{1,0:T(8,128)S(1)} %copy-done.7), channel_id=1, source_target_pairs={{0,16},{2,18},{4,20},{6,22},{8,24},{10,26},{12,28},{14,30},{16,0},... | collective-permute-start | bytes 589832 | tf_op jit(solution)/shard_map/ppermute | solution.py:302
  58.6 3.4 %shard_map.103 = (f32[528,512]{1,0:T(8,128)S(1)}, f32[528,512]{1,0:T(8,128)S(1)}) custom-call(f32[96,1664]{1,0:T(8,128)S(1)} %collective-permute-done.2.refs_0_, f32[32,1664]{1,0:T(8,128)S(1)} %collective-permute-done.6.refs_1_, f32[528,512]{1,0:T(8,128)S(1)} %get-tuple-element.68.refs_2_, f32[528,512]{1,0:T(8,128)S(1)} %get-tuple-element.69.refs_3_), custom_call_target="tpu_custom_call" | custom-call | flops 1000000 | bytes 1000000 | tf_op jit(solution)/shard_map/pallas_call | solution.py:284
  62.0 6.6 %collective-permute-done.8.refs_0_ = s32[16,3072]{1,0:T(8,128)S(1)} collective-permute-done((s32[16,3072]{1,0:T(8,128)S(1)}, s32[16,3072]{1,0:T(8,128)S(1)}, u32[]{:S(2)}, u32[]{:S(2)}) %collective-permute-start.8) | collective-permute-done | bytes 196640 | tf_op jit(solution)/shard_map/ppermute | solution.py:302
  68.6 3.5 %shard_map.104 = (f32[528,512]{1,0:T(8,128)S(1)}, f32[528,512]{1,0:T(8,128)S(1)}) custom-call(s32[16,3072]{1,0:T(8,128)S(1)} %collective-permute-done.8.refs_0_, f32[32,1664]{1,0:T(8,128)S(1)} %collective-permute-done.1.refs_1_, f32[32,1664]{1,0:T(8,128)S(1)} %collective-permute-done.9.refs_1_.refs_2_, f32[528,512]{1,0:T(8,128)S(1)} %get-tuple-element.70.refs_3_, ...), custom_call_target="tpu_custom_call" | custom-call | flops 1000000 | bytes 1000000 | tf_op jit(solution)/shard_map/pallas_call | solution.py:284
  72.1 3.5 %shard_map.105 = (f32[528,512]{1,0:T(8,128)S(1)}, f32[528,512]{1,0:T(8,128)S(1)}) custom-call(s32[16,3072]{1,0:T(8,128)S(1)} %collective-permute-done.refs_0_, f32[32,1664]{1,0:T(8,128)S(1)} %collective-permute-done.3.refs_1_, f32[32,1664]{1,0:T(8,128)S(1)} %collective-permute-done.7.refs_1_.refs_2_, f32[528,512]{1,0:T(8,128)S(1)} %get-tuple-element.72.refs_3_, ...), custom_call_target="tpu_custom_call" | custom-call | flops 1000000 | bytes 1000000 | tf_op jit(solution)/shard_map/pallas_call | solution.py:284
  78.5 4.5 %collective-permute-done.13.refs_1_ = f32[528,512]{1,0:T(8,128)S(1)} collective-permute-done((f32[528,512]{1,0:T(8,128)S(1)}, f32[528,512]{1,0:T(8,128)S(1)}, u32[]{:S(2)}, u32[]{:S(2)}) %collective-permute-start.13) | collective-permute-done | bytes 1081376 | tf_op jit(solution)/shard_map/ppermute | solution.py:302
  83.0 2.1 %shard_map.106 = f32[8,8,128]{2,1,0:T(8,128)} custom-call(f32[528,512]{1,0:T(8,128)S(1)} %pad_maximum_fusion.refs_0_, f32[528,512]{1,0:T(8,128)S(1)} %collective-permute-done.13.refs_1_, f32[528,512]{1,0:T(8,128)S(1)} %get-tuple-element.75.refs_2_), custom_call_target="tpu_custom_call" | custom-call | flops 1000000 | bytes 1000000 | tf_op jit(solution)/shard_map/pallas_call | solution.py:437
  86.6 4.8 %all-to-all-start = ((f32[8,8,128]{2,1,0:T(8,128)}), f32[8,8,128]{2,1,0:T(8,128)S(1)}, u32[]{:S(2)}, u32[]{:S(2)}) async-start(f32[8,8,128]{2,1,0:T(8,128)} %shard_map.106), calls=%async_computation | async-start | bytes 65536 | tf_op jit(solution)/shard_map/all_to_all | solution.py:458
  92.7 5.4 %all-to-all-done = f32[8,8,128]{2,1,0:T(8,128)S(1)} async-done(((f32[8,8,128]{2,1,0:T(8,128)}), f32[8,8,128]{2,1,0:T(8,128)S(1)}, u32[]{:S(2)}, u32[]{:S(2)}) %all-to-all-start) | async-done | bytes 32800 | tf_op jit(solution)/shard_map/all_to_all | solution.py:458
  (49 shorter events, 15.1 us)
Async XLA Ops:
  4.6 27.0 %collective-permute-start.2 = (f32[96,1664]{1,0:T(8,128)}, f32[96,1664]{1,0:T(8,128)S(1)}, u32[]{:S(2)}, u32[]{:S(2)}) collective-permute-start(f32[96,1664]{1,0:T(8,128)} %get-tuple-element.43), channel_id=1, source_target_pairs={{0,8},{2,10},{4,12},{6,14},{8,0},{10,2},{12,4},{14,6},{16,24},{18,... | collective-permute-start | bytes 1916936 | tf_op jit(solution)/shard_map/ppermute | solution.py:302
  7.7 19.7 %collective-permute-start.1 = (f32[32,1664]{1,0:T(8,128)}, f32[32,1664]{1,0:T(8,128)S(1)}, u32[]{:S(2)}, u32[]{:S(2)}) collective-permute-start(f32[32,1664]{1,0:T(8,128)} %get-tuple-element.42), channel_id=1, source_target_pairs={{0,16},{2,18},{4,20},{6,22},{8,24},{10,26},{12,28},{14,30},{16,0},... | collective-permute-start | bytes 638984 | tf_op jit(solution)/shard_map/ppermute | solution.py:302
  10.3 31.4 %collective-permute-start.5 = (s32[16,3456]{1,0:T(8,128)}, s32[16,3456]{1,0:T(8,128)S(1)}, u32[]{:S(2)}, u32[]{:S(2)}) collective-permute-start(s32[16,3456]{1,0:T(8,128)} %get-tuple-element.49), channel_id=1, source_target_pairs={{0,16},{2,18},{4,20},{6,22},{8,24},{10,26},{12,28},{14,30},{16,0},... | collective-permute-start | bytes 663560 | tf_op jit(solution)/shard_map/ppermute | solution.py:302
  10.6 32.9 %collective-permute-start.4 = (s32[16,3456]{1,0:T(8,128)}, s32[16,3456]{1,0:T(8,128)S(1)}, u32[]{:S(2)}, u32[]{:S(2)}) collective-permute-start(s32[16,3456]{1,0:T(8,128)} %get-tuple-element.48), channel_id=1, source_target_pairs={{0,24},{2,26},{4,28},{6,30},{8,16},{10,18},{12,20},{14,22},{16,8},... | collective-permute-start | bytes 663560 | tf_op jit(solution)/shard_map/ppermute | solution.py:302
  13.1 1.0 %copy-start = (f32[32,3328]{1,0:T(8,128)S(1)}, f32[32,3328]{1,0:T(8,128)}, u32[]{:S(2)}) copy-start(f32[32,3328]{1,0:T(8,128)} %get-tuple-element.45.refs_1_) | copy-start | bytes 1277956
  14.1 1.0 %copy-start.1 = (s32[32,3072]{1,0:T(8,128)S(1)}, s32[32,3072]{1,0:T(8,128)}, u32[]{:S(2)}) copy-start(s32[32,3072]{1,0:T(8,128)} %get-tuple-element.44.refs_0_) | copy-start | bytes 1179652
  31.6 8.3 %collective-permute-start.6 = (f32[32,1664]{1,0:T(8,128)S(1)}, f32[32,1664]{1,0:T(8,128)S(1)}, u32[]{:S(2)}, u32[]{:S(2)}) collective-permute-start(f32[32,1664]{1,0:T(8,128)S(1)} %slice.36), channel_id=1, source_target_pairs={{0,1},{1,0},{2,3},{3,2},{4,5},{5,4},{6,7},{7,6},{8,9},{9,8},{10,11... | collective-permute-start | bytes 638984 | tf_op jit(solution)/shard_map/ppermute | solution.py:302
  33.3 10.2 %collective-permute-start.3 = (f32[32,1664]{1,0:T(8,128)S(1)}, f32[32,1664]{1,0:T(8,128)S(1)}, u32[]{:S(2)}, u32[]{:S(2)}) collective-permute-start(f32[32,1664]{1,0:T(8,128)S(1)} %collective-permute-done.1.refs_1_), channel_id=1, source_target_pairs={{0,8},{2,10},{4,12},{6,14},{8,0},{10,2},{12,4},{14,6},{16,24},{18,... | collective-permute-start | bytes 638984 | tf_op jit(solution)/shard_map/ppermute | solution.py:302
  33.3 12.0 %collective-permute-start.9 = (f32[32,1664]{1,0:T(8,128)S(1)}, f32[32,1664]{1,0:T(8,128)S(1)}, u32[]{:S(2)}, u32[]{:S(2)}) collective-permute-start(f32[32,1664]{1,0:T(8,128)S(1)} %collective-permute-done.1.refs_1_), channel_id=1, source_target_pairs={{0,1},{1,0},{2,3},{3,2},{4,5},{5,4},{6,7},{7,6},{8,9},{9,8},{10,11... | collective-permute-start | bytes 638984 | tf_op jit(solution)/shard_map/ppermute | solution.py:302
  43.6 6.3 %collective-permute-start.7 = (f32[32,1664]{1,0:T(8,128)S(1)}, f32[32,1664]{1,0:T(8,128)S(1)}, u32[]{:S(2)}, u32[]{:S(2)}) collective-permute-start(f32[32,1664]{1,0:T(8,128)S(1)} %collective-permute-done.3.refs_1_), channel_id=1, source_target_pairs={{0,1},{1,0},{2,3},{3,2},{4,5},{5,4},{6,7},{7,6},{8,9},{9,8},{10,11... | collective-permute-start | bytes 638984 | tf_op jit(solution)/shard_map/ppermute | solution.py:302
  49.9 1.1 %copy-start.7 = (s32[16,3072]{1,0:T(8,128)S(1)}, s32[16,3072]{1,0:T(8,128)}, u32[]{:S(2)}) copy-start(s32[16,3072]{1,0:T(8,128)} %get-tuple-element.59) | copy-start | bytes 589828
  49.9 4.5 %copy-start.6 = (s32[16,3072]{1,0:T(8,128)S(1)}, s32[16,3072]{1,0:T(8,128)}, u32[]{:S(2)}) copy-start(s32[16,3072]{1,0:T(8,128)} %get-tuple-element.41) | copy-start | bytes 589828
  51.0 5.0 %collective-permute-start.10 = (f32[528,512]{1,0:T(8,128)S(1)}, f32[528,512]{1,0:T(8,128)S(1)}, u32[]{:S(2)}, u32[]{:S(2)}) collective-permute-start(f32[528,512]{1,0:T(8,128)S(1)} %shard_map.101), channel_id=1, source_target_pairs={{0,2},{2,0},{4,6},{6,4},{8,10},{10,8},{12,14},{14,12},{16,18},{18,... | collective-permute-start | bytes 3244040 | tf_op jit(solution)/shard_map/ppermute | solution.py:302
  51.1 17.6 %collective-permute-start.8 = (s32[16,3072]{1,0:T(8,128)S(1)}, s32[16,3072]{1,0:T(8,128)S(1)}, u32[]{:S(2)}, u32[]{:S(2)}) collective-permute-start(s32[16,3072]{1,0:T(8,128)S(1)} %copy-done.7), channel_id=1, source_target_pairs={{0,16},{2,18},{4,20},{6,22},{8,24},{10,26},{12,28},{14,30},{16,0},... | collective-permute-start | bytes 589832 | tf_op jit(solution)/shard_map/ppermute | solution.py:302
  54.4 17.6 %collective-permute-start = (s32[16,3072]{1,0:T(8,128)S(1)}, s32[16,3072]{1,0:T(8,128)S(1)}, u32[]{:S(2)}, u32[]{:S(2)}) collective-permute-start(s32[16,3072]{1,0:T(8,128)S(1)} %copy-done.6), channel_id=1, source_target_pairs={{0,24},{2,26},{4,28},{6,30},{8,16},{10,18},{12,20},{14,22},{16,8},... | collective-permute-start | bytes 589832 | tf_op jit(solution)/shard_map/ppermute | solution.py:302
  57.0 26.0 %collective-permute-start.13 = (f32[528,512]{1,0:T(8,128)S(1)}, f32[528,512]{1,0:T(8,128)S(1)}, u32[]{:S(2)}, u32[]{:S(2)}) collective-permute-start(f32[528,512]{1,0:T(8,128)S(1)} %shard_map.102), channel_id=1, source_target_pairs={{0,4},{2,6},{4,0},{6,2},{8,12},{10,14},{12,8},{14,10},{16,20},{18,... | collective-permute-start | bytes 3244040 | tf_op jit(solution)/shard_map/ppermute | solution.py:302
  75.6 2.0 %collective-permute-start.12 = (f32[264,512]{1,0:T(8,128)S(1)}, f32[264,512]{1,0:T(8,128)S(1)}, u32[]{:S(2)}, u32[]{:S(2)}) collective-permute-start(f32[264,512]{1,0:T(8,128)S(1)} %get-tuple-element.79), channel_id=1, source_target_pairs={{0,2},{2,0},{4,6},{6,4},{8,10},{10,8},{12,14},{14,12},{16,18},{18,... | collective-permute-start | bytes 1622024 | tf_op jit(solution)/shard_map/ppermute | solution.py:302
  75.7 2.7 %collective-permute-start.11 = (f32[264,512]{1,0:T(8,128)S(1)}, f32[264,512]{1,0:T(8,128)S(1)}, u32[]{:S(2)}, u32[]{:S(2)}) collective-permute-start(f32[264,512]{1,0:T(8,128)S(1)} %get-tuple-element.80), channel_id=1, source_target_pairs={{0,2},{2,0},{4,6},{6,4},{8,10},{10,8},{12,14},{14,12},{16,18},{18,... | collective-permute-start | bytes 1622024 | tf_op jit(solution)/shard_map/ppermute | solution.py:302
  83.0 2.1 %copy-start.4 = (f32[1,3072]{1,0:T(1,128)S(1)}, f32[1,3072]{1,0:T(1,128)}, u32[]{:S(2)}) copy-start(f32[1,3072]{1,0:T(1,128)} %get-tuple-element.77) | copy-start | bytes 36868
  83.0 8.5 %copy-start.3 = (s32[3072]{0:T(1024)S(1)}, s32[3072]{0:T(1024)}, u32[]{:S(2)}) copy-start(s32[3072]{0:T(1024)} %param.9) | copy-start | bytes 36868
  83.0 8.6 %copy-start.2 = (f32[3072,32]{0,1:T(8,128)S(1)}, f32[3072,32]{0,1:T(8,128)}, u32[]{:S(2)}) copy-start(f32[3072,32]{0,1:T(8,128)} %param.7) | copy-start | bytes 1179652
  85.1 6.3 %collective-permute-start.14 = (f32[32,128]{1,0:T(8,128)S(1)}, f32[32,128]{1,0:T(8,128)S(1)}, u32[]{:S(2)}, u32[]{:S(2)}) collective-permute-start(f32[32,128]{1,0:T(8,128)S(1)} %pad_maximum_fusion.1), channel_id=1, source_target_pairs={{0,1},{1,0},{2,3},{3,2},{4,5},{5,4},{6,7},{7,6},{8,9},{9,8},{10,11... | collective-permute-start | bytes 49160 | tf_op jit(solution)/shard_map/ppermute | solution.py:302
  86.6 11.4 %all-to-all-start = ((f32[8,8,128]{2,1,0:T(8,128)}), f32[8,8,128]{2,1,0:T(8,128)S(1)}, u32[]{:S(2)}, u32[]{:S(2)}) async-start(f32[8,8,128]{2,1,0:T(8,128)} %shard_map.106), calls=%async_computation | async-start | bytes 65536 | tf_op jit(solution)/shard_map/all_to_all | solution.py:458
  91.6 7.1 %copy-start.5 = (f32[8,2,32]{2,1,0:T(2,128)}, f32[8,2,32]{2,1,0:T(2,128)S(1)}, u32[]{:S(2)}) copy-start(f32[8,2,32]{2,1,0:T(2,128)S(1)} %fusion.5) | copy-start | bytes 6148
